TPU v7x, 32 devices: a whole 2x2x4 slice. The times are simulated.
32 devices in a mesh: lon: 16 (over z, y, core), lat: 2 (over x).
Axes of the slice: x: 2, y: 2, z: 4, core: 2. Of those that a mesh axis runs over, the one named last changes fastest.
Arguments:
- field_in: bfloat16 [4, 24, 36864], P(None, 'lat', 'lon'), may hold values from -6 to 6
- norm1_gain: float32 [192], replicated, may hold values from 0.25 to 1.75
- qkv_weight: bfloat16 [192, 576], replicated, may hold values from -0.4375 to 0.4375
- proj_weight: bfloat16 [192, 192], replicated, may hold values from -0.4375 to 0.4375
- earth_bias: float32 [4, 2, 6, 20736], P('lat'), may hold values from -4 to 320, as said below
- norm2_gain: float32 [192], replicated, may hold values from 0.25 to 1.75
- fc1_weight: bfloat16 [192, 768], replicated, may hold values from -0.4375 to 0.4375
- fc2_weight: bfloat16 [768, 192], replicated, may hold values from -0.21875 to 0.21875
Outputs:
- block_out: bfloat16 [4, 24, 36864], P(None, 'lat', 'lon')
Inputs may be any that keep to these rules, and one draw needn't show every extreme that they name: `earth_bias`: bias table entries.
All inputs are finite; a program needn't handle non-finite values.
Results may differ from a plain program's by a relative error of at most 0.014.
Values may be sent and summed in bfloat16 or wider, within the bound.
No kernel may reach another device: no remote copies, remote signals or barrier semaphores. Data moves between devices by JAX's collectives and lax.ppermute only.
A program may use at most 128 MiB of HBM per device.

v0:
```python
import jax
import jax.numpy as jnp
from jax import lax
from jax.sharding import PartitionSpec as P

WIN_LEV = 2
WIN_LAT = 6
WIN_LON = 12


def shifted(x, axis, by):
    devices = lax.axis_size(axis)
    return lax.ppermute(x, axis, [(i, (i + by) % devices) for i in range(devices)])


def row_regions(orig, total):
    tail = 2
    edge = WIN_LAT // 2
    return jnp.where(
        orig < 0,
        3,
        jnp.where(
            orig < edge, 2, jnp.where(orig < total - edge, 0, jnp.where(orig < total, 1, tail))
        ),
    )


def level_regions(levels):
    place = jnp.arange(levels)
    return jnp.where(place < levels - 2, 0, jnp.where(place == levels - 2, 1, 2))


def layer_norm(values, gain):
    center = values - jnp.mean(values, axis=-1, keepdims=True)
    spread = jnp.mean(center * center, axis=-1, keepdims=True)
    return center * lax.rsqrt(spread + 1e-05) * gain


def attend(tile, gain, qkv_weight, proj_weight, bias_types, level_lab, row_lab):
    levels, rows, flat = tile.shape
    chans = qkv_weight.shape[0]
    cols = flat // chans
    heads = bias_types.shape[2]
    head_dim = chans // heads
    zwin = levels // WIN_LEV
    rwin = rows // WIN_LAT
    cwin = cols // WIN_LON
    tokens = WIN_LEV * WIN_LAT * WIN_LON
    grid = tile.reshape(zwin, WIN_LEV, rwin, WIN_LAT, cwin, WIN_LON, chans)
    windows = grid.transpose(0, 2, 4, 1, 3, 5, 6).reshape(-1, chans)
    normed = layer_norm(windows.astype(jnp.float32), gain).astype(jnp.bfloat16)
    qkv = jnp.dot(normed, qkv_weight, preferred_element_type=jnp.float32).astype(jnp.bfloat16)
    qkv = qkv.reshape(zwin, rwin, cwin, tokens, 3, heads, head_dim)
    query = qkv[:, :, :, :, 0]
    keys = qkv[:, :, :, :, 1]
    values = qkv[:, :, :, :, 2]
    scores = jnp.einsum(
        "abcqhd,abckhd->bachqk", query, keys, preferred_element_type=jnp.float32
    ) * head_dim ** (-0.5)
    table = bias_types.reshape(rwin, zwin, heads, tokens, tokens)
    scores = scores + table[:, :, None]
    zlab = level_lab.reshape(zwin, WIN_LEV)
    rlab = row_lab.reshape(rwin, WIN_LAT)
    label = (
        zlab[None, :, :, None, None] * 8
        + rlab[:, None, None, :, None]
        + jnp.zeros((1, 1, 1, 1, WIN_LON), jnp.int32)
    )
    label = label.reshape(rwin, zwin, tokens)
    allowed = label[:, :, :, None] == label[:, :, None, :]
    scores = jnp.where(allowed[:, :, None, None], scores, -1000000000.0)
    probs = jax.nn.softmax(scores, axis=-1).astype(jnp.bfloat16)
    mixed = jnp.einsum("bachqk,abckhd->abcqhd", probs, values, preferred_element_type=jnp.float32)
    mixed = mixed.astype(jnp.bfloat16).reshape(-1, chans)
    proj = jnp.dot(mixed, proj_weight, preferred_element_type=jnp.float32).astype(jnp.bfloat16)
    back = proj.reshape(zwin, rwin, cwin, WIN_LEV, WIN_LAT, WIN_LON, chans).transpose(
        0, 3, 1, 4, 2, 5, 6
    )
    return back.reshape(levels, rows, flat)


def finish(tile, attn, gain, fc1_weight, fc2_weight):
    chans = fc1_weight.shape[0]
    resid = (tile.astype(jnp.float32) + attn.astype(jnp.float32)).astype(jnp.bfloat16)
    resid = lax.optimization_barrier(resid).reshape(-1, chans)
    normed = layer_norm(resid.astype(jnp.float32), gain).astype(jnp.bfloat16)
    hidden = jax.nn.gelu(jnp.dot(normed, fc1_weight, preferred_element_type=jnp.float32)).astype(
        jnp.bfloat16
    )
    result = resid.astype(jnp.float32) + jnp.dot(
        hidden, fc2_weight, preferred_element_type=jnp.float32
    )
    return result.astype(jnp.bfloat16).reshape(tile.shape)


def shards(
    field_in, norm1_gain, qkv_weight, proj_weight, earth_bias, norm2_gain, fc1_weight, fc2_weight
):
    levels, rows, flat = field_in.shape
    chans = qkv_weight.shape[0]
    half_lanes = WIN_LON // 2 * chans
    edge = WIN_LAT // 2
    total_rows = rows * lax.axis_size("lat")
    lat_place = lax.axis_index("lat")
    level_lab = level_regions(levels)
    incoming = shifted(field_in[:, :, :half_lanes], "lon", -1)
    tile = jnp.concatenate([field_in[:, :, half_lanes:], incoming], axis=2)
    above = shifted(tile[:, :edge], "lat", -1)
    tile = jnp.concatenate([tile[:, edge:], above], axis=1)
    tile = jnp.roll(tile, -1, axis=0)
    orig = lat_place * rows + edge + jnp.arange(rows)
    row_lab = row_regions(orig, total_rows)
    attn = attend(tile, norm1_gain, qkv_weight, proj_weight, earth_bias, level_lab, row_lab)
    done = jnp.roll(finish(tile, attn, norm2_gain, fc1_weight, fc2_weight), 1, axis=0)
    below = shifted(done[:, rows - edge :], "lat", 1)
    done = jnp.concatenate([below, done[:, : rows - edge]], axis=1)
    western = shifted(done[:, :, flat - half_lanes :], "lon", 1)
    return jnp.concatenate([western, done[:, :, : flat - half_lanes]], axis=2)


def solution(mesh):
    in_specs = (P(None, "lat", "lon"), P(), P(), P(), P("lat", None, None, None), P(), P(), P())
    out_specs = P(None, "lat", "lon")
    return jax.shard_map(shards, mesh=mesh, in_specs=in_specs, out_specs=out_specs, check_vma=False)
```

profile of v0, /device:TPU:0, one launch (start us, length us, event | category | flops | bytes accessed | tf_op | source)
XLA Modules:
  0.0 52.9 jit_solution(10645261376603028957)
XLA Ops:
  0.0 0.0 copy-start
  0.0 1.1 %fusion.45 = (bf16[4,12,1152]{2,0,1:T(4,128)(2,1)S(1)}, bf16[4,12,1152]{2,0,1:T(4,128)(2,1)S(1)}) fusion(bf16[4,12,2304]{2,0,1:T(4,128)(2,1)} %param.8), kind=kLoop, calls=%fused_computation.75 | loop fusion | bytes 442368 | tf_op jit(solution)/shard_map/slice | solution.py:107
  1.1 5.5 %collective-permute-start = (bf16[4,12,1152]{2,0,1:T(4,128)(2,1)S(1)}, bf16[4,12,1152]{2,0,1:T(4,128)(2,1)S(1)}, u32[]{:S(2)}, u32[]{:S(2)}) collective-permute-start(bf16[4,12,1152]{2,0,1:T(4,128)(2,1)S(1)} %get-tuple-element.9), channel_id=1, source_target_pairs={{0,30},{2,0},{4,2},{6,4},{8,6},{10,8},{12,10},{14,12},{16,14},{18,... | collective-permute-start | bytes 331784 | tf_op jit(solution)/shard_map/ppermute | solution.py:13
  6.6 0.1 broadcast_add_fusion
  6.7 0.1 add.90
  6.7 0.1 eq.28
  6.8 0.8 %broadcast_compare_fusion = pred[2,2,144,144]{2,3,1,0:T(8,128)(4,1)} fusion(s32[2,2,144]{2,1,0:T(2,128)S(1)} %eq.28), kind=kLoop, calls=%fused_computation.42 | loop fusion | flops 82944 | bytes 85248 | tf_op jit(solution)/shard_map/eq | solution.py:70
  7.7 5.2 %broadcast_in_dim_reshape.2 = f32[2,2,6,144,144]{4,3,1,2,0:T(8,128)} reshape(f32[2,2,6,20736]{3,1,2,0:T(2,128)} %param.12) | data formatting | bytes 3981312 | tf_op jit(solution)/shard_map/broadcast_in_dim;reshape | solution.py:61
  12.8 5.6 %copy.37 = f32[2,2,6,144,144]{3,4,2,1,0:T(8,128)} copy(f32[2,2,6,144,144]{4,3,1,2,0:T(8,128)} %broadcast_in_dim_reshape.2) | data formatting | bytes 3981312 | tf_op jit(solution)/shard_map/broadcast_in_dim;reshape | solution.py:61
  18.4 0.0 collective-permute-done
  18.5 1.6 %collective-permute-start.1 = (bf16[4,3,2304]{2,0,1:T(4,128)(2,1)S(1)}, bf16[4,3,2304]{2,0,1:T(4,128)(2,1)S(1)}, u32[]{:S(2)}, u32[]{:S(2)}) collective-permute-start(bf16[4,3,2304]{2,0,1:T(4,128)(2,1)S(1)} %pad_maximum_fusion.2), channel_id=1, source_target_pairs={{0,1},{1,0},{2,3},{3,2},{4,5},{5,4},{6,7},{7,6},{8,9},{9,8},{10,11... | collective-permute-start | bytes 165896 | tf_op jit(solution)/shard_map/ppermute | solution.py:13
  20.0 0.1 fusion.37
  20.1 2.6 %collective-permute-done.1 = bf16[4,3,2304]{2,0,1:T(4,128)(2,1)S(1)} collective-permute-done((bf16[4,3,2304]{2,0,1:T(4,128)(2,1)S(1)}, bf16[4,3,2304]{2,0,1:T(4,128)(2,1)S(1)}, u32[]{:S(2)}, u32[]{:S(2)}) %collective-permute-start.1) | collective-permute-done | bytes 55328 | tf_op jit(solution)/shard_map/ppermute | solution.py:13
  22.7 0.2 slice_maximum_fusion
  22.9 0.2 fusion.36
  23.1 0.4 reshape.166
  23.5 0.2 bitcast_reduce_fusion
  23.7 0.0 copy-start.1
  23.7 0.0 copy-start.4
  23.8 0.4 multiply_reduce_fusion
  24.2 0.1 rsqrt.20
  24.3 0.1 div.24
  24.4 0.1 copy.30
  24.5 0.1 reshape.162
  24.5 0.1 copy-done.1
  24.7 0.0 copy-done.4
  24.7 0.5 convolution_convert_fusion
  25.2 0.4 copy.33
  25.6 0.8 %reshape.157 = bf16[2,2,1,144,3,6,32]{3,1,0,6,5,4,2:T(2,128)(2,1)S(1)} reshape(bf16[576,576]{0,1:T(8,128)(2,1)S(1)} %copy.33) | data formatting | bytes 1327104 | tf_op jit(solution)/shard_map/reshape | solution.py:53
  26.3 0.0 copy-start.2
  26.4 1.0 %fusion.44 = (bf16[2,2,1,144,1,6,32]{3,1,0,6,5,4,2:T(2,128)(2,1)S(1)}, bf16[2,2,1,144,1,6,32]{3,1,0,6,5,4,2:T(2,128)(2,1)S(1)}, bf16[2,2,1,144,1,6,32]{3,1,0,6,5,4,2:T(2,128)(2,1)S(1)}) fusion(bf16[2,2,1,144,3,6,32]{3,1,0,6,5,4,2:T(2,128)(2,1)S(1)} %reshape.157), kind=kLoop, calls=%fused_computation.74 | loop fusion | bytes 1327104 | tf_op jit(solution)/shard_map/slice | solution.py:56
  27.4 0.0 copy-done.2
  27.4 5.4 %fusion.46 = (f32[2,2,6,144]{3,2,1,0:T(8,128)S(1)}, f32[2,2,6,144,144]{3,4,2,1,0:T(8,128)}) fusion(f32[2,2,6,144,144]{3,4,2,1,0:T(8,128)} %copy.37, pred[2,2,144,144]{2,3,1,0:T(8,128)(4,1)S(1)} %copy-done.2, bf16[2,2,1,144,1,6,32]{3,1,0,6,5,4,2:T(2,128)(2,1)S(1)} %get-tuple-element.6, bf16[2,2,1,144,1,6,32]{3,1,0,6,5,4,2:T(2,128)(2,1)S(1)} %get-tuple-element.7), kind=kOutput, calls=%fused_computation.76 | convolution fusion | flops 34338960 | bytes 4520448 | tf_op jit(solution)/shard_map/sub | solution.py:72
  32.8 2.4 %fusion.16 = bf16[2,2,1,144,6,32]{3,5,4,1,0,2:T(8,128)(2,1)S(1)} fusion(bf16[2,2,1,144,1,6,32]{3,1,0,6,5,4,2:T(2,128)(2,1)S(1)} %get-tuple-element.5, f32[2,2,6,144,144]{3,4,2,1,0:T(8,128)} %get-tuple-element.11, f32[2,2,6,144]{3,2,1,0:T(8,128)S(1)} %get-tuple-element.10), kind=kOutput, calls=%fused_computation.19 | convolution fusion | flops 32956416 | bytes 2446848 | tf_op jit(solution)/shard_map/bachqk,abckhd->abcqhd/dot_general | solution.py:73
  35.2 0.4 copy.39
  35.6 0.2 reshape.161
  35.8 0.0 copy-done.3
  35.9 0.3 fusion.20
  36.1 0.2 copy.40
  36.4 0.1 reshape.167
  36.4 0.1 copy.41
  36.5 0.4 reshape.163
  36.9 0.3 add_convert_fusion
  37.2 0.0 copy-start.5
  37.2 0.0 copy-start.6
  37.2 0.3 reshape.164
  37.6 0.2 copy.43
  37.8 0.2 reduce_sum.48
  38.0 0.3 multiply_reduce_fusion.1
  38.3 0.0 copy-done
  38.3 0.0 copy-done.5
  38.3 1.0 %fusion.19 = bf16[576,192]{0,1:T(8,128)(2,1)S(1)} fusion(f32[576,192]{0,1:T(8,128)S(1)} %copy.43, bf16[768,192]{0,1:T(8,128)(2,1)S(1)} %copy-done, bf16[192,768]{1,0:T(8,128)(2,1)S(1)} %copy-done.5, f32[576,192]{1,0:T(8,128)S(1)} %reshape.164, f32[192]{0:T(256)S(1)} %copy-done.6, f32[576]{0:T(1024)S(1)} %add_rsqrt_fusion.1, ...), kind=kOutput, calls=%fused_computation.20 | convolution fusion | flops 344383488 | bytes 1701120 | tf_op jit(solution)/shard_map/dot_general | solution.py:90
  39.3 0.1 slice.79
  39.5 0.1 copy.44
  39.6 0.1 slice.65
  39.7 0.1 copy.45
  39.8 0.3 slice.67
  40.2 1.6 %collective-permute-start.2 = (bf16[4,3,2304]{2,1,0:T(4,128)(2,1)S(1)}, bf16[4,3,2304]{2,1,0:T(4,128)(2,1)S(1)}, u32[]{:S(2)}, u32[]{:S(2)}) collective-permute-start(bf16[4,3,2304]{2,1,0:T(4,128)(2,1)S(1)} %slice.81), channel_id=1, source_target_pairs={{0,1},{1,0},{2,3},{3,2},{4,5},{5,4},{6,7},{7,6},{8,9},{9,8},{10,11... | collective-permute-start | bytes 165896 | tf_op jit(solution)/shard_map/ppermute | solution.py:13
  41.8 2.9 %collective-permute-done.2 = bf16[4,3,2304]{2,1,0:T(4,128)(2,1)S(1)} collective-permute-done((bf16[4,3,2304]{2,1,0:T(4,128)(2,1)S(1)}, bf16[4,3,2304]{2,1,0:T(4,128)(2,1)S(1)}, u32[]{:S(2)}, u32[]{:S(2)}) %collective-permute-start.2) | collective-permute-done | bytes 55328 | tf_op jit(solution)/shard_map/ppermute | solution.py:13
  44.6 0.1 fusion.38
  44.7 0.1 collective-permute-start.3
  44.7 7.3 %collective-permute-done.3 = bf16[4,12,1152]{2,1,0:T(8,128)(2,1)S(1)} collective-permute-done((bf16[4,12,1152]{2,1,0:T(8,128)(2,1)S(1)}, bf16[4,12,1152]{2,1,0:T(8,128)(2,1)S(1)}, u32[]{:S(2)}, u32[]{:S(2)}) %collective-permute-start.3) | collective-permute-done | bytes 110624 | tf_op jit(solution)/shard_map/ppermute | solution.py:13
  52.0 0.1 fusion.25
  52.1 0.8 %copy.46 = bf16[4,12,2304]{2,0,1:T(4,128)(2,1)} copy(bf16[4,12,2304]{2,1,0:T(8,128)(2,1)S(1)} %fusion.25) | data formatting | bytes 442368 | tf_op jit(solution)/shard_map/concatenate | solution.py:118
  (16 shorter events, 0.2 us)
Async XLA Ops:
  0.0 38.3 %copy-start = (bf16[768,192]{0,1:T(8,128)(2,1)S(1)}, bf16[768,192]{0,1:T(8,128)(2,1)}, u32[]{:S(2)}) copy-start(bf16[768,192]{0,1:T(8,128)(2,1)} %param.15) | copy-start | bytes 884740
  1.1 17.3 %collective-permute-start = (bf16[4,12,1152]{2,0,1:T(4,128)(2,1)S(1)}, bf16[4,12,1152]{2,0,1:T(4,128)(2,1)S(1)}, u32[]{:S(2)}, u32[]{:S(2)}) collective-permute-start(bf16[4,12,1152]{2,0,1:T(4,128)(2,1)S(1)} %get-tuple-element.9), channel_id=1, source_target_pairs={{0,30},{2,0},{4,2},{6,4},{8,6},{10,8},{12,10},{14,12},{16,14},{18,... | collective-permute-start | bytes 331784 | tf_op jit(solution)/shard_map/ppermute | solution.py:13
  18.5 4.2 %collective-permute-start.1 = (bf16[4,3,2304]{2,0,1:T(4,128)(2,1)S(1)}, bf16[4,3,2304]{2,0,1:T(4,128)(2,1)S(1)}, u32[]{:S(2)}, u32[]{:S(2)}) collective-permute-start(bf16[4,3,2304]{2,0,1:T(4,128)(2,1)S(1)} %pad_maximum_fusion.2), channel_id=1, source_target_pairs={{0,1},{1,0},{2,3},{3,2},{4,5},{5,4},{6,7},{7,6},{8,9},{9,8},{10,11... | collective-permute-start | bytes 165896 | tf_op jit(solution)/shard_map/ppermute | solution.py:13
  23.7 0.9 %copy-start.1 = (bf16[192,576]{1,0:T(8,128)(2,1)S(1)}, bf16[192,576]{1,0:T(8,128)(2,1)}, u32[]{:S(2)}) copy-start(bf16[192,576]{1,0:T(8,128)(2,1)} %param.10) | copy-start | bytes 663556
  23.7 0.9 %copy-start.4 = (f32[192]{0:T(256)S(1)}, f32[192]{0:T(256)}, u32[]{:S(2)}) copy-start(f32[192]{0:T(256)} %param.9) | copy-start | bytes 2308
  26.3 1.0 %copy-start.2 = (pred[2,2,144,144]{2,3,1,0:T(8,128)(4,1)S(1)}, pred[2,2,144,144]{2,3,1,0:T(8,128)(4,1)}, u32[]{:S(2)}) copy-start(pred[2,2,144,144]{2,3,1,0:T(8,128)(4,1)} %broadcast_compare_fusion) | copy-start | bytes 248836
  32.8 3.1 %copy-start.3 = (bf16[192,192]{1,0:T(8,128)(2,1)S(1)}, bf16[192,192]{1,0:T(8,128)(2,1)}, u32[]{:S(2)}) copy-start(bf16[192,192]{1,0:T(8,128)(2,1)} %param.11) | copy-start | bytes 221188
  37.2 1.1 %copy-start.5 = (bf16[192,768]{1,0:T(8,128)(2,1)S(1)}, bf16[192,768]{1,0:T(8,128)(2,1)}, u32[]{:S(2)}) copy-start(bf16[192,768]{1,0:T(8,128)(2,1)} %param.14) | copy-start | bytes 884740
  37.2 1.1 %copy-start.6 = (f32[192]{0:T(256)S(1)}, f32[192]{0:T(256)}, u32[]{:S(2)}) copy-start(f32[192]{0:T(256)} %param.13) | copy-start | bytes 2308
  40.2 4.4 %collective-permute-start.2 = (bf16[4,3,2304]{2,1,0:T(4,128)(2,1)S(1)}, bf16[4,3,2304]{2,1,0:T(4,128)(2,1)S(1)}, u32[]{:S(2)}, u32[]{:S(2)}) collective-permute-start(bf16[4,3,2304]{2,1,0:T(4,128)(2,1)S(1)} %slice.81), channel_id=1, source_target_pairs={{0,1},{1,0},{2,3},{3,2},{4,5},{5,4},{6,7},{7,6},{8,9},{9,8},{10,11... | collective-permute-start | bytes 165896 | tf_op jit(solution)/shard_map/ppermute | solution.py:13
  44.7 7.3 %collective-permute-start.3 = (bf16[4,12,1152]{2,1,0:T(8,128)(2,1)S(1)}, bf16[4,12,1152]{2,1,0:T(8,128)(2,1)S(1)}, u32[]{:S(2)}, u32[]{:S(2)}) collective-permute-start(bf16[4,12,1152]{2,1,0:T(8,128)(2,1)S(1)} %fusion.38), channel_id=1, source_target_pairs={{0,2},{2,4},{4,6},{6,8},{8,10},{10,12},{12,14},{14,16},{16,18},{18... | collective-permute-start | bytes 331784 | tf_op jit(solution)/shard_map/ppermute | solution.py:13
where the time goes:
time: 53.1 us; the launch traced here: 52.9 us
  local copies, waits for them, and re-layouts  18.6 us (35%)
  waiting for transfers between devices  12.7 us (24%)
  matrix products  9.59 us (18%)
  starting transfers between devices  8.67 us (16%)
  other arithmetic  2.9 us (5%)
    ppermute x4, waiting for transfers between devices, shifted(): lax.ppermute(x, axis, [(i, (i + by) % devices) for i in range(devices)])  12.7 us
    another operation x2, local copies, waits for them, and re-layouts, attend(): scores = scores + table[:, :, None]  10.8 us
    ppermute x4, starting transfers between devices, shifted(): lax.ppermute(x, axis, [(i, (i + by) % devices) for i in range(devices)])  8.67 us
    sub x1, matrix products, attend(): probs = jax.nn.softmax(scores, axis=-1).astype(jnp.bfloat16)  5.37 us
    dot_general x1, matrix products, attend(): jnp.einsum('bachqk,abckhd->abcqhd', probs, values, preferred_element_type...  2.39 us
    slice x1, local copies, waits for them, and re-layouts, shards(): tile = jnp.concatenate([field_in[:, :, half_lanes:], incoming], axis=2)  1.07 us
  transfers between devices with their start and end apart: 4, of which 3 were waited for; matrix products, arithmetic and copies ran while one was open for 23% of the time, Pallas kernels for 0%

commit v1 on v0

v1 whole, which is shorter than its diff:
```python
import functools

import jax
import jax.numpy as jnp
from jax import lax
from jax.experimental import pallas as pl
from jax.experimental.pallas import tpu as pltpu
from jax.sharding import PartitionSpec as P

LEVELS = 4
WIN_LEV = 2
WIN_LAT = 6
WIN_LON = 12
EDGE = WIN_LAT // 2
HALF = WIN_LON // 2
TOKENS = WIN_LEV * WIN_LAT * WIN_LON
QUERIES = TOKENS // 2
LOG2E = 1.4426950408889634
LANES = 128
SPARE = 64
NT = (((1,), (1,)), ((), ()))


def moved(x, lat_by, lon_by):
    lats, lons = lax.axis_size("lat"), lax.axis_size("lon")
    if lat_by == 0:
        return lax.ppermute(x, "lon", [(i, (i + lon_by) % lons) for i in range(lons)])
    if lon_by == 0:
        return lax.ppermute(x, "lat", [(i, (i + lat_by) % lats) for i in range(lats)])
    pairs = [
        (b * lats + a, (b + lon_by) % lons * lats + (a + lat_by) % lats)
        for b in range(lons)
        for a in range(lats)
    ]
    return lax.ppermute(x, ("lon", "lat"), pairs)


def table_kernel(last_ref, bias_ref, table_ref):
    heads = bias_ref.shape[2]
    width = 9 * LANES
    lane = lax.broadcasted_iota(jnp.int32, (1, LANES), 1)
    last = jnp.where(last_ref[0] > 0, -1e9, 0.0).astype(jnp.float32)

    def penalty(first, lev, side, wrap):
        key = lane + first
        key_lev = (key >= QUERIES).astype(jnp.int32)
        key_side = ((key - key_lev * QUERIES) >= QUERIES // 2).astype(jnp.int32)
        out = jnp.zeros((1, LANES), jnp.float32)
        if lev is not None:
            out = jnp.where(key_lev != lev, -1e9, out)
        if wrap:
            out = out + jnp.where(key_side != side, last, 0.0)
        return out

    for k in range(2):
        for p in range(2):
            masks = {}
            for lev in range(2):
                for side in range(2):
                    masks[lev, side] = [
                        penalty(first, lev if p == 1 else None, side, k == 1)
                        for first in (0, LANES)
                    ]
            for c in range(TOKENS // 8):
                tiles = [
                    bias_ref[k, p, :, c * width + u * LANES : c * width + (u + 1) * LANES]
                    for u in range(9)
                ]
                for r in range(8):
                    i = 8 * c + r
                    shift = 16 * r
                    nxt = tiles[r + 1]
                    main = tiles[r]
                    if r:
                        main = pltpu.roll(main, LANES - shift, 1)
                        nxt = pltpu.roll(nxt, LANES - shift, 1)
                        main = jnp.where(lane < LANES - shift, main, nxt)
                    lev = i // QUERIES
                    row = i % QUERIES // WIN_LON
                    col = i % WIN_LON
                    side = col // HALF
                    place = lev * 36 + row * HALF + col % HALF
                    mask = masks[lev, row // EDGE]
                    at = pl.ds(place, heads, stride=QUERIES)
                    table_ref[k, p, 1 - side, 0, at, :] = main * LOG2E + mask[0]
                    table_ref[k, p, 1 - side, 1, at, :] = nxt * LOG2E + mask[1]


def layer_norm(values, gain):
    center = values - jnp.mean(values, axis=-1, keepdims=True)
    spread = jnp.mean(center * center, axis=-1, keepdims=True)
    return center * lax.rsqrt(spread + 1e-05) * gain


def block_kernel(
    chans,
    heads,
    own_a,
    own_b,
    west_a,
    west_b,
    east_a,
    east_b,
    gain1_ref,
    wq_ref,
    wk_ref,
    wv_ref,
    proj_ref,
    table_ref,
    gain2_ref,
    fc1_ref,
    fc2_ref,
    out_ref,
    keys_ref,
    own_ref,
    res_ref,
):
    head_dim = chans // heads
    low = lax.broadcasted_iota(jnp.int32, (1, LANES), 1) < SPARE

    def tokens_of(ref, side, first, count):
        both = [ref[side, part, first : first + count] for part in range(2)]
        return jnp.concatenate([both[0], both[1][:, : chans - LANES]], axis=1)

    def fill(ref, row, col, cols):
        for pair in range(cols // 2):
            both = ref[row, :, pair * 2 * chans : (pair + 1) * 2 * chans].astype(jnp.float32)
            first, middle, final = (both[:, u * LANES : (u + 1) * LANES] for u in range(3))
            yield col + 2 * pair, (first, middle)
            middle, final = pltpu.roll(middle, SPARE, 1), pltpu.roll(final, SPARE, 1)
            yield col + 2 * pair + 1, (jnp.where(low, middle, final), final)

    for row in range(WIN_LAT):
        own, west, east = ((own_a, west_a, east_a), (own_b, west_b, east_b))[row // EDGE]
        r = row % EDGE
        blocks = list(fill(west, r, 0, HALF)) + list(fill(own, r, HALF, WIN_LON))
        blocks += list(fill(east, r, HALF + WIN_LON, HALF))
        for col, block in blocks:
            side = col // WIN_LON
            for part in range(2):
                at = pl.ds(row * WIN_LON + col % WIN_LON, LEVELS, stride=QUERIES)
                keys_ref[side, part, at, :] = block[part]
            mine = col - HALF
            if 0 <= mine < WIN_LON:
                side = mine // HALF
                place = row * HALF + mine % HALF
                for part in range(2):
                    own_ref[side, part, pl.ds(4 + place, LEVELS, stride=36), :] = block[part]
                    own_ref[side, part, pl.ds(148 + place, 1), :] = block[part][:1]

    gain1 = gain1_ref[...]
    lane = lax.broadcasted_iota(jnp.int32, (1, chans), 1)
    ones = (lax.broadcasted_iota(jnp.int32, (1, 2 * LANES), 1) == chans).astype(jnp.float32)
    mixed = []
    for side in range(2):
        normed = layer_norm(tokens_of(keys_ref, side, 0, LEVELS * QUERIES), gain1)
        normed = jnp.concatenate([normed[QUERIES:], normed[:QUERIES]], axis=0)
        normed = normed.astype(jnp.bfloat16)
        keys = jnp.dot(normed, wk_ref[...], preferred_element_type=jnp.float32)
        values = jnp.dot(normed, wv_ref[...], preferred_element_type=jnp.float32) + ones
        own = layer_norm(tokens_of(own_ref, side, 40, 144), gain1).astype(jnp.bfloat16)
        query = jnp.dot(own, wq_ref[...], preferred_element_type=jnp.float32)
        query = query * (head_dim ** (-0.5) * LOG2E)
        for p in range(2):
            q = query[p * QUERIES : (p + 1) * QUERIES]
            k = keys[p * TOKENS : (p + 1) * TOKENS].astype(jnp.bfloat16)
            v = values[p * TOKENS : (p + 1) * TOKENS].astype(jnp.bfloat16)
            picked = [
                jnp.where((lane >= h * head_dim) & (lane < (h + 1) * head_dim), q, 0.0)
                for h in range(heads)
            ]
            picked = jnp.concatenate(picked, axis=0).astype(jnp.bfloat16)
            scores = lax.dot_general(picked, k, NT, preferred_element_type=jnp.float32)
            bias = table_ref[0, p, side]
            scores = scores + jnp.concatenate([bias[0], bias[1, :, : TOKENS - LANES]], axis=1)
            top = jnp.max(scores, axis=1, keepdims=True)
            probs = jnp.exp2(scores - top).astype(jnp.bfloat16)
            got = jnp.dot(probs, v, preferred_element_type=jnp.float32)
            out = jnp.zeros((QUERIES, chans), jnp.float32)
            for h in range(heads):
                part = got[h * QUERIES : (h + 1) * QUERIES]
                scaled = part[:, :chans] * (1.0 / part[:, chans : chans + 1])
                inside = (lane >= h * head_dim) & (lane < (h + 1) * head_dim)
                out = jnp.where(inside, scaled, out)
            mixed.append(out)
    mixed = jnp.concatenate(mixed, axis=0).astype(jnp.bfloat16)
    attn = jnp.dot(mixed, proj_ref[...], preferred_element_type=jnp.float32)
    attn = attn.astype(jnp.bfloat16).astype(jnp.float32)
    resid = jnp.concatenate([tokens_of(own_ref, side, 40, 144) for side in range(2)], axis=0) + attn
    resid = resid.astype(jnp.bfloat16).astype(jnp.float32)
    normed = layer_norm(resid, gain2_ref[...]).astype(jnp.bfloat16)
    hidden = jnp.dot(normed, fc1_ref[...], preferred_element_type=jnp.float32)
    hidden = jax.nn.gelu(hidden).astype(jnp.bfloat16)
    result = resid + jnp.dot(hidden, fc2_ref[...], preferred_element_type=jnp.float32)
    for side in range(2):
        mine = result[side * 144 : (side + 1) * 144]
        for part, lanes in enumerate((slice(0, LANES), slice(LANES, chans))):
            width = min(LANES, chans - part * LANES)
            res_ref[side, part, 40:184, :width] = mine[:, lanes]
            res_ref[side, part, 0:40, :width] = mine[104:144, lanes]
    for row in range(WIN_LAT):
        for pair in range(WIN_LON // 2):
            tiles = []
            for col in (2 * pair, 2 * pair + 1):
                at = pl.ds(4 + row * HALF + col % HALF, LEVELS, stride=36)
                tiles += [res_ref[col // HALF, part, at, :] for part in range(2)]
            shifted = [pltpu.roll(x, SPARE, 1) for x in tiles[2:]]
            tiles = [tiles[0], jnp.where(low, tiles[1], shifted[0])]
            tiles.append(jnp.where(low, shifted[0], shifted[1]))
            tiles = jnp.concatenate(tiles, axis=1).astype(jnp.bfloat16)
            out_ref[row, :, pair * 2 * chans : (pair + 1) * 2 * chans] = tiles


def rows_of(ref_rows, at):
    shape = (EDGE,) + ref_rows.shape[1:]
    return pl.BlockSpec(shape, lambda _: (at, 0, 0))


def whole(x):
    return pl.BlockSpec(x.shape, lambda _: (0,) * x.ndim)


def run_block(pieces, table, at, weights, chans, heads):
    arrays = [x for x, _ in pieces]
    specs = [rows_of(x, where) for x, where in pieces]
    gain1, wq, wk, wv, proj, gain2, fc1, fc2 = weights
    table_spec = pl.BlockSpec((1,) + table.shape[1:], lambda _: (at, 0, 0, 0, 0, 0))
    before, after = (gain1, wq, wk, wv, proj), (gain2, fc1, fc2)
    out = jax.ShapeDtypeStruct((WIN_LAT,) + arrays[0].shape[1:], jnp.bfloat16)
    return pl.pallas_call(
        functools.partial(block_kernel, chans, heads),
        out_shape=out,
        grid=(1,),
        in_specs=specs + [whole(x) for x in before] + [table_spec] + [whole(x) for x in after],
        out_specs=whole(out),
        scratch_shapes=[
            pltpu.VMEM((2, 2, LEVELS * QUERIES, LANES), jnp.float32),
            pltpu.VMEM((2, 2, 184, LANES), jnp.float32),
            pltpu.VMEM((2, 2, 184, LANES), jnp.float32),
        ],
        compiler_params=pltpu.CompilerParams(vmem_limit_bytes=40 * 2**20),
        cost_estimate=pl.CostEstimate(flops=400_000_000, bytes_accessed=3_000_000, transcendentals=500_000),
        name="swin_rows",
    )(*arrays, *before, table, *after)


def shards(
    field_in, norm1_gain, qkv_weight, proj_weight, earth_bias, norm2_gain, fc1_weight, fc2_weight
):
    levels, rows, flat = field_in.shape
    chans = qkv_weight.shape[0]
    heads = earth_bias.shape[2]
    half = HALF * chans
    field = jnp.transpose(field_in, (1, 0, 2))
    east = moved(field[EDGE:, :, :half], 0, -1)
    west = moved(field[EDGE:, :, half:], 0, 1)
    south = moved(field[:EDGE], -1, 0)
    south_east = moved(field[:EDGE, :, :half], -1, -1)
    south_west = moved(field[:EDGE, :, half:], -1, 1)
    last = (lax.axis_index("lat") == lax.axis_size("lat") - 1).astype(jnp.int32).reshape(1)
    windows = rows // WIN_LAT
    table = pl.pallas_call(
        table_kernel,
        out_shape=jax.ShapeDtypeStruct((windows, 2, 2, 2, heads * QUERIES, LANES), jnp.float32),
        in_specs=[
            pl.BlockSpec(memory_space=pltpu.SMEM),
            pl.BlockSpec(memory_space=pltpu.VMEM),
        ],
        out_specs=pl.BlockSpec(memory_space=pltpu.VMEM),
        compiler_params=pltpu.CompilerParams(vmem_limit_bytes=40 * 2**20),
        cost_estimate=pl.CostEstimate(flops=4_000_000, bytes_accessed=6_000_000, transcendentals=0),
        name="bias_tables",
    )(last, earth_bias)
    wq = qkv_weight[:, :chans]
    wk = qkv_weight[:, chans : 2 * chans]
    wv = jnp.pad(qkv_weight[:, 2 * chans :], ((0, 0), (0, 2 * LANES - chans)))
    weights = (
        norm1_gain.reshape(1, chans),
        wq,
        wk,
        wv,
        proj_weight,
        norm2_gain.reshape(1, chans),
        fc1_weight,
        fc2_weight,
    )
    straddle = [(field, 3), (south, 0), (west, 2), (south_west, 0), (east, 2), (south_east, 0)]
    lower = run_block(straddle, table, 1, weights, chans, heads)
    top = moved(lower[EDGE:], 1, 0)
    inner = [(field, 1), (field, 2), (west, 0), (west, 1), (east, 0), (east, 1)]
    upper = run_block(inner, table, 0, weights, chans, heads)
    done = jnp.concatenate([top, upper, lower[:EDGE]], axis=0)
    return jnp.transpose(done, (1, 0, 2))


def solution(mesh):
    in_specs = (P(None, "lat", "lon"), P(), P(), P(), P("lat", None, None, None), P(), P(), P())
    out_specs = P(None, "lat", "lon")
    return jax.shard_map(shards, mesh=mesh, in_specs=in_specs, out_specs=out_specs, check_vma=False)
```

time: 53.1 us -> 32.6 us (0.61)
  waiting for transfers between devices: 12.7 us -> 1.1 us
  matrix products: 9.59 us -> 0 us
  local copies, waits for them, and re-layouts: 18.6 us -> 10.2 us
  Pallas kernels: 0 us -> 7.11 us
  starting transfers between devices: 8.67 us -> 12.9 us
  other arithmetic: 2.9 us -> 0.84 us
    ppermute x4 -> x6, waiting for transfers between devices: 12.7 us -> 1.1 us  [the longest x2 1.09 us: moved(): lax.ppermute(x, 'lat', [(i, (i + lat_by) % lats) for i in range(lats)])]
    another operation x2 -> x0, local copies, waits for them, and re-layouts: 10.8 us -> none  [attend(): scores = scores + table[:, :, None]]
    pallas_call x0 -> x3, Pallas kernels: none -> 7.11 us  [the longest x2 5.94 us: run_block(): pl.pallas_call(functools.partial(block_kernel, chans, heads), out_shape=o...]
    sub x1 -> x0, matrix products: 5.37 us -> none  [attend(): probs = jax.nn.softmax(scores, axis=-1).astype(jnp.bfloat16)]
    dot_general x4 -> x0, matrix products: 4.22 us -> none  [the longest x1 2.39 us: attend(): jnp.einsum('bachqk,abckhd->abcqhd', probs, values, preferred_element_type...]
    ppermute x4 -> x6, starting transfers between devices: 8.67 us -> 12.9 us  [the longest x2 5.45 us: moved(): lax.ppermute(x, 'lon', [(i, (i + lon_by) % lons) for i in range(lons)])]
    slice x9 -> x5, local copies, waits for them, and re-layouts: 2.89 us -> 6.2 us  [the longest x1 1.67 us: shards(): wv = jnp.pad(qkv_weight[:, 2 * chans:], ((0, 0), (0, 2 * LANES - chans)))]
    unnamed x15 -> x12, local copies, waits for them, and re-layouts: 0.19 us -> 3.06 us
  transfers between devices with their start and end apart: 4 -> 6, of which waited for: 3 -> 1; matrix products, arithmetic and copies ran while one was open for 23% -> 26% of each run, Pallas kernels for 0% -> 13%
where the time goes in v1:
time: 32.6 us; the launch traced here: 32.3 us
  starting transfers between devices  12.9 us (40%)
  local copies, waits for them, and re-layouts  10.2 us (31%)
  Pallas kernels  7.11 us (22%)
  waiting for transfers between devices  1.1 us (3%)
  other arithmetic  0.84 us (3%)
    pallas_call x2, Pallas kernels, run_block(): pl.pallas_call(functools.partial(block_kernel, chans, heads), out_shape=o...  5.94 us
    ppermute x2, starting transfers between devices, moved(): lax.ppermute(x, 'lon', [(i, (i + lon_by) % lons) for i in range(lons)])  5.45 us
    ppermute x2, starting transfers between devices, moved(): return lax.ppermute(x, ('lon', 'lat'), pairs)  5.34 us
    unnamed x12, local copies, waits for them, and re-layouts  3.06 us
    ppermute x2, starting transfers between devices, moved(): lax.ppermute(x, 'lat', [(i, (i + lat_by) % lats) for i in range(lats)])  2.09 us
    slice x1, local copies, waits for them, and re-layouts, shards(): wv = jnp.pad(qkv_weight[:, 2 * chans:], ((0, 0), (0, 2 * LANES - chans)))  1.67 us
    slice x1, local copies, waits for them, and re-layouts, shards(): east = moved(field[EDGE:, :, :half], 0, -1)  1.64 us
    slice x1, local copies, waits for them, and re-layouts, shards(): south = moved(field[:EDGE], -1, 0)  1.44 us
  transfers between devices with their start and end apart: 6, of which 1 were waited for; matrix products, arithmetic and copies ran while one was open for 26% of the time, Pallas kernels for 13%

profile of v1, /device:TPU:0, one launch (start us, length us, event | category | flops | bytes accessed | tf_op | source)
XLA Modules:
  0.0 32.3 jit_solution(9860257477772776595)
XLA Ops:
  0.0 1.6 %fusion.2 = (bf16[9,4,1152]{2,1,0:T(4,128)(2,1)}, bf16[9,4,1152]{2,1,0:T(4,128)(2,1)}) fusion(bf16[12,4,2304]{2,1,0:T(4,128)(2,1)} %bitcast.6), kind=kLoop, calls=%fused_computation.3 | loop fusion | bytes 331776 | tf_op jit(solution)/shard_map/slice | solution.py:255
  1.6 0.5 %collective-permute-start.1 = (bf16[9,4,1152]{2,1,0:T(4,128)(2,1)}, bf16[9,4,1152]{2,1,0:T(4,128)(2,1)S(1)}, u32[]{:S(2)}, u32[]{:S(2)}) collective-permute-start(bf16[9,4,1152]{2,1,0:T(4,128)(2,1)} %get-tuple-element.11), channel_id=1, source_target_pairs={{0,2},{2,4},{4,6},{6,8},{8,10},{10,12},{12,14},{14,16},{16,18},{18... | collective-permute-start | bytes 248840 | tf_op jit(solution)/shard_map/ppermute | solution.py:27
  2.1 5.0 %collective-permute-start.3 = (bf16[9,4,1152]{2,1,0:T(4,128)(2,1)}, bf16[9,4,1152]{2,1,0:T(4,128)(2,1)S(1)}, u32[]{:S(2)}, u32[]{:S(2)}) collective-permute-start(bf16[9,4,1152]{2,1,0:T(4,128)(2,1)} %get-tuple-element.10), channel_id=1, source_target_pairs={{0,30},{2,0},{4,2},{6,4},{8,6},{10,8},{12,10},{14,12},{16,14},{18,... | collective-permute-start | bytes 248840 | tf_op jit(solution)/shard_map/ppermute | solution.py:27
  7.1 1.4 %fusion.1 = (bf16[3,4,1152]{2,1,0:T(4,128)(2,1)}, bf16[3,4,1152]{2,1,0:T(4,128)(2,1)}) fusion(bf16[12,4,2304]{2,1,0:T(4,128)(2,1)} %bitcast.7), kind=kLoop, calls=%fused_computation.2 | loop fusion | bytes 110592 | tf_op jit(solution)/shard_map/slice | solution.py:258
  8.5 0.0 collective-permute-start.2
  8.5 5.3 %collective-permute-start.4 = (bf16[3,4,1152]{2,1,0:T(4,128)(2,1)}, bf16[3,4,1152]{2,1,0:T(4,128)(2,1)S(1)}, u32[]{:S(2)}, u32[]{:S(2)}) collective-permute-start(bf16[3,4,1152]{2,1,0:T(4,128)(2,1)} %get-tuple-element.8), channel_id=1, source_target_pairs={{0,31},{1,30},{2,1},{3,0},{4,3},{5,2},{6,5},{7,4},{8,7},{9,6},{10,... | collective-permute-start | bytes 82952 | tf_op jit(solution)/shard_map/ppermute | solution.py:35
  13.8 1.4 %slice.40 = bf16[3,4,2304]{2,1,0:T(4,128)(2,1)} slice(bf16[12,4,2304]{2,1,0:T(4,128)(2,1)} %bitcast.8), slice={[0:3], [0:4], [0:2304]} | slice | bytes 110592 | tf_op jit(solution)/shard_map/slice | solution.py:257
  15.3 1.9 %collective-permute-start = (bf16[3,4,2304]{2,1,0:T(4,128)(2,1)}, bf16[3,4,2304]{2,1,0:T(4,128)(2,1)S(1)}, u32[]{:S(2)}, u32[]{:S(2)}) collective-permute-start(bf16[3,4,2304]{2,1,0:T(4,128)(2,1)} %slice.40), channel_id=1, source_target_pairs={{0,1},{1,0},{2,3},{3,2},{4,5},{5,4},{6,7},{7,6},{8,9},{9,8},{10,11... | collective-permute-start | bytes 165896 | tf_op jit(solution)/shard_map/ppermute | solution.py:29
  17.2 1.7 %fusion = (bf16[192,192]{1,0:T(8,128)(2,1)}, bf16[192,192]{1,0:T(8,128)(2,1)S(1)}, bf16[192,192]{1,0:T(8,128)(2,1)S(1)}) fusion(bf16[192,576]{1,0:T(8,128)(2,1)} %param.10), kind=kLoop, calls=%fused_computation.1 | loop fusion | bytes 442368 | tf_op jit(solution)/shard_map/slice | solution.py:276
  18.9 1.9 %copy.9.bias_ref = f32[2,2,6,20736]{3,2,1,0:T(8,128)S(1)} copy(f32[2,2,6,20736]{3,1,2,0:T(2,128)} %param.12) | data formatting | bytes 3981312 | tf_op args[4]
  20.8 1.1 %copy.10.fc2_ref = bf16[768,192]{1,0:T(8,128)(2,1)S(1)} copy(bf16[768,192]{0,1:T(8,128)(2,1)} %param.15) | data formatting | bytes 589824 | tf_op args[7]
  21.9 0.9 %pad.4.wv_ref = bf16[192,256]{1,0:T(8,128)(2,1)S(1)} pad(bf16[192,192]{1,0:T(8,128)(2,1)} %get-tuple-element.5, bf16[]{:T(256)} %constant.3.clone.1), padding=0_0x0_64 | pad | bytes 172034 | tf_op jit(solution)/shard_map/jit(_pad)/pad | solution.py:276
  22.8 0.0 copy-start
  22.9 0.0 copy-start.1
  22.9 0.0 copy-start.2
  22.9 0.0 copy-start.3
  22.9 0.0 copy-start.4
  22.9 1.2 %bias_tables.1.table_ref = f32[2,2,2,2,432,128]{5,4,3,2,1,0:T(8,128)S(1)} custom-call(s32[1]{0:T(128)} %bitcast.2.last_ref, f32[2,2,6,20736]{3,2,1,0:T(8,128)S(1)} %copy.9.bias_ref), custom_call_target="tpu_custom_call" | custom-call | flops 4000000 | bytes 6000000 | tf_op jit(solution)/shard_map/bias_tables/pallas_call | solution.py:262
  24.1 0.0 collective-permute-done.2.west_b
  24.1 0.0 collective-permute-done.4.east_b
  24.1 0.0 collective-permute-done.own_b
  24.1 0.0 collective-permute-done.1.west_a.west_b
  24.1 0.0 collective-permute-done.3.east_a.east_b
  24.1 0.0 copy-done
  24.1 0.0 copy-done.1
  24.1 0.0 copy-done.2
  24.2 0.0 copy-done.3
  24.2 0.0 copy-done.4
  24.2 3.0 %swin_rows.2 = bf16[6,4,2304]{2,1,0:T(4,128)(2,1)S(1)} custom-call(bf16[12,4,2304]{2,1,0:T(4,128)(2,1)S(1)} %bitcast.9, bf16[3,4,2304]{2,1,0:T(4,128)(2,1)S(1)} %collective-permute-done.own_b, bf16[9,4,1152]{2,1,0:T(4,128)(2,1)S(1)} %collective-permute-done.1.west_a.west_b, bf16[3,4,1152]{2,1,0:T(4,128)(2,1)S(1)} %collective-permute-done.2.west_b, ...), custom_call_target="tpu_custom_call" | custom-call | flops 400000000 | bytes 3000000 | tf_op jit(solution)/shard_map/swin_rows/pallas_call | solution.py:230
  27.2 0.2 collective-permute-start.5
  27.4 3.0 %swin_rows.3 = bf16[6,4,2304]{2,1,0:T(4,128)(2,1)S(1)} custom-call(bf16[12,4,2304]{2,1,0:T(4,128)(2,1)S(1)} %bitcast.10, bf16[12,4,2304]{2,1,0:T(4,128)(2,1)S(1)} %bitcast.11, bf16[9,4,1152]{2,1,0:T(4,128)(2,1)S(1)} %collective-permute-done.1.west_a.west_b, bf16[9,4,1152]{2,1,0:T(4,128)(2,1)S(1)} %collective-permute-done.1.west_a.west_b, ...), custom_call_target="tpu_custom_call" | custom-call | flops 400000000 | bytes 3000000 | tf_op jit(solution)/shard_map/swin_rows/pallas_call | solution.py:230
  30.3 1.1 %collective-permute-done.5 = bf16[3,4,2304]{2,1,0:T(4,128)(2,1)S(1)} collective-permute-done((bf16[3,4,2304]{2,1,0:T(4,128)(2,1)S(1)}, bf16[3,4,2304]{2,1,0:T(4,128)(2,1)S(1)}, u32[]{:S(2)}, u32[]{:S(2)}) %collective-permute-start.5) | collective-permute-done | bytes 55328 | tf_op jit(solution)/shard_map/ppermute | solution.py:29
  31.4 0.8 %maximum_bitcast_fusion = bf16[4,12,2304]{2,0,1:T(4,128)(2,1)} fusion(bf16[3,4,2304]{2,1,0:T(4,128)(2,1)S(1)} %get-tuple-element.13, bf16[6,4,2304]{2,1,0:T(4,128)(2,1)S(1)} %swin_rows.3, bf16[3,4,2304]{2,1,0:T(4,128)(2,1)S(1)} %collective-permute-done.5), kind=kLoop, calls=%fused_computation | loop fusion | flops 221184 | bytes 442368 | tf_op jit(solution)/shard_map/transpose | solution.py:293
  (1 shorter events, 0.0 us)
Async XLA Ops:
  1.6 22.5 %collective-permute-start.1 = (bf16[9,4,1152]{2,1,0:T(4,128)(2,1)}, bf16[9,4,1152]{2,1,0:T(4,128)(2,1)S(1)}, u32[]{:S(2)}, u32[]{:S(2)}) collective-permute-start(bf16[9,4,1152]{2,1,0:T(4,128)(2,1)} %get-tuple-element.11), channel_id=1, source_target_pairs={{0,2},{2,4},{4,6},{6,8},{8,10},{10,12},{12,14},{14,16},{16,18},{18... | collective-permute-start | bytes 248840 | tf_op jit(solution)/shard_map/ppermute | solution.py:27
  2.1 22.0 %collective-permute-start.3 = (bf16[9,4,1152]{2,1,0:T(4,128)(2,1)}, bf16[9,4,1152]{2,1,0:T(4,128)(2,1)S(1)}, u32[]{:S(2)}, u32[]{:S(2)}) collective-permute-start(bf16[9,4,1152]{2,1,0:T(4,128)(2,1)} %get-tuple-element.10), channel_id=1, source_target_pairs={{0,30},{2,0},{4,2},{6,4},{8,6},{10,8},{12,10},{14,12},{16,14},{18,... | collective-permute-start | bytes 248840 | tf_op jit(solution)/shard_map/ppermute | solution.py:27
  8.5 15.6 %collective-permute-start.2 = (bf16[3,4,1152]{2,1,0:T(4,128)(2,1)}, bf16[3,4,1152]{2,1,0:T(4,128)(2,1)S(1)}, u32[]{:S(2)}, u32[]{:S(2)}) collective-permute-start(bf16[3,4,1152]{2,1,0:T(4,128)(2,1)} %get-tuple-element.9), channel_id=1, source_target_pairs={{0,3},{1,2},{2,5},{3,4},{4,7},{5,6},{6,9},{7,8},{8,11},{9,10},{10,... | collective-permute-start | bytes 82952 | tf_op jit(solution)/shard_map/ppermute | solution.py:35
  8.5 15.6 %collective-permute-start.4 = (bf16[3,4,1152]{2,1,0:T(4,128)(2,1)}, bf16[3,4,1152]{2,1,0:T(4,128)(2,1)S(1)}, u32[]{:S(2)}, u32[]{:S(2)}) collective-permute-start(bf16[3,4,1152]{2,1,0:T(4,128)(2,1)} %get-tuple-element.8), channel_id=1, source_target_pairs={{0,31},{1,30},{2,1},{3,0},{4,3},{5,2},{6,5},{7,4},{8,7},{9,6},{10,... | collective-permute-start | bytes 82952 | tf_op jit(solution)/shard_map/ppermute | solution.py:35
  15.3 8.8 %collective-permute-start = (bf16[3,4,2304]{2,1,0:T(4,128)(2,1)}, bf16[3,4,2304]{2,1,0:T(4,128)(2,1)S(1)}, u32[]{:S(2)}, u32[]{:S(2)}) collective-permute-start(bf16[3,4,2304]{2,1,0:T(4,128)(2,1)} %slice.40), channel_id=1, source_target_pairs={{0,1},{1,0},{2,3},{3,2},{4,5},{5,4},{6,7},{7,6},{8,9},{9,8},{10,11... | collective-permute-start | bytes 165896 | tf_op jit(solution)/shard_map/ppermute | solution.py:29
  22.8 1.3 %copy-start = (bf16[4,12,2304]{2,0,1:T(4,128)(2,1)S(1)}, bf16[4,12,2304]{2,0,1:T(4,128)(2,1)}, u32[]{:S(2)}) copy-start(bf16[4,12,2304]{2,0,1:T(4,128)(2,1)} %param.8) | copy-start | bytes 663556
  22.9 1.3 %copy-start.1 = (bf16[192,768]{1,0:T(8,128)(2,1)S(1)}, bf16[192,768]{1,0:T(8,128)(2,1)}, u32[]{:S(2)}) copy-start(bf16[192,768]{1,0:T(8,128)(2,1)} %fc1_ref.3) | copy-start | bytes 884740
  22.9 1.3 %copy-start.2 = (bf16[192,192]{1,0:T(8,128)(2,1)S(1)}, bf16[192,192]{1,0:T(8,128)(2,1)}, u32[]{:S(2)}) copy-start(bf16[192,192]{1,0:T(8,128)(2,1)} %proj_ref.3) | copy-start | bytes 221188
  22.9 1.3 %copy-start.3 = (f32[192]{0:T(256)S(1)}, f32[192]{0:T(256)}, u32[]{:S(2)}) copy-start(f32[192]{0:T(256)} %param.9) | copy-start | bytes 2308
  22.9 1.3 %copy-start.4 = (f32[192]{0:T(256)S(1)}, f32[192]{0:T(256)}, u32[]{:S(2)}) copy-start(f32[192]{0:T(256)} %param.13) | copy-start | bytes 2308
  27.2 4.2 %collective-permute-start.5 = (bf16[3,4,2304]{2,1,0:T(4,128)(2,1)S(1)}, bf16[3,4,2304]{2,1,0:T(4,128)(2,1)S(1)}, u32[]{:S(2)}, u32[]{:S(2)}) collective-permute-start(bf16[3,4,2304]{2,1,0:T(4,128)(2,1)S(1)} %get-tuple-element.12), channel_id=1, source_target_pairs={{0,1},{1,0},{2,3},{3,2},{4,5},{5,4},{6,7},{7,6},{8,9},{9,8},{10,11... | collective-permute-start | bytes 165896 | tf_op jit(solution)/shard_map/ppermute | solution.py:29

commit v2 on v1

v2 whole, which is shorter than its diff:
```python
import functools

import jax
import jax.numpy as jnp
from jax import lax
from jax.experimental import pallas as pl
from jax.experimental.pallas import tpu as pltpu
from jax.sharding import PartitionSpec as P

LEVELS = 4
WIN_LEV = 2
WIN_LAT = 6
WIN_LON = 12
EDGE = WIN_LAT // 2
HALF = WIN_LON // 2
TOKENS = WIN_LEV * WIN_LAT * WIN_LON
QUERIES = TOKENS // 2
LOG2E = 1.4426950408889634
LANES = 128
SPARE = 64
NT = (((1,), (1,)), ((), ()))


def moved(x, axis, by):
    size = lax.axis_size(axis)
    return lax.ppermute(x, axis, [(i, (i + by) % size) for i in range(size)])


def swapped(x, axis, first):
    size = lax.axis_size(axis)
    pairs = []
    for i in range(first, size, 2):
        j = (i + 1) % size
        pairs += [(i, j), (j, i)]
    return lax.ppermute(x, axis, pairs)


def table_kernel(last_ref, bias_ref, table_ref):
    heads = bias_ref.shape[2]
    width = 9 * LANES
    lane = lax.broadcasted_iota(jnp.int32, (1, LANES), 1)
    last = jnp.where(last_ref[0] > 0, -1e9, 0.0).astype(jnp.float32)

    def penalty(first, lev, side, wrap):
        key = lane + first
        key_lev = (key >= QUERIES).astype(jnp.int32)
        key_side = ((key - key_lev * QUERIES) >= QUERIES // 2).astype(jnp.int32)
        out = jnp.zeros((1, LANES), jnp.float32)
        if lev is not None:
            out = jnp.where(key_lev != lev, -1e9, out)
        if wrap:
            out = out + jnp.where(key_side != side, last, 0.0)
        return out

    for k in range(2):
        for p in range(2):
            masks = {}
            for lev in range(2):
                for side in range(2):
                    masks[lev, side] = [
                        penalty(first, lev if p == 1 else None, side, k == 1)
                        for first in (0, LANES)
                    ]
            for c in range(TOKENS // 8):
                tiles = [
                    bias_ref[k, p, :, c * width + u * LANES : c * width + (u + 1) * LANES]
                    for u in range(9)
                ]
                for r in range(8):
                    i = 8 * c + r
                    shift = 16 * r
                    nxt = tiles[r + 1]
                    main = tiles[r]
                    if r:
                        main = pltpu.roll(main, LANES - shift, 1)
                        nxt = pltpu.roll(nxt, LANES - shift, 1)
                        main = jnp.where(lane < LANES - shift, main, nxt)
                    lev = i // QUERIES
                    row = i % QUERIES // WIN_LON
                    col = i % WIN_LON
                    side = col // HALF
                    place = lev * 36 + row * HALF + col % HALF
                    mask = masks[lev, row // EDGE]
                    at = pl.ds(place, heads, stride=QUERIES)
                    table_ref[k, p, 1 - side, 0, at, :] = main * LOG2E + mask[0]
                    table_ref[k, p, 1 - side, 1, at, :] = nxt * LOG2E + mask[1]


def layer_norm(values, gain):
    center = values - jnp.mean(values, axis=-1, keepdims=True)
    spread = jnp.mean(center * center, axis=-1, keepdims=True)
    return center * lax.rsqrt(spread + 1e-05) * gain


def side_kernel(
    chans,
    heads,
    windows,
    right_ref,
    own_piece,
    halo_piece,
    gain1_ref,
    qkv_ref,
    proj_ref,
    table_ref,
    gain2_ref,
    fc1_ref,
    fc2_ref,
    out_ref,
    keys_ref,
    own_ref,
    res_ref,
):
    head_dim = chans // heads
    low = lax.broadcasted_iota(jnp.int32, (1, LANES), 1) < SPARE
    right = right_ref[0]
    halo_at = right * HALF
    own_at = HALF - halo_at

    def tokens_of(ref, at, first, count):
        both = [ref[at, part, first : first + count] for part in range(2)]
        return jnp.concatenate([both[0], both[1][:, : chans - LANES]], axis=1)

    def split(ref, row):
        for pair in range(HALF // 2):
            both = ref[row, :, pair * 2 * chans : (pair + 1) * 2 * chans].astype(jnp.float32)
            first, middle, final = (both[:, u * LANES : (u + 1) * LANES] for u in range(3))
            yield 2 * pair, (first, middle)
            middle, final = pltpu.roll(middle, SPARE, 1), pltpu.roll(final, SPARE, 1)
            yield 2 * pair + 1, (jnp.where(low, middle, final), final)

    for n in range(len(windows)):
        for row in range(WIN_LAT):
            for col, block in split(halo_piece, n * WIN_LAT + row):
                at = pl.ds(row * WIN_LON + col + halo_at, LEVELS, stride=QUERIES)
                for part in range(2):
                    keys_ref[n, part, at, :] = block[part]
            for col, block in split(own_piece, n * WIN_LAT + row):
                at = pl.ds(row * WIN_LON + col + own_at, LEVELS, stride=QUERIES)
                place = row * HALF + col
                for part in range(2):
                    keys_ref[n, part, at, :] = block[part]
                    own_ref[n, part, pl.ds(4 + place, LEVELS, stride=36), :] = block[part]
                    own_ref[n, part, pl.ds(148 + place, 1), :] = block[part][:1]

    gain1 = gain1_ref[...]
    lane = lax.broadcasted_iota(jnp.int32, (1, chans), 1)
    ones = jnp.ones((LEVELS * QUERIES, 2 * LANES - chans), jnp.float32)
    mixed = []
    for n in range(len(windows)):
        normed = layer_norm(tokens_of(keys_ref, n, 0, LEVELS * QUERIES), gain1)
        normed = jnp.concatenate([normed[QUERIES:], normed[:QUERIES]], axis=0)
        normed = normed.astype(jnp.bfloat16)
        keys = jnp.dot(normed, qkv_ref[:, chans : 2 * chans], preferred_element_type=jnp.float32)
        values = jnp.dot(normed, qkv_ref[:, 2 * chans :], preferred_element_type=jnp.float32)
        values = jnp.concatenate([values, ones], axis=1)
        own = layer_norm(tokens_of(own_ref, n, 40, 144), gain1).astype(jnp.bfloat16)
        query = jnp.dot(own, qkv_ref[:, :chans], preferred_element_type=jnp.float32)
        query = query * (head_dim ** (-0.5) * LOG2E)
        for p in range(2):
            q = query[p * QUERIES : (p + 1) * QUERIES]
            k = keys[p * TOKENS : (p + 1) * TOKENS].astype(jnp.bfloat16)
            v = values[p * TOKENS : (p + 1) * TOKENS].astype(jnp.bfloat16)
            picked = [
                jnp.where((lane >= h * head_dim) & (lane < (h + 1) * head_dim), q, 0.0)
                for h in range(heads)
            ]
            picked = jnp.concatenate(picked, axis=0).astype(jnp.bfloat16)
            scores = lax.dot_general(picked, k, NT, preferred_element_type=jnp.float32)
            table = [table_ref[windows[n], p, right, part] for part in range(2)]
            table = jnp.concatenate([table[0], table[1][:, : TOKENS - LANES]], axis=1)
            scores = scores + table
            top = jnp.max(scores, axis=1, keepdims=True)
            probs = jnp.exp2(scores - top).astype(jnp.bfloat16)
            got = jnp.dot(probs, v, preferred_element_type=jnp.float32)
            out = jnp.zeros((QUERIES, chans), jnp.float32)
            for h in range(heads):
                part = got[h * QUERIES : (h + 1) * QUERIES]
                scaled = part[:, :chans] * (1.0 / part[:, chans : chans + 1])
                inside = (lane >= h * head_dim) & (lane < (h + 1) * head_dim)
                out = jnp.where(inside, scaled, out)
            mixed.append(out)
    mixed = jnp.concatenate(mixed, axis=0).astype(jnp.bfloat16)
    attn = jnp.dot(mixed, proj_ref[...], preferred_element_type=jnp.float32)
    attn = attn.astype(jnp.bfloat16).astype(jnp.float32)
    tokens = [tokens_of(own_ref, n, 40, 144) for n in range(len(windows))]
    resid = jnp.concatenate(tokens, axis=0) + attn
    resid = resid.astype(jnp.bfloat16).astype(jnp.float32)
    normed = layer_norm(resid, gain2_ref[...]).astype(jnp.bfloat16)
    hidden = jnp.dot(normed, fc1_ref[...], preferred_element_type=jnp.float32)
    hidden = jax.nn.gelu(hidden).astype(jnp.bfloat16)
    result = lax.dot_general(hidden, fc2_ref[...], NT, preferred_element_type=jnp.float32)
    result = resid + result
    for n in range(len(windows)):
        mine = result[n * 144 : (n + 1) * 144]
        for part, lanes in enumerate((slice(0, LANES), slice(LANES, chans))):
            width = min(LANES, chans - part * LANES)
            res_ref[n, part, 40:184, :width] = mine[:, lanes]
            res_ref[n, part, 0:40, :width] = mine[104:144, lanes]
        for row in range(WIN_LAT):
            for pair in range(HALF // 2):
                tiles = []
                for col in (2 * pair, 2 * pair + 1):
                    at = pl.ds(4 + row * HALF + col, LEVELS, stride=36)
                    tiles += [res_ref[n, part, at, :] for part in range(2)]
                shifted = [pltpu.roll(x, SPARE, 1) for x in tiles[2:]]
                tiles = [tiles[0], jnp.where(low, tiles[1], shifted[0])]
                tiles.append(jnp.where(low, shifted[0], shifted[1]))
                tiles = jnp.concatenate(tiles, axis=1).astype(jnp.bfloat16)
                out_ref[n * WIN_LAT + row, :, pair * 2 * chans : (pair + 1) * 2 * chans] = tiles


def run_side(right, own, halo, table, windows, weights, chans, heads):
    count = len(windows)
    first = windows[0]
    assert list(windows) == list(range(first, first + count)) and first % count == 0
    rows = count * WIN_LAT
    piece = pl.BlockSpec((rows,) + own.shape[1:], lambda _: (first // count, 0, 0))

    def whole(x):
        return pl.BlockSpec(x.shape, lambda _: (0,) * len(x.shape))

    out = jax.ShapeDtypeStruct((rows,) + own.shape[1:], jnp.bfloat16)
    gain1, qkv, proj, gain2, fc1, fc2 = weights
    return pl.pallas_call(
        functools.partial(side_kernel, chans, heads, windows),
        out_shape=out,
        grid=(1,),
        in_specs=[pl.BlockSpec(memory_space=pltpu.SMEM), piece, piece]
        + [whole(x) for x in (gain1, qkv, proj, table, gain2, fc1, fc2)],
        out_specs=whole(out),
        scratch_shapes=[
            pltpu.VMEM((count, 2, LEVELS * QUERIES, LANES), jnp.float32),
            pltpu.VMEM((count, 2, 184, LANES), jnp.float32),
            pltpu.VMEM((count, 2, 184, LANES), jnp.float32),
        ],
        compiler_params=pltpu.CompilerParams(vmem_limit_bytes=32 * 2**20),
        cost_estimate=pl.CostEstimate(
            flops=200_000_000 * count, bytes_accessed=3_000_000, transcendentals=250_000 * count
        ),
        name="swin_side",
    )(right, own, halo, gain1, qkv, proj, table, gain2, fc1, fc2)


def shards(
    field_in, norm1_gain, qkv_weight, proj_weight, earth_bias, norm2_gain, fc1_weight, fc2_weight
):
    levels, rows, flat = field_in.shape
    chans = qkv_weight.shape[0]
    heads = earth_bias.shape[2]
    half = HALF * chans
    field = jnp.transpose(field_in, (1, 0, 2))
    south = moved(field[:EDGE], "lat", -1)
    odd = lax.axis_index("lon") % 2
    last = (lax.axis_index("lat") == lax.axis_size("lat") - 1).astype(jnp.int32).reshape(1)
    table = pl.pallas_call(
        table_kernel,
        out_shape=jax.ShapeDtypeStruct((2, 2, 2, 2, heads * QUERIES, LANES), jnp.float32),
        in_specs=[
            pl.BlockSpec(memory_space=pltpu.SMEM),
            pl.BlockSpec(memory_space=pltpu.VMEM),
        ],
        out_specs=pl.BlockSpec(memory_space=pltpu.VMEM),
        compiler_params=pltpu.CompilerParams(vmem_limit_bytes=32 * 2**20),
        cost_estimate=pl.CostEstimate(flops=4_000_000, bytes_accessed=6_000_000, transcendentals=0),
        name="bias_tables",
    )(last, earth_bias)
    tokens = jnp.concatenate([field[EDGE:], south], axis=0)
    left, right = tokens[:, :, :half], tokens[:, :, half:]
    near = jnp.where(odd == 1, left, right)
    far = jnp.where(odd == 1, right, left)
    far_halo = swapped(far, "lon", 1)
    near_halo = swapped(near, "lon", 0)
    weights = (
        norm1_gain.reshape(1, chans),
        qkv_weight,
        proj_weight,
        norm2_gain.reshape(1, chans),
        fc1_weight,
        jnp.transpose(fc2_weight),
    )
    near_right, far_right = (1 - odd).reshape(1), odd.reshape(1)
    near_done = run_side(near_right, near, near_halo, table, (0, 1), weights, chans, heads)
    far_low = run_side(far_right, far, far_halo, table, (1,), weights, chans, heads)
    top = moved(jnp.stack([near_done[WIN_LAT + EDGE :], far_low[EDGE:]]), "lat", 1)
    far_high = run_side(far_right, far, far_halo, table, (0,), weights, chans, heads)
    near_all = jnp.concatenate([top[0], near_done[: WIN_LAT + EDGE]], axis=0)
    far_all = jnp.concatenate([top[1], far_high, far_low[:EDGE]], axis=0)
    done = jnp.where(
        odd == 1,
        jnp.concatenate([near_all, far_all], axis=2),
        jnp.concatenate([far_all, near_all], axis=2),
    )
    return jnp.transpose(done, (1, 0, 2))


def solution(mesh):
    in_specs = (P(None, "lat", "lon"), P(), P(), P(), P("lat", None, None, None), P(), P(), P())
    out_specs = P(None, "lat", "lon")
    return jax.shard_map(shards, mesh=mesh, in_specs=in_specs, out_specs=out_specs, check_vma=False)
```

time: 32.6 us -> 23.7 us (0.73)
  local copies, waits for them, and re-layouts: 10.2 us -> 3.83 us
  starting transfers between devices: 12.9 us -> 8.6 us
  Pallas kernels: 7.11 us -> 8.43 us
    slice x5 -> x3, local copies, waits for them, and re-layouts: 6.2 us -> 1.84 us  [the longest x1 0.97 us: shards(): tokens = jnp.concatenate([field[EDGE:], south], axis=0)]
    ppermute x6 -> x4, starting transfers between devices: 12.9 us -> 8.6 us  [the longest x2 5.09 us: moved(): return lax.ppermute(x, axis, [(i, (i + by) % size) for i in range(size)])]
    pallas_call x3 -> x4, Pallas kernels: 7.11 us -> 8.43 us  [the longest x3 7.27 us: run_side(): pl.pallas_call(functools.partial(side_kernel, chans, heads, windows), out...]
    unnamed x12 -> x13, local copies, waits for them, and re-layouts: 3.06 us -> 1.93 us
    pad x1 -> x0, local copies, waits for them, and re-layouts: 0.91 us -> none  [shards(): wv = jnp.pad(qkv_weight[:, 2 * chans:], ((0, 0), (0, 2 * LANES - chans)))]
    ppermute x6 -> x4, waiting for transfers between devices: 1.1 us -> 1.42 us  [the longest x2 1.15 us: moved(): return lax.ppermute(x, axis, [(i, (i + by) % size) for i in range(size)])]
  transfers between devices with their start and end apart: 6 -> 4, of which waited for: 1 -> 2; matrix products, arithmetic and copies ran while one was open for 26% -> 12% of each run, Pallas kernels for 13% -> 23%
where the time goes in v2:
time: 23.7 us; the launch traced here: 23.5 us
  starting transfers between devices  8.6 us (36%)
  Pallas kernels  8.43 us (36%)
  local copies, waits for them, and re-layouts  3.83 us (16%)
  waiting for transfers between devices  1.42 us (6%)
  other arithmetic  1.02 us (4%)
    pallas_call x3, Pallas kernels, run_side(): pl.pallas_call(functools.partial(side_kernel, chans, heads, windows), out...  7.27 us
    ppermute x2, starting transfers between devices, moved(): return lax.ppermute(x, axis, [(i, (i + by) % size) for i in range(size)])  5.09 us
    ppermute x2, starting transfers between devices, swapped(): return lax.ppermute(x, axis, pairs)  3.51 us
    unnamed x13, local copies, waits for them, and re-layouts  1.93 us
    pallas_call x1, Pallas kernels, shards(): pl.pallas_call(table_kernel, out_shape=jax.ShapeDtypeStruct((2, 2, 2, 2,...  1.17 us
    ppermute x2, waiting for transfers between devices, moved(): return lax.ppermute(x, axis, [(i, (i + by) % size) for i in range(size)])  1.15 us
    slice x1, local copies, waits for them, and re-layouts, shards(): tokens = jnp.concatenate([field[EDGE:], south], axis=0)  0.97 us
    transpose x1, other arithmetic, shards(): return jnp.transpose(done, (1, 0, 2))  0.86 us
  transfers between devices with their start and end apart: 4, of which 2 were waited for; matrix products, arithmetic and copies ran while one was open for 12% of the time, Pallas kernels for 23%

profile of v2, /device:TPU:0, one launch (start us, length us, event | category | flops | bytes accessed | tf_op | source)
XLA Modules:
  0.0 23.5 jit_solution(16022982394768111717)
XLA Ops:
  0.0 0.8 %slice.41 = bf16[3,4,2304]{2,1,0:T(4,128)(2,1)S(1)} slice(bf16[12,4,2304]{2,1,0:T(4,128)(2,1)} %bitcast.26), slice={[0:3], [0:4], [0:2304]} | slice | bytes 110592 | tf_op jit(solution)/shard_map/slice | solution.py:253
  0.8 3.0 %collective-permute-start = (bf16[3,4,2304]{2,1,0:T(4,128)(2,1)S(1)}, bf16[3,4,2304]{2,1,0:T(4,128)(2,1)S(1)}, u32[]{:S(2)}, u32[]{:S(2)}) collective-permute-start(bf16[3,4,2304]{2,1,0:T(4,128)(2,1)S(1)} %slice.41), channel_id=1, source_target_pairs={{0,1},{1,0},{2,3},{3,2},{4,5},{5,4},{6,7},{7,6},{8,9},{9,8},{10,11... | collective-permute-start | bytes 165896 | tf_op jit(solution)/shard_map/ppermute | solution.py:26
  3.8 1.0 %slice.40 = bf16[9,4,2304]{2,1,0:T(4,128)(2,1)S(1)} slice(bf16[12,4,2304]{2,1,0:T(4,128)(2,1)} %bitcast.27), slice={[3:12], [0:4], [0:2304]} | slice | bytes 331776 | tf_op jit(solution)/shard_map/slice | solution.py:268
  4.8 1.1 %collective-permute-done = bf16[3,4,2304]{2,1,0:T(4,128)(2,1)S(1)} collective-permute-done((bf16[3,4,2304]{2,1,0:T(4,128)(2,1)S(1)}, bf16[3,4,2304]{2,1,0:T(4,128)(2,1)S(1)}, u32[]{:S(2)}, u32[]{:S(2)}) %collective-permute-start) | collective-permute-done | bytes 55328 | tf_op jit(solution)/shard_map/ppermute | solution.py:26
  6.0 0.1 broadcast_select_fusion.1
  6.1 3.4 %collective-permute-start.2 = (bf16[12,4,1152]{2,1,0:T(4,128)(2,1)S(1)}, bf16[12,4,1152]{2,1,0:T(4,128)(2,1)S(1)}, u32[]{:S(2)}, u32[]{:S(2)}) collective-permute-start(bf16[12,4,1152]{2,1,0:T(4,128)(2,1)S(1)} %get-tuple-element.6.own_piece), channel_id=1, source_target_pairs={{2,4},{4,2},{6,8},{8,6},{10,12},{12,10},{14,16},{16,14},{18,20},{2... | collective-permute-start | bytes 331784 | tf_op jit(solution)/shard_map/ppermute | solution.py:35
  9.5 1.9 %copy.9.bias_ref = f32[2,2,6,20736]{3,2,1,0:T(8,128)S(1)} copy(f32[2,2,6,20736]{3,1,2,0:T(2,128)} %param.12) | data formatting | bytes 3981312 | tf_op args[4]
  11.4 0.0 copy-start
  11.4 0.0 copy-start.1
  11.5 0.0 copy-start.2
  11.5 0.0 copy-start.3
  11.5 0.0 copy-start.4
  11.5 0.0 copy-start.5
  11.5 1.2 %bias_tables.1.table_ref = f32[2,2,2,2,432,128]{5,4,3,2,1,0:T(8,128)S(1)} custom-call(s32[1]{0:T(128)} %bitcast.3.last_ref, f32[2,2,6,20736]{3,2,1,0:T(8,128)S(1)} %copy.9.bias_ref), custom_call_target="tpu_custom_call" | custom-call | flops 4000000 | bytes 6000000 | tf_op jit(solution)/shard_map/bias_tables/pallas_call | solution.py:256
  12.7 0.1 collective-permute-start.1
  12.8 0.3 %collective-permute-done.2.halo_piece = bf16[12,4,1152]{2,1,0:T(4,128)(2,1)S(1)} collective-permute-done((bf16[12,4,1152]{2,1,0:T(4,128)(2,1)S(1)}, bf16[12,4,1152]{2,1,0:T(4,128)(2,1)S(1)}, u32[]{:S(2)}, u32[]{:S(2)}) %collective-permute-start.2) | collective-permute-done | bytes 110624 | tf_op jit(solution)/shard_map/ppermute | solution.py:35
  13.0 0.0 copy-done
  13.0 0.0 copy-done.1
  13.0 0.0 copy-done.2
  13.0 0.0 copy-done.3
  13.1 0.0 copy-done.4
  13.1 0.0 copy-done.5
  13.1 2.1 %swin_side.4 = bf16[6,4,1152]{2,1,0:T(4,128)(2,1)S(1)} custom-call(s32[1]{0:T(128)} %bitcast.7.right_ref, bf16[12,4,1152]{2,1,0:T(4,128)(2,1)S(1)} %get-tuple-element.6.own_piece, bf16[12,4,1152]{2,1,0:T(4,128)(2,1)S(1)} %collective-permute-done.2.halo_piece, f32[1,192]{1,0:T(1,128)S(1)} %bitcast.20, bf16[192,576]{1,0:T(8,128)(2,1)S(1)} %copy-done.2, ...), custom_call_target="tpu_custom_call" | custom-call | flops 200000000 | bytes 3000000 | tf_op jit(solution)/shard_map/swin_side/pallas_call | solution.py:225
  15.2 0.0 collective-permute-done.1.halo_piece
  15.2 3.1 %swin_side.3 = bf16[12,4,1152]{2,1,0:T(4,128)(2,1)S(1)} custom-call(s32[1]{0:T(128)} %bitcast.right_ref, bf16[12,4,1152]{2,1,0:T(4,128)(2,1)S(1)} %get-tuple-element.5.own_piece, bf16[12,4,1152]{2,1,0:T(4,128)(2,1)S(1)} %collective-permute-done.1.halo_piece, f32[1,192]{1,0:T(1,128)S(1)} %bitcast.21, bf16[192,576]{1,0:T(8,128)(2,1)S(1)} %copy-done.2, ...), custom_call_target="tpu_custom_call" | custom-call | flops 400000000 | bytes 3000000 | tf_op jit(solution)/shard_map/swin_side/pallas_call | solution.py:225
  18.4 2.1 %collective-permute-start.3 = (bf16[2,3,4,1152]{3,2,1,0:T(4,128)(2,1)S(1)}, bf16[2,3,4,1152]{3,2,1,0:T(4,128)(2,1)S(1)}, u32[]{:S(2)}, u32[]{:S(2)}) collective-permute-start(bf16[2,3,4,1152]{3,2,1,0:T(4,128)(2,1)S(1)} %pad_maximum_fusion.1), channel_id=1, source_target_pairs={{0,1},{1,0},{2,3},{3,2},{4,5},{5,4},{6,7},{7,6},{8,9},{9,8},{10,11... | collective-permute-start | bytes 165896 | tf_op jit(solution)/shard_map/ppermute | solution.py:26
  20.5 2.1 %swin_side.5 = bf16[6,4,1152]{2,1,0:T(4,128)(2,1)S(1)} custom-call(s32[1]{0:T(128)} %bitcast.7.right_ref, bf16[12,4,1152]{2,1,0:T(4,128)(2,1)S(1)} %get-tuple-element.6.own_piece, bf16[12,4,1152]{2,1,0:T(4,128)(2,1)S(1)} %collective-permute-done.2.halo_piece, f32[1,192]{1,0:T(1,128)S(1)} %bitcast.22, bf16[192,576]{1,0:T(8,128)(2,1)S(1)} %copy-done.2, ...), custom_call_target="tpu_custom_call" | custom-call | flops 200000000 | bytes 3000000 | tf_op jit(solution)/shard_map/swin_side/pallas_call | solution.py:225
  22.6 0.0 collective-permute-done.3
  22.6 0.9 %fusion = bf16[4,12,2304]{2,0,1:T(4,128)(2,1)} fusion(bf16[3,4,1152]{2,1,0:T(4,128)(2,1)S(1)} %get-tuple-element.10, bf16[6,4,1152]{2,1,0:T(4,128)(2,1)S(1)} %swin_side.5, bf16[3,4,1152]{2,1,0:T(4,128)(2,1)S(1)} %get-tuple-element.8, bf16[9,4,1152]{2,1,0:T(4,128)(2,1)S(1)} %slice.47, bf16[3,4,1152]{2,1,0:T(4,128)(2,1)S(1)} %get-tuple-element.7, pred[]{:T(512)S(6)} %eq.10), kind=kLoop, calls=%fused_computation.3 | loop fusion | flops 2322432 | bytes 442369 | tf_op jit(solution)/shard_map/transpose | solution.py:294
  (5 shorter events, 0.1 us)
Async XLA Ops:
  0.8 5.1 %collective-permute-start = (bf16[3,4,2304]{2,1,0:T(4,128)(2,1)S(1)}, bf16[3,4,2304]{2,1,0:T(4,128)(2,1)S(1)}, u32[]{:S(2)}, u32[]{:S(2)}) collective-permute-start(bf16[3,4,2304]{2,1,0:T(4,128)(2,1)S(1)} %slice.41), channel_id=1, source_target_pairs={{0,1},{1,0},{2,3},{3,2},{4,5},{5,4},{6,7},{7,6},{8,9},{9,8},{10,11... | collective-permute-start | bytes 165896 | tf_op jit(solution)/shard_map/ppermute | solution.py:26
  6.1 6.9 %collective-permute-start.2 = (bf16[12,4,1152]{2,1,0:T(4,128)(2,1)S(1)}, bf16[12,4,1152]{2,1,0:T(4,128)(2,1)S(1)}, u32[]{:S(2)}, u32[]{:S(2)}) collective-permute-start(bf16[12,4,1152]{2,1,0:T(4,128)(2,1)S(1)} %get-tuple-element.6.own_piece), channel_id=1, source_target_pairs={{2,4},{4,2},{6,8},{8,6},{10,12},{12,10},{14,16},{16,14},{18,20},{2... | collective-permute-start | bytes 331784 | tf_op jit(solution)/shard_map/ppermute | solution.py:35
  11.4 1.6 %copy-start = (bf16[192,768]{1,0:T(8,128)(2,1)S(1)}, bf16[192,768]{1,0:T(8,128)(2,1)}, u32[]{:S(2)}) copy-start(bf16[192,768]{1,0:T(8,128)(2,1)} %fc1_ref.5) | copy-start | bytes 884740
  11.4 1.6 %copy-start.1 = (bf16[768,192]{0,1:T(8,128)(2,1)S(1)}, bf16[768,192]{0,1:T(8,128)(2,1)}, u32[]{:S(2)}) copy-start(bf16[768,192]{0,1:T(8,128)(2,1)} %param.15) | copy-start | bytes 884740
  11.5 1.6 %copy-start.2 = (bf16[192,576]{1,0:T(8,128)(2,1)S(1)}, bf16[192,576]{1,0:T(8,128)(2,1)}, u32[]{:S(2)}) copy-start(bf16[192,576]{1,0:T(8,128)(2,1)} %qkv_ref.5) | copy-start | bytes 663556
  11.5 1.6 %copy-start.3 = (bf16[192,192]{1,0:T(8,128)(2,1)S(1)}, bf16[192,192]{1,0:T(8,128)(2,1)}, u32[]{:S(2)}) copy-start(bf16[192,192]{1,0:T(8,128)(2,1)} %proj_ref.5) | copy-start | bytes 221188
  11.5 1.6 %copy-start.4 = (f32[192]{0:T(256)S(1)}, f32[192]{0:T(256)}, u32[]{:S(2)}) copy-start(f32[192]{0:T(256)} %param.9) | copy-start | bytes 2308
  11.5 1.6 %copy-start.5 = (f32[192]{0:T(256)S(1)}, f32[192]{0:T(256)}, u32[]{:S(2)}) copy-start(f32[192]{0:T(256)} %param.13) | copy-start | bytes 2308
  12.7 2.5 %collective-permute-start.1 = (bf16[12,4,1152]{2,1,0:T(4,128)(2,1)S(1)}, bf16[12,4,1152]{2,1,0:T(4,128)(2,1)S(1)}, u32[]{:S(2)}, u32[]{:S(2)}) collective-permute-start(bf16[12,4,1152]{2,1,0:T(4,128)(2,1)S(1)} %get-tuple-element.5.own_piece), channel_id=1, source_target_pairs={{0,2},{2,0},{4,6},{6,4},{8,10},{10,8},{12,14},{14,12},{16,18},{18,... | collective-permute-start | bytes 331784 | tf_op jit(solution)/shard_map/ppermute | solution.py:35
  18.4 4.2 %collective-permute-start.3 = (bf16[2,3,4,1152]{3,2,1,0:T(4,128)(2,1)S(1)}, bf16[2,3,4,1152]{3,2,1,0:T(4,128)(2,1)S(1)}, u32[]{:S(2)}, u32[]{:S(2)}) collective-permute-start(bf16[2,3,4,1152]{3,2,1,0:T(4,128)(2,1)S(1)} %pad_maximum_fusion.1), channel_id=1, source_target_pairs={{0,1},{1,0},{2,3},{3,2},{4,5},{5,4},{6,7},{7,6},{8,9},{9,8},{10,11... | collective-permute-start | bytes 165896 | tf_op jit(solution)/shard_map/ppermute | solution.py:26

commit v3 on v2

--- a/solution.py
+++ b/solution.py
@@ -35,7 +35,8 @@
     return lax.ppermute(x, axis, pairs)
 
 
-def table_kernel(last_ref, bias_ref, table_ref):
+def table_kernel(last_ref, bias_ref, field_ref, table_ref, kept_ref):
+    kept_ref[...] = field_ref[EDGE:]
     heads = bias_ref.shape[2]
     width = 9 * LANES
     lane = lax.broadcasted_iota(jnp.int32, (1, LANES), 1)
@@ -131,11 +132,11 @@
 
     for n in range(len(windows)):
         for row in range(WIN_LAT):
-            for col, block in split(halo_piece, n * WIN_LAT + row):
+            for col, block in split(halo_piece, windows[n] * WIN_LAT + row):
                 at = pl.ds(row * WIN_LON + col + halo_at, LEVELS, stride=QUERIES)
                 for part in range(2):
                     keys_ref[n, part, at, :] = block[part]
-            for col, block in split(own_piece, n * WIN_LAT + row):
+            for col, block in split(own_piece, windows[n] * WIN_LAT + row):
                 at = pl.ds(row * WIN_LON + col + own_at, LEVELS, stride=QUERIES)
                 place = row * HALF + col
                 for part in range(2):
@@ -212,23 +213,14 @@
 
 def run_side(right, own, halo, table, windows, weights, chans, heads):
     count = len(windows)
-    first = windows[0]
-    assert list(windows) == list(range(first, first + count)) and first % count == 0
-    rows = count * WIN_LAT
-    piece = pl.BlockSpec((rows,) + own.shape[1:], lambda _: (first // count, 0, 0))
-
-    def whole(x):
-        return pl.BlockSpec(x.shape, lambda _: (0,) * len(x.shape))
-
-    out = jax.ShapeDtypeStruct((rows,) + own.shape[1:], jnp.bfloat16)
+    vmem = pl.BlockSpec(memory_space=pltpu.VMEM)
+    out = jax.ShapeDtypeStruct((count * WIN_LAT,) + own.shape[1:], jnp.bfloat16)
     gain1, qkv, proj, gain2, fc1, fc2 = weights
     return pl.pallas_call(
         functools.partial(side_kernel, chans, heads, windows),
         out_shape=out,
-        grid=(1,),
-        in_specs=[pl.BlockSpec(memory_space=pltpu.SMEM), piece, piece]
-        + [whole(x) for x in (gain1, qkv, proj, table, gain2, fc1, fc2)],
-        out_specs=whole(out),
+        in_specs=[pl.BlockSpec(memory_space=pltpu.SMEM)] + [vmem] * 9,
+        out_specs=vmem,
         scratch_shapes=[
             pltpu.VMEM((count, 2, LEVELS * QUERIES, LANES), jnp.float32),
             pltpu.VMEM((count, 2, 184, LANES), jnp.float32),
@@ -253,19 +245,20 @@
     south = moved(field[:EDGE], "lat", -1)
     odd = lax.axis_index("lon") % 2
     last = (lax.axis_index("lat") == lax.axis_size("lat") - 1).astype(jnp.int32).reshape(1)
-    table = pl.pallas_call(
+    vmem = pl.BlockSpec(memory_space=pltpu.VMEM)
+    table, kept = pl.pallas_call(
         table_kernel,
-        out_shape=jax.ShapeDtypeStruct((2, 2, 2, 2, heads * QUERIES, LANES), jnp.float32),
-        in_specs=[
-            pl.BlockSpec(memory_space=pltpu.SMEM),
-            pl.BlockSpec(memory_space=pltpu.VMEM),
+        out_shape=[
+            jax.ShapeDtypeStruct((2, 2, 2, 2, heads * QUERIES, LANES), jnp.float32),
+            jax.ShapeDtypeStruct((rows - EDGE, levels, flat), field.dtype),
         ],
-        out_specs=pl.BlockSpec(memory_space=pltpu.VMEM),
+        in_specs=[pl.BlockSpec(memory_space=pltpu.SMEM), vmem, vmem],
+        out_specs=[vmem, vmem],
         compiler_params=pltpu.CompilerParams(vmem_limit_bytes=32 * 2**20),
         cost_estimate=pl.CostEstimate(flops=4_000_000, bytes_accessed=6_000_000, transcendentals=0),
         name="bias_tables",
-    )(last, earth_bias)
-    tokens = jnp.concatenate([field[EDGE:], south], axis=0)
+    )(last, earth_bias, field)
+    tokens = jnp.concatenate([kept, south], axis=0)
     left, right = tokens[:, :, :half], tokens[:, :, half:]
     near = jnp.where(odd == 1, left, right)
     far = jnp.where(odd == 1, right, left)
@@ -281,6 +274,7 @@
     )
     near_right, far_right = (1 - odd).reshape(1), odd.reshape(1)
     near_done = run_side(near_right, near, near_halo, table, (0, 1), weights, chans, heads)
+    far_halo, near_done = lax.optimization_barrier((far_halo, near_done))
     far_low = run_side(far_right, far, far_halo, table, (1,), weights, chans, heads)
     top = moved(jnp.stack([near_done[WIN_LAT + EDGE :], far_low[EDGE:]]), "lat", 1)
     far_high = run_side(far_right, far, far_halo, table, (0,), weights, chans, heads)

time: 23.7 us -> 32.8 us (1.38)
  local copies, waits for them, and re-layouts: 3.83 us -> 9.43 us
  Pallas kernels: 8.43 us -> 11.4 us
  other arithmetic: 1.02 us -> 2.65 us
  waiting for transfers between devices: 1.42 us -> 0.48 us
  starting transfers between devices: 8.6 us -> 8.26 us
    unnamed x13 -> x20, local copies, waits for them, and re-layouts: 1.93 us -> 6.44 us
    pallas_call x3, Pallas kernels: 7.27 us -> 10.2 us  [run_side(): pl.pallas_call(functools.partial(side_kernel, chans, heads, windows), out...]
    select_n x1, other arithmetic: 0.12 us -> 1.75 us  [shards(): near = jnp.where(odd == 1, left, right)]
    ppermute x2, starting transfers between devices: 5.09 us -> 3.59 us  [moved(): return lax.ppermute(x, axis, [(i, (i + by) % size) for i in range(size)])]
    concatenate x0 -> x1, local copies, waits for them, and re-layouts: none -> 1.46 us  [shards(): tokens = jnp.concatenate([kept, south], axis=0)]
    ppermute x2, starting transfers between devices: 3.51 us -> 4.67 us  [swapped(): return lax.ppermute(x, axis, pairs)]
    slice x1 -> x0, local copies, waits for them, and re-layouts: 0.97 us -> none  [shards(): tokens = jnp.concatenate([field[EDGE:], south], axis=0)]
    ppermute x2, waiting for transfers between devices: 1.15 us -> 0.47 us  [moved(): return lax.ppermute(x, axis, [(i, (i + by) % size) for i in range(size)])]
  transfers between devices with their start and end apart: 4 -> 4, of which waited for: 2 -> 1; matrix products, arithmetic and copies ran while one was open for 12% -> 8% of each run, Pallas kernels for 23% -> 26%
where the time goes in v3:
time: 32.8 us; the launch traced here: 32.3 us
  Pallas kernels  11.4 us (35%)
  local copies, waits for them, and re-layouts  9.43 us (29%)
  starting transfers between devices  8.26 us (25%)
  other arithmetic  2.65 us (8%)
  waiting for transfers between devices  0.48 us (1%)
    pallas_call x3, Pallas kernels, run_side(): pl.pallas_call(functools.partial(side_kernel, chans, heads, windows), out...  10.2 us
    unnamed x20, local copies, waits for them, and re-layouts  6.44 us
    ppermute x2, starting transfers between devices, swapped(): return lax.ppermute(x, axis, pairs)  4.67 us
    ppermute x2, starting transfers between devices, moved(): return lax.ppermute(x, axis, [(i, (i + by) % size) for i in range(size)])  3.59 us
    select_n x1, other arithmetic, shards(): near = jnp.where(odd == 1, left, right)  1.75 us
    concatenate x1, local copies, waits for them, and re-layouts, shards(): tokens = jnp.concatenate([kept, south], axis=0)  1.46 us
    slice x1, local copies, waits for them, and re-layouts, shards(): south = moved(field[:EDGE], 'lat', -1)  1.45 us
    pallas_call x1, Pallas kernels, shards(): pl.pallas_call(table_kernel, out_shape=[jax.ShapeDtypeStruct((2, 2, 2, 2,...  1.18 us
  transfers between devices with their start and end apart: 4, of which 1 were waited for; matrix products, arithmetic and copies ran while one was open for 8% of the time, Pallas kernels for 26%

profile of v3, /device:TPU:0, one launch (start us, length us, event | category | flops | bytes accessed | tf_op | source)
XLA Modules:
  0.0 32.3 jit_solution(12818020179125818298)
XLA Ops:
  0.0 1.5 %slice.36 = bf16[3,4,2304]{2,1,0:T(4,128)(2,1)} slice(bf16[12,4,2304]{2,1,0:T(4,128)(2,1)} %bitcast.20), slice={[0:3], [0:4], [0:2304]} | slice | bytes 110592 | tf_op jit(solution)/shard_map/slice | solution.py:245
  1.5 2.9 %collective-permute-start = (bf16[3,4,2304]{2,1,0:T(4,128)(2,1)}, bf16[3,4,2304]{2,1,0:T(4,128)(2,1)}, u32[]{:S(2)}, u32[]{:S(2)}) collective-permute-start(bf16[3,4,2304]{2,1,0:T(4,128)(2,1)} %slice.36), channel_id=1, source_target_pairs={{0,1},{1,0},{2,3},{3,2},{4,5},{5,4},{6,7},{7,6},{8,9},{9,8},{10,11... | collective-permute-start | bytes 165896 | tf_op jit(solution)/shard_map/ppermute | solution.py:26
  4.4 0.0 copy-start.6
  4.4 1.9 %copy.9.bias_ref = f32[2,2,6,20736]{3,2,1,0:T(8,128)S(1)} copy(f32[2,2,6,20736]{3,1,2,0:T(2,128)} %param.12) | data formatting | bytes 3981312 | tf_op args[4]
  6.3 0.0 copy-start.7
  6.3 0.0 copy-start.8
  6.4 0.0 copy-done.6
  6.4 1.2 %bias_tables.1 = (f32[2,2,2,2,432,128]{5,4,3,2,1,0:T(8,128)S(1)}, bf16[9,4,2304]{2,1,0:T(4,128)(2,1)S(1)}) custom-call(s32[1]{0:T(128)} %bitcast.last_ref, f32[2,2,6,20736]{3,2,1,0:T(8,128)S(1)} %copy.9.bias_ref, bf16[12,4,2304]{2,1,0:T(4,128)(2,1)S(1)} %bitcast.21), custom_call_target="tpu_custom_call" | custom-call | flops 4000000 | bytes 6000000 | tf_op jit(solution)/shard_map/bias_tables/pallas_call | solution.py:249
  7.6 0.7 %constant_dynamic-update-slice_fusion.1 = bf16[12,4,2304]{2,1,0:T(4,128)(2,1)} fusion(bf16[9,4,2304]{2,1,0:T(4,128)(2,1)S(1)} %get-tuple-element.9), kind=kLoop, calls=%fused_computation.10 | loop fusion | bytes 331776
  8.3 0.0 collective-permute-done
  8.3 1.5 %constant_dynamic-update-slice_fusion = bf16[12,4,2304]{2,1,0:T(4,128)(2,1)} fusion(bf16[12,4,2304]{2,1,0:T(4,128)(2,1)} %constant_dynamic-update-slice_fusion.1, bf16[3,4,2304]{2,1,0:T(4,128)(2,1)} %collective-permute-done), kind=kLoop, calls=%fused_computation.9 | loop fusion | bytes 110592 | tf_op jit(solution)/shard_map/concatenate | solution.py:261
  9.7 1.7 %broadcast_select_fusion = (bf16[12,4,1152]{2,1,0:T(4,128)(2,1)}, bf16[12,4,1152]{2,1,0:T(4,128)(2,1)}) fusion(pred[]{:T(512)S(6)} %eq.10, bf16[12,4,2304]{2,1,0:T(4,128)(2,1)} %constant_dynamic-update-slice_fusion), kind=kLoop, calls=%fused_computation.2 | loop fusion | flops 110592 | bytes 442369 | tf_op jit(solution)/shard_map/jit(_where)/select_n | solution.py:263
  11.5 0.0 collective-permute-start.2
  11.5 4.7 %collective-permute-start.1 = (bf16[12,4,1152]{2,1,0:T(4,128)(2,1)}, bf16[12,4,1152]{2,1,0:T(4,128)(2,1)}, u32[]{:S(2)}, u32[]{:S(2)}) collective-permute-start(bf16[12,4,1152]{2,1,0:T(4,128)(2,1)} %get-tuple-element.14.own_piece), channel_id=1, source_target_pairs={{2,4},{4,2},{6,8},{8,6},{10,12},{12,10},{14,16},{16,14},{18,20},{2... | collective-permute-start | bytes 331784 | tf_op jit(solution)/shard_map/ppermute | solution.py:35
  16.2 0.0 collective-permute-done.2.halo_piece
  16.2 0.0 copy-done.7
  16.2 0.0 copy-done.8
  16.2 0.0 copy-start
  16.2 1.0 %copy-done = bf16[192,768]{1,0:T(8,128)(2,1)S(1)} copy-done((bf16[192,768]{1,0:T(8,128)(2,1)S(1)}, bf16[192,768]{1,0:T(8,128)(2,1)}, u32[]{:S(2)}) %copy-start) | copy-done | bytes 294936
  17.1 0.0 copy-start.2
  17.1 1.0 %copy-done.2 = bf16[768,192]{0,1:T(8,128)(2,1)S(1)} copy-done((bf16[768,192]{0,1:T(8,128)(2,1)S(1)}, bf16[768,192]{0,1:T(8,128)(2,1)}, u32[]{:S(2)}) %copy-start.2) | copy-done | bytes 294936
  18.1 0.0 copy-start.3
  18.1 0.9 %copy-done.3 = bf16[192,576]{1,0:T(8,128)(2,1)S(1)} copy-done((bf16[192,576]{1,0:T(8,128)(2,1)S(1)}, bf16[192,576]{1,0:T(8,128)(2,1)}, u32[]{:S(2)}) %copy-start.3) | copy-done | bytes 221208
  19.0 0.0 copy-start.5
  19.0 0.9 %copy-done.5 = bf16[192,192]{1,0:T(8,128)(2,1)S(1)} copy-done((bf16[192,192]{1,0:T(8,128)(2,1)S(1)}, bf16[192,192]{1,0:T(8,128)(2,1)}, u32[]{:S(2)}) %copy-start.5) | copy-done | bytes 73752
  19.9 0.0 copy-start.1
  19.9 0.0 copy-start.4
  19.9 4.1 %swin_side.3 = bf16[12,4,1152]{2,1,0:T(4,128)(2,1)S(1)} custom-call(s32[1]{0:T(128)} %bitcast.2.right_ref, bf16[12,4,1152]{2,1,0:T(4,128)(2,1)} %get-tuple-element.13.own_piece, bf16[12,4,1152]{2,1,0:T(4,128)(2,1)} %collective-permute-done.2.halo_piece, f32[1,192]{1,0:T(1,128)S(1)} %bitcast.22, bf16[192,576]{1,0:T(8,128)(2,1)S(1)} %copy-done.3, ...), custom_call_target="tpu_custom_call" | custom-call | flops 400000000 | bytes 3000000 | tf_op jit(solution)/shard_map/swin_side/pallas_call | solution.py:219
  24.0 0.0 collective-permute-done.1.halo_piece
  24.0 0.0 copy-done.1
  24.0 0.0 copy-done.4
  24.0 3.1 %swin_side.4 = bf16[6,4,1152]{2,1,0:T(4,128)(2,1)S(1)} custom-call(s32[1]{0:T(128)} %bitcast.7.right_ref, bf16[12,4,1152]{2,1,0:T(4,128)(2,1)} %get-tuple-element.14.own_piece, bf16[12,4,1152]{2,1,0:T(4,128)(2,1)} %collective-permute-done.1.halo_piece, f32[1,192]{1,0:T(1,128)S(1)} %bitcast.23, bf16[192,576]{1,0:T(8,128)(2,1)S(1)} %copy-done.4, ...), custom_call_target="tpu_custom_call" | custom-call | flops 200000000 | bytes 3000000 | tf_op jit(solution)/shard_map/swin_side/pallas_call | solution.py:219
  27.2 0.7 %collective-permute-start.3 = (bf16[2,3,4,1152]{3,2,1,0:T(4,128)(2,1)S(1)}, bf16[2,3,4,1152]{3,2,1,0:T(4,128)(2,1)S(1)}, u32[]{:S(2)}, u32[]{:S(2)}) collective-permute-start(bf16[2,3,4,1152]{3,2,1,0:T(4,128)(2,1)S(1)} %pad_maximum_fusion), channel_id=1, source_target_pairs={{0,1},{1,0},{2,3},{3,2},{4,5},{5,4},{6,7},{7,6},{8,9},{9,8},{10,11... | collective-permute-start | bytes 165896 | tf_op jit(solution)/shard_map/ppermute | solution.py:26
  27.9 3.1 %swin_side.5 = bf16[6,4,1152]{2,1,0:T(4,128)(2,1)S(1)} custom-call(s32[1]{0:T(128)} %bitcast.7.right_ref, bf16[12,4,1152]{2,1,0:T(4,128)(2,1)} %get-tuple-element.14.own_piece, bf16[12,4,1152]{2,1,0:T(4,128)(2,1)} %collective-permute-done.1.halo_piece, f32[1,192]{1,0:T(1,128)S(1)} %bitcast.24, bf16[192,576]{1,0:T(8,128)(2,1)S(1)} %copy-done.4, ...), custom_call_target="tpu_custom_call" | custom-call | flops 200000000 | bytes 3000000 | tf_op jit(solution)/shard_map/swin_side/pallas_call | solution.py:219
  31.0 0.5 %collective-permute-done.3 = bf16[2,3,4,1152]{3,2,1,0:T(4,128)(2,1)S(1)} collective-permute-done((bf16[2,3,4,1152]{3,2,1,0:T(4,128)(2,1)S(1)}, bf16[2,3,4,1152]{3,2,1,0:T(4,128)(2,1)S(1)}, u32[]{:S(2)}, u32[]{:S(2)}) %collective-permute-start.3) | collective-permute-done | bytes 55328 | tf_op jit(solution)/shard_map/ppermute | solution.py:26
  31.5 0.9 %fusion = bf16[4,12,2304]{2,0,1:T(4,128)(2,1)} fusion(bf16[3,4,1152]{2,1,0:T(4,128)(2,1)S(1)} %get-tuple-element.18, bf16[6,4,1152]{2,1,0:T(4,128)(2,1)S(1)} %swin_side.5, bf16[3,4,1152]{2,1,0:T(4,128)(2,1)S(1)} %get-tuple-element.16, bf16[9,4,1152]{2,1,0:T(4,128)(2,1)S(1)} %slice.33, bf16[3,4,1152]{2,1,0:T(4,128)(2,1)S(1)} %get-tuple-element.15, pred[]{:T(512)S(6)} %eq.10), kind=kLoop, calls=%fused_computation.1 | loop fusion | flops 2322432 | bytes 442369 | tf_op jit(solution)/shard_map/transpose | solution.py:288
  (5 shorter events, 0.1 us)
Async XLA Ops:
  1.5 6.8 %collective-permute-start = (bf16[3,4,2304]{2,1,0:T(4,128)(2,1)}, bf16[3,4,2304]{2,1,0:T(4,128)(2,1)}, u32[]{:S(2)}, u32[]{:S(2)}) collective-permute-start(bf16[3,4,2304]{2,1,0:T(4,128)(2,1)} %slice.36), channel_id=1, source_target_pairs={{0,1},{1,0},{2,3},{3,2},{4,5},{5,4},{6,7},{7,6},{8,9},{9,8},{10,11... | collective-permute-start | bytes 165896 | tf_op jit(solution)/shard_map/ppermute | solution.py:26
  4.4 2.0 %copy-start.6 = (bf16[4,12,2304]{2,0,1:T(4,128)(2,1)S(1)}, bf16[4,12,2304]{2,0,1:T(4,128)(2,1)}, u32[]{:S(2)}) copy-start(bf16[4,12,2304]{2,0,1:T(4,128)(2,1)} %param.8) | copy-start | bytes 663556
  6.3 9.8 %copy-start.7 = (f32[192]{0:T(256)S(1)}, f32[192]{0:T(256)}, u32[]{:S(2)}) copy-start(f32[192]{0:T(256)} %param.9) | copy-start | bytes 2308
  6.3 9.8 %copy-start.8 = (f32[192]{0:T(256)S(1)}, f32[192]{0:T(256)}, u32[]{:S(2)}) copy-start(f32[192]{0:T(256)} %param.13) | copy-start | bytes 2308
  11.5 4.7 %collective-permute-start.2 = (bf16[12,4,1152]{2,1,0:T(4,128)(2,1)}, bf16[12,4,1152]{2,1,0:T(4,128)(2,1)}, u32[]{:S(2)}, u32[]{:S(2)}) collective-permute-start(bf16[12,4,1152]{2,1,0:T(4,128)(2,1)} %get-tuple-element.13.own_piece), channel_id=1, source_target_pairs={{0,2},{2,0},{4,6},{6,4},{8,10},{10,8},{12,14},{14,12},{16,18},{18,... | collective-permute-start | bytes 331784 | tf_op jit(solution)/shard_map/ppermute | solution.py:35
  11.5 12.5 %collective-permute-start.1 = (bf16[12,4,1152]{2,1,0:T(4,128)(2,1)}, bf16[12,4,1152]{2,1,0:T(4,128)(2,1)}, u32[]{:S(2)}, u32[]{:S(2)}) collective-permute-start(bf16[12,4,1152]{2,1,0:T(4,128)(2,1)} %get-tuple-element.14.own_piece), channel_id=1, source_target_pairs={{2,4},{4,2},{6,8},{8,6},{10,12},{12,10},{14,16},{16,14},{18,20},{2... | collective-permute-start | bytes 331784 | tf_op jit(solution)/shard_map/ppermute | solution.py:35
  16.2 1.0 %copy-start = (bf16[192,768]{1,0:T(8,128)(2,1)S(1)}, bf16[192,768]{1,0:T(8,128)(2,1)}, u32[]{:S(2)}) copy-start(bf16[192,768]{1,0:T(8,128)(2,1)} %fc1_ref.5) | copy-start | bytes 884740
  17.1 1.0 %copy-start.2 = (bf16[768,192]{0,1:T(8,128)(2,1)S(1)}, bf16[768,192]{0,1:T(8,128)(2,1)}, u32[]{:S(2)}) copy-start(bf16[768,192]{0,1:T(8,128)(2,1)} %param.15) | copy-start | bytes 884740
  18.1 0.9 %copy-start.3 = (bf16[192,576]{1,0:T(8,128)(2,1)S(1)}, bf16[192,576]{1,0:T(8,128)(2,1)}, u32[]{:S(2)}) copy-start(bf16[192,576]{1,0:T(8,128)(2,1)} %qkv_ref.5) | copy-start | bytes 663556
  19.0 0.9 %copy-start.5 = (bf16[192,192]{1,0:T(8,128)(2,1)S(1)}, bf16[192,192]{1,0:T(8,128)(2,1)}, u32[]{:S(2)}) copy-start(bf16[192,192]{1,0:T(8,128)(2,1)} %proj_ref.5) | copy-start | bytes 221188
  19.9 4.1 %copy-start.1 = (bf16[192,768]{1,0:T(8,128)(2,1)S(1)}, bf16[192,768]{1,0:T(8,128)(2,1)}, u32[]{:S(2)}) copy-start(bf16[192,768]{1,0:T(8,128)(2,1)} %fc1_ref.5) | copy-start | bytes 884740
  19.9 4.1 %copy-start.4 = (bf16[192,576]{1,0:T(8,128)(2,1)S(1)}, bf16[192,576]{1,0:T(8,128)(2,1)}, u32[]{:S(2)}) copy-start(bf16[192,576]{1,0:T(8,128)(2,1)} %qkv_ref.5) | copy-start | bytes 663556
  27.2 4.2 %collective-permute-start.3 = (bf16[2,3,4,1152]{3,2,1,0:T(4,128)(2,1)S(1)}, bf16[2,3,4,1152]{3,2,1,0:T(4,128)(2,1)S(1)}, u32[]{:S(2)}, u32[]{:S(2)}) collective-permute-start(bf16[2,3,4,1152]{3,2,1,0:T(4,128)(2,1)S(1)} %pad_maximum_fusion), channel_id=1, source_target_pairs={{0,1},{1,0},{2,3},{3,2},{4,5},{5,4},{6,7},{7,6},{8,9},{9,8},{10,11... | collective-permute-start | bytes 165896 | tf_op jit(solution)/shard_map/ppermute | solution.py:26

commit v4 on v3

--- a/solution.py
+++ b/solution.py
@@ -35,7 +35,7 @@
     return lax.ppermute(x, axis, pairs)
 
 
-def table_kernel(last_ref, bias_ref, field_ref, table_ref, kept_ref):
+def table_kernel(last_ref, bias_ref, field_ref, table_out, kept_ref, table_ref, sems):
     kept_ref[...] = field_ref[EDGE:]
     heads = bias_ref.shape[2]
     width = 9 * LANES
@@ -53,6 +53,7 @@
             out = out + jnp.where(key_side != side, last, 0.0)
         return out
 
+    copies = []
     for k in range(2):
         for p in range(2):
             masks = {}
@@ -85,6 +86,10 @@
                     at = pl.ds(place, heads, stride=QUERIES)
                     table_ref[k, p, 1 - side, 0, at, :] = main * LOG2E + mask[0]
                     table_ref[k, p, 1 - side, 1, at, :] = nxt * LOG2E + mask[1]
+            copies.append(pltpu.make_async_copy(table_ref.at[k, p], table_out.at[k, p], sems.at[k, p]))
+            copies[-1].start()
+    for copy in copies:
+        copy.wait()
 
 
 def layer_norm(values, gain):
@@ -101,20 +106,43 @@
     own_piece,
     halo_piece,
     gain1_ref,
-    qkv_ref,
-    proj_ref,
-    table_ref,
     gain2_ref,
-    fc1_ref,
-    fc2_ref,
+    qkv_any,
+    table_any,
+    proj_any,
+    fc1_any,
+    fc2_any,
     out_ref,
     keys_ref,
     own_ref,
     res_ref,
+    qkv_ref,
+    table_ref,
+    proj_ref,
+    fc1_ref,
+    fc2_ref,
+    sems,
 ):
     head_dim = chans // heads
     low = lax.broadcasted_iota(jnp.int32, (1, LANES), 1) < SPARE
     right = right_ref[0]
+
+    def fetch(source, target, sem):
+        copy = pltpu.make_async_copy(source, target, sems.at[sem])
+        copy.start()
+        return copy
+
+    qkv_copy = fetch(qkv_any, qkv_ref, 0)
+    table_copies = {}
+    for n in range(len(windows)):
+        for p in range(2):
+            source = table_any.at[windows[n], p, right]
+            table_copies[n, p] = fetch(source, table_ref.at[n, p], 4 + 2 * n + p)
+    late_copies = [
+        fetch(proj_any, proj_ref, 1),
+        fetch(fc1_any, fc1_ref, 2),
+        fetch(fc2_any, fc2_ref, 3),
+    ]
     halo_at = right * HALF
     own_at = HALF - halo_at
 
@@ -148,6 +176,7 @@
     lane = lax.broadcasted_iota(jnp.int32, (1, chans), 1)
     ones = jnp.ones((LEVELS * QUERIES, 2 * LANES - chans), jnp.float32)
     mixed = []
+    qkv_copy.wait()
     for n in range(len(windows)):
         normed = layer_norm(tokens_of(keys_ref, n, 0, LEVELS * QUERIES), gain1)
         normed = jnp.concatenate([normed[QUERIES:], normed[:QUERIES]], axis=0)
@@ -168,7 +197,8 @@
             ]
             picked = jnp.concatenate(picked, axis=0).astype(jnp.bfloat16)
             scores = lax.dot_general(picked, k, NT, preferred_element_type=jnp.float32)
-            table = [table_ref[windows[n], p, right, part] for part in range(2)]
+            table_copies[n, p].wait()
+            table = [table_ref[n, p, part] for part in range(2)]
             table = jnp.concatenate([table[0], table[1][:, : TOKENS - LANES]], axis=1)
             scores = scores + table
             top = jnp.max(scores, axis=1, keepdims=True)
@@ -182,6 +212,8 @@
                 out = jnp.where(inside, scaled, out)
             mixed.append(out)
     mixed = jnp.concatenate(mixed, axis=0).astype(jnp.bfloat16)
+    for copy in late_copies:
+        copy.wait()
     attn = jnp.dot(mixed, proj_ref[...], preferred_element_type=jnp.float32)
     attn = attn.astype(jnp.bfloat16).astype(jnp.float32)
     tokens = [tokens_of(own_ref, n, 40, 144) for n in range(len(windows))]
@@ -219,19 +251,27 @@
     return pl.pallas_call(
         functools.partial(side_kernel, chans, heads, windows),
         out_shape=out,
-        in_specs=[pl.BlockSpec(memory_space=pltpu.SMEM)] + [vmem] * 9,
+        in_specs=[pl.BlockSpec(memory_space=pltpu.SMEM)]
+        + [vmem] * 4
+        + [pl.BlockSpec(memory_space=pl.ANY)] * 5,
         out_specs=vmem,
         scratch_shapes=[
             pltpu.VMEM((count, 2, LEVELS * QUERIES, LANES), jnp.float32),
             pltpu.VMEM((count, 2, 184, LANES), jnp.float32),
             pltpu.VMEM((count, 2, 184, LANES), jnp.float32),
+            pltpu.VMEM(qkv.shape, qkv.dtype),
+            pltpu.VMEM((count, 2) + table.shape[3:], table.dtype),
+            pltpu.VMEM(proj.shape, proj.dtype),
+            pltpu.VMEM(fc1.shape, fc1.dtype),
+            pltpu.VMEM(fc2.shape, fc2.dtype),
+            pltpu.SemaphoreType.DMA((4 + 2 * count,)),
         ],
-        compiler_params=pltpu.CompilerParams(vmem_limit_bytes=32 * 2**20),
+        compiler_params=pltpu.CompilerParams(vmem_limit_bytes=24 * 2**20),
         cost_estimate=pl.CostEstimate(
             flops=200_000_000 * count, bytes_accessed=3_000_000, transcendentals=250_000 * count
         ),
         name="swin_side",
-    )(right, own, halo, gain1, qkv, proj, table, gain2, fc1, fc2)
+    )(right, own, halo, gain1, gain2, qkv, table, proj, fc1, fc2)
 
 
 def shards(
@@ -246,14 +286,19 @@
     odd = lax.axis_index("lon") % 2
     last = (lax.axis_index("lat") == lax.axis_size("lat") - 1).astype(jnp.int32).reshape(1)
     vmem = pl.BlockSpec(memory_space=pltpu.VMEM)
+    table_shape = (2, 2, 2, 2, heads * QUERIES, LANES)
     table, kept = pl.pallas_call(
         table_kernel,
         out_shape=[
-            jax.ShapeDtypeStruct((2, 2, 2, 2, heads * QUERIES, LANES), jnp.float32),
+            jax.ShapeDtypeStruct(table_shape, jnp.float32),
             jax.ShapeDtypeStruct((rows - EDGE, levels, flat), field.dtype),
         ],
         in_specs=[pl.BlockSpec(memory_space=pltpu.SMEM), vmem, vmem],
-        out_specs=[vmem, vmem],
+        out_specs=[pl.BlockSpec(memory_space=pl.ANY), vmem],
+        scratch_shapes=[
+            pltpu.VMEM(table_shape, jnp.float32),
+            pltpu.SemaphoreType.DMA((2, 2)),
+        ],
         compiler_params=pltpu.CompilerParams(vmem_limit_bytes=32 * 2**20),
         cost_estimate=pl.CostEstimate(flops=4_000_000, bytes_accessed=6_000_000, transcendentals=0),
         name="bias_tables",

time: 32.8 us -> 39.3 us (1.20)
  Pallas kernels: 11.4 us -> 18.4 us
  waiting for transfers between devices: 0.48 us -> 0.01 us
    pallas_call x3, Pallas kernels: 10.2 us -> 16.3 us  [run_side(): pl.pallas_call(functools.partial(side_kernel, chans, heads, windows), out...]
    pallas_call x1, Pallas kernels: 1.18 us -> 2.11 us  [shards(): pl.pallas_call(table_kernel, out_shape=[jax.ShapeDtypeStruct(table_shape,...]
    ppermute x2, waiting for transfers between devices: 0.47 us -> 0.01 us  [moved(): return lax.ppermute(x, axis, [(i, (i + by) % size) for i in range(size)])]
  transfers between devices with their start and end apart: 4 -> 4, of which waited for: 1 -> 0; matrix products, arithmetic and copies ran while one was open for 8% -> 7% of each run, Pallas kernels for 26% -> 35%
where the time goes in v4:
time: 39.3 us; the launch traced here: 38.9 us
  Pallas kernels  18.4 us (47%)
  local copies, waits for them, and re-layouts  9.43 us (24%)
  starting transfers between devices  8.2 us (21%)
  other arithmetic  2.65 us (7%)
    pallas_call x3, Pallas kernels, run_side(): pl.pallas_call(functools.partial(side_kernel, chans, heads, windows), out...  16.3 us
    unnamed x20, local copies, waits for them, and re-layouts  6.44 us
    ppermute x2, starting transfers between devices, swapped(): return lax.ppermute(x, axis, pairs)  4.67 us
    ppermute x2, starting transfers between devices, moved(): return lax.ppermute(x, axis, [(i, (i + by) % size) for i in range(size)])  3.53 us
    pallas_call x1, Pallas kernels, shards(): pl.pallas_call(table_kernel, out_shape=[jax.ShapeDtypeStruct(table_shape,...  2.11 us
    select_n x1, other arithmetic, shards(): near = jnp.where(odd == 1, left, right)  1.75 us
    concatenate x1, local copies, waits for them, and re-layouts, shards(): tokens = jnp.concatenate([kept, south], axis=0)  1.46 us
    slice x1, local copies, waits for them, and re-layouts, shards(): south = moved(field[:EDGE], 'lat', -1)  1.45 us
  transfers between devices with their start and end apart: 4, of which 0 were waited for; matrix products, arithmetic and copies ran while one was open for 7% of the time, Pallas kernels for 35%

profile of v4, /device:TPU:0, one launch (start us, length us, event | category | flops | bytes accessed | tf_op | source)
XLA Modules:
  0.0 38.9 jit_solution(5147358455135377624)
XLA Ops:
  0.0 1.5 %slice.36 = bf16[3,4,2304]{2,1,0:T(4,128)(2,1)} slice(bf16[12,4,2304]{2,1,0:T(4,128)(2,1)} %bitcast.20), slice={[0:3], [0:4], [0:2304]} | slice | bytes 110592 | tf_op jit(solution)/shard_map/slice | solution.py:285
  1.5 2.9 %collective-permute-start = (bf16[3,4,2304]{2,1,0:T(4,128)(2,1)}, bf16[3,4,2304]{2,1,0:T(4,128)(2,1)}, u32[]{:S(2)}, u32[]{:S(2)}) collective-permute-start(bf16[3,4,2304]{2,1,0:T(4,128)(2,1)} %slice.36), channel_id=1, source_target_pairs={{0,1},{1,0},{2,3},{3,2},{4,5},{5,4},{6,7},{7,6},{8,9},{9,8},{10,11... | collective-permute-start | bytes 165896 | tf_op jit(solution)/shard_map/ppermute | solution.py:26
  4.4 0.0 copy-start.6
  4.4 1.9 %copy.9.bias_ref = f32[2,2,6,20736]{3,2,1,0:T(8,128)S(1)} copy(f32[2,2,6,20736]{3,1,2,0:T(2,128)} %param.12) | data formatting | bytes 3981312 | tf_op args[4]
  6.3 0.0 copy-start.7
  6.3 0.0 copy-start.8
  6.4 0.0 copy-done.6
  6.4 2.1 %bias_tables.1 = (f32[2,2,2,2,432,128]{5,4,3,2,1,0:T(8,128)S(1)}, bf16[9,4,2304]{2,1,0:T(4,128)(2,1)S(1)}) custom-call(s32[1]{0:T(128)} %bitcast.last_ref, f32[2,2,6,20736]{3,2,1,0:T(8,128)S(1)} %copy.9.bias_ref, bf16[12,4,2304]{2,1,0:T(4,128)(2,1)S(1)} %bitcast.21), custom_call_target="tpu_custom_call" | custom-call | flops 4000000 | bytes 6000000 | tf_op jit(solution)/shard_map/bias_tables/pallas_call | solution.py:290
  8.5 0.7 %constant_dynamic-update-slice_fusion.1 = bf16[12,4,2304]{2,1,0:T(4,128)(2,1)} fusion(bf16[9,4,2304]{2,1,0:T(4,128)(2,1)S(1)} %get-tuple-element.9), kind=kLoop, calls=%fused_computation.10 | loop fusion | bytes 331776
  9.2 0.0 collective-permute-done
  9.2 1.5 %constant_dynamic-update-slice_fusion = bf16[12,4,2304]{2,1,0:T(4,128)(2,1)} fusion(bf16[12,4,2304]{2,1,0:T(4,128)(2,1)} %constant_dynamic-update-slice_fusion.1, bf16[3,4,2304]{2,1,0:T(4,128)(2,1)} %collective-permute-done), kind=kLoop, calls=%fused_computation.9 | loop fusion | bytes 110592 | tf_op jit(solution)/shard_map/concatenate | solution.py:306
  10.7 1.7 %broadcast_select_fusion = (bf16[12,4,1152]{2,1,0:T(4,128)(2,1)}, bf16[12,4,1152]{2,1,0:T(4,128)(2,1)}) fusion(pred[]{:T(512)S(6)} %eq.10, bf16[12,4,2304]{2,1,0:T(4,128)(2,1)} %constant_dynamic-update-slice_fusion), kind=kLoop, calls=%fused_computation.2 | loop fusion | flops 110592 | bytes 442369 | tf_op jit(solution)/shard_map/jit(_where)/select_n | solution.py:308
  12.4 0.0 collective-permute-start.2
  12.4 4.7 %collective-permute-start.1 = (bf16[12,4,1152]{2,1,0:T(4,128)(2,1)}, bf16[12,4,1152]{2,1,0:T(4,128)(2,1)}, u32[]{:S(2)}, u32[]{:S(2)}) collective-permute-start(bf16[12,4,1152]{2,1,0:T(4,128)(2,1)} %get-tuple-element.14.own_piece), channel_id=1, source_target_pairs={{2,4},{4,2},{6,8},{8,6},{10,12},{12,10},{14,16},{16,14},{18,20},{2... | collective-permute-start | bytes 331784 | tf_op jit(solution)/shard_map/ppermute | solution.py:35
  17.1 0.0 collective-permute-done.2.halo_piece
  17.1 0.0 copy-done.7
  17.1 0.0 copy-done.8
  17.1 0.0 copy-start
  17.1 1.0 %copy-done = bf16[192,768]{1,0:T(8,128)(2,1)S(1)} copy-done((bf16[192,768]{1,0:T(8,128)(2,1)S(1)}, bf16[192,768]{1,0:T(8,128)(2,1)}, u32[]{:S(2)}) %copy-start) | copy-done | bytes 294936
  18.1 0.0 copy-start.2
  18.1 1.0 %copy-done.2 = bf16[768,192]{0,1:T(8,128)(2,1)S(1)} copy-done((bf16[768,192]{0,1:T(8,128)(2,1)S(1)}, bf16[768,192]{0,1:T(8,128)(2,1)}, u32[]{:S(2)}) %copy-start.2) | copy-done | bytes 294936
  19.0 0.0 copy-start.3
  19.0 0.9 %copy-done.3 = bf16[192,576]{1,0:T(8,128)(2,1)S(1)} copy-done((bf16[192,576]{1,0:T(8,128)(2,1)S(1)}, bf16[192,576]{1,0:T(8,128)(2,1)}, u32[]{:S(2)}) %copy-start.3) | copy-done | bytes 221208
  20.0 0.0 copy-start.5
  20.0 0.9 %copy-done.5 = bf16[192,192]{1,0:T(8,128)(2,1)S(1)} copy-done((bf16[192,192]{1,0:T(8,128)(2,1)S(1)}, bf16[192,192]{1,0:T(8,128)(2,1)}, u32[]{:S(2)}) %copy-start.5) | copy-done | bytes 73752
  20.9 0.0 copy-start.1
  20.9 0.0 copy-start.4
  20.9 6.8 %swin_side.3 = bf16[12,4,1152]{2,1,0:T(4,128)(2,1)S(1)} custom-call(s32[1]{0:T(128)} %bitcast.2.right_ref, bf16[12,4,1152]{2,1,0:T(4,128)(2,1)} %get-tuple-element.13.own_piece, bf16[12,4,1152]{2,1,0:T(4,128)(2,1)} %collective-permute-done.2.halo_piece, f32[1,192]{1,0:T(1,128)S(1)} %bitcast.22, f32[1,192]{1,0:T(1,128)S(1)} %bitcast.25, ...), custom_call_target="tpu_custom_call" | custom-call | flops 400000000 | bytes 3000000 | tf_op jit(solution)/shard_map/swin_side/pallas_call | solution.py:251
  27.7 0.0 collective-permute-done.1.halo_piece
  27.7 0.0 copy-done.1
  27.7 0.0 copy-done.4
  27.7 4.8 %swin_side.4 = bf16[6,4,1152]{2,1,0:T(4,128)(2,1)S(1)} custom-call(s32[1]{0:T(128)} %bitcast.7.right_ref, bf16[12,4,1152]{2,1,0:T(4,128)(2,1)} %get-tuple-element.14.own_piece, bf16[12,4,1152]{2,1,0:T(4,128)(2,1)} %collective-permute-done.1.halo_piece, f32[1,192]{1,0:T(1,128)S(1)} %bitcast.23, f32[1,192]{1,0:T(1,128)S(1)} %bitcast.26, ...), custom_call_target="tpu_custom_call" | custom-call | flops 200000000 | bytes 3000000 | tf_op jit(solution)/shard_map/swin_side/pallas_call | solution.py:251
  32.6 0.6 %collective-permute-start.3 = (bf16[2,3,4,1152]{3,2,1,0:T(4,128)(2,1)S(1)}, bf16[2,3,4,1152]{3,2,1,0:T(4,128)(2,1)S(1)}, u32[]{:S(2)}, u32[]{:S(2)}) collective-permute-start(bf16[2,3,4,1152]{3,2,1,0:T(4,128)(2,1)S(1)} %pad_maximum_fusion), channel_id=1, source_target_pairs={{0,1},{1,0},{2,3},{3,2},{4,5},{5,4},{6,7},{7,6},{8,9},{9,8},{10,11... | collective-permute-start | bytes 165896 | tf_op jit(solution)/shard_map/ppermute | solution.py:26
  33.2 4.8 %swin_side.5 = bf16[6,4,1152]{2,1,0:T(4,128)(2,1)S(1)} custom-call(s32[1]{0:T(128)} %bitcast.7.right_ref, bf16[12,4,1152]{2,1,0:T(4,128)(2,1)} %get-tuple-element.14.own_piece, bf16[12,4,1152]{2,1,0:T(4,128)(2,1)} %collective-permute-done.1.halo_piece, f32[1,192]{1,0:T(1,128)S(1)} %bitcast.24, f32[1,192]{1,0:T(1,128)S(1)} %bitcast.27, ...), custom_call_target="tpu_custom_call" | custom-call | flops 200000000 | bytes 3000000 | tf_op jit(solution)/shard_map/swin_side/pallas_call | solution.py:251
  38.0 0.0 collective-permute-done.3
  38.0 0.9 %fusion = bf16[4,12,2304]{2,0,1:T(4,128)(2,1)} fusion(bf16[3,4,1152]{2,1,0:T(4,128)(2,1)S(1)} %get-tuple-element.18, bf16[6,4,1152]{2,1,0:T(4,128)(2,1)S(1)} %swin_side.5, bf16[3,4,1152]{2,1,0:T(4,128)(2,1)S(1)} %get-tuple-element.16, bf16[9,4,1152]{2,1,0:T(4,128)(2,1)S(1)} %slice.33, bf16[3,4,1152]{2,1,0:T(4,128)(2,1)S(1)} %get-tuple-element.15, pred[]{:T(512)S(6)} %eq.10), kind=kLoop, calls=%fused_computation.1 | loop fusion | flops 2322432 | bytes 442369 | tf_op jit(solution)/shard_map/transpose | solution.py:333
  (5 shorter events, 0.1 us)
Async XLA Ops:
  1.5 7.8 %collective-permute-start = (bf16[3,4,2304]{2,1,0:T(4,128)(2,1)}, bf16[3,4,2304]{2,1,0:T(4,128)(2,1)}, u32[]{:S(2)}, u32[]{:S(2)}) collective-permute-start(bf16[3,4,2304]{2,1,0:T(4,128)(2,1)} %slice.36), channel_id=1, source_target_pairs={{0,1},{1,0},{2,3},{3,2},{4,5},{5,4},{6,7},{7,6},{8,9},{9,8},{10,11... | collective-permute-start | bytes 165896 | tf_op jit(solution)/shard_map/ppermute | solution.py:26
  4.4 2.0 %copy-start.6 = (bf16[4,12,2304]{2,0,1:T(4,128)(2,1)S(1)}, bf16[4,12,2304]{2,0,1:T(4,128)(2,1)}, u32[]{:S(2)}) copy-start(bf16[4,12,2304]{2,0,1:T(4,128)(2,1)} %param.8) | copy-start | bytes 663556
  6.3 10.8 %copy-start.7 = (f32[192]{0:T(256)S(1)}, f32[192]{0:T(256)}, u32[]{:S(2)}) copy-start(f32[192]{0:T(256)} %param.9) | copy-start | bytes 2308
  6.3 10.8 %copy-start.8 = (f32[192]{0:T(256)S(1)}, f32[192]{0:T(256)}, u32[]{:S(2)}) copy-start(f32[192]{0:T(256)} %param.13) | copy-start | bytes 2308
  12.4 4.7 %collective-permute-start.2 = (bf16[12,4,1152]{2,1,0:T(4,128)(2,1)}, bf16[12,4,1152]{2,1,0:T(4,128)(2,1)}, u32[]{:S(2)}, u32[]{:S(2)}) collective-permute-start(bf16[12,4,1152]{2,1,0:T(4,128)(2,1)} %get-tuple-element.13.own_piece), channel_id=1, source_target_pairs={{0,2},{2,0},{4,6},{6,4},{8,10},{10,8},{12,14},{14,12},{16,18},{18,... | collective-permute-start | bytes 331784 | tf_op jit(solution)/shard_map/ppermute | solution.py:35
  12.4 15.3 %collective-permute-start.1 = (bf16[12,4,1152]{2,1,0:T(4,128)(2,1)}, bf16[12,4,1152]{2,1,0:T(4,128)(2,1)}, u32[]{:S(2)}, u32[]{:S(2)}) collective-permute-start(bf16[12,4,1152]{2,1,0:T(4,128)(2,1)} %get-tuple-element.14.own_piece), channel_id=1, source_target_pairs={{2,4},{4,2},{6,8},{8,6},{10,12},{12,10},{14,16},{16,14},{18,20},{2... | collective-permute-start | bytes 331784 | tf_op jit(solution)/shard_map/ppermute | solution.py:35
  17.1 1.0 %copy-start = (bf16[192,768]{1,0:T(8,128)(2,1)S(1)}, bf16[192,768]{1,0:T(8,128)(2,1)}, u32[]{:S(2)}) copy-start(bf16[192,768]{1,0:T(8,128)(2,1)} %fc1_any.5) | copy-start | bytes 884740
  18.1 1.0 %copy-start.2 = (bf16[768,192]{0,1:T(8,128)(2,1)S(1)}, bf16[768,192]{0,1:T(8,128)(2,1)}, u32[]{:S(2)}) copy-start(bf16[768,192]{0,1:T(8,128)(2,1)} %param.15) | copy-start | bytes 884740
  19.0 0.9 %copy-start.3 = (bf16[192,576]{1,0:T(8,128)(2,1)S(1)}, bf16[192,576]{1,0:T(8,128)(2,1)}, u32[]{:S(2)}) copy-start(bf16[192,576]{1,0:T(8,128)(2,1)} %qkv_any.5) | copy-start | bytes 663556
  20.0 0.9 %copy-start.5 = (bf16[192,192]{1,0:T(8,128)(2,1)S(1)}, bf16[192,192]{1,0:T(8,128)(2,1)}, u32[]{:S(2)}) copy-start(bf16[192,192]{1,0:T(8,128)(2,1)} %proj_any.5) | copy-start | bytes 221188
  20.9 6.8 %copy-start.1 = (bf16[192,768]{1,0:T(8,128)(2,1)S(1)}, bf16[192,768]{1,0:T(8,128)(2,1)}, u32[]{:S(2)}) copy-start(bf16[192,768]{1,0:T(8,128)(2,1)} %fc1_any.5) | copy-start | bytes 884740
  20.9 6.8 %copy-start.4 = (bf16[192,576]{1,0:T(8,128)(2,1)S(1)}, bf16[192,576]{1,0:T(8,128)(2,1)}, u32[]{:S(2)}) copy-start(bf16[192,576]{1,0:T(8,128)(2,1)} %qkv_any.5) | copy-start | bytes 663556
  32.6 5.4 %collective-permute-start.3 = (bf16[2,3,4,1152]{3,2,1,0:T(4,128)(2,1)S(1)}, bf16[2,3,4,1152]{3,2,1,0:T(4,128)(2,1)S(1)}, u32[]{:S(2)}, u32[]{:S(2)}) collective-permute-start(bf16[2,3,4,1152]{3,2,1,0:T(4,128)(2,1)S(1)} %pad_maximum_fusion), channel_id=1, source_target_pairs={{0,1},{1,0},{2,3},{3,2},{4,5},{5,4},{6,7},{7,6},{8,9},{9,8},{10,11... | collective-permute-start | bytes 165896 | tf_op jit(solution)/shard_map/ppermute | solution.py:26

commit v5 on v2

--- a/solution.py
+++ b/solution.py
@@ -35,11 +35,40 @@
     return lax.ppermute(x, axis, pairs)
 
 
-def table_kernel(last_ref, bias_ref, table_ref):
+def half_places(place_ref, half):
+    odd = place_ref[1]
+    return pl.multiple_of((1 - odd) * half, LANES), pl.multiple_of(odd * half, LANES)
+
+
+def pack_kernel(place_ref, south_ref, near_in, far_in, near_ref, far_ref):
+    near_at, far_at = half_places(place_ref, near_ref.shape[2])
+    rows = near_ref.shape[0] - EDGE
+    near_ref[:rows] = near_in[:rows]
+    far_ref[:rows] = far_in[:rows]
+    near_ref[rows:] = south_ref[:, :, pl.ds(near_at, near_ref.shape[2])]
+    far_ref[rows:] = south_ref[:, :, pl.ds(far_at, far_ref.shape[2])]
+
+
+def last_kernel(place_ref, top_ref, done_ref, out_ref, sems):
+    half = top_ref.shape[3]
+    copies = []
+    for n, at in enumerate(half_places(place_ref, half)):
+        target = out_ref.at[:EDGE, :, pl.ds(at, half)]
+        copies.append(pltpu.make_async_copy(top_ref.at[n], target, sems.at[n]))
+        copies[-1].start()
+    for copy in copies:
+        copy.wait()
+
+
+def table_kernel(place_ref, bias_ref, field_ref, table_ref, near_ref, far_ref):
+    rows = field_ref.shape[0] - EDGE
+    near_at, far_at = half_places(place_ref, near_ref.shape[2])
+    near_ref[:rows] = field_ref[EDGE:, :, pl.ds(near_at, near_ref.shape[2])]
+    far_ref[:rows] = field_ref[EDGE:, :, pl.ds(far_at, far_ref.shape[2])]
     heads = bias_ref.shape[2]
     width = 9 * LANES
     lane = lax.broadcasted_iota(jnp.int32, (1, LANES), 1)
-    last = jnp.where(last_ref[0] > 0, -1e9, 0.0).astype(jnp.float32)
+    last = jnp.where(place_ref[0] > 0, -1e9, 0.0).astype(jnp.float32)
 
     def penalty(first, lev, side, wrap):
         key = lane + first
@@ -96,7 +125,8 @@
     chans,
     heads,
     windows,
-    right_ref,
+    part_of,
+    place_ref,
     own_piece,
     halo_piece,
     gain1_ref,
@@ -106,14 +136,34 @@
     gain2_ref,
     fc1_ref,
     fc2_ref,
-    out_ref,
-    keys_ref,
-    own_ref,
-    res_ref,
+    *rest,
 ):
+    if part_of == "near":
+        out_ref, keys_ref, own_ref, res_ref = rest
+    elif part_of == "low":
+        near_ref, out_ref, send_ref, keys_ref, own_ref, res_ref = rest
+    else:
+        near_ref, low_ref, done_ref, keys_ref, own_ref, res_ref, out_ref, sems = rest
+        half = near_ref.shape[2]
+        near_at, far_at = half_places(place_ref, half)
+        done_near = done_ref.at[:, :, pl.ds(near_at, half)]
+        done_far = done_ref.at[:, :, pl.ds(far_at, half)]
+        copies = [
+            pltpu.make_async_copy(
+                near_ref.at[: WIN_LAT + EDGE], done_near.at[EDGE:], sems.at[0]
+            ),
+            pltpu.make_async_copy(
+                low_ref.at[:EDGE], done_far.at[WIN_LAT + EDGE :], sems.at[1]
+            ),
+            pltpu.make_async_copy(
+                out_ref, done_far.at[EDGE : WIN_LAT + EDGE], sems.at[2]
+            ),
+        ]
+        for copy in copies[:2]:
+            copy.start()
     head_dim = chans // heads
     low = lax.broadcasted_iota(jnp.int32, (1, LANES), 1) < SPARE
-    right = right_ref[0]
+    right = 1 - place_ref[1] if part_of == "near" else place_ref[1]
     halo_at = right * HALF
     own_at = HALF - halo_at
 
@@ -208,9 +258,16 @@
                 tiles.append(jnp.where(low, shifted[0], shifted[1]))
                 tiles = jnp.concatenate(tiles, axis=1).astype(jnp.bfloat16)
                 out_ref[n * WIN_LAT + row, :, pair * 2 * chans : (pair + 1) * 2 * chans] = tiles
-
-
-def run_side(right, own, halo, table, windows, weights, chans, heads):
+    if part_of == "low":
+        send_ref[0] = near_ref[WIN_LAT + EDGE :]
+        send_ref[1] = out_ref[EDGE:]
+    elif part_of == "high":
+        copies[2].start()
+        for copy in copies:
+            copy.wait()
+
+
+def run_side(place, own, halo, table, windows, part_of, weights, chans, heads, before):
     count = len(windows)
     first = windows[0]
     assert list(windows) == list(range(first, first + count)) and first % count == 0
@@ -220,26 +277,33 @@
     def whole(x):
         return pl.BlockSpec(x.shape, lambda _: (0,) * len(x.shape))
 
-    out = jax.ShapeDtypeStruct((rows,) + own.shape[1:], jnp.bfloat16)
+    anywhere = pl.BlockSpec(memory_space=pl.ANY)
+    out = jax.ShapeDtypeStruct((rows,) + own.shape[1:], own.dtype)
+    send = jax.ShapeDtypeStruct((2, EDGE) + own.shape[1:], own.dtype)
+    done = jax.ShapeDtypeStruct(own.shape[:2] + (2 * own.shape[2],), own.dtype)
+    outs = {"near": [out], "low": [out, send], "high": [done]}[part_of]
+    extra = [pltpu.VMEM(out.shape, out.dtype), pltpu.SemaphoreType.DMA((3,))]
     gain1, qkv, proj, gain2, fc1, fc2 = weights
+    operands = (gain1, qkv, proj, table, gain2, fc1, fc2) + before
     return pl.pallas_call(
-        functools.partial(side_kernel, chans, heads, windows),
-        out_shape=out,
+        functools.partial(side_kernel, chans, heads, windows, part_of),
+        out_shape=outs,
         grid=(1,),
         in_specs=[pl.BlockSpec(memory_space=pltpu.SMEM), piece, piece]
-        + [whole(x) for x in (gain1, qkv, proj, table, gain2, fc1, fc2)],
-        out_specs=whole(out),
+        + [whole(x) for x in operands],
+        out_specs=[anywhere] if part_of == "high" else [whole(x) for x in outs],
         scratch_shapes=[
             pltpu.VMEM((count, 2, LEVELS * QUERIES, LANES), jnp.float32),
             pltpu.VMEM((count, 2, 184, LANES), jnp.float32),
             pltpu.VMEM((count, 2, 184, LANES), jnp.float32),
-        ],
+        ]
+        + (extra if part_of == "high" else []),
         compiler_params=pltpu.CompilerParams(vmem_limit_bytes=32 * 2**20),
         cost_estimate=pl.CostEstimate(
             flops=200_000_000 * count, bytes_accessed=3_000_000, transcendentals=250_000 * count
         ),
-        name="swin_side",
-    )(right, own, halo, gain1, qkv, proj, table, gain2, fc1, fc2)
+        name="swin_" + part_of,
+    )(place, own, halo, *operands)
 
 
 def shards(
@@ -252,23 +316,31 @@
     field = jnp.transpose(field_in, (1, 0, 2))
     south = moved(field[:EDGE], "lat", -1)
     odd = lax.axis_index("lon") % 2
-    last = (lax.axis_index("lat") == lax.axis_size("lat") - 1).astype(jnp.int32).reshape(1)
-    table = pl.pallas_call(
+    last = (lax.axis_index("lat") == lax.axis_size("lat") - 1).astype(jnp.int32)
+    place = jnp.stack([last, odd])
+    smem, vmem = (pl.BlockSpec(memory_space=m) for m in (pltpu.SMEM, pltpu.VMEM))
+    piece = jax.ShapeDtypeStruct((rows, levels, half), field.dtype)
+    table, near, far = pl.pallas_call(
         table_kernel,
-        out_shape=jax.ShapeDtypeStruct((2, 2, 2, 2, heads * QUERIES, LANES), jnp.float32),
-        in_specs=[
-            pl.BlockSpec(memory_space=pltpu.SMEM),
-            pl.BlockSpec(memory_space=pltpu.VMEM),
+        out_shape=[
+            jax.ShapeDtypeStruct((2, 2, 2, 2, heads * QUERIES, LANES), jnp.float32),
+            piece,
+            piece,
         ],
-        out_specs=pl.BlockSpec(memory_space=pltpu.VMEM),
+        in_specs=[smem, vmem, vmem],
+        out_specs=[vmem] * 3,
         compiler_params=pltpu.CompilerParams(vmem_limit_bytes=32 * 2**20),
         cost_estimate=pl.CostEstimate(flops=4_000_000, bytes_accessed=6_000_000, transcendentals=0),
         name="bias_tables",
-    )(last, earth_bias)
-    tokens = jnp.concatenate([field[EDGE:], south], axis=0)
-    left, right = tokens[:, :, :half], tokens[:, :, half:]
-    near = jnp.where(odd == 1, left, right)
-    far = jnp.where(odd == 1, right, left)
+    )(place, earth_bias, field)
+    near, far = pl.pallas_call(
+        pack_kernel,
+        out_shape=[piece, piece],
+        in_specs=[smem] + [vmem] * 3,
+        out_specs=[vmem] * 2,
+        cost_estimate=pl.CostEstimate(flops=0, bytes_accessed=500_000, transcendentals=0),
+        name="pack_halves",
+    )(place, south, near, far)
     far_halo = swapped(far, "lon", 1)
     near_halo = swapped(near, "lon", 0)
     weights = (
@@ -279,18 +351,27 @@
         fc1_weight,
         jnp.transpose(fc2_weight),
     )
-    near_right, far_right = (1 - odd).reshape(1), odd.reshape(1)
-    near_done = run_side(near_right, near, near_halo, table, (0, 1), weights, chans, heads)
-    far_low = run_side(far_right, far, far_halo, table, (1,), weights, chans, heads)
-    top = moved(jnp.stack([near_done[WIN_LAT + EDGE :], far_low[EDGE:]]), "lat", 1)
-    far_high = run_side(far_right, far, far_halo, table, (0,), weights, chans, heads)
-    near_all = jnp.concatenate([top[0], near_done[: WIN_LAT + EDGE]], axis=0)
-    far_all = jnp.concatenate([top[1], far_high, far_low[:EDGE]], axis=0)
-    done = jnp.where(
-        odd == 1,
-        jnp.concatenate([near_all, far_all], axis=2),
-        jnp.concatenate([far_all, near_all], axis=2),
+    (near_done,) = run_side(
+        place, near, near_halo, table, (0, 1), "near", weights, chans, heads, ()
     )
+    far_low, send = run_side(
+        place, far, far_halo, table, (1,), "low", weights, chans, heads, (near_done,)
+    )
+    top = moved(send, "lat", 1)
+    (done,) = run_side(
+        place, far, far_halo, table, (0,), "high", weights, chans, heads, (near_done, far_low)
+    )
+    anywhere = pl.BlockSpec(memory_space=pl.ANY)
+    done = pl.pallas_call(
+        last_kernel,
+        out_shape=jax.ShapeDtypeStruct(done.shape, done.dtype),
+        in_specs=[smem, anywhere, anywhere],
+        out_specs=anywhere,
+        scratch_shapes=[pltpu.SemaphoreType.DMA((2,))],
+        input_output_aliases={2: 0},
+        cost_estimate=pl.CostEstimate(flops=0, bytes_accessed=100_000, transcendentals=0),
+        name="last_rows",
+    )(place, top, done)
     return jnp.transpose(done, (1, 0, 2))
 
 

time: 23.7 us -> 35.7 us (1.51)
  Pallas kernels: 8.43 us -> 16.4 us
  local copies, waits for them, and re-layouts: 3.83 us -> 10 us
  waiting for transfers between devices: 1.42 us -> 0.44 us
  other arithmetic: 1.02 us -> 0.07 us
  starting transfers between devices: 8.6 us -> 8.21 us
    pallas_call x4 -> x6, Pallas kernels: 8.43 us -> 16.4 us  [the longest x3 9.54 us: run_side(): pl.pallas_call(functools.partial(side_kernel, chans, heads, windows, part...]
    unnamed x13 -> x33, local copies, waits for them, and re-layouts: 1.93 us -> 8.56 us
    ppermute x2, starting transfers between devices: 5.09 us -> 3.54 us  [moved(): return lax.ppermute(x, axis, [(i, (i + by) % size) for i in range(size)])]
    ppermute x2, starting transfers between devices: 3.51 us -> 4.67 us  [swapped(): return lax.ppermute(x, axis, pairs)]
    slice x2 -> x0, local copies, waits for them, and re-layouts: 1 us -> none  [the longest x1 0.97 us: shards(): tokens = jnp.concatenate([field[EDGE:], south], axis=0)]
    transpose x1 -> x0, other arithmetic: 0.86 us -> none  [shards(): return jnp.transpose(done, (1, 0, 2))]
    ppermute x2, waiting for transfers between devices: 1.15 us -> 0.43 us  [moved(): return lax.ppermute(x, axis, [(i, (i + by) % size) for i in range(size)])]
    slice x1, local copies, waits for them, and re-layouts: 0.83 us -> 1.45 us  [shards(): south = moved(field[:EDGE], 'lat', -1)]
  transfers between devices with their start and end apart: 4 -> 4, of which waited for: 2 -> 1; matrix products, arithmetic and copies ran while one was open for 12% -> 6% of each run, Pallas kernels for 23% -> 24%
where the time goes in v5:
time: 35.7 us; the launch traced here: 35.3 us
  Pallas kernels  16.4 us (46%)
  local copies, waits for them, and re-layouts  10 us (28%)
  starting transfers between devices  8.21 us (23%)
  waiting for transfers between devices  0.44 us (1%)
    pallas_call x3, Pallas kernels, run_side(): pl.pallas_call(functools.partial(side_kernel, chans, heads, windows, part...  9.54 us
    unnamed x33, local copies, waits for them, and re-layouts  8.56 us
    ppermute x2, starting transfers between devices, swapped(): return lax.ppermute(x, axis, pairs)  4.67 us
    ppermute x2, starting transfers between devices, moved(): return lax.ppermute(x, axis, [(i, (i + by) % size) for i in range(size)])  3.54 us
    pallas_call x1, Pallas kernels, shards(): pl.pallas_call(last_kernel, out_shape=jax.ShapeDtypeStruct(done.shape, do...  3.46 us
    pallas_call x1, Pallas kernels, shards(): pl.pallas_call(table_kernel, out_shape=[jax.ShapeDtypeStruct((2, 2, 2, 2,...  1.72 us
    pallas_call x1, Pallas kernels, shards(): pl.pallas_call(pack_kernel, out_shape=[piece, piece], in_specs=[smem] + [...  1.69 us
    slice x1, local copies, waits for them, and re-layouts, shards(): south = moved(field[:EDGE], 'lat', -1)  1.45 us
  transfers between devices with their start and end apart: 4, of which 1 were waited for; matrix products, arithmetic and copies ran while one was open for 6% of the time, Pallas kernels for 24%

profile of v5, /device:TPU:0, one launch (start us, length us, event | category | flops | bytes accessed | tf_op | source)
XLA Modules:
  0.0 35.3 jit_solution(14251096708813115391)
XLA Ops:
  0.0 1.4 %slice.4 = bf16[3,4,2304]{2,1,0:T(4,128)(2,1)} slice(bf16[12,4,2304]{2,1,0:T(4,128)(2,1)} %bitcast.10), slice={[0:3], [0:4], [0:2304]} | slice | bytes 110592 | tf_op jit(solution)/shard_map/slice | solution.py:317
  1.4 2.9 %collective-permute-start = (bf16[3,4,2304]{2,1,0:T(4,128)(2,1)}, bf16[3,4,2304]{2,1,0:T(4,128)(2,1)}, u32[]{:S(2)}, u32[]{:S(2)}) collective-permute-start(bf16[3,4,2304]{2,1,0:T(4,128)(2,1)} %slice.4), channel_id=1, source_target_pairs={{0,1},{1,0},{2,3},{3,2},{4,5},{5,4},{6,7},{7,6},{8,9},{9,8},{10,11... | collective-permute-start | bytes 165896 | tf_op jit(solution)/shard_map/ppermute | solution.py:26
  4.4 0.0 copy-start.8
  4.4 0.1 pad_add_fusion.place_ref
  4.5 0.0 copy-start.12
  4.5 1.9 %copy.10.bias_ref = f32[2,2,6,20736]{3,2,1,0:T(8,128)S(1)} copy(f32[2,2,6,20736]{3,1,2,0:T(2,128)} %param.12) | data formatting | bytes 3981312 | tf_op args[4]
  6.4 0.0 copy-done.8
  6.4 0.0 copy-start.14
  6.4 0.0 copy-start.15
  6.4 1.7 %bias_tables.1 = (f32[2,2,2,2,432,128]{5,4,3,2,1,0:T(8,128)S(1)}, bf16[12,4,1152]{2,1,0:T(4,128)(2,1)S(1)}, bf16[12,4,1152]{2,1,0:T(4,128)(2,1)S(1)}) custom-call(s32[2]{0:T(128)S(1)} %pad_add_fusion.place_ref, f32[2,2,6,20736]{3,2,1,0:T(8,128)S(1)} %copy.10.bias_ref, bf16[12,4,2304]{2,1,0:T(4,128)(2,1)S(1)} %bitcast.11), custom_call_target="tpu_custom_call" | custom-call | flops 4000000 | bytes 6000000 | tf_op jit(solution)/shard_map/bias_tables/pallas_call | solution.py:323
  8.2 0.0 copy-done.12
  8.2 0.0 copy-start.9
  8.2 0.6 %copy-done.9 = bf16[12,4,1152]{2,1,0:T(4,128)(2,1)} copy-done((bf16[12,4,1152]{2,1,0:T(4,128)(2,1)}, bf16[12,4,1152]{2,1,0:T(4,128)(2,1)S(1)}, u32[]{:S(2)}) %copy-start.9) | copy-done | bytes 110616
  8.8 0.0 copy-start.10
  8.8 0.6 %copy-done.10 = bf16[12,4,1152]{2,1,0:T(4,128)(2,1)} copy-done((bf16[12,4,1152]{2,1,0:T(4,128)(2,1)}, bf16[12,4,1152]{2,1,0:T(4,128)(2,1)S(1)}, u32[]{:S(2)}) %copy-start.10) | copy-done | bytes 110616
  9.5 0.0 collective-permute-done.south_ref
  9.5 1.7 %pack_halves.1 = (bf16[12,4,1152]{2,1,0:T(4,128)(2,1)}, bf16[12,4,1152]{2,1,0:T(4,128)(2,1)}) custom-call(s32[2]{0:T(128)} %copy-done.12, bf16[3,4,2304]{2,1,0:T(4,128)(2,1)} %collective-permute-done.south_ref, bf16[12,4,1152]{2,1,0:T(4,128)(2,1)} %copy-done.9, bf16[12,4,1152]{2,1,0:T(4,128)(2,1)} %copy-done.10), custom_call_target="tpu_custom_call" | custom-call | bytes 500000 | tf_op jit(solution)/shard_map/pack_halves/pallas_call | solution.py:336
  11.2 0.0 collective-permute-start.2
  11.2 4.7 %collective-permute-start.1 = (bf16[12,4,1152]{2,1,0:T(4,128)(2,1)}, bf16[12,4,1152]{2,1,0:T(4,128)(2,1)S(1)}, u32[]{:S(2)}, u32[]{:S(2)}) collective-permute-start(bf16[12,4,1152]{2,1,0:T(4,128)(2,1)} %get-tuple-element.14.own_piece), channel_id=1, source_target_pairs={{2,4},{4,2},{6,8},{8,6},{10,12},{12,10},{14,16},{16,14},{18,20},{2... | collective-permute-start | bytes 331784 | tf_op jit(solution)/shard_map/ppermute | solution.py:35
  15.8 0.0 collective-permute-done.2.halo_piece
  15.8 0.0 copy-done.14
  15.8 0.0 copy-done.15
  15.8 0.0 copy-start
  15.8 1.0 %copy-done = bf16[192,768]{1,0:T(8,128)(2,1)S(1)} copy-done((bf16[192,768]{1,0:T(8,128)(2,1)S(1)}, bf16[192,768]{1,0:T(8,128)(2,1)}, u32[]{:S(2)}) %copy-start) | copy-done | bytes 294936
  16.8 0.0 copy-start.2
  16.8 1.0 %copy-done.2 = bf16[768,192]{0,1:T(8,128)(2,1)S(1)} copy-done((bf16[768,192]{0,1:T(8,128)(2,1)S(1)}, bf16[768,192]{0,1:T(8,128)(2,1)}, u32[]{:S(2)}) %copy-start.2) | copy-done | bytes 294936
  17.8 0.0 copy-start.4
  17.8 0.9 %copy-done.4 = bf16[192,576]{1,0:T(8,128)(2,1)S(1)} copy-done((bf16[192,576]{1,0:T(8,128)(2,1)S(1)}, bf16[192,576]{1,0:T(8,128)(2,1)}, u32[]{:S(2)}) %copy-start.4) | copy-done | bytes 221208
  18.7 0.0 copy-start.6
  18.7 0.9 %copy-done.6 = bf16[192,192]{1,0:T(8,128)(2,1)S(1)} copy-done((bf16[192,192]{1,0:T(8,128)(2,1)S(1)}, bf16[192,192]{1,0:T(8,128)(2,1)}, u32[]{:S(2)}) %copy-start.6) | copy-done | bytes 73752
  19.6 0.0 copy-start.11
  19.6 0.9 %copy-done.11 = bf16[12,4,1152]{2,1,0:T(4,128)(2,1)S(1)} copy-done((bf16[12,4,1152]{2,1,0:T(4,128)(2,1)S(1)}, bf16[12,4,1152]{2,1,0:T(4,128)(2,1)}, u32[]{:S(2)}) %copy-start.11) | copy-done | bytes 110616
  20.5 0.0 copy-start.13
  20.5 0.7 %copy-done.13 = s32[2]{0:T(128)S(1)} copy-done((s32[2]{0:T(128)S(1)}, s32[2]{0:T(128)}, u32[]{:S(2)}) %copy-start.13) | copy-done | bytes 32
  21.2 0.0 copy-start.1
  21.2 0.0 copy-start.3
  21.2 0.0 copy-start.5
  21.2 0.0 copy-start.7
  21.2 3.6 %swin_near.1.rest_0_ = bf16[12,4,1152]{2,1,0:T(4,128)(2,1)S(1)} custom-call(s32[2]{0:T(128)S(1)} %copy-done.13, bf16[12,4,1152]{2,1,0:T(4,128)(2,1)S(1)} %copy-done.11, bf16[12,4,1152]{2,1,0:T(4,128)(2,1)S(1)} %collective-permute-done.2.halo_piece, f32[1,192]{1,0:T(1,128)S(1)} %bitcast.12, bf16[192,576]{1,0:T(8,128)(2,1)S(1)} %copy-done.4, ...), custom_call_target="tpu_custom_call" | custom-call | flops 400000000 | bytes 3000000 | tf_op jit(solution)/shard_map/swin_near/pallas_call | solution.py:288
  24.8 0.0 collective-permute-done.1.halo_piece
  24.8 0.0 copy-done.1
  24.8 0.0 copy-done.3
  24.8 0.0 copy-done.5
  24.8 0.0 copy-done.7
  24.8 2.6 %swin_low.1 = (bf16[6,4,1152]{2,1,0:T(4,128)(2,1)S(1)}, bf16[2,3,4,1152]{3,2,1,0:T(4,128)(2,1)S(1)}) custom-call(s32[2]{0:T(128)S(1)} %copy-done.13, bf16[12,4,1152]{2,1,0:T(4,128)(2,1)S(1)} %copy-done.7, bf16[12,4,1152]{2,1,0:T(4,128)(2,1)S(1)} %collective-permute-done.1.halo_piece, f32[1,192]{1,0:T(1,128)S(1)} %bitcast.13, bf16[192,576]{1,0:T(8,128)(2,1)S(1)} %copy-done.5, ...), custom_call_target="tpu_custom_call" | custom-call | flops 200000000 | bytes 3000000 | tf_op jit(solution)/shard_map/swin_low/pallas_call | solution.py:288
  27.5 0.6 %collective-permute-start.3 = (bf16[2,3,4,1152]{3,2,1,0:T(4,128)(2,1)S(1)}, bf16[2,3,4,1152]{3,2,1,0:T(4,128)(2,1)}, u32[]{:S(2)}, u32[]{:S(2)}) collective-permute-start(bf16[2,3,4,1152]{3,2,1,0:T(4,128)(2,1)S(1)} %get-tuple-element.17), channel_id=1, source_target_pairs={{0,1},{1,0},{2,3},{3,2},{4,5},{5,4},{6,7},{7,6},{8,9},{9,8},{10,11... | collective-permute-start | bytes 165896 | tf_op jit(solution)/shard_map/ppermute | solution.py:26
  28.1 3.3 %swin_high.1.done_ref = bf16[12,4,2304]{2,1,0:T(4,128)(2,1)} custom-call(s32[2]{0:T(128)S(1)} %copy-done.13, bf16[12,4,1152]{2,1,0:T(4,128)(2,1)S(1)} %copy-done.7, bf16[12,4,1152]{2,1,0:T(4,128)(2,1)S(1)} %collective-permute-done.1.halo_piece, f32[1,192]{1,0:T(1,128)S(1)} %bitcast.14, bf16[192,576]{1,0:T(8,128)(2,1)S(1)} %copy-done.5, ...), custom_call_target="tpu_custom_call" | custom-call | flops 200000000 | bytes 3000000 | tf_op jit(solution)/shard_map/swin_high/pallas_call | solution.py:288
  31.4 0.4 %collective-permute-done.3.top_ref = bf16[2,3,4,1152]{3,2,1,0:T(4,128)(2,1)} collective-permute-done((bf16[2,3,4,1152]{3,2,1,0:T(4,128)(2,1)S(1)}, bf16[2,3,4,1152]{3,2,1,0:T(4,128)(2,1)}, u32[]{:S(2)}, u32[]{:S(2)}) %collective-permute-start.3) | collective-permute-done | bytes 55328 | tf_op jit(solution)/shard_map/ppermute | solution.py:26
  31.8 3.5 %last_rows.1 = bf16[12,4,2304]{2,1,0:T(4,128)(2,1)} custom-call(s32[2]{0:T(128)} %copy-done.12, bf16[2,3,4,1152]{3,2,1,0:T(4,128)(2,1)} %collective-permute-done.3.top_ref, bf16[12,4,2304]{2,1,0:T(4,128)(2,1)} %swin_high.1.done_ref), custom_call_target="tpu_custom_call", output_to_operand_aliasing={{}: (2, {})} | custom-call | bytes 100000 | tf_op jit(solution)/shard_map/last_rows/pallas_call | solution.py:365
Async XLA Ops:
  1.4 8.0 %collective-permute-start = (bf16[3,4,2304]{2,1,0:T(4,128)(2,1)}, bf16[3,4,2304]{2,1,0:T(4,128)(2,1)}, u32[]{:S(2)}, u32[]{:S(2)}) collective-permute-start(bf16[3,4,2304]{2,1,0:T(4,128)(2,1)} %slice.4), channel_id=1, source_target_pairs={{0,1},{1,0},{2,3},{3,2},{4,5},{5,4},{6,7},{7,6},{8,9},{9,8},{10,11... | collective-permute-start | bytes 165896 | tf_op jit(solution)/shard_map/ppermute | solution.py:26
  4.4 2.0 %copy-start.8 = (bf16[4,12,2304]{2,0,1:T(4,128)(2,1)S(1)}, bf16[4,12,2304]{2,0,1:T(4,128)(2,1)}, u32[]{:S(2)}) copy-start(bf16[4,12,2304]{2,0,1:T(4,128)(2,1)} %param.8) | copy-start | bytes 663556
  4.5 3.7 %copy-start.12 = (s32[2]{0:T(128)}, s32[2]{0:T(128)S(1)}, u32[]{:S(2)}) copy-start(s32[2]{0:T(128)S(1)} %pad_add_fusion.place_ref) | copy-start | bytes 28
  6.4 9.4 %copy-start.14 = (f32[192]{0:T(256)S(1)}, f32[192]{0:T(256)}, u32[]{:S(2)}) copy-start(f32[192]{0:T(256)} %param.9) | copy-start | bytes 2308
  6.4 9.4 %copy-start.15 = (f32[192]{0:T(256)S(1)}, f32[192]{0:T(256)}, u32[]{:S(2)}) copy-start(f32[192]{0:T(256)} %param.13) | copy-start | bytes 2308
  8.2 0.6 %copy-start.9 = (bf16[12,4,1152]{2,1,0:T(4,128)(2,1)}, bf16[12,4,1152]{2,1,0:T(4,128)(2,1)S(1)}, u32[]{:S(2)}) copy-start(bf16[12,4,1152]{2,1,0:T(4,128)(2,1)S(1)} %get-tuple-element.12.near_in) | copy-start | bytes 331780
  8.8 0.6 %copy-start.10 = (bf16[12,4,1152]{2,1,0:T(4,128)(2,1)}, bf16[12,4,1152]{2,1,0:T(4,128)(2,1)S(1)}, u32[]{:S(2)}) copy-start(bf16[12,4,1152]{2,1,0:T(4,128)(2,1)S(1)} %get-tuple-element.13.far_in) | copy-start | bytes 331780
  11.2 4.7 %collective-permute-start.2 = (bf16[12,4,1152]{2,1,0:T(4,128)(2,1)}, bf16[12,4,1152]{2,1,0:T(4,128)(2,1)S(1)}, u32[]{:S(2)}, u32[]{:S(2)}) collective-permute-start(bf16[12,4,1152]{2,1,0:T(4,128)(2,1)} %get-tuple-element.16.own_piece), channel_id=1, source_target_pairs={{0,2},{2,0},{4,6},{6,4},{8,10},{10,8},{12,14},{14,12},{16,18},{18,... | collective-permute-start | bytes 331784 | tf_op jit(solution)/shard_map/ppermute | solution.py:35
  11.2 13.6 %collective-permute-start.1 = (bf16[12,4,1152]{2,1,0:T(4,128)(2,1)}, bf16[12,4,1152]{2,1,0:T(4,128)(2,1)S(1)}, u32[]{:S(2)}, u32[]{:S(2)}) collective-permute-start(bf16[12,4,1152]{2,1,0:T(4,128)(2,1)} %get-tuple-element.14.own_piece), channel_id=1, source_target_pairs={{2,4},{4,2},{6,8},{8,6},{10,12},{12,10},{14,16},{16,14},{18,20},{2... | collective-permute-start | bytes 331784 | tf_op jit(solution)/shard_map/ppermute | solution.py:35
  15.8 1.0 %copy-start = (bf16[192,768]{1,0:T(8,128)(2,1)S(1)}, bf16[192,768]{1,0:T(8,128)(2,1)}, u32[]{:S(2)}) copy-start(bf16[192,768]{1,0:T(8,128)(2,1)} %fc1_ref.5) | copy-start | bytes 884740
  16.8 1.0 %copy-start.2 = (bf16[768,192]{0,1:T(8,128)(2,1)S(1)}, bf16[768,192]{0,1:T(8,128)(2,1)}, u32[]{:S(2)}) copy-start(bf16[768,192]{0,1:T(8,128)(2,1)} %param.15) | copy-start | bytes 884740
  17.8 0.9 %copy-start.4 = (bf16[192,576]{1,0:T(8,128)(2,1)S(1)}, bf16[192,576]{1,0:T(8,128)(2,1)}, u32[]{:S(2)}) copy-start(bf16[192,576]{1,0:T(8,128)(2,1)} %qkv_ref.5) | copy-start | bytes 663556
  18.7 0.9 %copy-start.6 = (bf16[192,192]{1,0:T(8,128)(2,1)S(1)}, bf16[192,192]{1,0:T(8,128)(2,1)}, u32[]{:S(2)}) copy-start(bf16[192,192]{1,0:T(8,128)(2,1)} %proj_ref.5) | copy-start | bytes 221188
  19.6 0.9 %copy-start.11 = (bf16[12,4,1152]{2,1,0:T(4,128)(2,1)S(1)}, bf16[12,4,1152]{2,1,0:T(4,128)(2,1)}, u32[]{:S(2)}) copy-start(bf16[12,4,1152]{2,1,0:T(4,128)(2,1)} %get-tuple-element.16.own_piece) | copy-start | bytes 331780
  20.5 0.7 %copy-start.13 = (s32[2]{0:T(128)S(1)}, s32[2]{0:T(128)}, u32[]{:S(2)}) copy-start(s32[2]{0:T(128)} %copy-done.12) | copy-start | bytes 28
  21.2 3.6 %copy-start.1 = (bf16[192,768]{1,0:T(8,128)(2,1)S(1)}, bf16[192,768]{1,0:T(8,128)(2,1)}, u32[]{:S(2)}) copy-start(bf16[192,768]{1,0:T(8,128)(2,1)} %fc1_ref.5) | copy-start | bytes 884740
  21.2 3.6 %copy-start.3 = (bf16[768,192]{0,1:T(8,128)(2,1)S(1)}, bf16[768,192]{0,1:T(8,128)(2,1)}, u32[]{:S(2)}) copy-start(bf16[768,192]{0,1:T(8,128)(2,1)} %param.15) | copy-start | bytes 884740
  21.2 3.6 %copy-start.5 = (bf16[192,576]{1,0:T(8,128)(2,1)S(1)}, bf16[192,576]{1,0:T(8,128)(2,1)}, u32[]{:S(2)}) copy-start(bf16[192,576]{1,0:T(8,128)(2,1)} %qkv_ref.5) | copy-start | bytes 663556
  21.2 3.7 %copy-start.7 = (bf16[12,4,1152]{2,1,0:T(4,128)(2,1)S(1)}, bf16[12,4,1152]{2,1,0:T(4,128)(2,1)}, u32[]{:S(2)}) copy-start(bf16[12,4,1152]{2,1,0:T(4,128)(2,1)} %get-tuple-element.14.own_piece) | copy-start | bytes 331780
  27.5 4.3 %collective-permute-start.3 = (bf16[2,3,4,1152]{3,2,1,0:T(4,128)(2,1)S(1)}, bf16[2,3,4,1152]{3,2,1,0:T(4,128)(2,1)}, u32[]{:S(2)}, u32[]{:S(2)}) collective-permute-start(bf16[2,3,4,1152]{3,2,1,0:T(4,128)(2,1)S(1)} %get-tuple-element.17), channel_id=1, source_target_pairs={{0,1},{1,0},{2,3},{3,2},{4,5},{5,4},{6,7},{7,6},{8,9},{9,8},{10,11... | collective-permute-start | bytes 165896 | tf_op jit(solution)/shard_map/ppermute | solution.py:26

commit v6 on v5

--- a/solution.py
+++ b/solution.py
@@ -18,6 +18,7 @@
 LOG2E = 1.4426950408889634
 LANES = 128
 SPARE = 64
+VMEM_BYTES = 8 * 2**20
 NT = (((1,), (1,)), ((), ()))
 
 
@@ -298,7 +299,7 @@
             pltpu.VMEM((count, 2, 184, LANES), jnp.float32),
         ]
         + (extra if part_of == "high" else []),
-        compiler_params=pltpu.CompilerParams(vmem_limit_bytes=32 * 2**20),
+        compiler_params=pltpu.CompilerParams(vmem_limit_bytes=VMEM_BYTES),
         cost_estimate=pl.CostEstimate(
             flops=200_000_000 * count, bytes_accessed=3_000_000, transcendentals=250_000 * count
         ),
@@ -329,7 +330,7 @@
         ],
         in_specs=[smem, vmem, vmem],
         out_specs=[vmem] * 3,
-        compiler_params=pltpu.CompilerParams(vmem_limit_bytes=32 * 2**20),
+        compiler_params=pltpu.CompilerParams(vmem_limit_bytes=VMEM_BYTES),
         cost_estimate=pl.CostEstimate(flops=4_000_000, bytes_accessed=6_000_000, transcendentals=0),
         name="bias_tables",
     )(place, earth_bias, field)
@@ -338,6 +339,7 @@
         out_shape=[piece, piece],
         in_specs=[smem] + [vmem] * 3,
         out_specs=[vmem] * 2,
+        compiler_params=pltpu.CompilerParams(vmem_limit_bytes=VMEM_BYTES),
         cost_estimate=pl.CostEstimate(flops=0, bytes_accessed=500_000, transcendentals=0),
         name="pack_halves",
     )(place, south, near, far)
@@ -369,6 +371,7 @@
         out_specs=anywhere,
         scratch_shapes=[pltpu.SemaphoreType.DMA((2,))],
         input_output_aliases={2: 0},
+        compiler_params=pltpu.CompilerParams(vmem_limit_bytes=VMEM_BYTES),
         cost_estimate=pl.CostEstimate(flops=0, bytes_accessed=100_000, transcendentals=0),
         name="last_rows",
     )(place, top, done)

time: 35.7 us -> 24.9 us (0.70)
  local copies, waits for them, and re-layouts: 10 us -> 2.84 us
  Pallas kernels: 16.4 us -> 13 us
    unnamed x33 -> x15, local copies, waits for them, and re-layouts: 8.56 us -> 1.94 us
    pallas_call x1, Pallas kernels: 3.46 us -> 1.18 us  [shards(): pl.pallas_call(last_kernel, out_shape=jax.ShapeDtypeStruct(done.shape, do...]
    pallas_call x1, Pallas kernels: 1.69 us -> 0.56 us  [shards(): pl.pallas_call(pack_kernel, out_shape=[piece, piece], in_specs=[smem] + [...]
    slice x1, local copies, waits for them, and re-layouts: 1.45 us -> 0.91 us  [shards(): south = moved(field[:EDGE], 'lat', -1)]
  transfers between devices with their start and end apart: 4 -> 4, of which waited for: 1 -> 1; matrix products, arithmetic and copies ran while one was open for 6% -> 8% of each run, Pallas kernels for 24% -> 35%
where the time goes in v6:
time: 24.9 us; the launch traced here: 24.8 us
  Pallas kernels  13 us (52%)
  starting transfers between devices  8.34 us (33%)
  local copies, waits for them, and re-layouts  2.84 us (11%)
  waiting for transfers between devices  0.32 us (1%)
    pallas_call x3, Pallas kernels, run_side(): pl.pallas_call(functools.partial(side_kernel, chans, heads, windows, part...  9.56 us
    ppermute x2, starting transfers between devices, swapped(): return lax.ppermute(x, axis, pairs)  4.73 us
    ppermute x2, starting transfers between devices, moved(): return lax.ppermute(x, axis, [(i, (i + by) % size) for i in range(size)])  3.61 us
    unnamed x15, local copies, waits for them, and re-layouts  1.94 us
    pallas_call x1, Pallas kernels, shards(): pl.pallas_call(table_kernel, out_shape=[jax.ShapeDtypeStruct((2, 2, 2, 2,...  1.72 us
    pallas_call x1, Pallas kernels, shards(): pl.pallas_call(last_kernel, out_shape=jax.ShapeDtypeStruct(done.shape, do...  1.18 us
    slice x1, local copies, waits for them, and re-layouts, shards(): south = moved(field[:EDGE], 'lat', -1)  0.91 us
    pallas_call x1, Pallas kernels, shards(): pl.pallas_call(pack_kernel, out_shape=[piece, piece], in_specs=[smem] + [...  0.56 us
  transfers between devices with their start and end apart: 4, of which 1 were waited for; matrix products, arithmetic and copies ran while one was open for 8% of the time, Pallas kernels for 35%

profile of v6, /device:TPU:0, one launch (start us, length us, event | category | flops | bytes accessed | tf_op | source)
XLA Modules:
  0.0 24.8 jit_solution(5283315513959048800)
XLA Ops:
  0.0 0.0 copy-start.4
  0.0 0.9 %slice.4 = bf16[3,4,2304]{2,1,0:T(4,128)(2,1)S(1)} slice(bf16[12,4,2304]{2,1,0:T(4,128)(2,1)} %bitcast.10), slice={[0:3], [0:4], [0:2304]} | slice | bytes 110592 | tf_op jit(solution)/shard_map/slice | solution.py:318
  0.9 3.0 %collective-permute-start = (bf16[3,4,2304]{2,1,0:T(4,128)(2,1)S(1)}, bf16[3,4,2304]{2,1,0:T(4,128)(2,1)S(1)}, u32[]{:S(2)}, u32[]{:S(2)}) collective-permute-start(bf16[3,4,2304]{2,1,0:T(4,128)(2,1)S(1)} %slice.4), channel_id=1, source_target_pairs={{0,1},{1,0},{2,3},{3,2},{4,5},{5,4},{6,7},{7,6},{8,9},{9,8},{10,11... | collective-permute-start | bytes 165896 | tf_op jit(solution)/shard_map/ppermute | solution.py:27
  3.9 0.1 pad_add_fusion.place_ref
  4.0 1.9 %copy.10.bias_ref = f32[2,2,6,20736]{3,2,1,0:T(8,128)S(1)} copy(f32[2,2,6,20736]{3,1,2,0:T(2,128)} %param.12) | data formatting | bytes 3981312 | tf_op args[4]
  5.9 0.0 copy-done.4
  5.9 0.0 copy-start
  5.9 0.0 copy-start.1
  5.9 0.0 copy-start.2
  5.9 0.0 copy-start.3
  5.9 0.0 copy-start.5
  6.0 0.0 copy-start.6
  6.0 1.7 %bias_tables.1 = (f32[2,2,2,2,432,128]{5,4,3,2,1,0:T(8,128)S(1)}, bf16[12,4,1152]{2,1,0:T(4,128)(2,1)S(1)}, bf16[12,4,1152]{2,1,0:T(4,128)(2,1)S(1)}) custom-call(s32[2]{0:T(128)S(1)} %pad_add_fusion.place_ref, f32[2,2,6,20736]{3,2,1,0:T(8,128)S(1)} %copy.10.bias_ref, bf16[12,4,2304]{2,1,0:T(4,128)(2,1)S(1)} %bitcast.11), custom_call_target="tpu_custom_call" | custom-call | flops 4000000 | bytes 6000000 | tf_op jit(solution)/shard_map/bias_tables/pallas_call | solution.py:324
  7.7 0.0 collective-permute-done.south_ref
  7.7 0.6 %pack_halves.1 = (bf16[12,4,1152]{2,1,0:T(4,128)(2,1)S(1)}, bf16[12,4,1152]{2,1,0:T(4,128)(2,1)S(1)}) custom-call(s32[2]{0:T(128)S(1)} %pad_add_fusion.place_ref, bf16[3,4,2304]{2,1,0:T(4,128)(2,1)S(1)} %collective-permute-done.south_ref, bf16[12,4,1152]{2,1,0:T(4,128)(2,1)S(1)} %get-tuple-element.12.near_in, bf16[12,4,1152]{2,1,0:T(4,128)(2,1)S(1)} %get-tuple-element.13.far_in), custom_call_target="tpu_custom_call" | custom-call | bytes 500000 | tf_op jit(solution)/shard_map/pack_halves/pallas_call | solution.py:337
  8.3 0.1 collective-permute-start.2
  8.4 4.7 %collective-permute-start.1 = (bf16[12,4,1152]{2,1,0:T(4,128)(2,1)S(1)}, bf16[12,4,1152]{2,1,0:T(4,128)(2,1)S(1)}, u32[]{:S(2)}, u32[]{:S(2)}) collective-permute-start(bf16[12,4,1152]{2,1,0:T(4,128)(2,1)S(1)} %get-tuple-element.14.own_piece), channel_id=1, source_target_pairs={{2,4},{4,2},{6,8},{8,6},{10,12},{12,10},{14,16},{16,14},{18,20},{2... | collective-permute-start | bytes 331784 | tf_op jit(solution)/shard_map/ppermute | solution.py:36
  13.0 0.0 collective-permute-done.2.halo_piece
  13.0 0.0 copy-done
  13.0 0.0 copy-done.1
  13.0 0.0 copy-done.2
  13.0 0.0 copy-done.3
  13.0 0.0 copy-done.5
  13.1 0.0 copy-done.6
  13.1 3.6 %swin_near.1.rest_0_ = bf16[12,4,1152]{2,1,0:T(4,128)(2,1)S(1)} custom-call(s32[2]{0:T(128)S(1)} %pad_add_fusion.place_ref, bf16[12,4,1152]{2,1,0:T(4,128)(2,1)S(1)} %get-tuple-element.16.own_piece, bf16[12,4,1152]{2,1,0:T(4,128)(2,1)S(1)} %collective-permute-done.2.halo_piece, f32[1,192]{1,0:T(1,128)S(1)} %bitcast.12, bf16[192,576]{1,0:T(8,128)(2,1)S(1)} %copy-done.2, ...), custom_call_target="tpu_custom_call" | custom-call | flops 400000000 | bytes 3000000 | tf_op jit(solution)/shard_map/swin_near/pallas_call | solution.py:289
  16.7 0.0 collective-permute-done.1.halo_piece
  16.7 2.7 %swin_low.1 = (bf16[6,4,1152]{2,1,0:T(4,128)(2,1)S(1)}, bf16[2,3,4,1152]{3,2,1,0:T(4,128)(2,1)S(1)}) custom-call(s32[2]{0:T(128)S(1)} %pad_add_fusion.place_ref, bf16[12,4,1152]{2,1,0:T(4,128)(2,1)S(1)} %get-tuple-element.14.own_piece, bf16[12,4,1152]{2,1,0:T(4,128)(2,1)S(1)} %collective-permute-done.1.halo_piece, f32[1,192]{1,0:T(1,128)S(1)} %bitcast.13, ...), custom_call_target="tpu_custom_call" | custom-call | flops 200000000 | bytes 3000000 | tf_op jit(solution)/shard_map/swin_low/pallas_call | solution.py:289
  19.4 0.6 %collective-permute-start.3 = (bf16[2,3,4,1152]{3,2,1,0:T(4,128)(2,1)S(1)}, bf16[2,3,4,1152]{3,2,1,0:T(4,128)(2,1)S(1)}, u32[]{:S(2)}, u32[]{:S(2)}) collective-permute-start(bf16[2,3,4,1152]{3,2,1,0:T(4,128)(2,1)S(1)} %get-tuple-element.17), channel_id=1, source_target_pairs={{0,1},{1,0},{2,3},{3,2},{4,5},{5,4},{6,7},{7,6},{8,9},{9,8},{10,11... | collective-permute-start | bytes 165896 | tf_op jit(solution)/shard_map/ppermute | solution.py:27
  20.0 3.3 %swin_high.1.done_ref = bf16[12,4,2304]{2,1,0:T(4,128)(2,1)} custom-call(s32[2]{0:T(128)S(1)} %pad_add_fusion.place_ref, bf16[12,4,1152]{2,1,0:T(4,128)(2,1)S(1)} %get-tuple-element.14.own_piece, bf16[12,4,1152]{2,1,0:T(4,128)(2,1)S(1)} %collective-permute-done.1.halo_piece, f32[1,192]{1,0:T(1,128)S(1)} %bitcast.14, bf16[192,576]{1,0:T(8,128)(2,1)S(1)} %copy-done.2, ...), custom_call_target="tpu_custom_call" | custom-call | flops 200000000 | bytes 3000000 | tf_op jit(solution)/shard_map/swin_high/pallas_call | solution.py:289
  23.3 0.3 %collective-permute-done.3.top_ref = bf16[2,3,4,1152]{3,2,1,0:T(4,128)(2,1)S(1)} collective-permute-done((bf16[2,3,4,1152]{3,2,1,0:T(4,128)(2,1)S(1)}, bf16[2,3,4,1152]{3,2,1,0:T(4,128)(2,1)S(1)}, u32[]{:S(2)}, u32[]{:S(2)}) %collective-permute-start.3) | collective-permute-done | bytes 55328 | tf_op jit(solution)/shard_map/ppermute | solution.py:27
  23.6 1.2 %last_rows.1 = bf16[12,4,2304]{2,1,0:T(4,128)(2,1)} custom-call(s32[2]{0:T(128)S(1)} %pad_add_fusion.place_ref, bf16[2,3,4,1152]{3,2,1,0:T(4,128)(2,1)S(1)} %collective-permute-done.3.top_ref, bf16[12,4,2304]{2,1,0:T(4,128)(2,1)} %swin_high.1.done_ref), custom_call_target="tpu_custom_call", output_to_operand_aliasing={{}: (2, {})} | custom-call | bytes 100000 | tf_op jit(solution)/shard_map/last_rows/pallas_call | solution.py:367
Async XLA Ops:
  0.0 5.9 %copy-start.4 = (bf16[4,12,2304]{2,0,1:T(4,128)(2,1)S(1)}, bf16[4,12,2304]{2,0,1:T(4,128)(2,1)}, u32[]{:S(2)}) copy-start(bf16[4,12,2304]{2,0,1:T(4,128)(2,1)} %param.8) | copy-start | bytes 663556
  0.9 6.8 %collective-permute-start = (bf16[3,4,2304]{2,1,0:T(4,128)(2,1)S(1)}, bf16[3,4,2304]{2,1,0:T(4,128)(2,1)S(1)}, u32[]{:S(2)}, u32[]{:S(2)}) collective-permute-start(bf16[3,4,2304]{2,1,0:T(4,128)(2,1)S(1)} %slice.4), channel_id=1, source_target_pairs={{0,1},{1,0},{2,3},{3,2},{4,5},{5,4},{6,7},{7,6},{8,9},{9,8},{10,11... | collective-permute-start | bytes 165896 | tf_op jit(solution)/shard_map/ppermute | solution.py:27
  5.9 7.1 %copy-start = (bf16[192,768]{1,0:T(8,128)(2,1)S(1)}, bf16[192,768]{1,0:T(8,128)(2,1)}, u32[]{:S(2)}) copy-start(bf16[192,768]{1,0:T(8,128)(2,1)} %fc1_ref.5) | copy-start | bytes 884740
  5.9 7.1 %copy-start.1 = (bf16[768,192]{0,1:T(8,128)(2,1)S(1)}, bf16[768,192]{0,1:T(8,128)(2,1)}, u32[]{:S(2)}) copy-start(bf16[768,192]{0,1:T(8,128)(2,1)} %param.15) | copy-start | bytes 884740
  5.9 7.1 %copy-start.2 = (bf16[192,576]{1,0:T(8,128)(2,1)S(1)}, bf16[192,576]{1,0:T(8,128)(2,1)}, u32[]{:S(2)}) copy-start(bf16[192,576]{1,0:T(8,128)(2,1)} %qkv_ref.5) | copy-start | bytes 663556
  5.9 7.1 %copy-start.3 = (bf16[192,192]{1,0:T(8,128)(2,1)S(1)}, bf16[192,192]{1,0:T(8,128)(2,1)}, u32[]{:S(2)}) copy-start(bf16[192,192]{1,0:T(8,128)(2,1)} %proj_ref.5) | copy-start | bytes 221188
  5.9 7.1 %copy-start.5 = (f32[192]{0:T(256)S(1)}, f32[192]{0:T(256)}, u32[]{:S(2)}) copy-start(f32[192]{0:T(256)} %param.9) | copy-start | bytes 2308
  6.0 7.1 %copy-start.6 = (f32[192]{0:T(256)S(1)}, f32[192]{0:T(256)}, u32[]{:S(2)}) copy-start(f32[192]{0:T(256)} %param.13) | copy-start | bytes 2308
  8.3 4.7 %collective-permute-start.2 = (bf16[12,4,1152]{2,1,0:T(4,128)(2,1)S(1)}, bf16[12,4,1152]{2,1,0:T(4,128)(2,1)S(1)}, u32[]{:S(2)}, u32[]{:S(2)}) collective-permute-start(bf16[12,4,1152]{2,1,0:T(4,128)(2,1)S(1)} %get-tuple-element.16.own_piece), channel_id=1, source_target_pairs={{0,2},{2,0},{4,6},{6,4},{8,10},{10,8},{12,14},{14,12},{16,18},{18,... | collective-permute-start | bytes 331784 | tf_op jit(solution)/shard_map/ppermute | solution.py:36
  8.4 8.3 %collective-permute-start.1 = (bf16[12,4,1152]{2,1,0:T(4,128)(2,1)S(1)}, bf16[12,4,1152]{2,1,0:T(4,128)(2,1)S(1)}, u32[]{:S(2)}, u32[]{:S(2)}) collective-permute-start(bf16[12,4,1152]{2,1,0:T(4,128)(2,1)S(1)} %get-tuple-element.14.own_piece), channel_id=1, source_target_pairs={{2,4},{4,2},{6,8},{8,6},{10,12},{12,10},{14,16},{16,14},{18,20},{2... | collective-permute-start | bytes 331784 | tf_op jit(solution)/shard_map/ppermute | solution.py:36
  19.4 4.2 %collective-permute-start.3 = (bf16[2,3,4,1152]{3,2,1,0:T(4,128)(2,1)S(1)}, bf16[2,3,4,1152]{3,2,1,0:T(4,128)(2,1)S(1)}, u32[]{:S(2)}, u32[]{:S(2)}) collective-permute-start(bf16[2,3,4,1152]{3,2,1,0:T(4,128)(2,1)S(1)} %get-tuple-element.17), channel_id=1, source_target_pairs={{0,1},{1,0},{2,3},{3,2},{4,5},{5,4},{6,7},{7,6},{8,9},{9,8},{10,11... | collective-permute-start | bytes 165896 | tf_op jit(solution)/shard_map/ppermute | solution.py:27

commit v7 on v6

--- a/solution.py
+++ b/solution.py
@@ -16,6 +16,8 @@
 TOKENS = WIN_LEV * WIN_LAT * WIN_LON
 QUERIES = TOKENS // 2
 LOG2E = 1.4426950408889634
+GELU_0 = 0.7978845608028654
+GELU_1 = 0.044715 * GELU_0
 LANES = 128
 SPARE = 64
 VMEM_BYTES = 8 * 2**20
@@ -36,40 +38,44 @@
     return lax.ppermute(x, axis, pairs)
 
 
-def half_places(place_ref, half):
-    odd = place_ref[1]
+def half_places(half):
+    odd = lax.rem(lax.axis_index("lon"), 2)
     return pl.multiple_of((1 - odd) * half, LANES), pl.multiple_of(odd * half, LANES)
 
 
-def pack_kernel(place_ref, south_ref, near_in, far_in, near_ref, far_ref):
-    near_at, far_at = half_places(place_ref, near_ref.shape[2])
-    rows = near_ref.shape[0] - EDGE
-    near_ref[:rows] = near_in[:rows]
-    far_ref[:rows] = far_in[:rows]
-    near_ref[rows:] = south_ref[:, :, pl.ds(near_at, near_ref.shape[2])]
-    far_ref[rows:] = south_ref[:, :, pl.ds(far_at, far_ref.shape[2])]
-
-
-def last_kernel(place_ref, top_ref, done_ref, out_ref, sems):
+def pack_kernel(which, south_ref, kept_ref, *rest):
+    piece_ref = rest[-1]
+    at = half_places(piece_ref.shape[2])[which]
+    rows = piece_ref.shape[0] - EDGE
+    piece_ref[:rows] = kept_ref[:rows]
+    piece_ref[rows:] = south_ref[:, :, pl.ds(at, piece_ref.shape[2])]
+
+
+def last_kernel(top_ref, high_ref, done_ref, out_ref, sems):
     half = top_ref.shape[3]
-    copies = []
-    for n, at in enumerate(half_places(place_ref, half)):
-        target = out_ref.at[:EDGE, :, pl.ds(at, half)]
-        copies.append(pltpu.make_async_copy(top_ref.at[n], target, sems.at[n]))
-        copies[-1].start()
+    near_at, far_at = half_places(half)
+    near_out, far_out = (out_ref.at[:, :, pl.ds(at, half)] for at in (near_at, far_at))
+    copies = [
+        pltpu.make_async_copy(top_ref.at[0], near_out.at[:EDGE], sems.at[0]),
+        pltpu.make_async_copy(top_ref.at[1], far_out.at[:EDGE], sems.at[1]),
+        pltpu.make_async_copy(high_ref, far_out.at[EDGE : EDGE + WIN_LAT], sems.at[2]),
+    ]
+    for copy in copies:
+        copy.start()
     for copy in copies:
         copy.wait()
 
 
-def table_kernel(place_ref, bias_ref, field_ref, table_ref, near_ref, far_ref):
+def table_kernel(bias_ref, field_ref, table_ref, near_ref, far_ref):
     rows = field_ref.shape[0] - EDGE
-    near_at, far_at = half_places(place_ref, near_ref.shape[2])
+    near_at, far_at = half_places(near_ref.shape[2])
     near_ref[:rows] = field_ref[EDGE:, :, pl.ds(near_at, near_ref.shape[2])]
     far_ref[:rows] = field_ref[EDGE:, :, pl.ds(far_at, far_ref.shape[2])]
     heads = bias_ref.shape[2]
     width = 9 * LANES
     lane = lax.broadcasted_iota(jnp.int32, (1, LANES), 1)
-    last = jnp.where(place_ref[0] > 0, -1e9, 0.0).astype(jnp.float32)
+    is_last = lax.axis_index("lat") == lax.axis_size("lat") - 1
+    last = jnp.where(is_last, -1e9, 0.0).astype(jnp.float32)
 
     def penalty(first, lev, side, wrap):
         key = lane + first
@@ -122,12 +128,16 @@
     return center * lax.rsqrt(spread + 1e-05) * gain
 
 
+def gelu(x):
+    half = 0.5 * x
+    return half + half * jnp.tanh(x * (GELU_0 + GELU_1 * (x * x)))
+
+
 def side_kernel(
     chans,
     heads,
     windows,
     part_of,
-    place_ref,
     own_piece,
     halo_piece,
     gain1_ref,
@@ -144,9 +154,9 @@
     elif part_of == "low":
         near_ref, out_ref, send_ref, keys_ref, own_ref, res_ref = rest
     else:
-        near_ref, low_ref, done_ref, keys_ref, own_ref, res_ref, out_ref, sems = rest
+        near_ref, low_ref, out_ref, done_ref, keys_ref, own_ref, res_ref, sems = rest
         half = near_ref.shape[2]
-        near_at, far_at = half_places(place_ref, half)
+        near_at, far_at = half_places(half)
         done_near = done_ref.at[:, :, pl.ds(near_at, half)]
         done_far = done_ref.at[:, :, pl.ds(far_at, half)]
         copies = [
@@ -156,15 +166,13 @@
             pltpu.make_async_copy(
                 low_ref.at[:EDGE], done_far.at[WIN_LAT + EDGE :], sems.at[1]
             ),
-            pltpu.make_async_copy(
-                out_ref, done_far.at[EDGE : WIN_LAT + EDGE], sems.at[2]
-            ),
         ]
-        for copy in copies[:2]:
+        for copy in copies:
             copy.start()
     head_dim = chans // heads
     low = lax.broadcasted_iota(jnp.int32, (1, LANES), 1) < SPARE
-    right = 1 - place_ref[1] if part_of == "near" else place_ref[1]
+    odd = lax.rem(lax.axis_index("lon"), 2)
+    right = 1 - odd if part_of == "near" else odd
     halo_at = right * HALF
     own_at = HALF - halo_at
 
@@ -239,7 +247,7 @@
     resid = resid.astype(jnp.bfloat16).astype(jnp.float32)
     normed = layer_norm(resid, gain2_ref[...]).astype(jnp.bfloat16)
     hidden = jnp.dot(normed, fc1_ref[...], preferred_element_type=jnp.float32)
-    hidden = jax.nn.gelu(hidden).astype(jnp.bfloat16)
+    hidden = gelu(hidden).astype(jnp.bfloat16)
     result = lax.dot_general(hidden, fc2_ref[...], NT, preferred_element_type=jnp.float32)
     result = resid + result
     for n in range(len(windows)):
@@ -263,12 +271,11 @@
         send_ref[0] = near_ref[WIN_LAT + EDGE :]
         send_ref[1] = out_ref[EDGE:]
     elif part_of == "high":
-        copies[2].start()
         for copy in copies:
             copy.wait()
 
 
-def run_side(place, own, halo, table, windows, part_of, weights, chans, heads, before):
+def run_side(own, halo, table, windows, part_of, weights, chans, heads, before):
     count = len(windows)
     first = windows[0]
     assert list(windows) == list(range(first, first + count)) and first % count == 0
@@ -282,17 +289,16 @@
     out = jax.ShapeDtypeStruct((rows,) + own.shape[1:], own.dtype)
     send = jax.ShapeDtypeStruct((2, EDGE) + own.shape[1:], own.dtype)
     done = jax.ShapeDtypeStruct(own.shape[:2] + (2 * own.shape[2],), own.dtype)
-    outs = {"near": [out], "low": [out, send], "high": [done]}[part_of]
-    extra = [pltpu.VMEM(out.shape, out.dtype), pltpu.SemaphoreType.DMA((3,))]
+    outs = {"near": [out], "low": [out, send], "high": [out, done]}[part_of]
+    extra = [pltpu.SemaphoreType.DMA((2,))]
     gain1, qkv, proj, gain2, fc1, fc2 = weights
     operands = (gain1, qkv, proj, table, gain2, fc1, fc2) + before
     return pl.pallas_call(
         functools.partial(side_kernel, chans, heads, windows, part_of),
         out_shape=outs,
         grid=(1,),
-        in_specs=[pl.BlockSpec(memory_space=pltpu.SMEM), piece, piece]
-        + [whole(x) for x in operands],
-        out_specs=[anywhere] if part_of == "high" else [whole(x) for x in outs],
+        in_specs=[piece, piece] + [whole(x) for x in operands],
+        out_specs=[whole(out), anywhere] if part_of == "high" else [whole(x) for x in outs],
         scratch_shapes=[
             pltpu.VMEM((count, 2, LEVELS * QUERIES, LANES), jnp.float32),
             pltpu.VMEM((count, 2, 184, LANES), jnp.float32),
@@ -304,7 +310,7 @@
             flops=200_000_000 * count, bytes_accessed=3_000_000, transcendentals=250_000 * count
         ),
         name="swin_" + part_of,
-    )(place, own, halo, *operands)
+    )(own, halo, *operands)
 
 
 def shards(
@@ -316,10 +322,7 @@
     half = HALF * chans
     field = jnp.transpose(field_in, (1, 0, 2))
     south = moved(field[:EDGE], "lat", -1)
-    odd = lax.axis_index("lon") % 2
-    last = (lax.axis_index("lat") == lax.axis_size("lat") - 1).astype(jnp.int32)
-    place = jnp.stack([last, odd])
-    smem, vmem = (pl.BlockSpec(memory_space=m) for m in (pltpu.SMEM, pltpu.VMEM))
+    vmem = pl.BlockSpec(memory_space=pltpu.VMEM)
     piece = jax.ShapeDtypeStruct((rows, levels, half), field.dtype)
     table, near, far = pl.pallas_call(
         table_kernel,
@@ -328,21 +331,27 @@
             piece,
             piece,
         ],
-        in_specs=[smem, vmem, vmem],
+        in_specs=[vmem, vmem],
         out_specs=[vmem] * 3,
         compiler_params=pltpu.CompilerParams(vmem_limit_bytes=VMEM_BYTES),
         cost_estimate=pl.CostEstimate(flops=4_000_000, bytes_accessed=6_000_000, transcendentals=0),
         name="bias_tables",
-    )(place, earth_bias, field)
-    near, far = pl.pallas_call(
-        pack_kernel,
-        out_shape=[piece, piece],
-        in_specs=[smem] + [vmem] * 3,
-        out_specs=[vmem] * 2,
-        compiler_params=pltpu.CompilerParams(vmem_limit_bytes=VMEM_BYTES),
-        cost_estimate=pl.CostEstimate(flops=0, bytes_accessed=500_000, transcendentals=0),
-        name="pack_halves",
-    )(place, south, near, far)
+    )(earth_bias, field)
+    anywhere = pl.BlockSpec(memory_space=pl.ANY)
+
+    def pack(which, kept, *after):
+        return pl.pallas_call(
+            functools.partial(pack_kernel, which),
+            out_shape=piece,
+            in_specs=[vmem] * 2 + [anywhere] * len(after),
+            out_specs=vmem,
+            compiler_params=pltpu.CompilerParams(vmem_limit_bytes=VMEM_BYTES),
+            cost_estimate=pl.CostEstimate(flops=0, bytes_accessed=250_000, transcendentals=0),
+            name="pack_half",
+        )(south, kept, *after)
+
+    far = pack(1, far)
+    near = pack(0, near, far)
     far_halo = swapped(far, "lon", 1)
     near_halo = swapped(near, "lon", 0)
     weights = (
@@ -354,27 +363,26 @@
         jnp.transpose(fc2_weight),
     )
     (near_done,) = run_side(
-        place, near, near_halo, table, (0, 1), "near", weights, chans, heads, ()
+        near, near_halo, table, (0, 1), "near", weights, chans, heads, ()
     )
     far_low, send = run_side(
-        place, far, far_halo, table, (1,), "low", weights, chans, heads, (near_done,)
+        far, far_halo, table, (1,), "low", weights, chans, heads, (near_done,)
     )
     top = moved(send, "lat", 1)
-    (done,) = run_side(
-        place, far, far_halo, table, (0,), "high", weights, chans, heads, (near_done, far_low)
+    far_high, done = run_side(
+        far, far_halo, table, (0,), "high", weights, chans, heads, (near_done, far_low)
     )
-    anywhere = pl.BlockSpec(memory_space=pl.ANY)
     done = pl.pallas_call(
         last_kernel,
         out_shape=jax.ShapeDtypeStruct(done.shape, done.dtype),
-        in_specs=[smem, anywhere, anywhere],
+        in_specs=[anywhere] * 3,
         out_specs=anywhere,
-        scratch_shapes=[pltpu.SemaphoreType.DMA((2,))],
+        scratch_shapes=[pltpu.SemaphoreType.DMA((3,))],
         input_output_aliases={2: 0},
         compiler_params=pltpu.CompilerParams(vmem_limit_bytes=VMEM_BYTES),
-        cost_estimate=pl.CostEstimate(flops=0, bytes_accessed=100_000, transcendentals=0),
+        cost_estimate=pl.CostEstimate(flops=0, bytes_accessed=200_000, transcendentals=0),
         name="last_rows",
-    )(place, top, done)
+    )(top, far_high, done)
     return jnp.transpose(done, (1, 0, 2))
 
 

time: 24.9 us -> 22.2 us (0.89)
  Pallas kernels: 13 us -> 9.84 us
  starting transfers between devices: 8.34 us -> 8.78 us
    pallas_call x3, Pallas kernels: 9.56 us -> 7.96 us  [run_side(): pl.pallas_call(functools.partial(side_kernel, chans, heads, windows, part...]
    pallas_call x1, Pallas kernels: 1.72 us -> 1.17 us  [shards(): pl.pallas_call(table_kernel, out_shape=[jax.ShapeDtypeStruct((2, 2, 2, 2,...]
    pallas_call x1 -> x2, Pallas kernels: 0.56 us -> 0.04 us  [pack(): pl.pallas_call(functools.partial(pack_kernel, which), out_shape=piece, in...]
    pallas_call x1, Pallas kernels: 1.18 us -> 0.67 us  [shards(): pl.pallas_call(last_kernel, out_shape=jax.ShapeDtypeStruct(done.shape, do...]
    ppermute x2, starting transfers between devices: 3.61 us -> 4.05 us  [moved(): return lax.ppermute(x, axis, [(i, (i + by) % size) for i in range(size)])]
  transfers between devices with their start and end apart: 4 -> 4, of which waited for: 1 -> 1; matrix products, arithmetic and copies ran while one was open for 8% -> 9% of each run, Pallas kernels for 35% -> 32%
where the time goes in v7:
time: 22.2 us; the launch traced here: 22.1 us
  Pallas kernels  9.84 us (44%)
  starting transfers between devices  8.78 us (40%)
  local copies, waits for them, and re-layouts  2.84 us (13%)
  waiting for transfers between devices  0.46 us (2%)
    pallas_call x3, Pallas kernels, run_side(): pl.pallas_call(functools.partial(side_kernel, chans, heads, windows, part...  7.96 us
    ppermute x2, starting transfers between devices, swapped(): return lax.ppermute(x, axis, pairs)  4.73 us
    ppermute x2, starting transfers between devices, moved(): return lax.ppermute(x, axis, [(i, (i + by) % size) for i in range(size)])  4.05 us
    unnamed x15, local copies, waits for them, and re-layouts  1.94 us
    pallas_call x1, Pallas kernels, shards(): pl.pallas_call(table_kernel, out_shape=[jax.ShapeDtypeStruct((2, 2, 2, 2,...  1.17 us
    slice x1, local copies, waits for them, and re-layouts, shards(): south = moved(field[:EDGE], 'lat', -1)  0.91 us
    pallas_call x1, Pallas kernels, shards(): pl.pallas_call(last_kernel, out_shape=jax.ShapeDtypeStruct(done.shape, do...  0.67 us
    ppermute x2, waiting for transfers between devices, moved(): return lax.ppermute(x, axis, [(i, (i + by) % size) for i in range(size)])  0.45 us
  transfers between devices with their start and end apart: 4, of which 1 were waited for; matrix products, arithmetic and copies ran while one was open for 9% of the time, Pallas kernels for 32%

profile of v7, /device:TPU:0, one launch (start us, length us, event | category | flops | bytes accessed | tf_op | source)
XLA Modules:
  0.0 22.1 jit_solution(5229330514046437494)
XLA Ops:
  0.0 0.0 copy-start.4
  0.0 0.9 %slice.4 = bf16[3,4,2304]{2,1,0:T(4,128)(2,1)S(1)} slice(bf16[12,4,2304]{2,1,0:T(4,128)(2,1)} %bitcast.8), slice={[0:3], [0:4], [0:2304]} | slice | bytes 110592 | tf_op jit(solution)/shard_map/slice | solution.py:324
  0.9 3.0 %collective-permute-start = (bf16[3,4,2304]{2,1,0:T(4,128)(2,1)S(1)}, bf16[3,4,2304]{2,1,0:T(4,128)(2,1)S(1)}, u32[]{:S(2)}, u32[]{:S(2)}) collective-permute-start(bf16[3,4,2304]{2,1,0:T(4,128)(2,1)S(1)} %slice.4), channel_id=1, source_target_pairs={{0,1},{1,0},{2,3},{3,2},{4,5},{5,4},{6,7},{7,6},{8,9},{9,8},{10,11... | collective-permute-start | bytes 165896 | tf_op jit(solution)/shard_map/ppermute | solution.py:29
  3.9 1.9 %copy.10.bias_ref = f32[2,2,6,20736]{3,2,1,0:T(8,128)S(1)} copy(f32[2,2,6,20736]{3,1,2,0:T(2,128)} %param.12) | data formatting | bytes 3981312 | tf_op args[4]
  5.8 0.0 copy-done.4
  5.8 0.0 copy-start
  5.8 0.0 copy-start.1
  5.8 0.0 copy-start.2
  5.9 0.0 copy-start.3
  5.9 0.0 copy-start.5
  5.9 0.0 copy-start.6
  5.9 1.2 %bias_tables.1 = (f32[2,2,2,2,432,128]{5,4,3,2,1,0:T(8,128)S(1)}, bf16[12,4,1152]{2,1,0:T(4,128)(2,1)S(1)}, bf16[12,4,1152]{2,1,0:T(4,128)(2,1)S(1)}) custom-call(f32[2,2,6,20736]{3,2,1,0:T(8,128)S(1)} %copy.10.bias_ref, bf16[12,4,2304]{2,1,0:T(4,128)(2,1)S(1)} %bitcast.9), custom_call_target="tpu_custom_call" | custom-call | flops 4000000 | bytes 6000000 | tf_op jit(solution)/shard_map/bias_tables/pallas_call | solution.py:327
  7.1 0.0 collective-permute-done.south_ref
  7.1 0.1 collective-permute-start.2
  7.2 4.7 %collective-permute-start.1 = (bf16[12,4,1152]{2,1,0:T(4,128)(2,1)S(1)}, bf16[12,4,1152]{2,1,0:T(4,128)(2,1)S(1)}, u32[]{:S(2)}, u32[]{:S(2)}) collective-permute-start(bf16[12,4,1152]{2,1,0:T(4,128)(2,1)S(1)} %pack_half.2.rest_0_.own_piece), channel_id=1, source_target_pairs={{2,4},{4,2},{6,8},{8,6},{10,12},{12,10},{14,16},{16,14},{18,20},{2... | collective-permute-start | bytes 331784 | tf_op jit(solution)/shard_map/ppermute | solution.py:38
  11.9 0.0 collective-permute-done.2.halo_piece
  11.9 0.0 copy-done
  11.9 0.0 copy-done.1
  11.9 0.0 copy-done.2
  11.9 0.0 copy-done.3
  11.9 0.0 copy-done.5
  11.9 0.0 copy-done.6
  11.9 3.1 %swin_near.1.rest_0_ = bf16[12,4,1152]{2,1,0:T(4,128)(2,1)S(1)} custom-call(bf16[12,4,1152]{2,1,0:T(4,128)(2,1)S(1)} %pack_half.3.own_piece, bf16[12,4,1152]{2,1,0:T(4,128)(2,1)S(1)} %collective-permute-done.2.halo_piece, f32[1,192]{1,0:T(1,128)S(1)} %bitcast.10, bf16[192,576]{1,0:T(8,128)(2,1)S(1)} %copy-done.2, bf16[192,192]{1,0:T(8,128)(2,1)S(1)} %copy-done.3, ...), custom_call_target="tpu_custom_call" | custom-call | flops 400000000 | bytes 3000000 | tf_op jit(solution)/shard_map/swin_near/pallas_call | solution.py:296
  15.0 0.0 collective-permute-done.1.halo_piece
  15.1 2.1 %swin_low.1 = (bf16[6,4,1152]{2,1,0:T(4,128)(2,1)S(1)}, bf16[2,3,4,1152]{3,2,1,0:T(4,128)(2,1)S(1)}) custom-call(bf16[12,4,1152]{2,1,0:T(4,128)(2,1)S(1)} %pack_half.2.rest_0_.own_piece, bf16[12,4,1152]{2,1,0:T(4,128)(2,1)S(1)} %collective-permute-done.1.halo_piece, f32[1,192]{1,0:T(1,128)S(1)} %bitcast.11, bf16[192,576]{1,0:T(8,128)(2,1)S(1)} %copy-done.2, ...), custom_call_target="tpu_custom_call" | custom-call | flops 200000000 | bytes 3000000 | tf_op jit(solution)/shard_map/swin_low/pallas_call | solution.py:296
  17.2 1.0 %collective-permute-start.3 = (bf16[2,3,4,1152]{3,2,1,0:T(4,128)(2,1)S(1)}, bf16[2,3,4,1152]{3,2,1,0:T(4,128)(2,1)S(1)}, u32[]{:S(2)}, u32[]{:S(2)}) collective-permute-start(bf16[2,3,4,1152]{3,2,1,0:T(4,128)(2,1)S(1)} %get-tuple-element.15), channel_id=1, source_target_pairs={{0,1},{1,0},{2,3},{3,2},{4,5},{5,4},{6,7},{7,6},{8,9},{9,8},{10,11... | collective-permute-start | bytes 165896 | tf_op jit(solution)/shard_map/ppermute | solution.py:29
  18.3 2.7 %swin_high.1 = (bf16[6,4,1152]{2,1,0:T(4,128)(2,1)S(1)}, bf16[12,4,2304]{2,1,0:T(4,128)(2,1)}) custom-call(bf16[12,4,1152]{2,1,0:T(4,128)(2,1)S(1)} %pack_half.2.rest_0_.own_piece, bf16[12,4,1152]{2,1,0:T(4,128)(2,1)S(1)} %collective-permute-done.1.halo_piece, f32[1,192]{1,0:T(1,128)S(1)} %bitcast.12, bf16[192,576]{1,0:T(8,128)(2,1)S(1)} %copy-done.2, ...), custom_call_target="tpu_custom_call" | custom-call | flops 200000000 | bytes 3000000 | tf_op jit(solution)/shard_map/swin_high/pallas_call | solution.py:296
  21.0 0.4 %collective-permute-done.3.top_ref = bf16[2,3,4,1152]{3,2,1,0:T(4,128)(2,1)S(1)} collective-permute-done((bf16[2,3,4,1152]{3,2,1,0:T(4,128)(2,1)S(1)}, bf16[2,3,4,1152]{3,2,1,0:T(4,128)(2,1)S(1)}, u32[]{:S(2)}, u32[]{:S(2)}) %collective-permute-start.3) | collective-permute-done | bytes 55328 | tf_op jit(solution)/shard_map/ppermute | solution.py:29
  21.4 0.7 %last_rows.1 = bf16[12,4,2304]{2,1,0:T(4,128)(2,1)} custom-call(bf16[2,3,4,1152]{3,2,1,0:T(4,128)(2,1)S(1)} %collective-permute-done.3.top_ref, bf16[6,4,1152]{2,1,0:T(4,128)(2,1)S(1)} %get-tuple-element.17.high_ref, bf16[12,4,2304]{2,1,0:T(4,128)(2,1)} %get-tuple-element.18.done_ref), custom_call_target="tpu_custom_call", output_to_operand_aliasing={{}: (2, {})} | custom-call | bytes 200000 | tf_op jit(solution)/shard_map/last_rows/pallas_call | solution.py:375
  (2 shorter events, 0.0 us)
Async XLA Ops:
  0.0 5.8 %copy-start.4 = (bf16[4,12,2304]{2,0,1:T(4,128)(2,1)S(1)}, bf16[4,12,2304]{2,0,1:T(4,128)(2,1)}, u32[]{:S(2)}) copy-start(bf16[4,12,2304]{2,0,1:T(4,128)(2,1)} %param.8) | copy-start | bytes 663556
  0.9 6.2 %collective-permute-start = (bf16[3,4,2304]{2,1,0:T(4,128)(2,1)S(1)}, bf16[3,4,2304]{2,1,0:T(4,128)(2,1)S(1)}, u32[]{:S(2)}, u32[]{:S(2)}) collective-permute-start(bf16[3,4,2304]{2,1,0:T(4,128)(2,1)S(1)} %slice.4), channel_id=1, source_target_pairs={{0,1},{1,0},{2,3},{3,2},{4,5},{5,4},{6,7},{7,6},{8,9},{9,8},{10,11... | collective-permute-start | bytes 165896 | tf_op jit(solution)/shard_map/ppermute | solution.py:29
  5.8 6.1 %copy-start = (bf16[192,768]{1,0:T(8,128)(2,1)S(1)}, bf16[192,768]{1,0:T(8,128)(2,1)}, u32[]{:S(2)}) copy-start(bf16[192,768]{1,0:T(8,128)(2,1)} %fc1_ref.5) | copy-start | bytes 884740
  5.8 6.1 %copy-start.1 = (bf16[768,192]{0,1:T(8,128)(2,1)S(1)}, bf16[768,192]{0,1:T(8,128)(2,1)}, u32[]{:S(2)}) copy-start(bf16[768,192]{0,1:T(8,128)(2,1)} %param.15) | copy-start | bytes 884740
  5.8 6.0 %copy-start.2 = (bf16[192,576]{1,0:T(8,128)(2,1)S(1)}, bf16[192,576]{1,0:T(8,128)(2,1)}, u32[]{:S(2)}) copy-start(bf16[192,576]{1,0:T(8,128)(2,1)} %qkv_ref.5) | copy-start | bytes 663556
  5.9 6.0 %copy-start.3 = (bf16[192,192]{1,0:T(8,128)(2,1)S(1)}, bf16[192,192]{1,0:T(8,128)(2,1)}, u32[]{:S(2)}) copy-start(bf16[192,192]{1,0:T(8,128)(2,1)} %proj_ref.5) | copy-start | bytes 221188
  5.9 6.0 %copy-start.5 = (f32[192]{0:T(256)S(1)}, f32[192]{0:T(256)}, u32[]{:S(2)}) copy-start(f32[192]{0:T(256)} %param.9) | copy-start | bytes 2308
  5.9 6.0 %copy-start.6 = (f32[192]{0:T(256)S(1)}, f32[192]{0:T(256)}, u32[]{:S(2)}) copy-start(f32[192]{0:T(256)} %param.13) | copy-start | bytes 2308
  7.1 4.7 %collective-permute-start.2 = (bf16[12,4,1152]{2,1,0:T(4,128)(2,1)S(1)}, bf16[12,4,1152]{2,1,0:T(4,128)(2,1)S(1)}, u32[]{:S(2)}, u32[]{:S(2)}) collective-permute-start(bf16[12,4,1152]{2,1,0:T(4,128)(2,1)S(1)} %pack_half.3.own_piece), channel_id=1, source_target_pairs={{0,2},{2,0},{4,6},{6,4},{8,10},{10,8},{12,14},{14,12},{16,18},{18,... | collective-permute-start | bytes 331784 | tf_op jit(solution)/shard_map/ppermute | solution.py:38
  7.2 7.8 %collective-permute-start.1 = (bf16[12,4,1152]{2,1,0:T(4,128)(2,1)S(1)}, bf16[12,4,1152]{2,1,0:T(4,128)(2,1)S(1)}, u32[]{:S(2)}, u32[]{:S(2)}) collective-permute-start(bf16[12,4,1152]{2,1,0:T(4,128)(2,1)S(1)} %pack_half.2.rest_0_.own_piece), channel_id=1, source_target_pairs={{2,4},{4,2},{6,8},{8,6},{10,12},{12,10},{14,16},{16,14},{18,20},{2... | collective-permute-start | bytes 331784 | tf_op jit(solution)/shard_map/ppermute | solution.py:38
  17.2 4.2 %collective-permute-start.3 = (bf16[2,3,4,1152]{3,2,1,0:T(4,128)(2,1)S(1)}, bf16[2,3,4,1152]{3,2,1,0:T(4,128)(2,1)S(1)}, u32[]{:S(2)}, u32[]{:S(2)}) collective-permute-start(bf16[2,3,4,1152]{3,2,1,0:T(4,128)(2,1)S(1)} %get-tuple-element.15), channel_id=1, source_target_pairs={{0,1},{1,0},{2,3},{3,2},{4,5},{5,4},{6,7},{7,6},{8,9},{9,8},{10,11... | collective-permute-start | bytes 165896 | tf_op jit(solution)/shard_map/ppermute | solution.py:29

commit v8 on v7

--- a/solution.py
+++ b/solution.py
@@ -66,14 +66,33 @@
         copy.wait()
 
 
-def table_kernel(bias_ref, field_ref, table_ref, near_ref, far_ref):
-    rows = field_ref.shape[0] - EDGE
-    near_at, far_at = half_places(near_ref.shape[2])
-    near_ref[:rows] = field_ref[EDGE:, :, pl.ds(near_at, near_ref.shape[2])]
-    far_ref[:rows] = field_ref[EDGE:, :, pl.ds(far_at, far_ref.shape[2])]
-    heads = bias_ref.shape[2]
+def table_kernel(count, *refs):
+    bias_any, field_any, *weights_any = refs[: 2 + count]
+    table_ref, near_ref, far_ref, *weights_ref = refs[2 + count : 5 + 2 * count]
+    bias_ref, sems, side_sems = refs[5 + 2 * count :]
+    windows, heads = bias_any.shape[:2]
+    copies = {}
+    for k in range(windows):
+        for h in range(heads):
+            target = bias_ref.at[k, pl.ds(2 * h, 2)]
+            copies[k, h] = pltpu.make_async_copy(bias_any.at[k, h], target, sems.at[k, h])
+            copies[k, h].start()
+    rows, half = field_any.shape[0] - EDGE, near_ref.shape[2]
+    near_at, far_at = half_places(half)
+    fetches = [
+        (field_any.at[EDGE:, :, pl.ds(far_at, half)], far_ref.at[:rows]),
+        (field_any.at[EDGE:, :, pl.ds(near_at, half)], near_ref.at[:rows]),
+    ]
+    fetches += list(zip(weights_any, weights_ref))
+    fetches = [
+        pltpu.make_async_copy(source, target, side_sems.at[n])
+        for n, (source, target) in enumerate(fetches)
+    ]
+    for copy in fetches:
+        copy.start()
     width = 9 * LANES
-    lane = lax.broadcasted_iota(jnp.int32, (1, LANES), 1)
+    lane = lax.broadcasted_iota(jnp.int32, (8, LANES), 1)
+    upper = lax.rem(lax.broadcasted_iota(jnp.int32, (8, LANES), 0), 2) == 1
     is_last = lax.axis_index("lat") == lax.axis_size("lat") - 1
     last = jnp.where(is_last, -1e9, 0.0).astype(jnp.float32)
 
@@ -81,27 +100,27 @@
         key = lane + first
         key_lev = (key >= QUERIES).astype(jnp.int32)
         key_side = ((key - key_lev * QUERIES) >= QUERIES // 2).astype(jnp.int32)
-        out = jnp.zeros((1, LANES), jnp.float32)
-        if lev is not None:
-            out = jnp.where(key_lev != lev, -1e9, out)
+        out = jnp.where(upper & (key_lev != lev), -1e9, jnp.zeros((8, LANES), jnp.float32))
         if wrap:
             out = out + jnp.where(key_side != side, last, 0.0)
         return out
 
-    for k in range(2):
-        for p in range(2):
-            masks = {}
-            for lev in range(2):
-                for side in range(2):
-                    masks[lev, side] = [
-                        penalty(first, lev if p == 1 else None, side, k == 1)
-                        for first in (0, LANES)
-                    ]
+    for k in range(windows):
+        masks = {
+            (lev, side, part): penalty(part * LANES, lev, side, k == windows - 1)
+            for lev in range(2)
+            for side in range(2)
+            for part in range(2)
+        }
+        for h in range(heads):
+            copies[k, h].wait()
+        for first in range(0, 2 * heads, 8):
+            count = min(8, 2 * heads - first)
             for c in range(TOKENS // 8):
-                tiles = [
-                    bias_ref[k, p, :, c * width + u * LANES : c * width + (u + 1) * LANES]
-                    for u in range(9)
-                ]
+                tiles = []
+                for u in range(9):
+                    at = c * width + u * LANES
+                    tiles.append(bias_ref[k, first : first + count, at : at + LANES] * LOG2E)
                 for r in range(8):
                     i = 8 * c + r
                     shift = 16 * r
@@ -110,16 +129,18 @@
                     if r:
                         main = pltpu.roll(main, LANES - shift, 1)
                         nxt = pltpu.roll(nxt, LANES - shift, 1)
-                        main = jnp.where(lane < LANES - shift, main, nxt)
+                        main = jnp.where(lane[:count] < LANES - shift, main, nxt)
                     lev = i // QUERIES
                     row = i % QUERIES // WIN_LON
                     col = i % WIN_LON
                     side = col // HALF
-                    place = lev * 36 + row * HALF + col % HALF
-                    mask = masks[lev, row // EDGE]
-                    at = pl.ds(place, heads, stride=QUERIES)
-                    table_ref[k, p, 1 - side, 0, at, :] = main * LOG2E + mask[0]
-                    table_ref[k, p, 1 - side, 1, at, :] = nxt * LOG2E + mask[1]
+                    place = first * QUERIES + lev * 36 + row * HALF + col % HALF
+                    at = pl.ds(place, count, stride=QUERIES)
+                    for part, piece in enumerate((main, nxt)):
+                        mask = masks[lev, row // EDGE, part]
+                        table_ref[k, 1 - side, part, at, :] = piece + mask[:count]
+    for copy in fetches:
+        copy.wait()
 
 
 def layer_norm(values, gain):
@@ -226,7 +247,11 @@
             ]
             picked = jnp.concatenate(picked, axis=0).astype(jnp.bfloat16)
             scores = lax.dot_general(picked, k, NT, preferred_element_type=jnp.float32)
-            table = [table_ref[windows[n], p, right, part] for part in range(2)]
+            table = []
+            for part in range(2):
+                firsts = [(2 * h + p) * QUERIES for h in range(heads)]
+                pieces = [table_ref[windows[n], right, part, f : f + QUERIES] for f in firsts]
+                table.append(jnp.concatenate(pieces, axis=0))
             table = jnp.concatenate([table[0], table[1][:, : TOKENS - LANES]], axis=1)
             scores = scores + table
             top = jnp.max(scores, axis=1, keepdims=True)
@@ -322,22 +347,35 @@
     half = HALF * chans
     field = jnp.transpose(field_in, (1, 0, 2))
     south = moved(field[:EDGE], "lat", -1)
+    weights = (
+        norm1_gain.reshape(1, chans),
+        qkv_weight,
+        proj_weight,
+        norm2_gain.reshape(1, chans),
+        fc1_weight,
+        jnp.transpose(fc2_weight),
+    )
     vmem = pl.BlockSpec(memory_space=pltpu.VMEM)
+    anywhere = pl.BlockSpec(memory_space=pl.ANY)
     piece = jax.ShapeDtypeStruct((rows, levels, half), field.dtype)
-    table, near, far = pl.pallas_call(
-        table_kernel,
-        out_shape=[
-            jax.ShapeDtypeStruct((2, 2, 2, 2, heads * QUERIES, LANES), jnp.float32),
-            piece,
-            piece,
+    table = jax.ShapeDtypeStruct((2, 2, 2, 2 * heads * QUERIES, LANES), jnp.float32)
+    sources = (jnp.transpose(earth_bias, (0, 2, 1, 3)), field) + weights
+    sources = [pltpu.with_memory_space_constraint(x, pltpu.HBM) for x in sources]
+    outs = [table, piece, piece] + [jax.ShapeDtypeStruct(x.shape, x.dtype) for x in weights]
+    table, near, far, *weights = pl.pallas_call(
+        functools.partial(table_kernel, len(weights)),
+        out_shape=outs,
+        in_specs=[pl.BlockSpec(memory_space=pltpu.HBM)] * len(sources),
+        out_specs=[vmem] * len(outs),
+        scratch_shapes=[
+            pltpu.VMEM((2, 2 * heads, earth_bias.shape[3]), jnp.float32),
+            pltpu.SemaphoreType.DMA((2, heads)),
+            pltpu.SemaphoreType.DMA((2 + len(weights),)),
         ],
-        in_specs=[vmem, vmem],
-        out_specs=[vmem] * 3,
         compiler_params=pltpu.CompilerParams(vmem_limit_bytes=VMEM_BYTES),
         cost_estimate=pl.CostEstimate(flops=4_000_000, bytes_accessed=6_000_000, transcendentals=0),
         name="bias_tables",
-    )(earth_bias, field)
-    anywhere = pl.BlockSpec(memory_space=pl.ANY)
+    )(*sources)
 
     def pack(which, kept, *after):
         return pl.pallas_call(
@@ -354,14 +392,6 @@
     near = pack(0, near, far)
     far_halo = swapped(far, "lon", 1)
     near_halo = swapped(near, "lon", 0)
-    weights = (
-        norm1_gain.reshape(1, chans),
-        qkv_weight,
-        proj_weight,
-        norm2_gain.reshape(1, chans),
-        fc1_weight,
-        jnp.transpose(fc2_weight),
-    )
     (near_done,) = run_side(
         near, near_halo, table, (0, 1), "near", weights, chans, heads, ()
     )

time: 22.2 us -> 21.8 us (0.982)
  local copies, waits for them, and re-layouts: 2.84 us -> 0.83 us
  Pallas kernels: 9.84 us -> 11.4 us
  waiting for transfers between devices: 0.46 us -> 0.04 us
  starting transfers between devices: 8.78 us -> 9.19 us
    unnamed x15 -> x0, local copies, waits for them, and re-layouts: 1.94 us -> none
    pallas_call x1, Pallas kernels: 1.17 us -> 2.74 us  [shards(): pl.pallas_call(functools.partial(table_kernel, len(weights)), out_shape=o...]
    ppermute x2, waiting for transfers between devices: 0.45 us -> 0.04 us  [moved(): return lax.ppermute(x, axis, [(i, (i + by) % size) for i in range(size)])]
    ppermute x2, starting transfers between devices: 4.05 us -> 4.46 us  [moved(): return lax.ppermute(x, axis, [(i, (i + by) % size) for i in range(size)])]
  transfers between devices with their start and end apart: 4 -> 4, of which waited for: 1 -> 0; matrix products, arithmetic and copies ran while one was open for 9% -> 0% of each run, Pallas kernels for 32% -> 40%
where the time goes in v8:
time: 21.8 us; the launch traced here: 21.6 us
  Pallas kernels  11.4 us (52%)
  starting transfers between devices  9.19 us (42%)
  local copies, waits for them, and re-layouts  0.83 us (4%)
    pallas_call x3, Pallas kernels, run_side(): pl.pallas_call(functools.partial(side_kernel, chans, heads, windows, part...  7.97 us
    ppermute x2, starting transfers between devices, swapped(): return lax.ppermute(x, axis, pairs)  4.73 us
    ppermute x2, starting transfers between devices, moved(): return lax.ppermute(x, axis, [(i, (i + by) % size) for i in range(size)])  4.46 us
    pallas_call x1, Pallas kernels, shards(): pl.pallas_call(functools.partial(table_kernel, len(weights)), out_shape=o...  2.74 us
    slice x1, local copies, waits for them, and re-layouts, shards(): south = moved(field[:EDGE], 'lat', -1)  0.83 us
    pallas_call x1, Pallas kernels, shards(): pl.pallas_call(last_kernel, out_shape=jax.ShapeDtypeStruct(done.shape, do...  0.67 us
  transfers between devices with their start and end apart: 4, of which 0 were waited for; matrix products, arithmetic and copies ran while one was open for 0% of the time, Pallas kernels for 40%

profile of v8, /device:TPU:0, one launch (start us, length us, event | category | flops | bytes accessed | tf_op | source)
XLA Modules:
  0.0 21.6 jit_solution(6094936423557343684)
XLA Ops:
  0.0 0.8 %slice.4 = bf16[3,4,2304]{2,1,0:T(4,128)(2,1)S(1)} slice(bf16[12,4,2304]{2,1,0:T(4,128)(2,1)} %bitcast.7), slice={[0:3], [0:4], [0:2304]} | slice | bytes 110592 | tf_op jit(solution)/shard_map/slice | solution.py:349
  0.8 3.0 %collective-permute-start = (bf16[3,4,2304]{2,1,0:T(4,128)(2,1)S(1)}, bf16[3,4,2304]{2,1,0:T(4,128)(2,1)S(1)}, u32[]{:S(2)}, u32[]{:S(2)}) collective-permute-start(bf16[3,4,2304]{2,1,0:T(4,128)(2,1)S(1)} %slice.4), channel_id=1, source_target_pairs={{0,1},{1,0},{2,3},{3,2},{4,5},{5,4},{6,7},{7,6},{8,9},{9,8},{10,11... | collective-permute-start | bytes 165896 | tf_op jit(solution)/shard_map/ppermute | solution.py:29
  3.8 2.7 %bias_tables.1 = (f32[2,2,2,864,128]{4,3,2,1,0:T(8,128)S(1)}, bf16[12,4,1152]{2,1,0:T(4,128)(2,1)S(1)}, bf16[12,4,1152]{2,1,0:T(4,128)(2,1)S(1)}, f32[1,192]{1,0...) custom-call(f32[2,6,2,20736]{3,2,1,0:T(2,128)} %bitcast.6, ...), custom_call_target="tpu_custom_call" | custom-call | flops 4000000 | bytes 6000000 | tf_op jit(solution)/shard_map/bias_tables/pallas_call | solution.py:365
  6.6 0.0 collective-permute-done.south_ref
  6.7 0.1 collective-permute-start.2
  6.7 4.7 %collective-permute-start.1 = (bf16[12,4,1152]{2,1,0:T(4,128)(2,1)S(1)}, bf16[12,4,1152]{2,1,0:T(4,128)(2,1)S(1)}, u32[]{:S(2)}, u32[]{:S(2)}) collective-permute-start(bf16[12,4,1152]{2,1,0:T(4,128)(2,1)S(1)} %pack_half.2.rest_0_.own_piece), channel_id=1, source_target_pairs={{2,4},{4,2},{6,8},{8,6},{10,12},{12,10},{14,16},{16,14},{18,20},{2... | collective-permute-start | bytes 331784 | tf_op jit(solution)/shard_map/ppermute | solution.py:38
  11.4 0.0 collective-permute-done.2.halo_piece
  11.4 3.1 %swin_near.1.rest_0_ = bf16[12,4,1152]{2,1,0:T(4,128)(2,1)S(1)} custom-call(bf16[12,4,1152]{2,1,0:T(4,128)(2,1)S(1)} %pack_half.3.own_piece, bf16[12,4,1152]{2,1,0:T(4,128)(2,1)S(1)} %collective-permute-done.2.halo_piece, f32[1,192]{1,0:T(1,128)S(1)} %get-tuple-element.19.gain1_ref, bf16[192,576]{1,0:T(8,128)(2,1)S(1)} %get-tuple-element.20.qkv_ref, ...), custom_call_target="tpu_custom_call" | custom-call | flops 400000000 | bytes 3000000 | tf_op jit(solution)/shard_map/swin_near/pallas_call | solution.py:321
  14.5 0.0 collective-permute-done.1.halo_piece
  14.5 2.1 %swin_low.1 = (bf16[6,4,1152]{2,1,0:T(4,128)(2,1)S(1)}, bf16[2,3,4,1152]{3,2,1,0:T(4,128)(2,1)S(1)}) custom-call(bf16[12,4,1152]{2,1,0:T(4,128)(2,1)S(1)} %pack_half.2.rest_0_.own_piece, bf16[12,4,1152]{2,1,0:T(4,128)(2,1)S(1)} %collective-permute-done.1.halo_piece, f32[1,192]{1,0:T(1,128)S(1)} %get-tuple-element.19.gain1_ref, ...), custom_call_target="tpu_custom_call" | custom-call | flops 200000000 | bytes 3000000 | tf_op jit(solution)/shard_map/swin_low/pallas_call | solution.py:321
  16.7 1.5 %collective-permute-start.3 = (bf16[2,3,4,1152]{3,2,1,0:T(4,128)(2,1)S(1)}, bf16[2,3,4,1152]{3,2,1,0:T(4,128)(2,1)S(1)}, u32[]{:S(2)}, u32[]{:S(2)}) collective-permute-start(bf16[2,3,4,1152]{3,2,1,0:T(4,128)(2,1)S(1)} %get-tuple-element.27), channel_id=1, source_target_pairs={{0,1},{1,0},{2,3},{3,2},{4,5},{5,4},{6,7},{7,6},{8,9},{9,8},{10,11... | collective-permute-start | bytes 165896 | tf_op jit(solution)/shard_map/ppermute | solution.py:29
  18.1 2.7 %swin_high.1 = (bf16[6,4,1152]{2,1,0:T(4,128)(2,1)S(1)}, bf16[12,4,2304]{2,1,0:T(4,128)(2,1)}) custom-call(bf16[12,4,1152]{2,1,0:T(4,128)(2,1)S(1)} %pack_half.2.rest_0_.own_piece, bf16[12,4,1152]{2,1,0:T(4,128)(2,1)S(1)} %collective-permute-done.1.halo_piece, f32[1,192]{1,0:T(1,128)S(1)} %get-tuple-element.19.gain1_ref, ...), custom_call_target="tpu_custom_call" | custom-call | flops 200000000 | bytes 3000000 | tf_op jit(solution)/shard_map/swin_high/pallas_call | solution.py:321
  20.9 0.0 collective-permute-done.3.top_ref
  20.9 0.7 %last_rows.1 = bf16[12,4,2304]{2,1,0:T(4,128)(2,1)} custom-call(bf16[2,3,4,1152]{3,2,1,0:T(4,128)(2,1)S(1)} %collective-permute-done.3.top_ref, bf16[6,4,1152]{2,1,0:T(4,128)(2,1)S(1)} %get-tuple-element.29.high_ref, bf16[12,4,2304]{2,1,0:T(4,128)(2,1)} %get-tuple-element.30.done_ref), custom_call_target="tpu_custom_call", output_to_operand_aliasing={{}: (2, {})} | custom-call | bytes 200000 | tf_op jit(solution)/shard_map/last_rows/pallas_call | solution.py:405
  (2 shorter events, 0.0 us)
Async XLA Ops:
  0.8 5.8 %collective-permute-start = (bf16[3,4,2304]{2,1,0:T(4,128)(2,1)S(1)}, bf16[3,4,2304]{2,1,0:T(4,128)(2,1)S(1)}, u32[]{:S(2)}, u32[]{:S(2)}) collective-permute-start(bf16[3,4,2304]{2,1,0:T(4,128)(2,1)S(1)} %slice.4), channel_id=1, source_target_pairs={{0,1},{1,0},{2,3},{3,2},{4,5},{5,4},{6,7},{7,6},{8,9},{9,8},{10,11... | collective-permute-start | bytes 165896 | tf_op jit(solution)/shard_map/ppermute | solution.py:29
  6.7 4.7 %collective-permute-start.2 = (bf16[12,4,1152]{2,1,0:T(4,128)(2,1)S(1)}, bf16[12,4,1152]{2,1,0:T(4,128)(2,1)S(1)}, u32[]{:S(2)}, u32[]{:S(2)}) collective-permute-start(bf16[12,4,1152]{2,1,0:T(4,128)(2,1)S(1)} %pack_half.3.own_piece), channel_id=1, source_target_pairs={{0,2},{2,0},{4,6},{6,4},{8,10},{10,8},{12,14},{14,12},{16,18},{18,... | collective-permute-start | bytes 331784 | tf_op jit(solution)/shard_map/ppermute | solution.py:38
  6.7 7.8 %collective-permute-start.1 = (bf16[12,4,1152]{2,1,0:T(4,128)(2,1)S(1)}, bf16[12,4,1152]{2,1,0:T(4,128)(2,1)S(1)}, u32[]{:S(2)}, u32[]{:S(2)}) collective-permute-start(bf16[12,4,1152]{2,1,0:T(4,128)(2,1)S(1)} %pack_half.2.rest_0_.own_piece), channel_id=1, source_target_pairs={{2,4},{4,2},{6,8},{8,6},{10,12},{12,10},{14,16},{16,14},{18,20},{2... | collective-permute-start | bytes 331784 | tf_op jit(solution)/shard_map/ppermute | solution.py:38
  16.7 4.2 %collective-permute-start.3 = (bf16[2,3,4,1152]{3,2,1,0:T(4,128)(2,1)S(1)}, bf16[2,3,4,1152]{3,2,1,0:T(4,128)(2,1)S(1)}, u32[]{:S(2)}, u32[]{:S(2)}) collective-permute-start(bf16[2,3,4,1152]{3,2,1,0:T(4,128)(2,1)S(1)} %get-tuple-element.27), channel_id=1, source_target_pairs={{0,1},{1,0},{2,3},{3,2},{4,5},{5,4},{6,7},{7,6},{8,9},{9,8},{10,11... | collective-permute-start | bytes 165896 | tf_op jit(solution)/shard_map/ppermute | solution.py:29

commit v9 on v8

--- a/solution.py
+++ b/solution.py
@@ -29,12 +29,12 @@
     return lax.ppermute(x, axis, [(i, (i + by) % size) for i in range(size)])
 
 
-def swapped(x, axis, first):
+def swapped(x, axis, first, ways=(True, True)):
     size = lax.axis_size(axis)
     pairs = []
     for i in range(first, size, 2):
         j = (i + 1) % size
-        pairs += [(i, j), (j, i)]
+        pairs += [(i, j)] * ways[0] + [(j, i)] * ways[1]
     return lax.ppermute(x, axis, pairs)
 
 
@@ -49,6 +49,18 @@
     rows = piece_ref.shape[0] - EDGE
     piece_ref[:rows] = kept_ref[:rows]
     piece_ref[rows:] = south_ref[:, :, pl.ds(at, piece_ref.shape[2])]
+
+
+def pick_kernel(even_ref, odd_ref, out_ref):
+    odd = lax.rem(lax.axis_index("lon"), 2)
+
+    @pl.when(odd == 0)
+    def _():
+        out_ref[...] = even_ref[...]
+
+    @pl.when(odd == 1)
+    def _():
+        out_ref[...] = odd_ref[...]
 
 
 def last_kernel(top_ref, high_ref, done_ref, out_ref, sems):
@@ -112,10 +124,10 @@
             for side in range(2)
             for part in range(2)
         }
-        for h in range(heads):
-            copies[k, h].wait()
         for first in range(0, 2 * heads, 8):
             count = min(8, 2 * heads - first)
+            for h in range(first // 2, (first + count) // 2):
+                copies[k, h].wait()
             for c in range(TOKENS // 8):
                 tiles = []
                 for u in range(9):
@@ -155,6 +167,40 @@
 
 
 def side_kernel(
+    chans,
+    heads,
+    windows,
+    part_of,
+    own_piece,
+    *rest,
+):
+    lon = lax.axis_index("lon")
+    if part_of == "seam":
+        halo_piece, *rest, far_in, out_ref, far_out, keys_ref, own_ref, res_ref = rest
+        refs = rest + [out_ref, keys_ref, own_ref, res_ref]
+        far_out[...] = far_in[...]
+
+        @pl.when(lon == 0)
+        def _():
+            side_body(chans, heads, windows, "near", own_piece, halo_piece, *refs)
+
+    elif part_of == "near":
+        halo_piece, *rest, seam_ref, out_ref, keys_ref, own_ref, res_ref = rest
+        refs = rest + [out_ref, keys_ref, own_ref, res_ref]
+
+        @pl.when(lon != 0)
+        def _():
+            side_body(chans, heads, windows, "near", own_piece, halo_piece, *refs)
+
+        @pl.when(lon == 0)
+        def _():
+            out_ref[...] = seam_ref[...]
+
+    else:
+        side_body(chans, heads, windows, part_of, own_piece, *rest)
+
+
+def side_body(
     chans,
     heads,
     windows,
@@ -314,13 +360,13 @@
     out = jax.ShapeDtypeStruct((rows,) + own.shape[1:], own.dtype)
     send = jax.ShapeDtypeStruct((2, EDGE) + own.shape[1:], own.dtype)
     done = jax.ShapeDtypeStruct(own.shape[:2] + (2 * own.shape[2],), own.dtype)
-    outs = {"near": [out], "low": [out, send], "high": [out, done]}[part_of]
+    outs = {"seam": [out, own], "near": [out], "low": [out, send], "high": [out, done]}[part_of]
     extra = [pltpu.SemaphoreType.DMA((2,))]
     gain1, qkv, proj, gain2, fc1, fc2 = weights
     operands = (gain1, qkv, proj, table, gain2, fc1, fc2) + before
     return pl.pallas_call(
         functools.partial(side_kernel, chans, heads, windows, part_of),
-        out_shape=outs,
+        out_shape=[jax.ShapeDtypeStruct(x.shape, x.dtype) for x in outs],
         grid=(1,),
         in_specs=[piece, piece] + [whole(x) for x in operands],
         out_specs=[whole(out), anywhere] if part_of == "high" else [whole(x) for x in outs],
@@ -388,13 +434,29 @@
             name="pack_half",
         )(south, kept, *after)
 
+    def pick(even, odd):
+        return pl.pallas_call(
+            pick_kernel,
+            out_shape=piece,
+            in_specs=[vmem] * 2,
+            out_specs=vmem,
+            compiler_params=pltpu.CompilerParams(vmem_limit_bytes=VMEM_BYTES),
+            cost_estimate=pl.CostEstimate(flops=0, bytes_accessed=350_000, transcendentals=0),
+            name="pick_halo",
+        )(even, odd)
+
     far = pack(1, far)
     near = pack(0, near, far)
-    far_halo = swapped(far, "lon", 1)
     near_halo = swapped(near, "lon", 0)
+    halo_even = swapped(far, "lon", 1, (True, False))
+    seam_done, far_later = run_side(
+        near, near_halo, table, (0, 1), "seam", weights, chans, heads, (far,)
+    )
+    halo_odd = swapped(far_later, "lon", 1, (False, True))
     (near_done,) = run_side(
-        near, near_halo, table, (0, 1), "near", weights, chans, heads, ()
+        near, near_halo, table, (0, 1), "near", weights, chans, heads, (seam_done,)
     )
+    far_halo = pick(halo_even, halo_odd)
     far_low, send = run_side(
         far, far_halo, table, (1,), "low", weights, chans, heads, (near_done,)
     )

time: 21.8 us -> 24.6 us (1.13)
  waiting for transfers between devices: 0.04 us -> 2.3 us
  starting transfers between devices: 9.19 us -> 9.71 us
    ppermute x2 -> x3, waiting for transfers between devices: 0.01 us -> 2.27 us  [swapped(): return lax.ppermute(x, axis, pairs)]
    ppermute x2 -> x3, starting transfers between devices: 4.73 us -> 5.25 us  [swapped(): return lax.ppermute(x, axis, pairs)]
    pallas_call x3 -> x4, Pallas kernels: 7.97 us -> 8.01 us  [run_side(): pl.pallas_call(functools.partial(side_kernel, chans, heads, windows, part...]
  transfers between devices with their start and end apart: 4 -> 5, of which waited for: 0 -> 2; matrix products, arithmetic and copies ran while one was open for 0% -> 0% of each run, Pallas kernels for 40% -> 35%
where the time goes in v9:
time: 24.6 us; the launch traced here: 24.4 us
  Pallas kernels  11.5 us (47%)
  starting transfers between devices  9.71 us (39%)
  waiting for transfers between devices  2.3 us (9%)
  local copies, waits for them, and re-layouts  0.83 us (3%)
    pallas_call x4, Pallas kernels, run_side(): pl.pallas_call(functools.partial(side_kernel, chans, heads, windows, part...  8.01 us
    ppermute x3, starting transfers between devices, swapped(): return lax.ppermute(x, axis, pairs)  5.25 us
    ppermute x2, starting transfers between devices, moved(): return lax.ppermute(x, axis, [(i, (i + by) % size) for i in range(size)])  4.46 us
    pallas_call x1, Pallas kernels, shards(): pl.pallas_call(functools.partial(table_kernel, len(weights)), out_shape=o...  2.74 us
    ppermute x3, waiting for transfers between devices, swapped(): return lax.ppermute(x, axis, pairs)  2.27 us
    slice x1, local copies, waits for them, and re-layouts, shards(): south = moved(field[:EDGE], 'lat', -1)  0.83 us
    pallas_call x1, Pallas kernels, shards(): pl.pallas_call(last_kernel, out_shape=jax.ShapeDtypeStruct(done.shape, do...  0.67 us
  transfers between devices with their start and end apart: 5, of which 2 were waited for; matrix products, arithmetic and copies ran while one was open for 0% of the time, Pallas kernels for 35%

profile of v9, /device:TPU:0, one launch (start us, length us, event | category | flops | bytes accessed | tf_op | source)
XLA Modules:
  0.0 24.4 jit_solution(16121042847762582118)
XLA Ops:
  0.0 0.8 %slice.4 = bf16[3,4,2304]{2,1,0:T(4,128)(2,1)S(1)} slice(bf16[12,4,2304]{2,1,0:T(4,128)(2,1)} %bitcast.7), slice={[0:3], [0:4], [0:2304]} | slice | bytes 110592 | tf_op jit(solution)/shard_map/slice | solution.py:395
  0.8 3.0 %collective-permute-start = (bf16[3,4,2304]{2,1,0:T(4,128)(2,1)S(1)}, bf16[3,4,2304]{2,1,0:T(4,128)(2,1)S(1)}, u32[]{:S(2)}, u32[]{:S(2)}) collective-permute-start(bf16[3,4,2304]{2,1,0:T(4,128)(2,1)S(1)} %slice.4), channel_id=1, source_target_pairs={{0,1},{1,0},{2,3},{3,2},{4,5},{5,4},{6,7},{7,6},{8,9},{9,8},{10,11... | collective-permute-start | bytes 165896 | tf_op jit(solution)/shard_map/ppermute | solution.py:29
  3.8 2.7 %bias_tables.1 = (f32[2,2,2,864,128]{4,3,2,1,0:T(8,128)S(1)}, bf16[12,4,1152]{2,1,0:T(4,128)(2,1)S(1)}, bf16[12,4,1152]{2,1,0:T(4,128)(2,1)S(1)}, f32[1,192]{1,0...) custom-call(f32[2,6,2,20736]{3,2,1,0:T(2,128)} %bitcast.6, ...), custom_call_target="tpu_custom_call" | custom-call | flops 4000000 | bytes 6000000 | tf_op jit(solution)/shard_map/bias_tables/pallas_call | solution.py:411
  6.6 0.0 collective-permute-done.south_ref
  6.7 0.1 collective-permute-start.2
  6.7 1.3 %collective-permute-start.1 = (bf16[12,4,1152]{2,1,0:T(4,128)(2,1)S(1)}, bf16[12,4,1152]{2,1,0:T(4,128)(2,1)S(1)}, u32[]{:S(2)}, u32[]{:S(2)}) collective-permute-start(bf16[12,4,1152]{2,1,0:T(4,128)(2,1)S(1)} %pack_half.2.rest_0_.rest_8_.own_piece), channel_id=1, source_target_pairs={{2,4},{6,8},{10,12},{14,16},{18,20},{22,24},{26,28},{30,0},{3,5},{... | collective-permute-start | bytes 331784 | tf_op jit(solution)/shard_map/ppermute | solution.py:38
  8.0 0.0 collective-permute-done.2.rest_0_
  8.0 3.1 %swin_seam.1 = (bf16[12,4,1152]{2,1,0:T(4,128)(2,1)S(1)}, bf16[12,4,1152]{2,1,0:T(4,128)(2,1)S(1)}) custom-call(bf16[12,4,1152]{2,1,0:T(4,128)(2,1)S(1)} %pack_half.3.own_piece, bf16[12,4,1152]{2,1,0:T(4,128)(2,1)S(1)} %collective-permute-done.2.rest_0_, f32[1,192]{1,0:T(1,128)S(1)} %get-tuple-element.22.rest_1_, ...), custom_call_target="tpu_custom_call" | custom-call | flops 400000000 | bytes 3000000 | tf_op jit(solution)/shard_map/swin_seam/pallas_call | solution.py:367
  11.2 3.9 %collective-permute-start.3 = (bf16[12,4,1152]{2,1,0:T(4,128)(2,1)S(1)}, bf16[12,4,1152]{2,1,0:T(4,128)(2,1)S(1)}, u32[]{:S(2)}, u32[]{:S(2)}) collective-permute-start(bf16[12,4,1152]{2,1,0:T(4,128)(2,1)S(1)} %get-tuple-element.29), channel_id=1, source_target_pairs={{4,2},{8,6},{12,10},{16,14},{20,18},{24,22},{28,26},{0,30},{5,3},{... | collective-permute-start | bytes 331784 | tf_op jit(solution)/shard_map/ppermute | solution.py:38
  15.1 0.4 %collective-permute-done.1.even_ref = bf16[12,4,1152]{2,1,0:T(4,128)(2,1)S(1)} collective-permute-done((bf16[12,4,1152]{2,1,0:T(4,128)(2,1)S(1)}, bf16[12,4,1152]{2,1,0:T(4,128)(2,1)S(1)}, u32[]{:S(2)}, u32[]{:S(2)}) %collective-permute-start.1) | collective-permute-done | bytes 110624 | tf_op jit(solution)/shard_map/ppermute | solution.py:38
  15.5 1.8 %collective-permute-done.3.odd_ref = bf16[12,4,1152]{2,1,0:T(4,128)(2,1)S(1)} collective-permute-done((bf16[12,4,1152]{2,1,0:T(4,128)(2,1)S(1)}, bf16[12,4,1152]{2,1,0:T(4,128)(2,1)S(1)}, u32[]{:S(2)}, u32[]{:S(2)}) %collective-permute-start.3) | collective-permute-done | bytes 110624 | tf_op jit(solution)/shard_map/ppermute | solution.py:38
  17.4 2.1 %swin_low.1 = (bf16[6,4,1152]{2,1,0:T(4,128)(2,1)S(1)}, bf16[2,3,4,1152]{3,2,1,0:T(4,128)(2,1)S(1)}) custom-call(bf16[12,4,1152]{2,1,0:T(4,128)(2,1)S(1)} %pack_half.2.rest_0_.rest_8_.own_piece, bf16[12,4,1152]{2,1,0:T(4,128)(2,1)S(1)} %pick_halo.1.rest_0_, f32[1,192]{1,0:T(1,128)S(1)} %get-tuple-element.22.rest_1_, ...), custom_call_target="tpu_custom_call" | custom-call | flops 200000000 | bytes 3000000 | tf_op jit(solution)/shard_map/swin_low/pallas_call | solution.py:367
  19.5 1.5 %collective-permute-start.4 = (bf16[2,3,4,1152]{3,2,1,0:T(4,128)(2,1)S(1)}, bf16[2,3,4,1152]{3,2,1,0:T(4,128)(2,1)S(1)}, u32[]{:S(2)}, u32[]{:S(2)}) collective-permute-start(bf16[2,3,4,1152]{3,2,1,0:T(4,128)(2,1)S(1)} %get-tuple-element.31), channel_id=1, source_target_pairs={{0,1},{1,0},{2,3},{3,2},{4,5},{5,4},{6,7},{7,6},{8,9},{9,8},{10,11... | collective-permute-start | bytes 165896 | tf_op jit(solution)/shard_map/ppermute | solution.py:29
  21.0 2.7 %swin_high.1 = (bf16[6,4,1152]{2,1,0:T(4,128)(2,1)S(1)}, bf16[12,4,2304]{2,1,0:T(4,128)(2,1)}) custom-call(bf16[12,4,1152]{2,1,0:T(4,128)(2,1)S(1)} %pack_half.2.rest_0_.rest_8_.own_piece, bf16[12,4,1152]{2,1,0:T(4,128)(2,1)S(1)} %pick_halo.1.rest_0_, f32[1,192]{1,0:T(1,128)S(1)} %get-tuple-element.22.rest_1_, ...), custom_call_target="tpu_custom_call" | custom-call | flops 200000000 | bytes 3000000 | tf_op jit(solution)/shard_map/swin_high/pallas_call | solution.py:367
  23.7 0.0 collective-permute-done.4.top_ref
  23.8 0.7 %last_rows.1 = bf16[12,4,2304]{2,1,0:T(4,128)(2,1)} custom-call(bf16[2,3,4,1152]{3,2,1,0:T(4,128)(2,1)S(1)} %collective-permute-done.4.top_ref, bf16[6,4,1152]{2,1,0:T(4,128)(2,1)S(1)} %get-tuple-element.33.high_ref, bf16[12,4,2304]{2,1,0:T(4,128)(2,1)} %get-tuple-element.34.done_ref), custom_call_target="tpu_custom_call", output_to_operand_aliasing={{}: (2, {})} | custom-call | bytes 200000 | tf_op jit(solution)/shard_map/last_rows/pallas_call | solution.py:467
  (4 shorter events, 0.1 us)
Async XLA Ops:
  0.8 5.8 %collective-permute-start = (bf16[3,4,2304]{2,1,0:T(4,128)(2,1)S(1)}, bf16[3,4,2304]{2,1,0:T(4,128)(2,1)S(1)}, u32[]{:S(2)}, u32[]{:S(2)}) collective-permute-start(bf16[3,4,2304]{2,1,0:T(4,128)(2,1)S(1)} %slice.4), channel_id=1, source_target_pairs={{0,1},{1,0},{2,3},{3,2},{4,5},{5,4},{6,7},{7,6},{8,9},{9,8},{10,11... | collective-permute-start | bytes 165896 | tf_op jit(solution)/shard_map/ppermute | solution.py:29
  6.7 1.4 %collective-permute-start.2 = (bf16[12,4,1152]{2,1,0:T(4,128)(2,1)S(1)}, bf16[12,4,1152]{2,1,0:T(4,128)(2,1)S(1)}, u32[]{:S(2)}, u32[]{:S(2)}) collective-permute-start(bf16[12,4,1152]{2,1,0:T(4,128)(2,1)S(1)} %pack_half.3.own_piece), channel_id=1, source_target_pairs={{0,2},{2,0},{4,6},{6,4},{8,10},{10,8},{12,14},{14,12},{16,18},{18,... | collective-permute-start | bytes 331784 | tf_op jit(solution)/shard_map/ppermute | solution.py:38
  6.7 8.8 %collective-permute-start.1 = (bf16[12,4,1152]{2,1,0:T(4,128)(2,1)S(1)}, bf16[12,4,1152]{2,1,0:T(4,128)(2,1)S(1)}, u32[]{:S(2)}, u32[]{:S(2)}) collective-permute-start(bf16[12,4,1152]{2,1,0:T(4,128)(2,1)S(1)} %pack_half.2.rest_0_.rest_8_.own_piece), channel_id=1, source_target_pairs={{2,4},{6,8},{10,12},{14,16},{18,20},{22,24},{26,28},{30,0},{3,5},{... | collective-permute-start | bytes 331784 | tf_op jit(solution)/shard_map/ppermute | solution.py:38
  11.2 6.2 %collective-permute-start.3 = (bf16[12,4,1152]{2,1,0:T(4,128)(2,1)S(1)}, bf16[12,4,1152]{2,1,0:T(4,128)(2,1)S(1)}, u32[]{:S(2)}, u32[]{:S(2)}) collective-permute-start(bf16[12,4,1152]{2,1,0:T(4,128)(2,1)S(1)} %get-tuple-element.29), channel_id=1, source_target_pairs={{4,2},{8,6},{12,10},{16,14},{20,18},{24,22},{28,26},{0,30},{5,3},{... | collective-permute-start | bytes 331784 | tf_op jit(solution)/shard_map/ppermute | solution.py:38
  19.5 4.2 %collective-permute-start.4 = (bf16[2,3,4,1152]{3,2,1,0:T(4,128)(2,1)S(1)}, bf16[2,3,4,1152]{3,2,1,0:T(4,128)(2,1)S(1)}, u32[]{:S(2)}, u32[]{:S(2)}) collective-permute-start(bf16[2,3,4,1152]{3,2,1,0:T(4,128)(2,1)S(1)} %get-tuple-element.31), channel_id=1, source_target_pairs={{0,1},{1,0},{2,3},{3,2},{4,5},{5,4},{6,7},{7,6},{8,9},{9,8},{10,11... | collective-permute-start | bytes 165896 | tf_op jit(solution)/shard_map/ppermute | solution.py:29

commit v10 on v8

v10 whole, which is shorter than its diff:
```python
import functools

import jax
import jax.numpy as jnp
from jax import lax
from jax.experimental import pallas as pl
from jax.experimental.pallas import tpu as pltpu
from jax.sharding import PartitionSpec as P

LEVELS = 4
WIN_LEV = 2
WIN_LAT = 6
WIN_LON = 12
EDGE = WIN_LAT // 2
HALF = WIN_LON // 2
TOKENS = WIN_LEV * WIN_LAT * WIN_LON
QUERIES = TOKENS // 2
LOG2E = 1.4426950408889634
GELU_0 = 0.7978845608028654
GELU_1 = 0.044715 * GELU_0
LANES = 128
SPARE = 64
VMEM_BYTES = 8 * 2**20
NT = (((1,), (1,)), ((), ()))


def moved(x, axis, by):
    size = lax.axis_size(axis)
    return lax.ppermute(x, axis, [(i, (i + by) % size) for i in range(size)])


def swapped(x, axis, first):
    size = lax.axis_size(axis)
    pairs = []
    for i in range(first, size, 2):
        j = (i + 1) % size
        pairs += [(i, j), (j, i)]
    return lax.ppermute(x, axis, pairs)


def half_places(half):
    odd = lax.rem(lax.axis_index("lon"), 2)
    return pl.multiple_of((1 - odd) * half, LANES), pl.multiple_of(odd * half, LANES)


def pack_kernel(which, south_ref, kept_ref, *rest):
    piece_ref = rest[-1]
    at = half_places(piece_ref.shape[2])[which]
    rows = piece_ref.shape[0] - EDGE
    piece_ref[:rows] = kept_ref[:rows]
    piece_ref[rows:] = south_ref[:, :, pl.ds(at, piece_ref.shape[2])]


def last_kernel(top_ref, high_ref, near_low_ref, far_low_ref, out_ref, sems):
    half = top_ref.shape[3]
    copies = []
    for n, at in enumerate(half_places(half)):
        target = out_ref.at[:, :, pl.ds(at, half)]
        low_ref = (near_low_ref, far_low_ref)[n]
        for source, first in (
            (high_ref.at[n], EDGE),
            (low_ref.at[0, :EDGE], EDGE + WIN_LAT),
            (top_ref.at[n], 0),
        ):
            rows = pl.ds(first, source.shape[0])
            copy = pltpu.make_async_copy(source, target.at[rows], sems.at[len(copies)])
            copy.start()
            copies.append(copy)
    for copy in copies:
        copy.wait()


def table_kernel(count, *refs):
    bias_any, field_any, *weights_any = refs[: 2 + count]
    table_ref, near_ref, far_ref, *weights_ref = refs[2 + count : 5 + 2 * count]
    bias_ref, sems, side_sems = refs[5 + 2 * count :]
    windows, heads, tiles = bias_any.shape[:3]
    lines = bias_ref.shape[0]
    flat = bias_any.reshape(lines, LANES)
    parts = 2 * windows
    copies = []
    for n in range(parts):
        at = pl.ds(n * (lines // parts), lines // parts)
        copies.append(pltpu.make_async_copy(flat.at[at], bias_ref.at[at], sems.at[n]))
        copies[-1].start()
    rows, half = field_any.shape[0] - EDGE, near_ref.shape[2]
    near_at, far_at = half_places(half)
    fetches = [
        (field_any.at[EDGE:, :, pl.ds(far_at, half)], far_ref.at[:rows]),
        (field_any.at[EDGE:, :, pl.ds(near_at, half)], near_ref.at[:rows]),
    ]
    fetches += list(zip(weights_any, weights_ref))
    fetches = [
        pltpu.make_async_copy(source, target, side_sems.at[n])
        for n, (source, target) in enumerate(fetches)
    ]
    for copy in fetches:
        copy.start()
    blocks = WIN_LEV * WIN_LAT // 2
    lane = lax.broadcasted_iota(jnp.int32, (blocks, LANES), 1)
    block = lax.broadcasted_iota(jnp.int32, (blocks, LANES), 0)
    is_last = lax.axis_index("lat") == lax.axis_size("lat") - 1
    last = jnp.where(is_last, -1e9, 0.0).astype(jnp.float32)

    def penalty(part, second, levels, wrap):
        key = lane + part * LANES
        key_lev = key // QUERIES
        key_side = (key - key_lev * QUERIES) // (QUERIES // 2)
        row = 2 * block + second
        lev = row // WIN_LAT
        side = (row - lev * WIN_LAT) // EDGE
        out = jnp.zeros((blocks, LANES), jnp.float32)
        if levels:
            out = jnp.where(key_lev != lev, -1e9, out)
        if wrap:
            out = out + jnp.where(key_side != side, last, 0.0)
        return out

    for k in range(windows):
        masks = {
            (p, part, second): penalty(part, second, p == 1, k == windows - 1)
            for p in range(2)
            for part in range(2)
            for second in range(2)
        }
        for h in range(heads):
            if h % (heads // 2) == 0:
                copies[2 * k + h // (heads // 2)].wait()
            for p in range(2):
                base = (k * heads + h) * 2 * tiles + p
                for third in range(3):
                    line = base + third * 18
                    pieces = [
                        bias_ref[pl.ds(line + 2 * u, blocks, stride=54), :] * LOG2E
                        for u in range(9)
                    ]
                    for r in range(8):
                        shift = 16 * r
                        main, nxt = pieces[r], pieces[r + 1]
                        if r:
                            main = pltpu.roll(main, LANES - shift, 1)
                            nxt = pltpu.roll(nxt, LANES - shift, 1)
                            main = jnp.where(lane < LANES - shift, main, nxt)
                        second, col = divmod(8 * third + r, WIN_LON)
                        side = col // HALF
                        place = h * QUERIES + HALF * second + col % HALF
                        at = pl.ds(place, blocks, stride=WIN_LON)
                        for part, piece in enumerate((main, nxt)):
                            filled = piece + masks[p, part, second]
                            table_ref[k, p, 1 - side, part, at, :] = filled
    for copy in fetches:
        copy.wait()


def layer_norm(values, gain):
    center = values - jnp.mean(values, axis=-1, keepdims=True)
    spread = jnp.mean(center * center, axis=-1, keepdims=True)
    return center * lax.rsqrt(spread + 1e-05) * gain


def gelu(x):
    half = 0.5 * x
    return half + half * jnp.tanh(x * (GELU_0 + GELU_1 * (x * x)))


def units_kernel(chans, heads, units, lower, *refs):
    count = len(units)
    pieces, refs = refs[: 2 * count], refs[2 * count :]
    gain1_ref, qkv_ref, proj_ref, gain2_ref, fc1_ref, fc2_ref, table_ref, *refs = refs
    if lower:
        lower_ref, out_ref, send_ref, keys_ref, own_ref, res_ref = refs
    else:
        out_ref, keys_ref, own_ref, res_ref = refs
    head_dim = chans // heads
    low = lax.broadcasted_iota(jnp.int32, (1, LANES), 1) < SPARE
    odd = lax.rem(lax.axis_index("lon"), 2)
    rights = [1 - odd if near else odd for near, _ in units]

    def tokens_of(ref, at, first, count):
        both = [ref[at, part, first : first + count] for part in range(2)]
        return jnp.concatenate([both[0], both[1][:, : chans - LANES]], axis=1)

    def split(ref, row):
        for pair in range(HALF // 2):
            both = ref[row, :, pair * 2 * chans : (pair + 1) * 2 * chans].astype(jnp.float32)
            first, middle, final = (both[:, u * LANES : (u + 1) * LANES] for u in range(3))
            yield 2 * pair, (first, middle)
            middle, final = pltpu.roll(middle, SPARE, 1), pltpu.roll(final, SPARE, 1)
            yield 2 * pair + 1, (jnp.where(low, middle, final), final)

    for n, (_, window) in enumerate(units):
        own_piece, halo_piece = pieces[2 * n], pieces[2 * n + 1]
        halo_at = rights[n] * HALF
        own_at = HALF - halo_at
        for row in range(WIN_LAT):
            for col, block in split(halo_piece, window * WIN_LAT + row):
                at = pl.ds(row * WIN_LON + col + halo_at, LEVELS, stride=QUERIES)
                for part in range(2):
                    keys_ref[n, part, at, :] = block[part]
            for col, block in split(own_piece, window * WIN_LAT + row):
                at = pl.ds(row * WIN_LON + col + own_at, LEVELS, stride=QUERIES)
                place = row * HALF + col
                for part in range(2):
                    keys_ref[n, part, at, :] = block[part]
                    own_ref[n, part, pl.ds(4 + place, LEVELS, stride=36), :] = block[part]
                    own_ref[n, part, pl.ds(148 + place, 1), :] = block[part][:1]

    gain1 = gain1_ref[...]
    lane = lax.broadcasted_iota(jnp.int32, (1, chans), 1)
    ones = jnp.ones((LEVELS * QUERIES, 2 * LANES - chans), jnp.float32)
    mixed = []
    for n, (_, window) in enumerate(units):
        normed = layer_norm(tokens_of(keys_ref, n, 0, LEVELS * QUERIES), gain1)
        normed = jnp.concatenate([normed[QUERIES:], normed[:QUERIES]], axis=0)
        normed = normed.astype(jnp.bfloat16)
        keys = jnp.dot(normed, qkv_ref[:, chans : 2 * chans], preferred_element_type=jnp.float32)
        values = jnp.dot(normed, qkv_ref[:, 2 * chans :], preferred_element_type=jnp.float32)
        values = jnp.concatenate([values, ones], axis=1)
        own = layer_norm(tokens_of(own_ref, n, 40, 144), gain1).astype(jnp.bfloat16)
        query = jnp.dot(own, qkv_ref[:, :chans], preferred_element_type=jnp.float32)
        query = query * (head_dim ** (-0.5) * LOG2E)
        for p in range(2):
            q = query[p * QUERIES : (p + 1) * QUERIES]
            k = keys[p * TOKENS : (p + 1) * TOKENS].astype(jnp.bfloat16)
            v = values[p * TOKENS : (p + 1) * TOKENS].astype(jnp.bfloat16)
            picked = [
                jnp.where((lane >= h * head_dim) & (lane < (h + 1) * head_dim), q, 0.0)
                for h in range(heads)
            ]
            picked = jnp.concatenate(picked, axis=0).astype(jnp.bfloat16)
            scores = lax.dot_general(picked, k, NT, preferred_element_type=jnp.float32)
            table = [table_ref[window, p, rights[n], part] for part in range(2)]
            table = jnp.concatenate([table[0], table[1][:, : TOKENS - LANES]], axis=1)
            scores = scores + table
            top = jnp.max(scores, axis=1, keepdims=True)
            probs = jnp.exp2(scores - top).astype(jnp.bfloat16)
            got = jnp.dot(probs, v, preferred_element_type=jnp.float32)
            out = jnp.zeros((QUERIES, chans), jnp.float32)
            for h in range(heads):
                part = got[h * QUERIES : (h + 1) * QUERIES]
                scaled = part[:, :chans] * (1.0 / part[:, chans : chans + 1])
                inside = (lane >= h * head_dim) & (lane < (h + 1) * head_dim)
                out = jnp.where(inside, scaled, out)
            mixed.append(out)
    mixed = jnp.concatenate(mixed, axis=0).astype(jnp.bfloat16)
    attn = jnp.dot(mixed, proj_ref[...], preferred_element_type=jnp.float32)
    attn = attn.astype(jnp.bfloat16).astype(jnp.float32)
    tokens = [tokens_of(own_ref, n, 40, 144) for n in range(count)]
    resid = jnp.concatenate(tokens, axis=0) + attn
    resid = resid.astype(jnp.bfloat16).astype(jnp.float32)
    normed = layer_norm(resid, gain2_ref[...]).astype(jnp.bfloat16)
    hidden = jnp.dot(normed, fc1_ref[...], preferred_element_type=jnp.float32)
    hidden = gelu(hidden).astype(jnp.bfloat16)
    result = lax.dot_general(hidden, fc2_ref[...], NT, preferred_element_type=jnp.float32)
    result = resid + result
    for n in range(count):
        mine = result[n * 144 : (n + 1) * 144]
        for part, lanes in enumerate((slice(0, LANES), slice(LANES, chans))):
            width = min(LANES, chans - part * LANES)
            res_ref[n, part, 40:184, :width] = mine[:, lanes]
            res_ref[n, part, 0:40, :width] = mine[104:144, lanes]
        for row in range(WIN_LAT):
            for pair in range(HALF // 2):
                tiles = []
                for col in (2 * pair, 2 * pair + 1):
                    at = pl.ds(4 + row * HALF + col, LEVELS, stride=36)
                    tiles += [res_ref[n, part, at, :] for part in range(2)]
                shifted = [pltpu.roll(x, SPARE, 1) for x in tiles[2:]]
                tiles = [tiles[0], jnp.where(low, tiles[1], shifted[0])]
                tiles.append(jnp.where(low, shifted[0], shifted[1]))
                tiles = jnp.concatenate(tiles, axis=1).astype(jnp.bfloat16)
                out_ref[n, row, :, pair * 2 * chans : (pair + 1) * 2 * chans] = tiles
    if lower:
        send_ref[0] = lower_ref[0, EDGE:]
        send_ref[1] = out_ref[0, EDGE:]


def run_units(units, near, far, table, weights, chans, heads, *lower):
    count = len(units)
    pieces = [x for is_near, _ in units for x in (near if is_near else far)]
    piece = pieces[0]
    out = jax.ShapeDtypeStruct((count, WIN_LAT) + piece.shape[1:], piece.dtype)
    send = jax.ShapeDtypeStruct((2, EDGE) + piece.shape[1:], piece.dtype)
    operands = (*pieces, *weights, table, *lower)
    vmem = pl.BlockSpec(memory_space=pltpu.VMEM)
    outs = [out, send] if lower else [out]
    return pl.pallas_call(
        functools.partial(units_kernel, chans, heads, units, bool(lower)),
        out_shape=outs,
        in_specs=[vmem] * len(operands),
        out_specs=[vmem] * len(outs),
        scratch_shapes=[
            pltpu.VMEM((count, 2, LEVELS * QUERIES, LANES), jnp.float32),
            pltpu.VMEM((count, 2, 184, LANES), jnp.float32),
            pltpu.VMEM((count, 2, 184, LANES), jnp.float32),
        ],
        compiler_params=pltpu.CompilerParams(vmem_limit_bytes=VMEM_BYTES),
        cost_estimate=pl.CostEstimate(
            flops=200_000_000 * count, bytes_accessed=3_000_000, transcendentals=250_000 * count
        ),
        name="swin_windows",
    )(*operands)


def shards(
    field_in, norm1_gain, qkv_weight, proj_weight, earth_bias, norm2_gain, fc1_weight, fc2_weight
):
    levels, rows, flat = field_in.shape
    chans = qkv_weight.shape[0]
    heads = earth_bias.shape[2]
    half = HALF * chans
    field = jnp.transpose(field_in, (1, 0, 2))
    south = moved(field[:EDGE], "lat", -1)
    weights = (
        norm1_gain.reshape(1, chans),
        qkv_weight,
        proj_weight,
        norm2_gain.reshape(1, chans),
        fc1_weight,
        jnp.transpose(fc2_weight),
    )
    vmem = pl.BlockSpec(memory_space=pltpu.VMEM)
    anywhere = pl.BlockSpec(memory_space=pl.ANY)
    piece = jax.ShapeDtypeStruct((rows, levels, half), field.dtype)
    table = jax.ShapeDtypeStruct((2, 2, 2, 2, heads * QUERIES, LANES), jnp.float32)
    windows, zwin, _, entries = earth_bias.shape
    tiles = entries // LANES
    bias = earth_bias.reshape(windows, zwin, heads, tiles, LANES).transpose(0, 2, 3, 1, 4)
    sources = (bias, field) + weights
    sources = [pltpu.with_memory_space_constraint(x, pltpu.HBM) for x in sources]
    outs = [table, piece, piece] + [jax.ShapeDtypeStruct(x.shape, x.dtype) for x in weights]
    table, near, far, *weights = pl.pallas_call(
        functools.partial(table_kernel, len(weights)),
        out_shape=outs,
        in_specs=[pl.BlockSpec(memory_space=pltpu.HBM)] * len(sources),
        out_specs=[vmem] * len(outs),
        scratch_shapes=[
            pltpu.VMEM((bias.size // LANES, LANES), jnp.float32),
            pltpu.SemaphoreType.DMA((2 * windows,)),
            pltpu.SemaphoreType.DMA((2 + len(weights),)),
        ],
        compiler_params=pltpu.CompilerParams(vmem_limit_bytes=VMEM_BYTES),
        cost_estimate=pl.CostEstimate(flops=4_000_000, bytes_accessed=6_000_000, transcendentals=0),
        name="bias_tables",
    )(*sources)

    def pack(which, kept, *after):
        return pl.pallas_call(
            functools.partial(pack_kernel, which),
            out_shape=piece,
            in_specs=[vmem] * 2 + [anywhere] * len(after),
            out_specs=vmem,
            compiler_params=pltpu.CompilerParams(vmem_limit_bytes=VMEM_BYTES),
            cost_estimate=pl.CostEstimate(flops=0, bytes_accessed=250_000, transcendentals=0),
            name="pack_half",
        )(south, kept, *after)

    far = pack(1, far)
    near = pack(0, near, far)
    far_halo = swapped(far, "lon", 1)
    near_halo = swapped(near, "lon", 0)
    near, far = (near, near_halo), (far, far_halo)
    common = (near, far, table, weights, chans, heads)
    (near_low,) = run_units(((True, 1),), *common)
    far_low, send = run_units(((False, 1),), *common, near_low)
    top = moved(send, "lat", 1)
    (high,) = run_units(((True, 0), (False, 0)), *common)
    done = pl.pallas_call(
        last_kernel,
        out_shape=jax.ShapeDtypeStruct(field.shape, field.dtype),
        in_specs=[vmem] * 4,
        out_specs=anywhere,
        scratch_shapes=[pltpu.SemaphoreType.DMA((6,))],
        compiler_params=pltpu.CompilerParams(vmem_limit_bytes=VMEM_BYTES),
        cost_estimate=pl.CostEstimate(flops=0, bytes_accessed=400_000, transcendentals=0),
        name="last_rows",
    )(top, high, near_low, far_low)
    return jnp.transpose(done, (1, 0, 2))


def solution(mesh):
    in_specs = (P(None, "lat", "lon"), P(), P(), P(), P("lat", None, None, None), P(), P(), P())
    out_specs = P(None, "lat", "lon")
    return jax.shard_map(shards, mesh=mesh, in_specs=in_specs, out_specs=out_specs, check_vma=False)
```

time: 21.8 us -> 21.5 us (0.986)
  Pallas kernels: 11.4 us -> 10.7 us
  waiting for transfers between devices: 0.04 us -> 0.29 us
    pallas_call x4, Pallas kernels: 8.64 us -> 8.1 us  [the longest x3 7.36 us: run_units(): pl.pallas_call(functools.partial(units_kernel, chans, heads, units, bool(...]
    ppermute x2, waiting for transfers between devices: 0.01 us -> 0.29 us  [swapped(): return lax.ppermute(x, axis, pairs)]
  transfers between devices with their start and end apart: 4 -> 4, of which waited for: 0 -> 1; matrix products, arithmetic and copies ran while one was open for 0% -> 0% of each run, Pallas kernels for 40% -> 37%
where the time goes in v10:
time: 21.5 us; the launch traced here: 21.3 us
  Pallas kernels  10.7 us (50%)
  starting transfers between devices  9.37 us (44%)
  local copies, waits for them, and re-layouts  0.83 us (4%)
  waiting for transfers between devices  0.29 us (1%)
    pallas_call x3, Pallas kernels, run_units(): pl.pallas_call(functools.partial(units_kernel, chans, heads, units, bool(...  7.36 us
    ppermute x2, starting transfers between devices, swapped(): return lax.ppermute(x, axis, pairs)  4.81 us
    ppermute x2, starting transfers between devices, moved(): return lax.ppermute(x, axis, [(i, (i + by) % size) for i in range(size)])  4.56 us
    pallas_call x1, Pallas kernels, shards(): pl.pallas_call(functools.partial(table_kernel, len(weights)), out_shape=o...  2.56 us
    slice x1, local copies, waits for them, and re-layouts, shards(): south = moved(field[:EDGE], 'lat', -1)  0.83 us
    pallas_call x1, Pallas kernels, shards(): pl.pallas_call(last_kernel, out_shape=jax.ShapeDtypeStruct(field.shape, f...  0.74 us
  transfers between devices with their start and end apart: 4, of which 1 were waited for; matrix products, arithmetic and copies ran while one was open for 0% of the time, Pallas kernels for 37%

profile of v10, /device:TPU:0, one launch (start us, length us, event | category | flops | bytes accessed | tf_op | source)
XLA Modules:
  0.0 21.3 jit_solution(193860279558263126)
XLA Ops:
  0.0 0.8 %slice.4 = bf16[3,4,2304]{2,1,0:T(4,128)(2,1)S(1)} slice(bf16[12,4,2304]{2,1,0:T(4,128)(2,1)} %bitcast.9), slice={[0:3], [0:4], [0:2304]} | slice | bytes 110592 | tf_op jit(solution)/shard_map/slice | solution.py:313
  0.8 3.0 %collective-permute-start = (bf16[3,4,2304]{2,1,0:T(4,128)(2,1)S(1)}, bf16[3,4,2304]{2,1,0:T(4,128)(2,1)S(1)}, u32[]{:S(2)}, u32[]{:S(2)}) collective-permute-start(bf16[3,4,2304]{2,1,0:T(4,128)(2,1)S(1)} %slice.4), channel_id=1, source_target_pairs={{0,1},{1,0},{2,3},{3,2},{4,5},{5,4},{6,7},{7,6},{8,9},{9,8},{10,11... | collective-permute-start | bytes 165896 | tf_op jit(solution)/shard_map/ppermute | solution.py:29
  3.8 2.6 %bias_tables.1 = (f32[2,2,2,2,432,128]{5,4,3,2,1,0:T(8,128)S(1)}, bf16[12,4,1152]{2,1,0:T(4,128)(2,1)S(1)}, bf16[12,4,1152]{2,1,0:T(4,128)(2,1)S(1)}, f32[1,192]...) custom-call(f32[2,6,162,2,128]{4,3,2,1,0:T(2,128)} %bitcast.8, ...), custom_call_target="tpu_custom_call" | custom-call | flops 4000000 | bytes 6000000 | tf_op jit(solution)/shard_map/bias_tables/pallas_call | solution.py:332
  6.4 0.0 collective-permute-done.south_ref
  6.5 0.1 collective-permute-start.2
  6.6 4.7 %collective-permute-start.1 = (bf16[12,4,1152]{2,1,0:T(4,128)(2,1)S(1)}, bf16[12,4,1152]{2,1,0:T(4,128)(2,1)S(1)}, u32[]{:S(2)}, u32[]{:S(2)}) collective-permute-start(bf16[12,4,1152]{2,1,0:T(4,128)(2,1)S(1)} %pack_half.2.rest_0_.refs_0_.refs_2_), channel_id=1, source_target_pairs={{2,4},{4,2},{6,8},{8,6},{10,12},{12,10},{14,16},{16,14},{18,20},{2... | collective-permute-start | bytes 331784 | tf_op jit(solution)/shard_map/ppermute | solution.py:38
  11.3 0.0 collective-permute-done.2.refs_1_
  11.3 2.1 %swin_windows.3.refs_9_.near_low_ref = bf16[1,6,4,1152]{3,2,1,0:T(4,128)(2,1)S(1)} custom-call(bf16[12,4,1152]{2,1,0:T(4,128)(2,1)S(1)} %pack_half.3.refs_0_, bf16[12,4,1152]{2,1,0:T(4,128)(2,1)S(1)} %collective-permute-done.2.refs_1_, f32[1,192]{1,0:T(1,128)S(1)} %get-tuple-element.17.refs_2_.refs_4_, ...), custom_call_target="tpu_custom_call" | custom-call | flops 200000000 | bytes 3000000 | tf_op jit(solution)/shard_map/swin_windows/pallas_call | solution.py:287
  13.4 0.3 %collective-permute-done.1.refs_1_.refs_3_ = bf16[12,4,1152]{2,1,0:T(4,128)(2,1)S(1)} collective-permute-done((bf16[12,4,1152]{2,1,0:T(4,128)(2,1)S(1)}, bf16[12,4,1152]{2,1,0:T(4,128)(2,1)S(1)}, u32[]{:S(2)}, u32[]{:S(2)}) %collective-permute-start.1) | collective-permute-done | bytes 110624 | tf_op jit(solution)/shard_map/ppermute | solution.py:38
  13.7 2.1 %swin_windows.4 = (bf16[1,6,4,1152]{3,2,1,0:T(4,128)(2,1)S(1)}, bf16[2,3,4,1152]{3,2,1,0:T(4,128)(2,1)S(1)}) custom-call(bf16[12,4,1152]{2,1,0:T(4,128)(2,1)S(1)} %pack_half.2.rest_0_.refs_0_.refs_2_, bf16[12,4,1152]{2,1,0:T(4,128)(2,1)S(1)} %collective-permute-done.1.refs_1_.refs_3_, f32[1,192]{1,0:T(1,128)S(1)} %get-tuple-element.17.refs_2_.refs_4_, ...), custom_call_target="tpu_custom_call" | custom-call | flops 200000000 | bytes 3000000 | tf_op jit(solution)/shard_map/swin_windows/pallas_call | solution.py:287
  15.9 1.6 %collective-permute-start.3 = (bf16[2,3,4,1152]{3,2,1,0:T(4,128)(2,1)S(1)}, bf16[2,3,4,1152]{3,2,1,0:T(4,128)(2,1)S(1)}, u32[]{:S(2)}, u32[]{:S(2)}) collective-permute-start(bf16[2,3,4,1152]{3,2,1,0:T(4,128)(2,1)S(1)} %get-tuple-element.25), channel_id=1, source_target_pairs={{0,1},{1,0},{2,3},{3,2},{4,5},{5,4},{6,7},{7,6},{8,9},{9,8},{10,11... | collective-permute-start | bytes 165896 | tf_op jit(solution)/shard_map/ppermute | solution.py:29
  17.4 3.1 %swin_windows.5.high_ref = bf16[2,6,4,1152]{3,2,1,0:T(4,128)(2,1)S(1)} custom-call(bf16[12,4,1152]{2,1,0:T(4,128)(2,1)S(1)} %pack_half.3.refs_0_, bf16[12,4,1152]{2,1,0:T(4,128)(2,1)S(1)} %collective-permute-done.2.refs_1_, bf16[12,4,1152]{2,1,0:T(4,128)(2,1)S(1)} %pack_half.2.rest_0_.refs_0_.refs_2_, ...), custom_call_target="tpu_custom_call" | custom-call | flops 400000000 | bytes 3000000 | tf_op jit(solution)/shard_map/swin_windows/pallas_call | solution.py:287
  20.5 0.0 collective-permute-done.3.top_ref
  20.5 0.7 %last_rows.1 = bf16[12,4,2304]{2,1,0:T(4,128)(2,1)} custom-call(bf16[2,3,4,1152]{3,2,1,0:T(4,128)(2,1)S(1)} %collective-permute-done.3.top_ref, bf16[2,6,4,1152]{3,2,1,0:T(4,128)(2,1)S(1)} %swin_windows.5.high_ref, bf16[1,6,4,1152]{3,2,1,0:T(4,128)(2,1)S(1)} %swin_windows.3.refs_9_.near_low_ref, bf16[1,6,4,1152]{3,2,1,0:T(4,128)(2,1)S(1)} %get-tuple-element.26.far_low_ref), custom_call_target="tpu_custom_call" | custom-call | bytes 400000 | tf_op jit(solution)/shard_map/last_rows/pallas_call | solution.py:368
  (2 shorter events, 0.0 us)
Async XLA Ops:
  0.8 5.6 %collective-permute-start = (bf16[3,4,2304]{2,1,0:T(4,128)(2,1)S(1)}, bf16[3,4,2304]{2,1,0:T(4,128)(2,1)S(1)}, u32[]{:S(2)}, u32[]{:S(2)}) collective-permute-start(bf16[3,4,2304]{2,1,0:T(4,128)(2,1)S(1)} %slice.4), channel_id=1, source_target_pairs={{0,1},{1,0},{2,3},{3,2},{4,5},{5,4},{6,7},{7,6},{8,9},{9,8},{10,11... | collective-permute-start | bytes 165896 | tf_op jit(solution)/shard_map/ppermute | solution.py:29
  6.5 4.8 %collective-permute-start.2 = (bf16[12,4,1152]{2,1,0:T(4,128)(2,1)S(1)}, bf16[12,4,1152]{2,1,0:T(4,128)(2,1)S(1)}, u32[]{:S(2)}, u32[]{:S(2)}) collective-permute-start(bf16[12,4,1152]{2,1,0:T(4,128)(2,1)S(1)} %pack_half.3.refs_0_), channel_id=1, source_target_pairs={{0,2},{2,0},{4,6},{6,4},{8,10},{10,8},{12,14},{14,12},{16,18},{18,... | collective-permute-start | bytes 331784 | tf_op jit(solution)/shard_map/ppermute | solution.py:38
  6.6 7.2 %collective-permute-start.1 = (bf16[12,4,1152]{2,1,0:T(4,128)(2,1)S(1)}, bf16[12,4,1152]{2,1,0:T(4,128)(2,1)S(1)}, u32[]{:S(2)}, u32[]{:S(2)}) collective-permute-start(bf16[12,4,1152]{2,1,0:T(4,128)(2,1)S(1)} %pack_half.2.rest_0_.refs_0_.refs_2_), channel_id=1, source_target_pairs={{2,4},{4,2},{6,8},{8,6},{10,12},{12,10},{14,16},{16,14},{18,20},{2... | collective-permute-start | bytes 331784 | tf_op jit(solution)/shard_map/ppermute | solution.py:38
  15.9 4.7 %collective-permute-start.3 = (bf16[2,3,4,1152]{3,2,1,0:T(4,128)(2,1)S(1)}, bf16[2,3,4,1152]{3,2,1,0:T(4,128)(2,1)S(1)}, u32[]{:S(2)}, u32[]{:S(2)}) collective-permute-start(bf16[2,3,4,1152]{3,2,1,0:T(4,128)(2,1)S(1)} %get-tuple-element.25), channel_id=1, source_target_pairs={{0,1},{1,0},{2,3},{3,2},{4,5},{5,4},{6,7},{7,6},{8,9},{9,8},{10,11... | collective-permute-start | bytes 165896 | tf_op jit(solution)/shard_map/ppermute | solution.py:29

commit v11 on v10

--- a/solution.py
+++ b/solution.py
@@ -77,7 +77,7 @@
     windows, heads, tiles = bias_any.shape[:3]
     lines = bias_ref.shape[0]
     flat = bias_any.reshape(lines, LANES)
-    parts = 2 * windows
+    parts = heads * windows
     copies = []
     for n in range(parts):
         at = pl.ds(n * (lines // parts), lines // parts)
@@ -124,8 +124,7 @@
             for second in range(2)
         }
         for h in range(heads):
-            if h % (heads // 2) == 0:
-                copies[2 * k + h // (heads // 2)].wait()
+            copies[k * heads + h].wait()
             for p in range(2):
                 base = (k * heads + h) * 2 * tiles + p
                 for third in range(3):
@@ -153,9 +152,15 @@
 
 
 def layer_norm(values, gain):
-    center = values - jnp.mean(values, axis=-1, keepdims=True)
-    spread = jnp.mean(center * center, axis=-1, keepdims=True)
-    return center * lax.rsqrt(spread + 1e-05) * gain
+    chans = values.shape[1]
+    ones = jnp.ones((chans, chans), jnp.bfloat16)
+
+    def mean(x):
+        total = jnp.dot(x.astype(jnp.bfloat16), ones, preferred_element_type=jnp.float32)
+        return total * (1.0 / chans)
+
+    center = values - mean(values)
+    return center * lax.rsqrt(mean(center * center) + 1e-05) * gain
 
 
 def gelu(x):
@@ -235,13 +240,12 @@
             top = jnp.max(scores, axis=1, keepdims=True)
             probs = jnp.exp2(scores - top).astype(jnp.bfloat16)
             got = jnp.dot(probs, v, preferred_element_type=jnp.float32)
-            out = jnp.zeros((QUERIES, chans), jnp.float32)
-            for h in range(heads):
+            out, total = got[:QUERIES, :chans], got[:QUERIES, chans : chans + 1]
+            for h in range(1, heads):
                 part = got[h * QUERIES : (h + 1) * QUERIES]
-                scaled = part[:, :chans] * (1.0 / part[:, chans : chans + 1])
-                inside = (lane >= h * head_dim) & (lane < (h + 1) * head_dim)
-                out = jnp.where(inside, scaled, out)
-            mixed.append(out)
+                out = jnp.where(lane >= h * head_dim, part[:, :chans], out)
+                total = jnp.where(lane >= h * head_dim, part[:, chans : chans + 1], total)
+            mixed.append(out / total)
     mixed = jnp.concatenate(mixed, axis=0).astype(jnp.bfloat16)
     attn = jnp.dot(mixed, proj_ref[...], preferred_element_type=jnp.float32)
     attn = attn.astype(jnp.bfloat16).astype(jnp.float32)
@@ -336,7 +340,7 @@
         out_specs=[vmem] * len(outs),
         scratch_shapes=[
             pltpu.VMEM((bias.size // LANES, LANES), jnp.float32),
-            pltpu.SemaphoreType.DMA((2 * windows,)),
+            pltpu.SemaphoreType.DMA((heads * windows,)),
             pltpu.SemaphoreType.DMA((2 + len(weights),)),
         ],
         compiler_params=pltpu.CompilerParams(vmem_limit_bytes=VMEM_BYTES),

time: 21.5 us -> 22.4 us (1.042)
  Pallas kernels: 10.7 us -> 12.4 us
  starting transfers between devices: 9.37 us -> 8.86 us
  waiting for transfers between devices: 0.29 us -> 0.04 us
    pallas_call x3, Pallas kernels: 7.36 us -> 8.57 us  [run_units(): pl.pallas_call(functools.partial(units_kernel, chans, heads, units, bool(...]
    pallas_call x1, Pallas kernels: 2.56 us -> 3.07 us  [shards(): pl.pallas_call(functools.partial(table_kernel, len(weights)), out_shape=o...]
    ppermute x2, starting transfers between devices: 4.56 us -> 4.13 us  [moved(): return lax.ppermute(x, axis, [(i, (i + by) % size) for i in range(size)])]
    ppermute x2, waiting for transfers between devices: 0.29 us -> 0.04 us  [swapped(): return lax.ppermute(x, axis, pairs)]
  transfers between devices with their start and end apart: 4 -> 4, of which waited for: 1 -> 0; matrix products, arithmetic and copies ran while one was open for 0% -> 0% of each run, Pallas kernels for 37% -> 42%
where the time goes in v11:
time: 22.4 us; the launch traced here: 22.2 us
  Pallas kernels  12.4 us (55%)
  starting transfers between devices  8.86 us (40%)
  local copies, waits for them, and re-layouts  0.83 us (4%)
    pallas_call x3, Pallas kernels, run_units(): pl.pallas_call(functools.partial(units_kernel, chans, heads, units, bool(...  8.57 us
    ppermute x2, starting transfers between devices, swapped(): return lax.ppermute(x, axis, pairs)  4.73 us
    ppermute x2, starting transfers between devices, moved(): return lax.ppermute(x, axis, [(i, (i + by) % size) for i in range(size)])  4.13 us
    pallas_call x1, Pallas kernels, shards(): pl.pallas_call(functools.partial(table_kernel, len(weights)), out_shape=o...  3.07 us
    slice x1, local copies, waits for them, and re-layouts, shards(): south = moved(field[:EDGE], 'lat', -1)  0.83 us
    pallas_call x1, Pallas kernels, shards(): pl.pallas_call(last_kernel, out_shape=jax.ShapeDtypeStruct(field.shape, f...  0.74 us
  transfers between devices with their start and end apart: 4, of which 0 were waited for; matrix products, arithmetic and copies ran while one was open for 0% of the time, Pallas kernels for 42%

profile of v11, /device:TPU:0, one launch (start us, length us, event | category | flops | bytes accessed | tf_op | source)
XLA Modules:
  0.0 22.2 jit_solution(16803160187767523879)
XLA Ops:
  0.0 0.8 %slice.4 = bf16[3,4,2304]{2,1,0:T(4,128)(2,1)S(1)} slice(bf16[12,4,2304]{2,1,0:T(4,128)(2,1)} %bitcast.9), slice={[0:3], [0:4], [0:2304]} | slice | bytes 110592 | tf_op jit(solution)/shard_map/slice | solution.py:317
  0.8 3.0 %collective-permute-start = (bf16[3,4,2304]{2,1,0:T(4,128)(2,1)S(1)}, bf16[3,4,2304]{2,1,0:T(4,128)(2,1)S(1)}, u32[]{:S(2)}, u32[]{:S(2)}) collective-permute-start(bf16[3,4,2304]{2,1,0:T(4,128)(2,1)S(1)} %slice.4), channel_id=1, source_target_pairs={{0,1},{1,0},{2,3},{3,2},{4,5},{5,4},{6,7},{7,6},{8,9},{9,8},{10,11... | collective-permute-start | bytes 165896 | tf_op jit(solution)/shard_map/ppermute | solution.py:29
  3.8 3.1 %bias_tables.1 = (f32[2,2,2,2,432,128]{5,4,3,2,1,0:T(8,128)S(1)}, bf16[12,4,1152]{2,1,0:T(4,128)(2,1)S(1)}, bf16[12,4,1152]{2,1,0:T(4,128)(2,1)S(1)}, f32[1,192]...) custom-call(f32[2,6,162,2,128]{4,3,2,1,0:T(2,128)} %bitcast.8, ...), custom_call_target="tpu_custom_call" | custom-call | flops 4000000 | bytes 6000000 | tf_op jit(solution)/shard_map/bias_tables/pallas_call | solution.py:336
  6.9 0.0 collective-permute-done.south_ref
  7.0 0.1 collective-permute-start.2
  7.1 4.7 %collective-permute-start.1 = (bf16[12,4,1152]{2,1,0:T(4,128)(2,1)S(1)}, bf16[12,4,1152]{2,1,0:T(4,128)(2,1)S(1)}, u32[]{:S(2)}, u32[]{:S(2)}) collective-permute-start(bf16[12,4,1152]{2,1,0:T(4,128)(2,1)S(1)} %pack_half.2.rest_0_.refs_0_.refs_2_), channel_id=1, source_target_pairs={{2,4},{4,2},{6,8},{8,6},{10,12},{12,10},{14,16},{16,14},{18,20},{2... | collective-permute-start | bytes 331784 | tf_op jit(solution)/shard_map/ppermute | solution.py:38
  11.7 0.0 collective-permute-done.2.refs_1_
  11.7 2.4 %swin_windows.3.refs_9_.near_low_ref = bf16[1,6,4,1152]{3,2,1,0:T(4,128)(2,1)S(1)} custom-call(bf16[12,4,1152]{2,1,0:T(4,128)(2,1)S(1)} %pack_half.3.refs_0_, bf16[12,4,1152]{2,1,0:T(4,128)(2,1)S(1)} %collective-permute-done.2.refs_1_, f32[1,192]{1,0:T(1,128)S(1)} %get-tuple-element.17.refs_2_.refs_4_, ...), custom_call_target="tpu_custom_call" | custom-call | flops 200000000 | bytes 3000000 | tf_op jit(solution)/shard_map/swin_windows/pallas_call | solution.py:291
  14.1 0.0 collective-permute-done.1.refs_1_.refs_3_
  14.2 2.4 %swin_windows.4 = (bf16[1,6,4,1152]{3,2,1,0:T(4,128)(2,1)S(1)}, bf16[2,3,4,1152]{3,2,1,0:T(4,128)(2,1)S(1)}) custom-call(bf16[12,4,1152]{2,1,0:T(4,128)(2,1)S(1)} %pack_half.2.rest_0_.refs_0_.refs_2_, bf16[12,4,1152]{2,1,0:T(4,128)(2,1)S(1)} %collective-permute-done.1.refs_1_.refs_3_, f32[1,192]{1,0:T(1,128)S(1)} %get-tuple-element.17.refs_2_.refs_4_, ...), custom_call_target="tpu_custom_call" | custom-call | flops 200000000 | bytes 3000000 | tf_op jit(solution)/shard_map/swin_windows/pallas_call | solution.py:291
  16.6 1.1 %collective-permute-start.3 = (bf16[2,3,4,1152]{3,2,1,0:T(4,128)(2,1)S(1)}, bf16[2,3,4,1152]{3,2,1,0:T(4,128)(2,1)S(1)}, u32[]{:S(2)}, u32[]{:S(2)}) collective-permute-start(bf16[2,3,4,1152]{3,2,1,0:T(4,128)(2,1)S(1)} %get-tuple-element.25), channel_id=1, source_target_pairs={{0,1},{1,0},{2,3},{3,2},{4,5},{5,4},{6,7},{7,6},{8,9},{9,8},{10,11... | collective-permute-start | bytes 165896 | tf_op jit(solution)/shard_map/ppermute | solution.py:29
  17.7 3.8 %swin_windows.5.high_ref = bf16[2,6,4,1152]{3,2,1,0:T(4,128)(2,1)S(1)} custom-call(bf16[12,4,1152]{2,1,0:T(4,128)(2,1)S(1)} %pack_half.3.refs_0_, bf16[12,4,1152]{2,1,0:T(4,128)(2,1)S(1)} %collective-permute-done.2.refs_1_, bf16[12,4,1152]{2,1,0:T(4,128)(2,1)S(1)} %pack_half.2.rest_0_.refs_0_.refs_2_, ...), custom_call_target="tpu_custom_call" | custom-call | flops 400000000 | bytes 3000000 | tf_op jit(solution)/shard_map/swin_windows/pallas_call | solution.py:291
  21.5 0.0 collective-permute-done.3.top_ref
  21.5 0.7 %last_rows.1 = bf16[12,4,2304]{2,1,0:T(4,128)(2,1)} custom-call(bf16[2,3,4,1152]{3,2,1,0:T(4,128)(2,1)S(1)} %collective-permute-done.3.top_ref, bf16[2,6,4,1152]{3,2,1,0:T(4,128)(2,1)S(1)} %swin_windows.5.high_ref, bf16[1,6,4,1152]{3,2,1,0:T(4,128)(2,1)S(1)} %swin_windows.3.refs_9_.near_low_ref, bf16[1,6,4,1152]{3,2,1,0:T(4,128)(2,1)S(1)} %get-tuple-element.26.far_low_ref), custom_call_target="tpu_custom_call" | custom-call | bytes 400000 | tf_op jit(solution)/shard_map/last_rows/pallas_call | solution.py:372
  (2 shorter events, 0.0 us)
Async XLA Ops:
  0.8 6.1 %collective-permute-start = (bf16[3,4,2304]{2,1,0:T(4,128)(2,1)S(1)}, bf16[3,4,2304]{2,1,0:T(4,128)(2,1)S(1)}, u32[]{:S(2)}, u32[]{:S(2)}) collective-permute-start(bf16[3,4,2304]{2,1,0:T(4,128)(2,1)S(1)} %slice.4), channel_id=1, source_target_pairs={{0,1},{1,0},{2,3},{3,2},{4,5},{5,4},{6,7},{7,6},{8,9},{9,8},{10,11... | collective-permute-start | bytes 165896 | tf_op jit(solution)/shard_map/ppermute | solution.py:29
  7.0 4.7 %collective-permute-start.2 = (bf16[12,4,1152]{2,1,0:T(4,128)(2,1)S(1)}, bf16[12,4,1152]{2,1,0:T(4,128)(2,1)S(1)}, u32[]{:S(2)}, u32[]{:S(2)}) collective-permute-start(bf16[12,4,1152]{2,1,0:T(4,128)(2,1)S(1)} %pack_half.3.refs_0_), channel_id=1, source_target_pairs={{0,2},{2,0},{4,6},{6,4},{8,10},{10,8},{12,14},{14,12},{16,18},{18,... | collective-permute-start | bytes 331784 | tf_op jit(solution)/shard_map/ppermute | solution.py:38
  7.1 7.1 %collective-permute-start.1 = (bf16[12,4,1152]{2,1,0:T(4,128)(2,1)S(1)}, bf16[12,4,1152]{2,1,0:T(4,128)(2,1)S(1)}, u32[]{:S(2)}, u32[]{:S(2)}) collective-permute-start(bf16[12,4,1152]{2,1,0:T(4,128)(2,1)S(1)} %pack_half.2.rest_0_.refs_0_.refs_2_), channel_id=1, source_target_pairs={{2,4},{4,2},{6,8},{8,6},{10,12},{12,10},{14,16},{16,14},{18,20},{2... | collective-permute-start | bytes 331784 | tf_op jit(solution)/shard_map/ppermute | solution.py:38
  16.6 4.9 %collective-permute-start.3 = (bf16[2,3,4,1152]{3,2,1,0:T(4,128)(2,1)S(1)}, bf16[2,3,4,1152]{3,2,1,0:T(4,128)(2,1)S(1)}, u32[]{:S(2)}, u32[]{:S(2)}) collective-permute-start(bf16[2,3,4,1152]{3,2,1,0:T(4,128)(2,1)S(1)} %get-tuple-element.25), channel_id=1, source_target_pairs={{0,1},{1,0},{2,3},{3,2},{4,5},{5,4},{6,7},{7,6},{8,9},{9,8},{10,11... | collective-permute-start | bytes 165896 | tf_op jit(solution)/shard_map/ppermute | solution.py:29

commit v12 on v10

--- a/solution.py
+++ b/solution.py
@@ -77,7 +77,7 @@
     windows, heads, tiles = bias_any.shape[:3]
     lines = bias_ref.shape[0]
     flat = bias_any.reshape(lines, LANES)
-    parts = 2 * windows
+    parts = windows
     copies = []
     for n in range(parts):
         at = pl.ds(n * (lines // parts), lines // parts)
@@ -123,9 +123,8 @@
             for part in range(2)
             for second in range(2)
         }
+        copies[k].wait()
         for h in range(heads):
-            if h % (heads // 2) == 0:
-                copies[2 * k + h // (heads // 2)].wait()
             for p in range(2):
                 base = (k * heads + h) * 2 * tiles + p
                 for third in range(3):
@@ -207,52 +206,63 @@
 
     gain1 = gain1_ref[...]
     lane = lax.broadcasted_iota(jnp.int32, (1, chans), 1)
-    ones = jnp.ones((LEVELS * QUERIES, 2 * LANES - chans), jnp.float32)
+    ones = jnp.ones((TOKENS, 2 * LANES - chans), jnp.float32)
     mixed = []
     for n, (_, window) in enumerate(units):
-        normed = layer_norm(tokens_of(keys_ref, n, 0, LEVELS * QUERIES), gain1)
-        normed = jnp.concatenate([normed[QUERIES:], normed[:QUERIES]], axis=0)
-        normed = normed.astype(jnp.bfloat16)
+        normed = []
+        for p in range(2):
+            levels = [(2 * p + 1 + lev) % LEVELS for lev in range(WIN_LEV)]
+            parts = [tokens_of(keys_ref, n, lev * QUERIES, QUERIES) for lev in levels]
+            parts = [layer_norm(x, gain1) for x in parts]
+            normed.append(jnp.concatenate(parts, axis=0).astype(jnp.bfloat16))
+        normed = jnp.concatenate(normed, axis=0)
         keys = jnp.dot(normed, qkv_ref[:, chans : 2 * chans], preferred_element_type=jnp.float32)
         values = jnp.dot(normed, qkv_ref[:, 2 * chans :], preferred_element_type=jnp.float32)
-        values = jnp.concatenate([values, ones], axis=1)
         own = layer_norm(tokens_of(own_ref, n, 40, 144), gain1).astype(jnp.bfloat16)
         query = jnp.dot(own, qkv_ref[:, :chans], preferred_element_type=jnp.float32)
         query = query * (head_dim ** (-0.5) * LOG2E)
         for p in range(2):
             q = query[p * QUERIES : (p + 1) * QUERIES]
             k = keys[p * TOKENS : (p + 1) * TOKENS].astype(jnp.bfloat16)
-            v = values[p * TOKENS : (p + 1) * TOKENS].astype(jnp.bfloat16)
+            v = jnp.concatenate([values[p * TOKENS : (p + 1) * TOKENS], ones], axis=1)
+            v = v.astype(jnp.bfloat16)
             picked = [
                 jnp.where((lane >= h * head_dim) & (lane < (h + 1) * head_dim), q, 0.0)
                 for h in range(heads)
             ]
             picked = jnp.concatenate(picked, axis=0).astype(jnp.bfloat16)
             scores = lax.dot_general(picked, k, NT, preferred_element_type=jnp.float32)
-            table = [table_ref[window, p, rights[n], part] for part in range(2)]
-            table = jnp.concatenate([table[0], table[1][:, : TOKENS - LANES]], axis=1)
-            scores = scores + table
-            top = jnp.max(scores, axis=1, keepdims=True)
-            probs = jnp.exp2(scores - top).astype(jnp.bfloat16)
+            probs = []
+            for h in range(heads):
+                at = slice(h * QUERIES, (h + 1) * QUERIES)
+                bias = [table_ref[window, p, rights[n], part, at] for part in range(2)]
+                bias = jnp.concatenate([bias[0], bias[1][:, : TOKENS - LANES]], axis=1)
+                part = scores[at] + bias
+                probs.append(jnp.exp2(part - jnp.max(part, axis=1, keepdims=True)))
+            probs = jnp.concatenate(probs, axis=0).astype(jnp.bfloat16)
             got = jnp.dot(probs, v, preferred_element_type=jnp.float32)
-            out = jnp.zeros((QUERIES, chans), jnp.float32)
+            out = None
             for h in range(heads):
                 part = got[h * QUERIES : (h + 1) * QUERIES]
                 scaled = part[:, :chans] * (1.0 / part[:, chans : chans + 1])
-                inside = (lane >= h * head_dim) & (lane < (h + 1) * head_dim)
-                out = jnp.where(inside, scaled, out)
+                out = jnp.where(lane >= h * head_dim, scaled, out) if h else scaled
             mixed.append(out)
     mixed = jnp.concatenate(mixed, axis=0).astype(jnp.bfloat16)
     attn = jnp.dot(mixed, proj_ref[...], preferred_element_type=jnp.float32)
     attn = attn.astype(jnp.bfloat16).astype(jnp.float32)
-    tokens = [tokens_of(own_ref, n, 40, 144) for n in range(count)]
-    resid = jnp.concatenate(tokens, axis=0) + attn
-    resid = resid.astype(jnp.bfloat16).astype(jnp.float32)
-    normed = layer_norm(resid, gain2_ref[...]).astype(jnp.bfloat16)
-    hidden = jnp.dot(normed, fc1_ref[...], preferred_element_type=jnp.float32)
-    hidden = gelu(hidden).astype(jnp.bfloat16)
-    result = lax.dot_general(hidden, fc2_ref[...], NT, preferred_element_type=jnp.float32)
-    result = resid + result
+    resid, normed = [], []
+    for n in range(count):
+        part = tokens_of(own_ref, n, 40, 144) + attn[n * 144 : (n + 1) * 144]
+        resid.append(part.astype(jnp.bfloat16).astype(jnp.float32))
+        normed.append(layer_norm(resid[n], gain2_ref[...]).astype(jnp.bfloat16))
+    result, normed = jnp.concatenate(resid, axis=0), jnp.concatenate(normed, axis=0)
+    for first in range(0, fc1_ref.shape[1], 2 * LANES):
+        units_at = slice(first, first + 2 * LANES)
+        hidden = jnp.dot(normed, fc1_ref[:, units_at], preferred_element_type=jnp.float32)
+        hidden = gelu(hidden).astype(jnp.bfloat16)
+        result = result + lax.dot_general(
+            hidden, fc2_ref[:, units_at], NT, preferred_element_type=jnp.float32
+        )
     for n in range(count):
         mine = result[n * 144 : (n + 1) * 144]
         for part, lanes in enumerate((slice(0, LANES), slice(LANES, chans))):

time: 21.5 us -> 21.2 us (0.986)
    pallas_call x3, Pallas kernels: 7.36 us -> 7.08 us  [run_units(): pl.pallas_call(functools.partial(units_kernel, chans, heads, units, bool(...]
  transfers between devices with their start and end apart: 4 -> 4, of which waited for: 1 -> 1; matrix products, arithmetic and copies ran while one was open for 0% -> 0% of each run, Pallas kernels for 37% -> 36%
where the time goes in v12:
time: 21.2 us; the launch traced here: 21 us
  Pallas kernels  10.5 us (50%)
  starting transfers between devices  9.34 us (44%)
  local copies, waits for them, and re-layouts  0.83 us (4%)
  waiting for transfers between devices  0.33 us (2%)
    pallas_call x3, Pallas kernels, run_units(): pl.pallas_call(functools.partial(units_kernel, chans, heads, units, bool(...  7.08 us
    ppermute x2, starting transfers between devices, swapped(): return lax.ppermute(x, axis, pairs)  4.78 us
    ppermute x2, starting transfers between devices, moved(): return lax.ppermute(x, axis, [(i, (i + by) % size) for i in range(size)])  4.56 us
    pallas_call x1, Pallas kernels, shards(): pl.pallas_call(functools.partial(table_kernel, len(weights)), out_shape=o...  2.59 us
    slice x1, local copies, waits for them, and re-layouts, shards(): south = moved(field[:EDGE], 'lat', -1)  0.83 us
    pallas_call x1, Pallas kernels, shards(): pl.pallas_call(last_kernel, out_shape=jax.ShapeDtypeStruct(field.shape, f...  0.74 us
  transfers between devices with their start and end apart: 4, of which 1 were waited for; matrix products, arithmetic and copies ran while one was open for 0% of the time, Pallas kernels for 36%

profile of v12, /device:TPU:0, one launch (start us, length us, event | category | flops | bytes accessed | tf_op | source)
XLA Modules:
  0.0 21.0 jit_solution(15492993567145812362)
XLA Ops:
  0.0 0.8 %slice.4 = bf16[3,4,2304]{2,1,0:T(4,128)(2,1)S(1)} slice(bf16[12,4,2304]{2,1,0:T(4,128)(2,1)} %bitcast.9), slice={[0:3], [0:4], [0:2304]} | slice | bytes 110592 | tf_op jit(solution)/shard_map/slice | solution.py:323
  0.8 3.0 %collective-permute-start = (bf16[3,4,2304]{2,1,0:T(4,128)(2,1)S(1)}, bf16[3,4,2304]{2,1,0:T(4,128)(2,1)S(1)}, u32[]{:S(2)}, u32[]{:S(2)}) collective-permute-start(bf16[3,4,2304]{2,1,0:T(4,128)(2,1)S(1)} %slice.4), channel_id=1, source_target_pairs={{0,1},{1,0},{2,3},{3,2},{4,5},{5,4},{6,7},{7,6},{8,9},{9,8},{10,11... | collective-permute-start | bytes 165896 | tf_op jit(solution)/shard_map/ppermute | solution.py:29
  3.8 2.6 %bias_tables.1 = (f32[2,2,2,2,432,128]{5,4,3,2,1,0:T(8,128)S(1)}, bf16[12,4,1152]{2,1,0:T(4,128)(2,1)S(1)}, bf16[12,4,1152]{2,1,0:T(4,128)(2,1)S(1)}, f32[1,192]...) custom-call(f32[2,6,162,2,128]{4,3,2,1,0:T(2,128)} %bitcast.8, ...), custom_call_target="tpu_custom_call" | custom-call | flops 4000000 | bytes 6000000 | tf_op jit(solution)/shard_map/bias_tables/pallas_call | solution.py:342
  6.4 0.0 collective-permute-done.south_ref
  6.5 0.1 collective-permute-start.2
  6.6 4.7 %collective-permute-start.1 = (bf16[12,4,1152]{2,1,0:T(4,128)(2,1)S(1)}, bf16[12,4,1152]{2,1,0:T(4,128)(2,1)S(1)}, u32[]{:S(2)}, u32[]{:S(2)}) collective-permute-start(bf16[12,4,1152]{2,1,0:T(4,128)(2,1)S(1)} %pack_half.2.rest_0_.refs_0_.refs_2_), channel_id=1, source_target_pairs={{2,4},{4,2},{6,8},{8,6},{10,12},{12,10},{14,16},{16,14},{18,20},{2... | collective-permute-start | bytes 331784 | tf_op jit(solution)/shard_map/ppermute | solution.py:38
  11.3 0.0 collective-permute-done.2.refs_1_
  11.3 2.1 %swin_windows.3.refs_9_.near_low_ref = bf16[1,6,4,1152]{3,2,1,0:T(4,128)(2,1)S(1)} custom-call(bf16[12,4,1152]{2,1,0:T(4,128)(2,1)S(1)} %pack_half.3.refs_0_, bf16[12,4,1152]{2,1,0:T(4,128)(2,1)S(1)} %collective-permute-done.2.refs_1_, f32[1,192]{1,0:T(1,128)S(1)} %get-tuple-element.17.refs_2_.refs_4_, ...), custom_call_target="tpu_custom_call" | custom-call | flops 200000000 | bytes 3000000 | tf_op jit(solution)/shard_map/swin_windows/pallas_call | solution.py:297
  13.4 0.3 %collective-permute-done.1.refs_1_.refs_3_ = bf16[12,4,1152]{2,1,0:T(4,128)(2,1)S(1)} collective-permute-done((bf16[12,4,1152]{2,1,0:T(4,128)(2,1)S(1)}, bf16[12,4,1152]{2,1,0:T(4,128)(2,1)S(1)}, u32[]{:S(2)}, u32[]{:S(2)}) %collective-permute-start.1) | collective-permute-done | bytes 110624 | tf_op jit(solution)/shard_map/ppermute | solution.py:38
  13.7 2.1 %swin_windows.4 = (bf16[1,6,4,1152]{3,2,1,0:T(4,128)(2,1)S(1)}, bf16[2,3,4,1152]{3,2,1,0:T(4,128)(2,1)S(1)}) custom-call(bf16[12,4,1152]{2,1,0:T(4,128)(2,1)S(1)} %pack_half.2.rest_0_.refs_0_.refs_2_, bf16[12,4,1152]{2,1,0:T(4,128)(2,1)S(1)} %collective-permute-done.1.refs_1_.refs_3_, f32[1,192]{1,0:T(1,128)S(1)} %get-tuple-element.17.refs_2_.refs_4_, ...), custom_call_target="tpu_custom_call" | custom-call | flops 200000000 | bytes 3000000 | tf_op jit(solution)/shard_map/swin_windows/pallas_call | solution.py:297
  15.8 1.6 %collective-permute-start.3 = (bf16[2,3,4,1152]{3,2,1,0:T(4,128)(2,1)S(1)}, bf16[2,3,4,1152]{3,2,1,0:T(4,128)(2,1)S(1)}, u32[]{:S(2)}, u32[]{:S(2)}) collective-permute-start(bf16[2,3,4,1152]{3,2,1,0:T(4,128)(2,1)S(1)} %get-tuple-element.25), channel_id=1, source_target_pairs={{0,1},{1,0},{2,3},{3,2},{4,5},{5,4},{6,7},{7,6},{8,9},{9,8},{10,11... | collective-permute-start | bytes 165896 | tf_op jit(solution)/shard_map/ppermute | solution.py:29
  17.4 2.9 %swin_windows.5.high_ref = bf16[2,6,4,1152]{3,2,1,0:T(4,128)(2,1)S(1)} custom-call(bf16[12,4,1152]{2,1,0:T(4,128)(2,1)S(1)} %pack_half.3.refs_0_, bf16[12,4,1152]{2,1,0:T(4,128)(2,1)S(1)} %collective-permute-done.2.refs_1_, bf16[12,4,1152]{2,1,0:T(4,128)(2,1)S(1)} %pack_half.2.rest_0_.refs_0_.refs_2_, ...), custom_call_target="tpu_custom_call" | custom-call | flops 400000000 | bytes 3000000 | tf_op jit(solution)/shard_map/swin_windows/pallas_call | solution.py:297
  20.3 0.0 collective-permute-done.3.top_ref
  20.3 0.7 %last_rows.1 = bf16[12,4,2304]{2,1,0:T(4,128)(2,1)} custom-call(bf16[2,3,4,1152]{3,2,1,0:T(4,128)(2,1)S(1)} %collective-permute-done.3.top_ref, bf16[2,6,4,1152]{3,2,1,0:T(4,128)(2,1)S(1)} %swin_windows.5.high_ref, bf16[1,6,4,1152]{3,2,1,0:T(4,128)(2,1)S(1)} %swin_windows.3.refs_9_.near_low_ref, bf16[1,6,4,1152]{3,2,1,0:T(4,128)(2,1)S(1)} %get-tuple-element.26.far_low_ref), custom_call_target="tpu_custom_call" | custom-call | bytes 400000 | tf_op jit(solution)/shard_map/last_rows/pallas_call | solution.py:378
  (2 shorter events, 0.0 us)
Async XLA Ops:
  0.8 5.6 %collective-permute-start = (bf16[3,4,2304]{2,1,0:T(4,128)(2,1)S(1)}, bf16[3,4,2304]{2,1,0:T(4,128)(2,1)S(1)}, u32[]{:S(2)}, u32[]{:S(2)}) collective-permute-start(bf16[3,4,2304]{2,1,0:T(4,128)(2,1)S(1)} %slice.4), channel_id=1, source_target_pairs={{0,1},{1,0},{2,3},{3,2},{4,5},{5,4},{6,7},{7,6},{8,9},{9,8},{10,11... | collective-permute-start | bytes 165896 | tf_op jit(solution)/shard_map/ppermute | solution.py:29
  6.5 4.8 %collective-permute-start.2 = (bf16[12,4,1152]{2,1,0:T(4,128)(2,1)S(1)}, bf16[12,4,1152]{2,1,0:T(4,128)(2,1)S(1)}, u32[]{:S(2)}, u32[]{:S(2)}) collective-permute-start(bf16[12,4,1152]{2,1,0:T(4,128)(2,1)S(1)} %pack_half.3.refs_0_), channel_id=1, source_target_pairs={{0,2},{2,0},{4,6},{6,4},{8,10},{10,8},{12,14},{14,12},{16,18},{18,... | collective-permute-start | bytes 331784 | tf_op jit(solution)/shard_map/ppermute | solution.py:38
  6.6 7.1 %collective-permute-start.1 = (bf16[12,4,1152]{2,1,0:T(4,128)(2,1)S(1)}, bf16[12,4,1152]{2,1,0:T(4,128)(2,1)S(1)}, u32[]{:S(2)}, u32[]{:S(2)}) collective-permute-start(bf16[12,4,1152]{2,1,0:T(4,128)(2,1)S(1)} %pack_half.2.rest_0_.refs_0_.refs_2_), channel_id=1, source_target_pairs={{2,4},{4,2},{6,8},{8,6},{10,12},{12,10},{14,16},{16,14},{18,20},{2... | collective-permute-start | bytes 331784 | tf_op jit(solution)/shard_map/ppermute | solution.py:38
  15.8 4.4 %collective-permute-start.3 = (bf16[2,3,4,1152]{3,2,1,0:T(4,128)(2,1)S(1)}, bf16[2,3,4,1152]{3,2,1,0:T(4,128)(2,1)S(1)}, u32[]{:S(2)}, u32[]{:S(2)}) collective-permute-start(bf16[2,3,4,1152]{3,2,1,0:T(4,128)(2,1)S(1)} %get-tuple-element.25), channel_id=1, source_target_pairs={{0,1},{1,0},{2,3},{3,2},{4,5},{5,4},{6,7},{7,6},{8,9},{9,8},{10,11... | collective-permute-start | bytes 165896 | tf_op jit(solution)/shard_map/ppermute | solution.py:29

commit v13 on v12

--- a/solution.py
+++ b/solution.py
@@ -70,39 +70,15 @@
         copy.wait()
 
 
-def table_kernel(count, *refs):
-    bias_any, field_any, *weights_any = refs[: 2 + count]
-    table_ref, near_ref, far_ref, *weights_ref = refs[2 + count : 5 + 2 * count]
-    bias_ref, sems, side_sems = refs[5 + 2 * count :]
-    windows, heads, tiles = bias_any.shape[:3]
-    lines = bias_ref.shape[0]
-    flat = bias_any.reshape(lines, LANES)
-    parts = windows
-    copies = []
-    for n in range(parts):
-        at = pl.ds(n * (lines // parts), lines // parts)
-        copies.append(pltpu.make_async_copy(flat.at[at], bias_ref.at[at], sems.at[n]))
-        copies[-1].start()
-    rows, half = field_any.shape[0] - EDGE, near_ref.shape[2]
-    near_at, far_at = half_places(half)
-    fetches = [
-        (field_any.at[EDGE:, :, pl.ds(far_at, half)], far_ref.at[:rows]),
-        (field_any.at[EDGE:, :, pl.ds(near_at, half)], near_ref.at[:rows]),
-    ]
-    fetches += list(zip(weights_any, weights_ref))
-    fetches = [
-        pltpu.make_async_copy(source, target, side_sems.at[n])
-        for n, (source, target) in enumerate(fetches)
-    ]
-    for copy in fetches:
-        copy.start()
+def build_tables(bias_ref, table_ref, heads, wrap):
+    lines = bias_ref.shape[0] // heads
     blocks = WIN_LEV * WIN_LAT // 2
     lane = lax.broadcasted_iota(jnp.int32, (blocks, LANES), 1)
     block = lax.broadcasted_iota(jnp.int32, (blocks, LANES), 0)
     is_last = lax.axis_index("lat") == lax.axis_size("lat") - 1
     last = jnp.where(is_last, -1e9, 0.0).astype(jnp.float32)
 
-    def penalty(part, second, levels, wrap):
+    def penalty(part, second, levels):
         key = lane + part * LANES
         key_lev = key // QUERIES
         key_side = (key - key_lev * QUERIES) // (QUERIES // 2)
@@ -116,38 +92,58 @@
             out = out + jnp.where(key_side != side, last, 0.0)
         return out
 
-    for k in range(windows):
-        masks = {
-            (p, part, second): penalty(part, second, p == 1, k == windows - 1)
-            for p in range(2)
-            for part in range(2)
-            for second in range(2)
-        }
-        copies[k].wait()
-        for h in range(heads):
-            for p in range(2):
-                base = (k * heads + h) * 2 * tiles + p
-                for third in range(3):
-                    line = base + third * 18
-                    pieces = [
-                        bias_ref[pl.ds(line + 2 * u, blocks, stride=54), :] * LOG2E
-                        for u in range(9)
-                    ]
-                    for r in range(8):
-                        shift = 16 * r
-                        main, nxt = pieces[r], pieces[r + 1]
-                        if r:
-                            main = pltpu.roll(main, LANES - shift, 1)
-                            nxt = pltpu.roll(nxt, LANES - shift, 1)
-                            main = jnp.where(lane < LANES - shift, main, nxt)
-                        second, col = divmod(8 * third + r, WIN_LON)
-                        side = col // HALF
-                        place = h * QUERIES + HALF * second + col % HALF
-                        at = pl.ds(place, blocks, stride=WIN_LON)
-                        for part, piece in enumerate((main, nxt)):
-                            filled = piece + masks[p, part, second]
-                            table_ref[k, p, 1 - side, part, at, :] = filled
+    masks = {
+        (p, part, second): penalty(part, second, p == 1)
+        for p in range(2)
+        for part in range(2)
+        for second in range(2)
+    }
+    for h in range(heads):
+        for p in range(2):
+            for third in range(3):
+                line = h * lines + p + third * 18
+                pieces = [
+                    bias_ref[pl.ds(line + 2 * u, blocks, stride=54), :] * LOG2E for u in range(9)
+                ]
+                for r in range(8):
+                    shift = 16 * r
+                    main, nxt = pieces[r], pieces[r + 1]
+                    if r:
+                        main = pltpu.roll(main, LANES - shift, 1)
+                        nxt = pltpu.roll(nxt, LANES - shift, 1)
+                        main = jnp.where(lane < LANES - shift, main, nxt)
+                    second, col = divmod(8 * third + r, WIN_LON)
+                    side = col // HALF
+                    place = h * QUERIES + HALF * second + col % HALF
+                    at = pl.ds(place, blocks, stride=WIN_LON)
+                    for part, piece in enumerate((main, nxt)):
+                        table_ref[p, 1 - side, part, at, :] = piece + masks[p, part, second]
+
+
+def table_kernel(count, heads, *refs):
+    bias_any, field_any, *weights_any = refs[: 2 + count]
+    table_ref, inner_ref, near_ref, far_ref, *weights_ref = refs[2 + count : 6 + 2 * count]
+    bias_ref, sems = refs[6 + 2 * count :]
+    lines = bias_ref.shape[0]
+    flat = bias_any.reshape(2 * lines, LANES)
+    rows, half = field_any.shape[0] - EDGE, near_ref.shape[2]
+    near_at, far_at = half_places(half)
+    fetches = [
+        (flat.at[pl.ds(lines, lines)], bias_ref),
+        (field_any.at[EDGE:, :, pl.ds(far_at, half)], far_ref.at[:rows]),
+        (field_any.at[EDGE:, :, pl.ds(near_at, half)], near_ref.at[:rows]),
+        (flat.at[pl.ds(0, lines)], inner_ref),
+    ]
+    fetches += list(zip(weights_any, weights_ref))
+    fetches = [
+        pltpu.make_async_copy(source, target, sems.at[n])
+        for n, (source, target) in enumerate(fetches)
+    ]
     for copy in fetches:
+        copy.start()
+    fetches[0].wait()
+    build_tables(bias_ref, table_ref, heads, True)
+    for copy in fetches[1:]:
         copy.wait()
 
 
@@ -162,14 +158,16 @@
     return half + half * jnp.tanh(x * (GELU_0 + GELU_1 * (x * x)))
 
 
-def units_kernel(chans, heads, units, lower, *refs):
+def units_kernel(chans, heads, units, extra, *refs):
     count = len(units)
     pieces, refs = refs[: 2 * count], refs[2 * count :]
     gain1_ref, qkv_ref, proj_ref, gain2_ref, fc1_ref, fc2_ref, table_ref, *refs = refs
-    if lower:
-        lower_ref, out_ref, send_ref, keys_ref, own_ref, res_ref = refs
+    if extra:
+        extra_ref, out_ref, extra_out, keys_ref, own_ref, res_ref = refs
     else:
         out_ref, keys_ref, own_ref, res_ref = refs
+    if extra == "tables":
+        build_tables(extra_ref, extra_out, heads, False)
     head_dim = chans // heads
     low = lax.broadcasted_iota(jnp.int32, (1, LANES), 1) < SPARE
     odd = lax.rem(lax.axis_index("lon"), 2)
@@ -235,7 +233,7 @@
             probs = []
             for h in range(heads):
                 at = slice(h * QUERIES, (h + 1) * QUERIES)
-                bias = [table_ref[window, p, rights[n], part, at] for part in range(2)]
+                bias = [table_ref[p, rights[n], part, at] for part in range(2)]
                 bias = jnp.concatenate([bias[0], bias[1][:, : TOKENS - LANES]], axis=1)
                 part = scores[at] + bias
                 probs.append(jnp.exp2(part - jnp.max(part, axis=1, keepdims=True)))
@@ -280,22 +278,26 @@
                 tiles.append(jnp.where(low, shifted[0], shifted[1]))
                 tiles = jnp.concatenate(tiles, axis=1).astype(jnp.bfloat16)
                 out_ref[n, row, :, pair * 2 * chans : (pair + 1) * 2 * chans] = tiles
-    if lower:
-        send_ref[0] = lower_ref[0, EDGE:]
-        send_ref[1] = out_ref[0, EDGE:]
-
-
-def run_units(units, near, far, table, weights, chans, heads, *lower):
+    if extra == "send":
+        extra_out[0] = extra_ref[0, EDGE:]
+        extra_out[1] = out_ref[0, EDGE:]
+
+
+def run_units(units, near, far, weights, chans, heads, table, extra=None, extra_in=None):
     count = len(units)
     pieces = [x for is_near, _ in units for x in (near if is_near else far)]
     piece = pieces[0]
-    out = jax.ShapeDtypeStruct((count, WIN_LAT) + piece.shape[1:], piece.dtype)
-    send = jax.ShapeDtypeStruct((2, EDGE) + piece.shape[1:], piece.dtype)
-    operands = (*pieces, *weights, table, *lower)
+    outs = [jax.ShapeDtypeStruct((count, WIN_LAT) + piece.shape[1:], piece.dtype)]
+    operands = (*pieces, *weights, table)
+    if extra == "send":
+        outs.append(jax.ShapeDtypeStruct((2, EDGE) + piece.shape[1:], piece.dtype))
+    elif extra == "tables":
+        outs.append(jax.ShapeDtypeStruct(table.shape, table.dtype))
+    if extra:
+        operands += (extra_in,)
     vmem = pl.BlockSpec(memory_space=pltpu.VMEM)
-    outs = [out, send] if lower else [out]
     return pl.pallas_call(
-        functools.partial(units_kernel, chans, heads, units, bool(lower)),
+        functools.partial(units_kernel, chans, heads, units, extra),
         out_shape=outs,
         in_specs=[vmem] * len(operands),
         out_specs=[vmem] * len(outs),
@@ -332,22 +334,22 @@
     vmem = pl.BlockSpec(memory_space=pltpu.VMEM)
     anywhere = pl.BlockSpec(memory_space=pl.ANY)
     piece = jax.ShapeDtypeStruct((rows, levels, half), field.dtype)
-    table = jax.ShapeDtypeStruct((2, 2, 2, 2, heads * QUERIES, LANES), jnp.float32)
+    table = jax.ShapeDtypeStruct((2, 2, 2, heads * QUERIES, LANES), jnp.float32)
     windows, zwin, _, entries = earth_bias.shape
     tiles = entries // LANES
     bias = earth_bias.reshape(windows, zwin, heads, tiles, LANES).transpose(0, 2, 3, 1, 4)
     sources = (bias, field) + weights
+    raw = jax.ShapeDtypeStruct((bias.size // windows // LANES, LANES), bias.dtype)
     sources = [pltpu.with_memory_space_constraint(x, pltpu.HBM) for x in sources]
-    outs = [table, piece, piece] + [jax.ShapeDtypeStruct(x.shape, x.dtype) for x in weights]
-    table, near, far, *weights = pl.pallas_call(
-        functools.partial(table_kernel, len(weights)),
+    outs = [table, raw, piece, piece] + [jax.ShapeDtypeStruct(x.shape, x.dtype) for x in weights]
+    table, inner, near, far, *weights = pl.pallas_call(
+        functools.partial(table_kernel, len(weights), heads),
         out_shape=outs,
         in_specs=[pl.BlockSpec(memory_space=pltpu.HBM)] * len(sources),
         out_specs=[vmem] * len(outs),
         scratch_shapes=[
-            pltpu.VMEM((bias.size // LANES, LANES), jnp.float32),
-            pltpu.SemaphoreType.DMA((2 * windows,)),
-            pltpu.SemaphoreType.DMA((2 + len(weights),)),
+            pltpu.VMEM(raw.shape, raw.dtype),
+            pltpu.SemaphoreType.DMA((4 + len(weights),)),
         ],
         compiler_params=pltpu.CompilerParams(vmem_limit_bytes=VMEM_BYTES),
         cost_estimate=pl.CostEstimate(flops=4_000_000, bytes_accessed=6_000_000, transcendentals=0),
@@ -370,11 +372,11 @@
     far_halo = swapped(far, "lon", 1)
     near_halo = swapped(near, "lon", 0)
     near, far = (near, near_halo), (far, far_halo)
-    common = (near, far, table, weights, chans, heads)
-    (near_low,) = run_units(((True, 1),), *common)
-    far_low, send = run_units(((False, 1),), *common, near_low)
+    common = (near, far, weights, chans, heads)
+    near_low, inner = run_units(((True, 1),), *common, table, "tables", inner)
+    far_low, send = run_units(((False, 1),), *common, table, "send", near_low)
     top = moved(send, "lat", 1)
-    (high,) = run_units(((True, 0), (False, 0)), *common)
+    (high,) = run_units(((True, 0), (False, 0)), *common, inner)
     done = pl.pallas_call(
         last_kernel,
         out_shape=jax.ShapeDtypeStruct(field.shape, field.dtype),

time: 21.2 us -> 21.2 us (level)
  Pallas kernels: 10.5 us -> 9.91 us
  starting transfers between devices: 9.34 us -> 9.82 us
    pallas_call x4, Pallas kernels: 9.67 us -> 9.13 us  [the longest x3 7.19 us: run_units(): pl.pallas_call(functools.partial(units_kernel, chans, heads, units, extra...]
    ppermute x2, starting transfers between devices: 4.78 us -> 5.26 us  [swapped(): return lax.ppermute(x, axis, pairs)]
  transfers between devices with their start and end apart: 4 -> 4, of which waited for: 1 -> 2; matrix products, arithmetic and copies ran while one was open for 0% -> 0% of each run, Pallas kernels for 36% -> 33%
where the time goes in v13:
time: 21.2 us; the launch traced here: 21 us
  Pallas kernels  9.91 us (47%)
  starting transfers between devices  9.82 us (46%)
  local copies, waits for them, and re-layouts  0.83 us (4%)
  waiting for transfers between devices  0.4 us (2%)
    pallas_call x3, Pallas kernels, run_units(): pl.pallas_call(functools.partial(units_kernel, chans, heads, units, extra...  7.19 us
    ppermute x2, starting transfers between devices, swapped(): return lax.ppermute(x, axis, pairs)  5.26 us
    ppermute x2, starting transfers between devices, moved(): return lax.ppermute(x, axis, [(i, (i + by) % size) for i in range(size)])  4.56 us
    pallas_call x1, Pallas kernels, shards(): pl.pallas_call(functools.partial(table_kernel, len(weights), heads), out_...  1.95 us
    slice x1, local copies, waits for them, and re-layouts, shards(): south = moved(field[:EDGE], 'lat', -1)  0.83 us
    pallas_call x1, Pallas kernels, shards(): pl.pallas_call(last_kernel, out_shape=jax.ShapeDtypeStruct(field.shape, f...  0.74 us
  transfers between devices with their start and end apart: 4, of which 2 were waited for; matrix products, arithmetic and copies ran while one was open for 0% of the time, Pallas kernels for 33%

profile of v13, /device:TPU:0, one launch (start us, length us, event | category | flops | bytes accessed | tf_op | source)
XLA Modules:
  0.0 21.0 jit_solution(18162586702353409794)
XLA Ops:
  0.0 0.8 %slice.4 = bf16[3,4,2304]{2,1,0:T(4,128)(2,1)S(1)} slice(bf16[12,4,2304]{2,1,0:T(4,128)(2,1)} %bitcast.9), slice={[0:3], [0:4], [0:2304]} | slice | bytes 110592 | tf_op jit(solution)/shard_map/slice | solution.py:325
  0.8 3.0 %collective-permute-start = (bf16[3,4,2304]{2,1,0:T(4,128)(2,1)S(1)}, bf16[3,4,2304]{2,1,0:T(4,128)(2,1)S(1)}, u32[]{:S(2)}, u32[]{:S(2)}) collective-permute-start(bf16[3,4,2304]{2,1,0:T(4,128)(2,1)S(1)} %slice.4), channel_id=1, source_target_pairs={{0,1},{1,0},{2,3},{3,2},{4,5},{5,4},{6,7},{7,6},{8,9},{9,8},{10,11... | collective-permute-start | bytes 165896 | tf_op jit(solution)/shard_map/ppermute | solution.py:29
  3.8 1.9 %bias_tables.1 = (f32[2,2,2,432,128]{4,3,2,1,0:T(8,128)S(1)}, f32[1944,128]{1,0:T(8,128)S(1)}, bf16[12,4,1152]{2,1,0:T(4,128)(2,1)S(1)}, bf16[12,4,1152]{2,1,0:T...) custom-call(f32[2,6,162,2,128]{4,3,2,1,0:T(2,128)} %bitcast.8, ...), custom_call_target="tpu_custom_call" | custom-call | flops 4000000 | bytes 6000000 | tf_op jit(solution)/shard_map/bias_tables/pallas_call | solution.py:345
  5.8 0.2 collective-permute-done.south_ref
  6.0 0.1 collective-permute-start.2
  6.1 5.2 %collective-permute-start.1 = (bf16[12,4,1152]{2,1,0:T(4,128)(2,1)S(1)}, bf16[12,4,1152]{2,1,0:T(4,128)(2,1)S(1)}, u32[]{:S(2)}, u32[]{:S(2)}) collective-permute-start(bf16[12,4,1152]{2,1,0:T(4,128)(2,1)S(1)} %pack_half.2.rest_0_.refs_0_.refs_2_), channel_id=1, source_target_pairs={{2,4},{4,2},{6,8},{8,6},{10,12},{12,10},{14,16},{16,14},{18,20},{2... | collective-permute-start | bytes 331784 | tf_op jit(solution)/shard_map/ppermute | solution.py:38
  11.3 0.0 collective-permute-done.2.refs_1_
  11.3 2.2 %swin_windows.3 = (bf16[1,6,4,1152]{3,2,1,0:T(4,128)(2,1)S(1)}, f32[2,2,2,432,128]{4,3,2,1,0:T(8,128)S(1)}) custom-call(bf16[12,4,1152]{2,1,0:T(4,128)(2,1)S(1)} %pack_half.3.refs_0_, bf16[12,4,1152]{2,1,0:T(4,128)(2,1)S(1)} %collective-permute-done.2.refs_1_, f32[1,192]{1,0:T(1,128)S(1)} %get-tuple-element.20.refs_2_.refs_4_, ...), custom_call_target="tpu_custom_call" | custom-call | flops 200000000 | bytes 3000000 | tf_op jit(solution)/shard_map/swin_windows/pallas_call | solution.py:299
  13.5 0.2 %collective-permute-done.1.refs_1_.refs_3_ = bf16[12,4,1152]{2,1,0:T(4,128)(2,1)S(1)} collective-permute-done((bf16[12,4,1152]{2,1,0:T(4,128)(2,1)S(1)}, bf16[12,4,1152]{2,1,0:T(4,128)(2,1)S(1)}, u32[]{:S(2)}, u32[]{:S(2)}) %collective-permute-start.1) | collective-permute-done | bytes 110624 | tf_op jit(solution)/shard_map/ppermute | solution.py:38
  13.7 2.1 %swin_windows.4 = (bf16[1,6,4,1152]{3,2,1,0:T(4,128)(2,1)S(1)}, bf16[2,3,4,1152]{3,2,1,0:T(4,128)(2,1)S(1)}) custom-call(bf16[12,4,1152]{2,1,0:T(4,128)(2,1)S(1)} %pack_half.2.rest_0_.refs_0_.refs_2_, bf16[12,4,1152]{2,1,0:T(4,128)(2,1)S(1)} %collective-permute-done.1.refs_1_.refs_3_, f32[1,192]{1,0:T(1,128)S(1)} %get-tuple-element.20.refs_2_.refs_4_, ...), custom_call_target="tpu_custom_call" | custom-call | flops 200000000 | bytes 3000000 | tf_op jit(solution)/shard_map/swin_windows/pallas_call | solution.py:299
  15.8 1.6 %collective-permute-start.3 = (bf16[2,3,4,1152]{3,2,1,0:T(4,128)(2,1)S(1)}, bf16[2,3,4,1152]{3,2,1,0:T(4,128)(2,1)S(1)}, u32[]{:S(2)}, u32[]{:S(2)}) collective-permute-start(bf16[2,3,4,1152]{3,2,1,0:T(4,128)(2,1)S(1)} %get-tuple-element.30), channel_id=1, source_target_pairs={{0,1},{1,0},{2,3},{3,2},{4,5},{5,4},{6,7},{7,6},{8,9},{9,8},{10,11... | collective-permute-start | bytes 165896 | tf_op jit(solution)/shard_map/ppermute | solution.py:29
  17.4 2.9 %swin_windows.5.high_ref = bf16[2,6,4,1152]{3,2,1,0:T(4,128)(2,1)S(1)} custom-call(bf16[12,4,1152]{2,1,0:T(4,128)(2,1)S(1)} %pack_half.3.refs_0_, bf16[12,4,1152]{2,1,0:T(4,128)(2,1)S(1)} %collective-permute-done.2.refs_1_, bf16[12,4,1152]{2,1,0:T(4,128)(2,1)S(1)} %pack_half.2.rest_0_.refs_0_.refs_2_, ...), custom_call_target="tpu_custom_call" | custom-call | flops 400000000 | bytes 3000000 | tf_op jit(solution)/shard_map/swin_windows/pallas_call | solution.py:299
  20.3 0.0 collective-permute-done.3.top_ref
  20.3 0.7 %last_rows.1 = bf16[12,4,2304]{2,1,0:T(4,128)(2,1)} custom-call(bf16[2,3,4,1152]{3,2,1,0:T(4,128)(2,1)S(1)} %collective-permute-done.3.top_ref, bf16[2,6,4,1152]{3,2,1,0:T(4,128)(2,1)S(1)} %swin_windows.5.high_ref, bf16[1,6,4,1152]{3,2,1,0:T(4,128)(2,1)S(1)} %get-tuple-element.29.refs_9_.near_low_ref, bf16[1,6,4,1152]{3,2,1,0:T(4,128)(2,1)S(1)} %get-tuple-element.32.far_low_ref), custom_call_target="tpu_custom_call" | custom-call | bytes 400000 | tf_op jit(solution)/shard_map/last_rows/pallas_call | solution.py:380
  (2 shorter events, 0.0 us)
Async XLA Ops:
  0.8 5.1 %collective-permute-start = (bf16[3,4,2304]{2,1,0:T(4,128)(2,1)S(1)}, bf16[3,4,2304]{2,1,0:T(4,128)(2,1)S(1)}, u32[]{:S(2)}, u32[]{:S(2)}) collective-permute-start(bf16[3,4,2304]{2,1,0:T(4,128)(2,1)S(1)} %slice.4), channel_id=1, source_target_pairs={{0,1},{1,0},{2,3},{3,2},{4,5},{5,4},{6,7},{7,6},{8,9},{9,8},{10,11... | collective-permute-start | bytes 165896 | tf_op jit(solution)/shard_map/ppermute | solution.py:29
  6.0 5.3 %collective-permute-start.2 = (bf16[12,4,1152]{2,1,0:T(4,128)(2,1)S(1)}, bf16[12,4,1152]{2,1,0:T(4,128)(2,1)S(1)}, u32[]{:S(2)}, u32[]{:S(2)}) collective-permute-start(bf16[12,4,1152]{2,1,0:T(4,128)(2,1)S(1)} %pack_half.3.refs_0_), channel_id=1, source_target_pairs={{0,2},{2,0},{4,6},{6,4},{8,10},{10,8},{12,14},{14,12},{16,18},{18,... | collective-permute-start | bytes 331784 | tf_op jit(solution)/shard_map/ppermute | solution.py:38
  6.1 7.6 %collective-permute-start.1 = (bf16[12,4,1152]{2,1,0:T(4,128)(2,1)S(1)}, bf16[12,4,1152]{2,1,0:T(4,128)(2,1)S(1)}, u32[]{:S(2)}, u32[]{:S(2)}) collective-permute-start(bf16[12,4,1152]{2,1,0:T(4,128)(2,1)S(1)} %pack_half.2.rest_0_.refs_0_.refs_2_), channel_id=1, source_target_pairs={{2,4},{4,2},{6,8},{8,6},{10,12},{12,10},{14,16},{16,14},{18,20},{2... | collective-permute-start | bytes 331784 | tf_op jit(solution)/shard_map/ppermute | solution.py:38
  15.8 4.4 %collective-permute-start.3 = (bf16[2,3,4,1152]{3,2,1,0:T(4,128)(2,1)S(1)}, bf16[2,3,4,1152]{3,2,1,0:T(4,128)(2,1)S(1)}, u32[]{:S(2)}, u32[]{:S(2)}) collective-permute-start(bf16[2,3,4,1152]{3,2,1,0:T(4,128)(2,1)S(1)} %get-tuple-element.30), channel_id=1, source_target_pairs={{0,1},{1,0},{2,3},{3,2},{4,5},{5,4},{6,7},{7,6},{8,9},{9,8},{10,11... | collective-permute-start | bytes 165896 | tf_op jit(solution)/shard_map/ppermute | solution.py:29

commit v14 on v13

--- a/solution.py
+++ b/solution.py
@@ -49,6 +49,13 @@
     rows = piece_ref.shape[0] - EDGE
     piece_ref[:rows] = kept_ref[:rows]
     piece_ref[rows:] = south_ref[:, :, pl.ds(at, piece_ref.shape[2])]
+
+
+def pick_kernel(both_ref, out_ref, sem):
+    odd = lax.rem(lax.axis_index("lon"), 2)
+    copy = pltpu.make_async_copy(both_ref.at[1 - odd], out_ref, sem)
+    copy.start()
+    copy.wait()
 
 
 def last_kernel(top_ref, high_ref, near_low_ref, far_low_ref, out_ref, sems):
@@ -370,7 +377,18 @@
     far = pack(1, far)
     near = pack(0, near, far)
     far_halo = swapped(far, "lon", 1)
-    near_halo = swapped(near, "lon", 0)
+    lons = lax.axis_size("lon")
+    both = lax.all_gather(near, "lon", axis_index_groups=[[i, i + 1] for i in range(0, lons, 2)])
+    near_halo = pl.pallas_call(
+        pick_kernel,
+        out_shape=piece,
+        in_specs=[anywhere],
+        out_specs=vmem,
+        scratch_shapes=[pltpu.SemaphoreType.DMA],
+        compiler_params=pltpu.CompilerParams(vmem_limit_bytes=VMEM_BYTES),
+        cost_estimate=pl.CostEstimate(flops=0, bytes_accessed=250_000, transcendentals=0),
+        name="pick_halo",
+    )(both)
     near, far = (near, near_halo), (far, far_halo)
     common = (near, far, weights, chans, heads)
     near_low, inner = run_units(((True, 1),), *common, table, "tables", inner)

time: 21.2 us -> 21.3 us (level)
  blocking collectives: 0 us -> 1.96 us
  starting transfers between devices: 9.82 us -> 8 us
    all_gather x0 -> x1, blocking collectives: none -> 1.96 us  [shards(): lax.all_gather(near, 'lon', axis_index_groups=[[i, i + 1] for i in range(...]
    ppermute x2 -> x1, starting transfers between devices: 5.26 us -> 3.62 us  [swapped(): return lax.ppermute(x, axis, pairs)]
    ppermute x2 -> x1, waiting for transfers between devices: 0.22 us -> 0.01 us  [swapped(): return lax.ppermute(x, axis, pairs)]
  transfers between devices with their start and end apart: 4 -> 3, of which waited for: 2 -> 1; matrix products, arithmetic and copies ran while one was open for 0% -> 0% of each run, Pallas kernels for 33% -> 34%
where the time goes in v14:
time: 21.3 us; the launch traced here: 21.1 us
  Pallas kernels  10 us (47%)
  starting transfers between devices  8 us (38%)
  blocking collectives  1.96 us (9%)
  local copies, waits for them, and re-layouts  0.83 us (4%)
    pallas_call x3, Pallas kernels, run_units(): pl.pallas_call(functools.partial(units_kernel, chans, heads, units, extra...  7.19 us
    ppermute x2, starting transfers between devices, moved(): return lax.ppermute(x, axis, [(i, (i + by) % size) for i in range(size)])  4.39 us
    ppermute x1, starting transfers between devices, swapped(): return lax.ppermute(x, axis, pairs)  3.62 us
    all_gather x1, blocking collectives, shards(): lax.all_gather(near, 'lon', axis_index_groups=[[i, i + 1] for i in range(...  1.96 us
    pallas_call x1, Pallas kernels, shards(): pl.pallas_call(functools.partial(table_kernel, len(weights), heads), out_...  1.95 us
    slice x1, local copies, waits for them, and re-layouts, shards(): south = moved(field[:EDGE], 'lat', -1)  0.83 us
    pallas_call x1, Pallas kernels, shards(): pl.pallas_call(last_kernel, out_shape=jax.ShapeDtypeStruct(field.shape, f...  0.74 us
  transfers between devices with their start and end apart: 3, of which 1 were waited for; matrix products, arithmetic and copies ran while one was open for 0% of the time, Pallas kernels for 34%

profile of v14, /device:TPU:0, one launch (start us, length us, event | category | flops | bytes accessed | tf_op | source)
XLA Modules:
  0.0 21.1 jit_solution(3331727299387684283)
XLA Ops:
  0.0 0.8 %slice.4 = bf16[3,4,2304]{2,1,0:T(4,128)(2,1)S(1)} slice(bf16[12,4,2304]{2,1,0:T(4,128)(2,1)} %bitcast.11), slice={[0:3], [0:4], [0:2304]} | slice | bytes 110592 | tf_op jit(solution)/shard_map/slice | solution.py:332
  0.8 3.0 %collective-permute-start = (bf16[3,4,2304]{2,1,0:T(4,128)(2,1)S(1)}, bf16[3,4,2304]{2,1,0:T(4,128)(2,1)S(1)}, u32[]{:S(2)}, u32[]{:S(2)}) collective-permute-start(bf16[3,4,2304]{2,1,0:T(4,128)(2,1)S(1)} %slice.4), channel_id=1, source_target_pairs={{0,1},{1,0},{2,3},{3,2},{4,5},{5,4},{6,7},{7,6},{8,9},{9,8},{10,11... | collective-permute-start | bytes 165896 | tf_op jit(solution)/shard_map/ppermute | solution.py:29
  3.8 1.9 %bias_tables.1 = (f32[2,2,2,432,128]{4,3,2,1,0:T(8,128)S(1)}, f32[1944,128]{1,0:T(8,128)S(1)}, bf16[12,4,1152]{2,1,0:T(4,128)(2,1)S(1)}, bf16[12,4,1152]{2,1,0:T...) custom-call(f32[2,6,162,2,128]{4,3,2,1,0:T(2,128)} %bitcast.10, ...), custom_call_target="tpu_custom_call" | custom-call | flops 4000000 | bytes 6000000 | tf_op jit(solution)/shard_map/bias_tables/pallas_call | solution.py:352
  5.8 0.2 collective-permute-done.south_ref
  6.0 3.6 %collective-permute-start.1 = (bf16[12,4,1152]{2,1,0:T(4,128)(2,1)S(1)}, bf16[12,4,1152]{2,1,0:T(4,128)(2,1)S(1)}, u32[]{:S(2)}, u32[]{:S(2)}) collective-permute-start(bf16[12,4,1152]{2,1,0:T(4,128)(2,1)S(1)} %pack_half.2.rest_0_.refs_0_.refs_2_), channel_id=1, source_target_pairs={{2,4},{4,2},{6,8},{8,6},{10,12},{12,10},{14,16},{16,14},{18,20},{2... | collective-permute-start | bytes 331784 | tf_op jit(solution)/shard_map/ppermute | solution.py:38
  9.6 2.0 %all-gather = bf16[24,4,1152]{2,1,0:T(4,128)(2,1)S(1)} all-gather(bf16[12,4,1152]{2,1,0:T(4,128)(2,1)S(1)} %pack_half.3.refs_0_), channel_id=2, replica_groups={{0,2},{4,6},{8,10},{12,14},{16,18},{20,22},{24,26},{28,30},{1,3},{5,7},..., dimensions={0}, use_global_device_ids=true | all-gather | bytes 331776 | tf_op jit(solution)/shard_map/all_gather | solution.py:381
  11.6 0.1 pick_halo.1.refs_1_
  11.7 2.2 %swin_windows.3 = (bf16[1,6,4,1152]{3,2,1,0:T(4,128)(2,1)S(1)}, f32[2,2,2,432,128]{4,3,2,1,0:T(8,128)S(1)}) custom-call(bf16[12,4,1152]{2,1,0:T(4,128)(2,1)S(1)} %pack_half.3.refs_0_, bf16[12,4,1152]{2,1,0:T(4,128)(2,1)S(1)} %pick_halo.1.refs_1_, f32[1,192]{1,0:T(1,128)S(1)} %get-tuple-element.20.refs_2_.refs_4_, ...), custom_call_target="tpu_custom_call" | custom-call | flops 200000000 | bytes 3000000 | tf_op jit(solution)/shard_map/swin_windows/pallas_call | solution.py:306
  14.0 0.0 collective-permute-done.1.refs_1_.refs_3_
  14.0 2.1 %swin_windows.4 = (bf16[1,6,4,1152]{3,2,1,0:T(4,128)(2,1)S(1)}, bf16[2,3,4,1152]{3,2,1,0:T(4,128)(2,1)S(1)}) custom-call(bf16[12,4,1152]{2,1,0:T(4,128)(2,1)S(1)} %pack_half.2.rest_0_.refs_0_.refs_2_, bf16[12,4,1152]{2,1,0:T(4,128)(2,1)S(1)} %collective-permute-done.1.refs_1_.refs_3_, f32[1,192]{1,0:T(1,128)S(1)} %get-tuple-element.20.refs_2_.refs_4_, ...), custom_call_target="tpu_custom_call" | custom-call | flops 200000000 | bytes 3000000 | tf_op jit(solution)/shard_map/swin_windows/pallas_call | solution.py:306
  16.1 1.4 %collective-permute-start.2 = (bf16[2,3,4,1152]{3,2,1,0:T(4,128)(2,1)S(1)}, bf16[2,3,4,1152]{3,2,1,0:T(4,128)(2,1)S(1)}, u32[]{:S(2)}, u32[]{:S(2)}) collective-permute-start(bf16[2,3,4,1152]{3,2,1,0:T(4,128)(2,1)S(1)} %get-tuple-element.30), channel_id=1, source_target_pairs={{0,1},{1,0},{2,3},{3,2},{4,5},{5,4},{6,7},{7,6},{8,9},{9,8},{10,11... | collective-permute-start | bytes 165896 | tf_op jit(solution)/shard_map/ppermute | solution.py:29
  17.5 2.9 %swin_windows.5.high_ref = bf16[2,6,4,1152]{3,2,1,0:T(4,128)(2,1)S(1)} custom-call(bf16[12,4,1152]{2,1,0:T(4,128)(2,1)S(1)} %pack_half.3.refs_0_, bf16[12,4,1152]{2,1,0:T(4,128)(2,1)S(1)} %pick_halo.1.refs_1_, bf16[12,4,1152]{2,1,0:T(4,128)(2,1)S(1)} %pack_half.2.rest_0_.refs_0_.refs_2_, bf16[12,4,1152]{2,1,0:T(4,128)(2,1)S(1)} %collective-permute-done.1.refs_1_.refs_3_, ...), custom_call_target="tpu_custom_call" | custom-call | flops 400000000 | bytes 3000000 | tf_op jit(solution)/shard_map/swin_windows/pallas_call | solution.py:306
  20.3 0.0 collective-permute-done.2.top_ref
  20.4 0.7 %last_rows.1 = bf16[12,4,2304]{2,1,0:T(4,128)(2,1)} custom-call(bf16[2,3,4,1152]{3,2,1,0:T(4,128)(2,1)S(1)} %collective-permute-done.2.top_ref, bf16[2,6,4,1152]{3,2,1,0:T(4,128)(2,1)S(1)} %swin_windows.5.high_ref, bf16[1,6,4,1152]{3,2,1,0:T(4,128)(2,1)S(1)} %get-tuple-element.29.refs_9_.near_low_ref, bf16[1,6,4,1152]{3,2,1,0:T(4,128)(2,1)S(1)} %get-tuple-element.32.far_low_ref), custom_call_target="tpu_custom_call" | custom-call | bytes 400000 | tf_op jit(solution)/shard_map/last_rows/pallas_call | solution.py:398
  (2 shorter events, 0.0 us)
Async XLA Ops:
  0.8 5.1 %collective-permute-start = (bf16[3,4,2304]{2,1,0:T(4,128)(2,1)S(1)}, bf16[3,4,2304]{2,1,0:T(4,128)(2,1)S(1)}, u32[]{:S(2)}, u32[]{:S(2)}) collective-permute-start(bf16[3,4,2304]{2,1,0:T(4,128)(2,1)S(1)} %slice.4), channel_id=1, source_target_pairs={{0,1},{1,0},{2,3},{3,2},{4,5},{5,4},{6,7},{7,6},{8,9},{9,8},{10,11... | collective-permute-start | bytes 165896 | tf_op jit(solution)/shard_map/ppermute | solution.py:29
  6.0 8.0 %collective-permute-start.1 = (bf16[12,4,1152]{2,1,0:T(4,128)(2,1)S(1)}, bf16[12,4,1152]{2,1,0:T(4,128)(2,1)S(1)}, u32[]{:S(2)}, u32[]{:S(2)}) collective-permute-start(bf16[12,4,1152]{2,1,0:T(4,128)(2,1)S(1)} %pack_half.2.rest_0_.refs_0_.refs_2_), channel_id=1, source_target_pairs={{2,4},{4,2},{6,8},{8,6},{10,12},{12,10},{14,16},{16,14},{18,20},{2... | collective-permute-start | bytes 331784 | tf_op jit(solution)/shard_map/ppermute | solution.py:38
  16.1 4.3 %collective-permute-start.2 = (bf16[2,3,4,1152]{3,2,1,0:T(4,128)(2,1)S(1)}, bf16[2,3,4,1152]{3,2,1,0:T(4,128)(2,1)S(1)}, u32[]{:S(2)}, u32[]{:S(2)}) collective-permute-start(bf16[2,3,4,1152]{3,2,1,0:T(4,128)(2,1)S(1)} %get-tuple-element.30), channel_id=1, source_target_pairs={{0,1},{1,0},{2,3},{3,2},{4,5},{5,4},{6,7},{7,6},{8,9},{9,8},{10,11... | collective-permute-start | bytes 165896 | tf_op jit(solution)/shard_map/ppermute | solution.py:29

commit v15 on v10

--- a/solution.py
+++ b/solution.py
@@ -77,7 +77,7 @@
     windows, heads, tiles = bias_any.shape[:3]
     lines = bias_ref.shape[0]
     flat = bias_any.reshape(lines, LANES)
-    parts = 2 * windows
+    parts = windows
     copies = []
     for n in range(parts):
         at = pl.ds(n * (lines // parts), lines // parts)
@@ -123,9 +123,8 @@
             for part in range(2)
             for second in range(2)
         }
+        copies[k].wait()
         for h in range(heads):
-            if h % (heads // 2) == 0:
-                copies[2 * k + h // (heads // 2)].wait()
             for p in range(2):
                 base = (k * heads + h) * 2 * tiles + p
                 for third in range(3):
@@ -205,60 +204,66 @@
                     own_ref[n, part, pl.ds(4 + place, LEVELS, stride=36), :] = block[part]
                     own_ref[n, part, pl.ds(148 + place, 1), :] = block[part][:1]
 
-    gain1 = gain1_ref[...]
+    gain1, gain2 = gain1_ref[...], gain2_ref[...]
     lane = lax.broadcasted_iota(jnp.int32, (1, chans), 1)
-    ones = jnp.ones((LEVELS * QUERIES, 2 * LANES - chans), jnp.float32)
-    mixed = []
-    for n, (_, window) in enumerate(units):
-        normed = layer_norm(tokens_of(keys_ref, n, 0, LEVELS * QUERIES), gain1)
-        normed = jnp.concatenate([normed[QUERIES:], normed[:QUERIES]], axis=0)
-        normed = normed.astype(jnp.bfloat16)
-        keys = jnp.dot(normed, qkv_ref[:, chans : 2 * chans], preferred_element_type=jnp.float32)
-        values = jnp.dot(normed, qkv_ref[:, 2 * chans :], preferred_element_type=jnp.float32)
-        values = jnp.concatenate([values, ones], axis=1)
-        own = layer_norm(tokens_of(own_ref, n, 40, 144), gain1).astype(jnp.bfloat16)
-        query = jnp.dot(own, qkv_ref[:, :chans], preferred_element_type=jnp.float32)
-        query = query * (head_dim ** (-0.5) * LOG2E)
-        for p in range(2):
-            q = query[p * QUERIES : (p + 1) * QUERIES]
-            k = keys[p * TOKENS : (p + 1) * TOKENS].astype(jnp.bfloat16)
-            v = values[p * TOKENS : (p + 1) * TOKENS].astype(jnp.bfloat16)
-            picked = [
-                jnp.where((lane >= h * head_dim) & (lane < (h + 1) * head_dim), q, 0.0)
-                for h in range(heads)
-            ]
-            picked = jnp.concatenate(picked, axis=0).astype(jnp.bfloat16)
-            scores = lax.dot_general(picked, k, NT, preferred_element_type=jnp.float32)
-            table = [table_ref[window, p, rights[n], part] for part in range(2)]
-            table = jnp.concatenate([table[0], table[1][:, : TOKENS - LANES]], axis=1)
-            scores = scores + table
-            top = jnp.max(scores, axis=1, keepdims=True)
-            probs = jnp.exp2(scores - top).astype(jnp.bfloat16)
-            got = jnp.dot(probs, v, preferred_element_type=jnp.float32)
-            out = jnp.zeros((QUERIES, chans), jnp.float32)
-            for h in range(heads):
-                part = got[h * QUERIES : (h + 1) * QUERIES]
-                scaled = part[:, :chans] * (1.0 / part[:, chans : chans + 1])
-                inside = (lane >= h * head_dim) & (lane < (h + 1) * head_dim)
-                out = jnp.where(inside, scaled, out)
-            mixed.append(out)
-    mixed = jnp.concatenate(mixed, axis=0).astype(jnp.bfloat16)
-    attn = jnp.dot(mixed, proj_ref[...], preferred_element_type=jnp.float32)
-    attn = attn.astype(jnp.bfloat16).astype(jnp.float32)
-    tokens = [tokens_of(own_ref, n, 40, 144) for n in range(count)]
-    resid = jnp.concatenate(tokens, axis=0) + attn
-    resid = resid.astype(jnp.bfloat16).astype(jnp.float32)
-    normed = layer_norm(resid, gain2_ref[...]).astype(jnp.bfloat16)
-    hidden = jnp.dot(normed, fc1_ref[...], preferred_element_type=jnp.float32)
-    hidden = gelu(hidden).astype(jnp.bfloat16)
-    result = lax.dot_general(hidden, fc2_ref[...], NT, preferred_element_type=jnp.float32)
-    result = resid + result
-    for n in range(count):
-        mine = result[n * 144 : (n + 1) * 144]
+    ones = jnp.ones((TOKENS, 2 * LANES - chans), jnp.float32)
+
+    def level_window(n, window, p):
+        levels = [(2 * p + 1 + lev) % LEVELS for lev in range(WIN_LEV)]
+        parts = [tokens_of(keys_ref, n, lev * QUERIES, QUERIES) for lev in levels]
+        parts = [layer_norm(x, gain1) for x in parts]
+        normed = jnp.concatenate(parts, axis=0).astype(jnp.bfloat16)
+        k = jnp.dot(normed, qkv_ref[:, chans : 2 * chans], preferred_element_type=jnp.float32)
+        k = k.astype(jnp.bfloat16)
+        v = jnp.dot(normed, qkv_ref[:, 2 * chans :], preferred_element_type=jnp.float32)
+        v = jnp.concatenate([v, ones], axis=1).astype(jnp.bfloat16)
+        tokens = tokens_of(own_ref, n, 40 + p * QUERIES, QUERIES)
+        own = layer_norm(tokens, gain1).astype(jnp.bfloat16)
+        q = jnp.dot(own, qkv_ref[:, :chans], preferred_element_type=jnp.float32)
+        q = q * (head_dim ** (-0.5) * LOG2E)
+        picked = [
+            jnp.where((lane >= h * head_dim) & (lane < (h + 1) * head_dim), q, 0.0)
+            for h in range(heads)
+        ]
+        picked = jnp.concatenate(picked, axis=0).astype(jnp.bfloat16)
+        scores = lax.dot_general(picked, k, NT, preferred_element_type=jnp.float32)
+        probs = []
+        for h in range(heads):
+            at = slice(h * QUERIES, (h + 1) * QUERIES)
+            bias = [table_ref[window, p, rights[n], part, at] for part in range(2)]
+            bias = jnp.concatenate([bias[0], bias[1][:, : TOKENS - LANES]], axis=1)
+            part = scores[at] + bias
+            probs.append(jnp.exp2(part - jnp.max(part, axis=1, keepdims=True)))
+        probs = jnp.concatenate(probs, axis=0).astype(jnp.bfloat16)
+        got = jnp.dot(probs, v, preferred_element_type=jnp.float32)
+        mixed = None
+        for h in range(heads):
+            part = got[h * QUERIES : (h + 1) * QUERIES]
+            scaled = part[:, :chans] * (1.0 / part[:, chans : chans + 1])
+            mixed = jnp.where(lane >= h * head_dim, scaled, mixed) if h else scaled
+        mixed = mixed.astype(jnp.bfloat16)
+        attn = jnp.dot(mixed, proj_ref[...], preferred_element_type=jnp.float32)
+        resid = tokens + attn.astype(jnp.bfloat16).astype(jnp.float32)
+        result = resid = resid.astype(jnp.bfloat16).astype(jnp.float32)
+        normed = layer_norm(resid, gain2).astype(jnp.bfloat16)
+        for first in range(0, fc1_ref.shape[1], 2 * LANES):
+            units_at = slice(first, first + 2 * LANES)
+            hidden = jnp.dot(normed, fc1_ref[:, units_at], preferred_element_type=jnp.float32)
+            hidden = gelu(hidden).astype(jnp.bfloat16)
+            result = result + lax.dot_general(
+                hidden, fc2_ref[:, units_at], NT, preferred_element_type=jnp.float32
+            )
         for part, lanes in enumerate((slice(0, LANES), slice(LANES, chans))):
             width = min(LANES, chans - part * LANES)
-            res_ref[n, part, 40:184, :width] = mine[:, lanes]
-            res_ref[n, part, 0:40, :width] = mine[104:144, lanes]
+            first = 40 + p * QUERIES
+            res_ref[n, part, first : first + QUERIES, :width] = result[:, lanes]
+            if p == 1:
+                res_ref[n, part, 0:40, :width] = result[QUERIES - 40 :, lanes]
+
+    for n, (_, window) in enumerate(units):
+        for p in range(2):
+            level_window(n, window, p)
+    for n in range(count):
         for row in range(WIN_LAT):
             for pair in range(HALF // 2):
                 tiles = []

time: 21.5 us -> 25.4 us (1.18)
  Pallas kernels: 10.7 us -> 14.9 us
  waiting for transfers between devices: 0.29 us -> 0.01 us
    pallas_call x3, Pallas kernels: 7.36 us -> 11.5 us  [run_units(): pl.pallas_call(functools.partial(units_kernel, chans, heads, units, bool(...]
    ppermute x2, waiting for transfers between devices: 0.29 us -> 0.01 us  [swapped(): return lax.ppermute(x, axis, pairs)]
  transfers between devices with their start and end apart: 4 -> 4, of which waited for: 1 -> 0; matrix products, arithmetic and copies ran while one was open for 0% -> 0% of each run, Pallas kernels for 37% -> 44%
where the time goes in v15:
time: 25.4 us; the launch traced here: 25.2 us
  Pallas kernels  14.9 us (59%)
  starting transfers between devices  9.34 us (37%)
  local copies, waits for them, and re-layouts  0.83 us (3%)
    pallas_call x3, Pallas kernels, run_units(): pl.pallas_call(functools.partial(units_kernel, chans, heads, units, bool(...  11.5 us
    ppermute x2, starting transfers between devices, swapped(): return lax.ppermute(x, axis, pairs)  4.78 us
    ppermute x2, starting transfers between devices, moved(): return lax.ppermute(x, axis, [(i, (i + by) % size) for i in range(size)])  4.56 us
    pallas_call x1, Pallas kernels, shards(): pl.pallas_call(functools.partial(table_kernel, len(weights)), out_shape=o...  2.59 us
    slice x1, local copies, waits for them, and re-layouts, shards(): south = moved(field[:EDGE], 'lat', -1)  0.83 us
    pallas_call x1, Pallas kernels, shards(): pl.pallas_call(last_kernel, out_shape=jax.ShapeDtypeStruct(field.shape, f...  0.74 us
  transfers between devices with their start and end apart: 4, of which 0 were waited for; matrix products, arithmetic and copies ran while one was open for 0% of the time, Pallas kernels for 44%

profile of v15, /device:TPU:0, one launch (start us, length us, event | category | flops | bytes accessed | tf_op | source)
XLA Modules:
  0.0 25.2 jit_solution(1023003197233715390)
XLA Ops:
  0.0 0.8 %slice.4 = bf16[3,4,2304]{2,1,0:T(4,128)(2,1)S(1)} slice(bf16[12,4,2304]{2,1,0:T(4,128)(2,1)} %bitcast.9), slice={[0:3], [0:4], [0:2304]} | slice | bytes 110592 | tf_op jit(solution)/shard_map/slice | solution.py:318
  0.8 3.0 %collective-permute-start = (bf16[3,4,2304]{2,1,0:T(4,128)(2,1)S(1)}, bf16[3,4,2304]{2,1,0:T(4,128)(2,1)S(1)}, u32[]{:S(2)}, u32[]{:S(2)}) collective-permute-start(bf16[3,4,2304]{2,1,0:T(4,128)(2,1)S(1)} %slice.4), channel_id=1, source_target_pairs={{0,1},{1,0},{2,3},{3,2},{4,5},{5,4},{6,7},{7,6},{8,9},{9,8},{10,11... | collective-permute-start | bytes 165896 | tf_op jit(solution)/shard_map/ppermute | solution.py:29
  3.8 2.6 %bias_tables.1 = (f32[2,2,2,2,432,128]{5,4,3,2,1,0:T(8,128)S(1)}, bf16[12,4,1152]{2,1,0:T(4,128)(2,1)S(1)}, bf16[12,4,1152]{2,1,0:T(4,128)(2,1)S(1)}, f32[1,192]...) custom-call(f32[2,6,162,2,128]{4,3,2,1,0:T(2,128)} %bitcast.8, ...), custom_call_target="tpu_custom_call" | custom-call | flops 4000000 | bytes 6000000 | tf_op jit(solution)/shard_map/bias_tables/pallas_call | solution.py:337
  6.4 0.0 collective-permute-done.south_ref
  6.5 0.1 collective-permute-start.2
  6.6 4.7 %collective-permute-start.1 = (bf16[12,4,1152]{2,1,0:T(4,128)(2,1)S(1)}, bf16[12,4,1152]{2,1,0:T(4,128)(2,1)S(1)}, u32[]{:S(2)}, u32[]{:S(2)}) collective-permute-start(bf16[12,4,1152]{2,1,0:T(4,128)(2,1)S(1)} %pack_half.2.rest_0_.refs_0_.refs_2_), channel_id=1, source_target_pairs={{2,4},{4,2},{6,8},{8,6},{10,12},{12,10},{14,16},{16,14},{18,20},{2... | collective-permute-start | bytes 331784 | tf_op jit(solution)/shard_map/ppermute | solution.py:38
  11.3 0.0 collective-permute-done.2.refs_1_
  11.3 3.1 %swin_windows.3.refs_9_.near_low_ref = bf16[1,6,4,1152]{3,2,1,0:T(4,128)(2,1)S(1)} custom-call(bf16[12,4,1152]{2,1,0:T(4,128)(2,1)S(1)} %pack_half.3.refs_0_, bf16[12,4,1152]{2,1,0:T(4,128)(2,1)S(1)} %collective-permute-done.2.refs_1_, f32[1,192]{1,0:T(1,128)S(1)} %get-tuple-element.17.refs_2_.refs_4_, ...), custom_call_target="tpu_custom_call" | custom-call | flops 200000000 | bytes 3000000 | tf_op jit(solution)/shard_map/swin_windows/pallas_call | solution.py:292
  14.4 0.0 collective-permute-done.1.refs_1_.refs_3_
  14.4 3.1 %swin_windows.4 = (bf16[1,6,4,1152]{3,2,1,0:T(4,128)(2,1)S(1)}, bf16[2,3,4,1152]{3,2,1,0:T(4,128)(2,1)S(1)}) custom-call(bf16[12,4,1152]{2,1,0:T(4,128)(2,1)S(1)} %pack_half.2.rest_0_.refs_0_.refs_2_, bf16[12,4,1152]{2,1,0:T(4,128)(2,1)S(1)} %collective-permute-done.1.refs_1_.refs_3_, f32[1,192]{1,0:T(1,128)S(1)} %get-tuple-element.17.refs_2_.refs_4_, ...), custom_call_target="tpu_custom_call" | custom-call | flops 200000000 | bytes 3000000 | tf_op jit(solution)/shard_map/swin_windows/pallas_call | solution.py:292
  17.5 1.6 %collective-permute-start.3 = (bf16[2,3,4,1152]{3,2,1,0:T(4,128)(2,1)S(1)}, bf16[2,3,4,1152]{3,2,1,0:T(4,128)(2,1)S(1)}, u32[]{:S(2)}, u32[]{:S(2)}) collective-permute-start(bf16[2,3,4,1152]{3,2,1,0:T(4,128)(2,1)S(1)} %get-tuple-element.25), channel_id=1, source_target_pairs={{0,1},{1,0},{2,3},{3,2},{4,5},{5,4},{6,7},{7,6},{8,9},{9,8},{10,11... | collective-permute-start | bytes 165896 | tf_op jit(solution)/shard_map/ppermute | solution.py:29
  19.0 5.4 %swin_windows.5.high_ref = bf16[2,6,4,1152]{3,2,1,0:T(4,128)(2,1)S(1)} custom-call(bf16[12,4,1152]{2,1,0:T(4,128)(2,1)S(1)} %pack_half.3.refs_0_, bf16[12,4,1152]{2,1,0:T(4,128)(2,1)S(1)} %collective-permute-done.2.refs_1_, bf16[12,4,1152]{2,1,0:T(4,128)(2,1)S(1)} %pack_half.2.rest_0_.refs_0_.refs_2_, ...), custom_call_target="tpu_custom_call" | custom-call | flops 400000000 | bytes 3000000 | tf_op jit(solution)/shard_map/swin_windows/pallas_call | solution.py:292
  24.4 0.0 collective-permute-done.3.top_ref
  24.4 0.7 %last_rows.1 = bf16[12,4,2304]{2,1,0:T(4,128)(2,1)} custom-call(bf16[2,3,4,1152]{3,2,1,0:T(4,128)(2,1)S(1)} %collective-permute-done.3.top_ref, bf16[2,6,4,1152]{3,2,1,0:T(4,128)(2,1)S(1)} %swin_windows.5.high_ref, bf16[1,6,4,1152]{3,2,1,0:T(4,128)(2,1)S(1)} %swin_windows.3.refs_9_.near_low_ref, bf16[1,6,4,1152]{3,2,1,0:T(4,128)(2,1)S(1)} %get-tuple-element.26.far_low_ref), custom_call_target="tpu_custom_call" | custom-call | bytes 400000 | tf_op jit(solution)/shard_map/last_rows/pallas_call | solution.py:373
  (2 shorter events, 0.0 us)
Async XLA Ops:
  0.8 5.6 %collective-permute-start = (bf16[3,4,2304]{2,1,0:T(4,128)(2,1)S(1)}, bf16[3,4,2304]{2,1,0:T(4,128)(2,1)S(1)}, u32[]{:S(2)}, u32[]{:S(2)}) collective-permute-start(bf16[3,4,2304]{2,1,0:T(4,128)(2,1)S(1)} %slice.4), channel_id=1, source_target_pairs={{0,1},{1,0},{2,3},{3,2},{4,5},{5,4},{6,7},{7,6},{8,9},{9,8},{10,11... | collective-permute-start | bytes 165896 | tf_op jit(solution)/shard_map/ppermute | solution.py:29
  6.5 4.8 %collective-permute-start.2 = (bf16[12,4,1152]{2,1,0:T(4,128)(2,1)S(1)}, bf16[12,4,1152]{2,1,0:T(4,128)(2,1)S(1)}, u32[]{:S(2)}, u32[]{:S(2)}) collective-permute-start(bf16[12,4,1152]{2,1,0:T(4,128)(2,1)S(1)} %pack_half.3.refs_0_), channel_id=1, source_target_pairs={{0,2},{2,0},{4,6},{6,4},{8,10},{10,8},{12,14},{14,12},{16,18},{18,... | collective-permute-start | bytes 331784 | tf_op jit(solution)/shard_map/ppermute | solution.py:38
  6.6 7.8 %collective-permute-start.1 = (bf16[12,4,1152]{2,1,0:T(4,128)(2,1)S(1)}, bf16[12,4,1152]{2,1,0:T(4,128)(2,1)S(1)}, u32[]{:S(2)}, u32[]{:S(2)}) collective-permute-start(bf16[12,4,1152]{2,1,0:T(4,128)(2,1)S(1)} %pack_half.2.rest_0_.refs_0_.refs_2_), channel_id=1, source_target_pairs={{2,4},{4,2},{6,8},{8,6},{10,12},{12,10},{14,16},{16,14},{18,20},{2... | collective-permute-start | bytes 331784 | tf_op jit(solution)/shard_map/ppermute | solution.py:38
  17.5 6.9 %collective-permute-start.3 = (bf16[2,3,4,1152]{3,2,1,0:T(4,128)(2,1)S(1)}, bf16[2,3,4,1152]{3,2,1,0:T(4,128)(2,1)S(1)}, u32[]{:S(2)}, u32[]{:S(2)}) collective-permute-start(bf16[2,3,4,1152]{3,2,1,0:T(4,128)(2,1)S(1)} %get-tuple-element.25), channel_id=1, source_target_pairs={{0,1},{1,0},{2,3},{3,2},{4,5},{5,4},{6,7},{7,6},{8,9},{9,8},{10,11... | collective-permute-start | bytes 165896 | tf_op jit(solution)/shard_map/ppermute | solution.py:29

commit v16 on v12

--- a/solution.py
+++ b/solution.py
@@ -207,8 +207,10 @@
     gain1 = gain1_ref[...]
     lane = lax.broadcasted_iota(jnp.int32, (1, chans), 1)
     ones = jnp.ones((TOKENS, 2 * LANES - chans), jnp.float32)
-    mixed = []
-    for n, (_, window) in enumerate(units):
+    scores, values, mixed = {}, {}, []
+    for n in range(count):
+        own = layer_norm(tokens_of(own_ref, n, 40, 144), gain1).astype(jnp.bfloat16)
+        query = jnp.dot(own, qkv_ref[:, :chans], preferred_element_type=jnp.float32)
         normed = []
         for p in range(2):
             levels = [(2 * p + 1 + lev) % LEVELS for lev in range(WIN_LEV)]
@@ -217,33 +219,36 @@
             normed.append(jnp.concatenate(parts, axis=0).astype(jnp.bfloat16))
         normed = jnp.concatenate(normed, axis=0)
         keys = jnp.dot(normed, qkv_ref[:, chans : 2 * chans], preferred_element_type=jnp.float32)
-        values = jnp.dot(normed, qkv_ref[:, 2 * chans :], preferred_element_type=jnp.float32)
-        own = layer_norm(tokens_of(own_ref, n, 40, 144), gain1).astype(jnp.bfloat16)
-        query = jnp.dot(own, qkv_ref[:, :chans], preferred_element_type=jnp.float32)
         query = query * (head_dim ** (-0.5) * LOG2E)
         for p in range(2):
             q = query[p * QUERIES : (p + 1) * QUERIES]
-            k = keys[p * TOKENS : (p + 1) * TOKENS].astype(jnp.bfloat16)
-            v = jnp.concatenate([values[p * TOKENS : (p + 1) * TOKENS], ones], axis=1)
-            v = v.astype(jnp.bfloat16)
             picked = [
                 jnp.where((lane >= h * head_dim) & (lane < (h + 1) * head_dim), q, 0.0)
                 for h in range(heads)
             ]
             picked = jnp.concatenate(picked, axis=0).astype(jnp.bfloat16)
-            scores = lax.dot_general(picked, k, NT, preferred_element_type=jnp.float32)
+            k = keys[p * TOKENS : (p + 1) * TOKENS].astype(jnp.bfloat16)
+            scores[n, p] = lax.dot_general(picked, k, NT, preferred_element_type=jnp.float32)
+        values[n] = jnp.dot(normed, qkv_ref[:, 2 * chans :], preferred_element_type=jnp.float32)
+    got = {}
+    for n, (_, window) in enumerate(units):
+        for p in range(2):
             probs = []
             for h in range(heads):
                 at = slice(h * QUERIES, (h + 1) * QUERIES)
                 bias = [table_ref[window, p, rights[n], part, at] for part in range(2)]
                 bias = jnp.concatenate([bias[0], bias[1][:, : TOKENS - LANES]], axis=1)
-                part = scores[at] + bias
+                part = scores[n, p][at] + bias
                 probs.append(jnp.exp2(part - jnp.max(part, axis=1, keepdims=True)))
             probs = jnp.concatenate(probs, axis=0).astype(jnp.bfloat16)
-            got = jnp.dot(probs, v, preferred_element_type=jnp.float32)
+            v = jnp.concatenate([values[n][p * TOKENS : (p + 1) * TOKENS], ones], axis=1)
+            v = v.astype(jnp.bfloat16)
+            got[n, p] = jnp.dot(probs, v, preferred_element_type=jnp.float32)
+    for n in range(count):
+        for p in range(2):
             out = None
             for h in range(heads):
-                part = got[h * QUERIES : (h + 1) * QUERIES]
+                part = got[n, p][h * QUERIES : (h + 1) * QUERIES]
                 scaled = part[:, :chans] * (1.0 / part[:, chans : chans + 1])
                 out = jnp.where(lane >= h * head_dim, scaled, out) if h else scaled
             mixed.append(out)
@@ -256,13 +261,19 @@
         resid.append(part.astype(jnp.bfloat16).astype(jnp.float32))
         normed.append(layer_norm(resid[n], gain2_ref[...]).astype(jnp.bfloat16))
     result, normed = jnp.concatenate(resid, axis=0), jnp.concatenate(normed, axis=0)
-    for first in range(0, fc1_ref.shape[1], 2 * LANES):
-        units_at = slice(first, first + 2 * LANES)
-        hidden = jnp.dot(normed, fc1_ref[:, units_at], preferred_element_type=jnp.float32)
-        hidden = gelu(hidden).astype(jnp.bfloat16)
+    blocks = [slice(f, f + 2 * LANES) for f in range(0, fc1_ref.shape[1], 2 * LANES)]
+
+    def first_product(at):
+        return jnp.dot(normed, fc1_ref[:, at], preferred_element_type=jnp.float32)
+
+    hidden = first_product(blocks[0])
+    for b, at in enumerate(blocks):
+        following = first_product(blocks[b + 1]) if b + 1 < len(blocks) else None
+        active = gelu(hidden).astype(jnp.bfloat16)
         result = result + lax.dot_general(
-            hidden, fc2_ref[:, units_at], NT, preferred_element_type=jnp.float32
+            active, fc2_ref[:, at], NT, preferred_element_type=jnp.float32
         )
+        hidden = following
     for n in range(count):
         mine = result[n * 144 : (n + 1) * 144]
         for part, lanes in enumerate((slice(0, LANES), slice(LANES, chans))):

time: 21.2 us -> 21.2 us (level)
  no operation moved by 1% of the time
where the time goes in v16:
time: 21.2 us; the launch traced here: 21 us
  Pallas kernels  10.4 us (49%)
  starting transfers between devices  9.34 us (44%)
  local copies, waits for them, and re-layouts  0.83 us (4%)
  waiting for transfers between devices  0.34 us (2%)
    pallas_call x3, Pallas kernels, run_units(): pl.pallas_call(functools.partial(units_kernel, chans, heads, units, bool(...  7.02 us
    ppermute x2, starting transfers between devices, swapped(): return lax.ppermute(x, axis, pairs)  4.78 us
    ppermute x2, starting transfers between devices, moved(): return lax.ppermute(x, axis, [(i, (i + by) % size) for i in range(size)])  4.56 us
    pallas_call x1, Pallas kernels, shards(): pl.pallas_call(functools.partial(table_kernel, len(weights)), out_shape=o...  2.59 us
    slice x1, local copies, waits for them, and re-layouts, shards(): south = moved(field[:EDGE], 'lat', -1)  0.83 us
    pallas_call x1, Pallas kernels, shards(): pl.pallas_call(last_kernel, out_shape=jax.ShapeDtypeStruct(field.shape, f...  0.74 us
  transfers between devices with their start and end apart: 4, of which 1 were waited for; matrix products, arithmetic and copies ran while one was open for 0% of the time, Pallas kernels for 36%

profile of v16, /device:TPU:0, one launch (start us, length us, event | category | flops | bytes accessed | tf_op | source)
XLA Modules:
  0.0 21.0 jit_solution(10239279678917852307)
XLA Ops:
  0.0 0.8 %slice.4 = bf16[3,4,2304]{2,1,0:T(4,128)(2,1)S(1)} slice(bf16[12,4,2304]{2,1,0:T(4,128)(2,1)} %bitcast.9), slice={[0:3], [0:4], [0:2304]} | slice | bytes 110592 | tf_op jit(solution)/shard_map/slice | solution.py:334
  0.8 3.0 %collective-permute-start = (bf16[3,4,2304]{2,1,0:T(4,128)(2,1)S(1)}, bf16[3,4,2304]{2,1,0:T(4,128)(2,1)S(1)}, u32[]{:S(2)}, u32[]{:S(2)}) collective-permute-start(bf16[3,4,2304]{2,1,0:T(4,128)(2,1)S(1)} %slice.4), channel_id=1, source_target_pairs={{0,1},{1,0},{2,3},{3,2},{4,5},{5,4},{6,7},{7,6},{8,9},{9,8},{10,11... | collective-permute-start | bytes 165896 | tf_op jit(solution)/shard_map/ppermute | solution.py:29
  3.8 2.6 %bias_tables.1 = (f32[2,2,2,2,432,128]{5,4,3,2,1,0:T(8,128)S(1)}, bf16[12,4,1152]{2,1,0:T(4,128)(2,1)S(1)}, bf16[12,4,1152]{2,1,0:T(4,128)(2,1)S(1)}, f32[1,192]...) custom-call(f32[2,6,162,2,128]{4,3,2,1,0:T(2,128)} %bitcast.8, ...), custom_call_target="tpu_custom_call" | custom-call | flops 4000000 | bytes 6000000 | tf_op jit(solution)/shard_map/bias_tables/pallas_call | solution.py:353
  6.4 0.0 collective-permute-done.south_ref
  6.5 0.1 collective-permute-start.2
  6.6 4.7 %collective-permute-start.1 = (bf16[12,4,1152]{2,1,0:T(4,128)(2,1)S(1)}, bf16[12,4,1152]{2,1,0:T(4,128)(2,1)S(1)}, u32[]{:S(2)}, u32[]{:S(2)}) collective-permute-start(bf16[12,4,1152]{2,1,0:T(4,128)(2,1)S(1)} %pack_half.2.rest_0_.refs_0_.refs_2_), channel_id=1, source_target_pairs={{2,4},{4,2},{6,8},{8,6},{10,12},{12,10},{14,16},{16,14},{18,20},{2... | collective-permute-start | bytes 331784 | tf_op jit(solution)/shard_map/ppermute | solution.py:38
  11.3 0.0 collective-permute-done.2.refs_1_
  11.3 2.1 %swin_windows.3.refs_9_.near_low_ref = bf16[1,6,4,1152]{3,2,1,0:T(4,128)(2,1)S(1)} custom-call(bf16[12,4,1152]{2,1,0:T(4,128)(2,1)S(1)} %pack_half.3.refs_0_, bf16[12,4,1152]{2,1,0:T(4,128)(2,1)S(1)} %collective-permute-done.2.refs_1_, f32[1,192]{1,0:T(1,128)S(1)} %get-tuple-element.17.refs_2_.refs_4_, ...), custom_call_target="tpu_custom_call" | custom-call | flops 200000000 | bytes 3000000 | tf_op jit(solution)/shard_map/swin_windows/pallas_call | solution.py:308
  13.4 0.3 %collective-permute-done.1.refs_1_.refs_3_ = bf16[12,4,1152]{2,1,0:T(4,128)(2,1)S(1)} collective-permute-done((bf16[12,4,1152]{2,1,0:T(4,128)(2,1)S(1)}, bf16[12,4,1152]{2,1,0:T(4,128)(2,1)S(1)}, u32[]{:S(2)}, u32[]{:S(2)}) %collective-permute-start.1) | collective-permute-done | bytes 110624 | tf_op jit(solution)/shard_map/ppermute | solution.py:38
  13.7 2.1 %swin_windows.4 = (bf16[1,6,4,1152]{3,2,1,0:T(4,128)(2,1)S(1)}, bf16[2,3,4,1152]{3,2,1,0:T(4,128)(2,1)S(1)}) custom-call(bf16[12,4,1152]{2,1,0:T(4,128)(2,1)S(1)} %pack_half.2.rest_0_.refs_0_.refs_2_, bf16[12,4,1152]{2,1,0:T(4,128)(2,1)S(1)} %collective-permute-done.1.refs_1_.refs_3_, f32[1,192]{1,0:T(1,128)S(1)} %get-tuple-element.17.refs_2_.refs_4_, ...), custom_call_target="tpu_custom_call" | custom-call | flops 200000000 | bytes 3000000 | tf_op jit(solution)/shard_map/swin_windows/pallas_call | solution.py:308
  15.8 1.6 %collective-permute-start.3 = (bf16[2,3,4,1152]{3,2,1,0:T(4,128)(2,1)S(1)}, bf16[2,3,4,1152]{3,2,1,0:T(4,128)(2,1)S(1)}, u32[]{:S(2)}, u32[]{:S(2)}) collective-permute-start(bf16[2,3,4,1152]{3,2,1,0:T(4,128)(2,1)S(1)} %get-tuple-element.25), channel_id=1, source_target_pairs={{0,1},{1,0},{2,3},{3,2},{4,5},{5,4},{6,7},{7,6},{8,9},{9,8},{10,11... | collective-permute-start | bytes 165896 | tf_op jit(solution)/shard_map/ppermute | solution.py:29
  17.4 2.8 %swin_windows.5.high_ref = bf16[2,6,4,1152]{3,2,1,0:T(4,128)(2,1)S(1)} custom-call(bf16[12,4,1152]{2,1,0:T(4,128)(2,1)S(1)} %pack_half.3.refs_0_, bf16[12,4,1152]{2,1,0:T(4,128)(2,1)S(1)} %collective-permute-done.2.refs_1_, bf16[12,4,1152]{2,1,0:T(4,128)(2,1)S(1)} %pack_half.2.rest_0_.refs_0_.refs_2_, ...), custom_call_target="tpu_custom_call" | custom-call | flops 400000000 | bytes 3000000 | tf_op jit(solution)/shard_map/swin_windows/pallas_call | solution.py:308
  20.2 0.0 collective-permute-done.3.top_ref
  20.2 0.7 %last_rows.1 = bf16[12,4,2304]{2,1,0:T(4,128)(2,1)} custom-call(bf16[2,3,4,1152]{3,2,1,0:T(4,128)(2,1)S(1)} %collective-permute-done.3.top_ref, bf16[2,6,4,1152]{3,2,1,0:T(4,128)(2,1)S(1)} %swin_windows.5.high_ref, bf16[1,6,4,1152]{3,2,1,0:T(4,128)(2,1)S(1)} %swin_windows.3.refs_9_.near_low_ref, bf16[1,6,4,1152]{3,2,1,0:T(4,128)(2,1)S(1)} %get-tuple-element.26.far_low_ref), custom_call_target="tpu_custom_call" | custom-call | bytes 400000 | tf_op jit(solution)/shard_map/last_rows/pallas_call | solution.py:389
  (2 shorter events, 0.0 us)
Async XLA Ops:
  0.8 5.6 %collective-permute-start = (bf16[3,4,2304]{2,1,0:T(4,128)(2,1)S(1)}, bf16[3,4,2304]{2,1,0:T(4,128)(2,1)S(1)}, u32[]{:S(2)}, u32[]{:S(2)}) collective-permute-start(bf16[3,4,2304]{2,1,0:T(4,128)(2,1)S(1)} %slice.4), channel_id=1, source_target_pairs={{0,1},{1,0},{2,3},{3,2},{4,5},{5,4},{6,7},{7,6},{8,9},{9,8},{10,11... | collective-permute-start | bytes 165896 | tf_op jit(solution)/shard_map/ppermute | solution.py:29
  6.5 4.8 %collective-permute-start.2 = (bf16[12,4,1152]{2,1,0:T(4,128)(2,1)S(1)}, bf16[12,4,1152]{2,1,0:T(4,128)(2,1)S(1)}, u32[]{:S(2)}, u32[]{:S(2)}) collective-permute-start(bf16[12,4,1152]{2,1,0:T(4,128)(2,1)S(1)} %pack_half.3.refs_0_), channel_id=1, source_target_pairs={{0,2},{2,0},{4,6},{6,4},{8,10},{10,8},{12,14},{14,12},{16,18},{18,... | collective-permute-start | bytes 331784 | tf_op jit(solution)/shard_map/ppermute | solution.py:38
  6.6 7.1 %collective-permute-start.1 = (bf16[12,4,1152]{2,1,0:T(4,128)(2,1)S(1)}, bf16[12,4,1152]{2,1,0:T(4,128)(2,1)S(1)}, u32[]{:S(2)}, u32[]{:S(2)}) collective-permute-start(bf16[12,4,1152]{2,1,0:T(4,128)(2,1)S(1)} %pack_half.2.rest_0_.refs_0_.refs_2_), channel_id=1, source_target_pairs={{2,4},{4,2},{6,8},{8,6},{10,12},{12,10},{14,16},{16,14},{18,20},{2... | collective-permute-start | bytes 331784 | tf_op jit(solution)/shard_map/ppermute | solution.py:38
  15.8 4.4 %collective-permute-start.3 = (bf16[2,3,4,1152]{3,2,1,0:T(4,128)(2,1)S(1)}, bf16[2,3,4,1152]{3,2,1,0:T(4,128)(2,1)S(1)}, u32[]{:S(2)}, u32[]{:S(2)}) collective-permute-start(bf16[2,3,4,1152]{3,2,1,0:T(4,128)(2,1)S(1)} %get-tuple-element.25), channel_id=1, source_target_pairs={{0,1},{1,0},{2,3},{3,2},{4,5},{5,4},{6,7},{7,6},{8,9},{9,8},{10,11... | collective-permute-start | bytes 165896 | tf_op jit(solution)/shard_map/ppermute | solution.py:29

commit v17 on v13

--- a/solution.py
+++ b/solution.py
@@ -43,12 +43,18 @@
     return pl.multiple_of((1 - odd) * half, LANES), pl.multiple_of(odd * half, LANES)
 
 
-def pack_kernel(which, south_ref, kept_ref, *rest):
-    piece_ref = rest[-1]
-    at = half_places(piece_ref.shape[2])[which]
-    rows = piece_ref.shape[0] - EDGE
-    piece_ref[:rows] = kept_ref[:rows]
-    piece_ref[rows:] = south_ref[:, :, pl.ds(at, piece_ref.shape[2])]
+def pack_far_kernel(south_ref, kept_ref, far_ref):
+    at = half_places(far_ref.shape[2])[1]
+    rows = far_ref.shape[0] - EDGE
+    far_ref[:rows] = kept_ref[:rows]
+    far_ref[rows:] = south_ref[:, :, pl.ds(at, far_ref.shape[2])]
+
+
+def pack_near_kernel(south_ref, kept_ref, _, low_ref, high_ref):
+    at = half_places(low_ref.shape[2])[0]
+    high_ref[...] = kept_ref[:WIN_LAT]
+    low_ref[:EDGE] = kept_ref[WIN_LAT : WIN_LAT + EDGE]
+    low_ref[EDGE:] = south_ref[:, :, pl.ds(at, low_ref.shape[2])]
 
 
 def last_kernel(top_ref, high_ref, near_low_ref, far_low_ref, out_ref, sems):
@@ -185,16 +191,17 @@
             middle, final = pltpu.roll(middle, SPARE, 1), pltpu.roll(final, SPARE, 1)
             yield 2 * pair + 1, (jnp.where(low, middle, final), final)
 
-    for n, (_, window) in enumerate(units):
+    for n, (near, window) in enumerate(units):
         own_piece, halo_piece = pieces[2 * n], pieces[2 * n + 1]
+        first = 0 if near else window * WIN_LAT
         halo_at = rights[n] * HALF
         own_at = HALF - halo_at
         for row in range(WIN_LAT):
-            for col, block in split(halo_piece, window * WIN_LAT + row):
+            for col, block in split(halo_piece, first + row):
                 at = pl.ds(row * WIN_LON + col + halo_at, LEVELS, stride=QUERIES)
                 for part in range(2):
                     keys_ref[n, part, at, :] = block[part]
-            for col, block in split(own_piece, window * WIN_LAT + row):
+            for col, block in split(own_piece, first + row):
                 at = pl.ds(row * WIN_LON + col + own_at, LEVELS, stride=QUERIES)
                 place = row * HALF + col
                 for part in range(2):
@@ -205,8 +212,10 @@
     gain1 = gain1_ref[...]
     lane = lax.broadcasted_iota(jnp.int32, (1, chans), 1)
     ones = jnp.ones((TOKENS, 2 * LANES - chans), jnp.float32)
-    mixed = []
-    for n, (_, window) in enumerate(units):
+    scores, values, mixed = {}, {}, []
+    for n in range(count):
+        own = layer_norm(tokens_of(own_ref, n, 40, 144), gain1).astype(jnp.bfloat16)
+        query = jnp.dot(own, qkv_ref[:, :chans], preferred_element_type=jnp.float32)
         normed = []
         for p in range(2):
             levels = [(2 * p + 1 + lev) % LEVELS for lev in range(WIN_LEV)]
@@ -215,33 +224,36 @@
             normed.append(jnp.concatenate(parts, axis=0).astype(jnp.bfloat16))
         normed = jnp.concatenate(normed, axis=0)
         keys = jnp.dot(normed, qkv_ref[:, chans : 2 * chans], preferred_element_type=jnp.float32)
-        values = jnp.dot(normed, qkv_ref[:, 2 * chans :], preferred_element_type=jnp.float32)
-        own = layer_norm(tokens_of(own_ref, n, 40, 144), gain1).astype(jnp.bfloat16)
-        query = jnp.dot(own, qkv_ref[:, :chans], preferred_element_type=jnp.float32)
         query = query * (head_dim ** (-0.5) * LOG2E)
         for p in range(2):
             q = query[p * QUERIES : (p + 1) * QUERIES]
-            k = keys[p * TOKENS : (p + 1) * TOKENS].astype(jnp.bfloat16)
-            v = jnp.concatenate([values[p * TOKENS : (p + 1) * TOKENS], ones], axis=1)
-            v = v.astype(jnp.bfloat16)
             picked = [
                 jnp.where((lane >= h * head_dim) & (lane < (h + 1) * head_dim), q, 0.0)
                 for h in range(heads)
             ]
             picked = jnp.concatenate(picked, axis=0).astype(jnp.bfloat16)
-            scores = lax.dot_general(picked, k, NT, preferred_element_type=jnp.float32)
+            k = keys[p * TOKENS : (p + 1) * TOKENS].astype(jnp.bfloat16)
+            scores[n, p] = lax.dot_general(picked, k, NT, preferred_element_type=jnp.float32)
+        values[n] = jnp.dot(normed, qkv_ref[:, 2 * chans :], preferred_element_type=jnp.float32)
+    got = {}
+    for n, (_, window) in enumerate(units):
+        for p in range(2):
             probs = []
             for h in range(heads):
                 at = slice(h * QUERIES, (h + 1) * QUERIES)
                 bias = [table_ref[p, rights[n], part, at] for part in range(2)]
                 bias = jnp.concatenate([bias[0], bias[1][:, : TOKENS - LANES]], axis=1)
-                part = scores[at] + bias
+                part = scores[n, p][at] + bias
                 probs.append(jnp.exp2(part - jnp.max(part, axis=1, keepdims=True)))
             probs = jnp.concatenate(probs, axis=0).astype(jnp.bfloat16)
-            got = jnp.dot(probs, v, preferred_element_type=jnp.float32)
+            v = jnp.concatenate([values[n][p * TOKENS : (p + 1) * TOKENS], ones], axis=1)
+            v = v.astype(jnp.bfloat16)
+            got[n, p] = jnp.dot(probs, v, preferred_element_type=jnp.float32)
+    for n in range(count):
+        for p in range(2):
             out = None
             for h in range(heads):
-                part = got[h * QUERIES : (h + 1) * QUERIES]
+                part = got[n, p][h * QUERIES : (h + 1) * QUERIES]
                 scaled = part[:, :chans] * (1.0 / part[:, chans : chans + 1])
                 out = jnp.where(lane >= h * head_dim, scaled, out) if h else scaled
             mixed.append(out)
@@ -254,13 +266,19 @@
         resid.append(part.astype(jnp.bfloat16).astype(jnp.float32))
         normed.append(layer_norm(resid[n], gain2_ref[...]).astype(jnp.bfloat16))
     result, normed = jnp.concatenate(resid, axis=0), jnp.concatenate(normed, axis=0)
-    for first in range(0, fc1_ref.shape[1], 2 * LANES):
-        units_at = slice(first, first + 2 * LANES)
-        hidden = jnp.dot(normed, fc1_ref[:, units_at], preferred_element_type=jnp.float32)
-        hidden = gelu(hidden).astype(jnp.bfloat16)
+    blocks = [slice(f, f + 2 * LANES) for f in range(0, fc1_ref.shape[1], 2 * LANES)]
+
+    def first_product(at):
+        return jnp.dot(normed, fc1_ref[:, at], preferred_element_type=jnp.float32)
+
+    hidden = first_product(blocks[0])
+    for b, at in enumerate(blocks):
+        following = first_product(blocks[b + 1]) if b + 1 < len(blocks) else None
+        active = gelu(hidden).astype(jnp.bfloat16)
         result = result + lax.dot_general(
-            hidden, fc2_ref[:, units_at], NT, preferred_element_type=jnp.float32
+            active, fc2_ref[:, at], NT, preferred_element_type=jnp.float32
         )
+        hidden = following
     for n in range(count):
         mine = result[n * 144 : (n + 1) * 144]
         for part, lanes in enumerate((slice(0, LANES), slice(LANES, chans))):
@@ -285,7 +303,7 @@
 
 def run_units(units, near, far, weights, chans, heads, table, extra=None, extra_in=None):
     count = len(units)
-    pieces = [x for is_near, _ in units for x in (near if is_near else far)]
+    pieces = [x for is_near, w in units for x in (near[w] if is_near else far)]
     piece = pieces[0]
     outs = [jax.ShapeDtypeStruct((count, WIN_LAT) + piece.shape[1:], piece.dtype)]
     operands = (*pieces, *weights, table)
@@ -356,22 +374,23 @@
         name="bias_tables",
     )(*sources)
 
-    def pack(which, kept, *after):
+    def pack(kernel, outs, *operands):
         return pl.pallas_call(
-            functools.partial(pack_kernel, which),
-            out_shape=piece,
-            in_specs=[vmem] * 2 + [anywhere] * len(after),
-            out_specs=vmem,
+            kernel,
+            out_shape=outs,
+            in_specs=[vmem] * 2 + [anywhere] * (len(operands) - 2),
+            out_specs=[vmem] * len(outs),
             compiler_params=pltpu.CompilerParams(vmem_limit_bytes=VMEM_BYTES),
             cost_estimate=pl.CostEstimate(flops=0, bytes_accessed=250_000, transcendentals=0),
             name="pack_half",
-        )(south, kept, *after)
-
-    far = pack(1, far)
-    near = pack(0, near, far)
+        )(*operands)
+
+    (far,) = pack(pack_far_kernel, [piece], south, far)
     far_halo = swapped(far, "lon", 1)
-    near_halo = swapped(near, "lon", 0)
-    near, far = (near, near_halo), (far, far_halo)
+    window = jax.ShapeDtypeStruct((WIN_LAT, levels, half), field.dtype)
+    near_parts = pack(pack_near_kernel, [window, window], south, near, far)
+    low, high = ((part, swapped(part, "lon", 0)) for part in near_parts)
+    near, far = (high, low), (far, far_halo)
     common = (near, far, weights, chans, heads)
     near_low, inner = run_units(((True, 1),), *common, table, "tables", inner)
     far_low, send = run_units(((False, 1),), *common, table, "send", near_low)

time: 21.2 us -> 20.9 us (0.986)
  starting transfers between devices: 9.82 us -> 9.13 us
  waiting for transfers between devices: 0.4 us -> 0.92 us
    ppermute x2 -> x3, starting transfers between devices: 5.26 us -> 4.18 us  [swapped(): return lax.ppermute(x, axis, pairs)]
    ppermute x2 -> x3, waiting for transfers between devices: 0.22 us -> 0.73 us  [swapped(): return lax.ppermute(x, axis, pairs)]
    ppermute x2, starting transfers between devices: 4.56 us -> 4.95 us  [moved(): return lax.ppermute(x, axis, [(i, (i + by) % size) for i in range(size)])]
  transfers between devices with their start and end apart: 4 -> 5, of which waited for: 2 -> 2; matrix products, arithmetic and copies ran while one was open for 0% -> 0% of each run, Pallas kernels for 33% -> 44%
where the time goes in v17:
time: 20.9 us; the launch traced here: 20.7 us
  Pallas kernels  9.77 us (47%)
  starting transfers between devices  9.13 us (44%)
  waiting for transfers between devices  0.92 us (4%)
  local copies, waits for them, and re-layouts  0.83 us (4%)
    pallas_call x3, Pallas kernels, run_units(): pl.pallas_call(functools.partial(units_kernel, chans, heads, units, extra...  7.05 us
    ppermute x2, starting transfers between devices, moved(): return lax.ppermute(x, axis, [(i, (i + by) % size) for i in range(size)])  4.95 us
    ppermute x3, starting transfers between devices, swapped(): return lax.ppermute(x, axis, pairs)  4.18 us
    pallas_call x1, Pallas kernels, shards(): pl.pallas_call(functools.partial(table_kernel, len(weights), heads), out_...  1.95 us
    slice x1, local copies, waits for them, and re-layouts, shards(): south = moved(field[:EDGE], 'lat', -1)  0.83 us
    pallas_call x1, Pallas kernels, shards(): pl.pallas_call(last_kernel, out_shape=jax.ShapeDtypeStruct(field.shape, f...  0.74 us
    ppermute x3, waiting for transfers between devices, swapped(): return lax.ppermute(x, axis, pairs)  0.73 us
  transfers between devices with their start and end apart: 5, of which 2 were waited for; matrix products, arithmetic and copies ran while one was open for 0% of the time, Pallas kernels for 44%

profile of v17, /device:TPU:0, one launch (start us, length us, event | category | flops | bytes accessed | tf_op | source)
XLA Modules:
  0.0 20.7 jit_solution(5967573267701632391)
XLA Ops:
  0.0 0.8 %slice.4 = bf16[3,4,2304]{2,1,0:T(4,128)(2,1)S(1)} slice(bf16[12,4,2304]{2,1,0:T(4,128)(2,1)} %bitcast.9), slice={[0:3], [0:4], [0:2304]} | slice | bytes 110592 | tf_op jit(solution)/shard_map/slice | solution.py:343
  0.8 3.0 %collective-permute-start = (bf16[3,4,2304]{2,1,0:T(4,128)(2,1)S(1)}, bf16[3,4,2304]{2,1,0:T(4,128)(2,1)S(1)}, u32[]{:S(2)}, u32[]{:S(2)}) collective-permute-start(bf16[3,4,2304]{2,1,0:T(4,128)(2,1)S(1)} %slice.4), channel_id=1, source_target_pairs={{0,1},{1,0},{2,3},{3,2},{4,5},{5,4},{6,7},{7,6},{8,9},{9,8},{10,11... | collective-permute-start | bytes 165896 | tf_op jit(solution)/shard_map/ppermute | solution.py:29
  3.8 1.9 %bias_tables.1 = (f32[2,2,2,432,128]{4,3,2,1,0:T(8,128)S(1)}, f32[1944,128]{1,0:T(8,128)S(1)}, bf16[12,4,1152]{2,1,0:T(4,128)(2,1)S(1)}, bf16[12,4,1152]{2,1,0:T...) custom-call(f32[2,6,162,2,128]{4,3,2,1,0:T(2,128)} %bitcast.8, ...), custom_call_target="tpu_custom_call" | custom-call | flops 4000000 | bytes 6000000 | tf_op jit(solution)/shard_map/bias_tables/pallas_call | solution.py:363
  5.8 0.2 collective-permute-done.south_ref
  6.0 3.6 %collective-permute-start.1 = (bf16[12,4,1152]{2,1,0:T(4,128)(2,1)S(1)}, bf16[12,4,1152]{2,1,0:T(4,128)(2,1)S(1)}, u32[]{:S(2)}, u32[]{:S(2)}) collective-permute-start(bf16[12,4,1152]{2,1,0:T(4,128)(2,1)S(1)} %pack_half.2._.refs_0_.refs_2_), channel_id=1, source_target_pairs={{2,4},{4,2},{6,8},{8,6},{10,12},{12,10},{14,16},{16,14},{18,20},{2... | collective-permute-start | bytes 331784 | tf_op jit(solution)/shard_map/ppermute | solution.py:38
  9.6 0.1 collective-permute-start.2
  9.7 0.5 %collective-permute-start.4 = (bf16[6,4,1152]{2,1,0:T(4,128)(2,1)S(1)}, bf16[6,4,1152]{2,1,0:T(4,128)(2,1)S(1)}, u32[]{:S(2)}, u32[]{:S(2)}) collective-permute-start(bf16[6,4,1152]{2,1,0:T(4,128)(2,1)S(1)} %get-tuple-element.34.refs_0_), channel_id=1, source_target_pairs={{0,2},{2,0},{4,6},{6,4},{8,10},{10,8},{12,14},{14,12},{16,18},{18,... | collective-permute-start | bytes 165896 | tf_op jit(solution)/shard_map/ppermute | solution.py:38
  10.2 0.7 %collective-permute-done.2.refs_1_ = bf16[6,4,1152]{2,1,0:T(4,128)(2,1)S(1)} collective-permute-done((bf16[6,4,1152]{2,1,0:T(4,128)(2,1)S(1)}, bf16[6,4,1152]{2,1,0:T(4,128)(2,1)S(1)}, u32[]{:S(2)}, u32[]{:S(2)}) %collective-permute-start.2) | collective-permute-done | bytes 55328 | tf_op jit(solution)/shard_map/ppermute | solution.py:38
  10.9 2.1 %swin_windows.3 = (bf16[1,6,4,1152]{3,2,1,0:T(4,128)(2,1)S(1)}, f32[2,2,2,432,128]{4,3,2,1,0:T(8,128)S(1)}) custom-call(bf16[6,4,1152]{2,1,0:T(4,128)(2,1)S(1)} %get-tuple-element.30.refs_0_, bf16[6,4,1152]{2,1,0:T(4,128)(2,1)S(1)} %collective-permute-done.2.refs_1_, f32[1,192]{1,0:T(1,128)S(1)} %get-tuple-element.22.refs_2_.refs_4_, ...), custom_call_target="tpu_custom_call" | custom-call | flops 200000000 | bytes 3000000 | tf_op jit(solution)/shard_map/swin_windows/pallas_call | solution.py:317
  13.1 0.0 collective-permute-done.1.refs_1_.refs_3_
  13.1 2.1 %swin_windows.4 = (bf16[1,6,4,1152]{3,2,1,0:T(4,128)(2,1)S(1)}, bf16[2,3,4,1152]{3,2,1,0:T(4,128)(2,1)S(1)}) custom-call(bf16[12,4,1152]{2,1,0:T(4,128)(2,1)S(1)} %pack_half.2._.refs_0_.refs_2_, bf16[12,4,1152]{2,1,0:T(4,128)(2,1)S(1)} %collective-permute-done.1.refs_1_.refs_3_, f32[1,192]{1,0:T(1,128)S(1)} %get-tuple-element.22.refs_2_.refs_4_, ...), custom_call_target="tpu_custom_call" | custom-call | flops 200000000 | bytes 3000000 | tf_op jit(solution)/shard_map/swin_windows/pallas_call | solution.py:317
  15.2 1.9 %collective-permute-start.3 = (bf16[2,3,4,1152]{3,2,1,0:T(4,128)(2,1)S(1)}, bf16[2,3,4,1152]{3,2,1,0:T(4,128)(2,1)S(1)}, u32[]{:S(2)}, u32[]{:S(2)}) collective-permute-start(bf16[2,3,4,1152]{3,2,1,0:T(4,128)(2,1)S(1)} %get-tuple-element.33), channel_id=1, source_target_pairs={{0,1},{1,0},{2,3},{3,2},{4,5},{5,4},{6,7},{7,6},{8,9},{9,8},{10,11... | collective-permute-start | bytes 165896 | tf_op jit(solution)/shard_map/ppermute | solution.py:29
  17.1 0.0 collective-permute-done.4.refs_1_
  17.1 2.8 %swin_windows.5.high_ref = bf16[2,6,4,1152]{3,2,1,0:T(4,128)(2,1)S(1)} custom-call(bf16[6,4,1152]{2,1,0:T(4,128)(2,1)S(1)} %get-tuple-element.34.refs_0_, bf16[6,4,1152]{2,1,0:T(4,128)(2,1)S(1)} %collective-permute-done.4.refs_1_, bf16[12,4,1152]{2,1,0:T(4,128)(2,1)S(1)} %pack_half.2._.refs_0_.refs_2_, ...), custom_call_target="tpu_custom_call" | custom-call | flops 400000000 | bytes 3000000 | tf_op jit(solution)/shard_map/swin_windows/pallas_call | solution.py:317
  20.0 0.0 collective-permute-done.3.top_ref
  20.0 0.7 %last_rows.1 = bf16[12,4,2304]{2,1,0:T(4,128)(2,1)} custom-call(bf16[2,3,4,1152]{3,2,1,0:T(4,128)(2,1)S(1)} %collective-permute-done.3.top_ref, bf16[2,6,4,1152]{3,2,1,0:T(4,128)(2,1)S(1)} %swin_windows.5.high_ref, bf16[1,6,4,1152]{3,2,1,0:T(4,128)(2,1)S(1)} %get-tuple-element.32.refs_9_.near_low_ref, bf16[1,6,4,1152]{3,2,1,0:T(4,128)(2,1)S(1)} %get-tuple-element.36.far_low_ref), custom_call_target="tpu_custom_call" | custom-call | bytes 400000 | tf_op jit(solution)/shard_map/last_rows/pallas_call | solution.py:399
  (2 shorter events, 0.0 us)
Async XLA Ops:
  0.8 5.1 %collective-permute-start = (bf16[3,4,2304]{2,1,0:T(4,128)(2,1)S(1)}, bf16[3,4,2304]{2,1,0:T(4,128)(2,1)S(1)}, u32[]{:S(2)}, u32[]{:S(2)}) collective-permute-start(bf16[3,4,2304]{2,1,0:T(4,128)(2,1)S(1)} %slice.4), channel_id=1, source_target_pairs={{0,1},{1,0},{2,3},{3,2},{4,5},{5,4},{6,7},{7,6},{8,9},{9,8},{10,11... | collective-permute-start | bytes 165896 | tf_op jit(solution)/shard_map/ppermute | solution.py:29
  6.0 7.1 %collective-permute-start.1 = (bf16[12,4,1152]{2,1,0:T(4,128)(2,1)S(1)}, bf16[12,4,1152]{2,1,0:T(4,128)(2,1)S(1)}, u32[]{:S(2)}, u32[]{:S(2)}) collective-permute-start(bf16[12,4,1152]{2,1,0:T(4,128)(2,1)S(1)} %pack_half.2._.refs_0_.refs_2_), channel_id=1, source_target_pairs={{2,4},{4,2},{6,8},{8,6},{10,12},{12,10},{14,16},{16,14},{18,20},{2... | collective-permute-start | bytes 331784 | tf_op jit(solution)/shard_map/ppermute | solution.py:38
  9.6 1.3 %collective-permute-start.2 = (bf16[6,4,1152]{2,1,0:T(4,128)(2,1)S(1)}, bf16[6,4,1152]{2,1,0:T(4,128)(2,1)S(1)}, u32[]{:S(2)}, u32[]{:S(2)}) collective-permute-start(bf16[6,4,1152]{2,1,0:T(4,128)(2,1)S(1)} %get-tuple-element.30.refs_0_), channel_id=1, source_target_pairs={{0,2},{2,0},{4,6},{6,4},{8,10},{10,8},{12,14},{14,12},{16,18},{18,... | collective-permute-start | bytes 165896 | tf_op jit(solution)/shard_map/ppermute | solution.py:38
  9.7 7.4 %collective-permute-start.4 = (bf16[6,4,1152]{2,1,0:T(4,128)(2,1)S(1)}, bf16[6,4,1152]{2,1,0:T(4,128)(2,1)S(1)}, u32[]{:S(2)}, u32[]{:S(2)}) collective-permute-start(bf16[6,4,1152]{2,1,0:T(4,128)(2,1)S(1)} %get-tuple-element.34.refs_0_), channel_id=1, source_target_pairs={{0,2},{2,0},{4,6},{6,4},{8,10},{10,8},{12,14},{14,12},{16,18},{18,... | collective-permute-start | bytes 165896 | tf_op jit(solution)/shard_map/ppermute | solution.py:38
  15.2 4.8 %collective-permute-start.3 = (bf16[2,3,4,1152]{3,2,1,0:T(4,128)(2,1)S(1)}, bf16[2,3,4,1152]{3,2,1,0:T(4,128)(2,1)S(1)}, u32[]{:S(2)}, u32[]{:S(2)}) collective-permute-start(bf16[2,3,4,1152]{3,2,1,0:T(4,128)(2,1)S(1)} %get-tuple-element.33), channel_id=1, source_target_pairs={{0,1},{1,0},{2,3},{3,2},{4,5},{5,4},{6,7},{7,6},{8,9},{9,8},{10,11... | collective-permute-start | bytes 165896 | tf_op jit(solution)/shard_map/ppermute | solution.py:29

commit v18 on v17

--- a/solution.py
+++ b/solution.py
@@ -168,12 +168,14 @@
     count = len(units)
     pieces, refs = refs[: 2 * count], refs[2 * count :]
     gain1_ref, qkv_ref, proj_ref, gain2_ref, fc1_ref, fc2_ref, table_ref, *refs = refs
-    if extra:
-        extra_ref, out_ref, extra_out, keys_ref, own_ref, res_ref = refs
+    *refs, keys_ref, own_ref, res_ref = refs
+    if extra == "ahead":
+        raw_ref, far_ref, out_ref, inner_ref, far_keys, far_own, far_picked = refs
+        build_tables(raw_ref, inner_ref, heads, False)
+    elif extra == "send":
+        far_keys, far_own, far_picked, lower_ref, out_ref, send_ref = refs
     else:
-        out_ref, keys_ref, own_ref, res_ref = refs
-    if extra == "tables":
-        build_tables(extra_ref, extra_out, heads, False)
+        (out_ref,) = refs
     head_dim = chans // heads
     low = lax.broadcasted_iota(jnp.int32, (1, LANES), 1) < SPARE
     odd = lax.rem(lax.axis_index("lon"), 2)
@@ -191,31 +193,52 @@
             middle, final = pltpu.roll(middle, SPARE, 1), pltpu.roll(final, SPARE, 1)
             yield 2 * pair + 1, (jnp.where(low, middle, final), final)
 
+    def place_keys(n, ref, first, column, into):
+        for row in range(WIN_LAT):
+            for col, block in split(ref, first + row):
+                at = pl.ds(row * WIN_LON + col + column, LEVELS, stride=QUERIES)
+                for part in range(2):
+                    into[n, part, at, :] = block[part]
+
+    def place_own(n, ref, first, column, into, own_into):
+        for row in range(WIN_LAT):
+            for col, block in split(ref, first + row):
+                at = pl.ds(row * WIN_LON + col + column, LEVELS, stride=QUERIES)
+                place = row * HALF + col
+                for part in range(2):
+                    into[n, part, at, :] = block[part]
+                    own_into[n, part, pl.ds(4 + place, LEVELS, stride=36), :] = block[part]
+                    own_into[n, part, pl.ds(148 + place, 1), :] = block[part][:1]
+
+    def queries(n, own_from):
+        own = layer_norm(tokens_of(own_from, n, 40, 144), gain1).astype(jnp.bfloat16)
+        query = jnp.dot(own, qkv_ref[:, :chans], preferred_element_type=jnp.float32)
+        query = query * (head_dim ** (-0.5) * LOG2E)
+        picked = []
+        for p in range(2):
+            q = query[p * QUERIES : (p + 1) * QUERIES]
+            picked += [
+                jnp.where((lane >= h * head_dim) & (lane < (h + 1) * head_dim), q, 0.0)
+                for h in range(heads)
+            ]
+        return jnp.concatenate(picked, axis=0).astype(jnp.bfloat16)
+
+    if extra == "send":
+        keys_ref[...] = far_keys[...]
+        own_ref = far_own
     for n, (near, window) in enumerate(units):
         own_piece, halo_piece = pieces[2 * n], pieces[2 * n + 1]
         first = 0 if near else window * WIN_LAT
-        halo_at = rights[n] * HALF
-        own_at = HALF - halo_at
-        for row in range(WIN_LAT):
-            for col, block in split(halo_piece, first + row):
-                at = pl.ds(row * WIN_LON + col + halo_at, LEVELS, stride=QUERIES)
-                for part in range(2):
-                    keys_ref[n, part, at, :] = block[part]
-            for col, block in split(own_piece, first + row):
-                at = pl.ds(row * WIN_LON + col + own_at, LEVELS, stride=QUERIES)
-                place = row * HALF + col
-                for part in range(2):
-                    keys_ref[n, part, at, :] = block[part]
-                    own_ref[n, part, pl.ds(4 + place, LEVELS, stride=36), :] = block[part]
-                    own_ref[n, part, pl.ds(148 + place, 1), :] = block[part][:1]
+        if extra != "send":
+            place_own(n, own_piece, first, HALF - rights[n] * HALF, keys_ref, own_ref)
+        place_keys(n, halo_piece, first, rights[n] * HALF, keys_ref)
 
     gain1 = gain1_ref[...]
     lane = lax.broadcasted_iota(jnp.int32, (1, chans), 1)
     ones = jnp.ones((TOKENS, 2 * LANES - chans), jnp.float32)
     scores, values, mixed = {}, {}, []
     for n in range(count):
-        own = layer_norm(tokens_of(own_ref, n, 40, 144), gain1).astype(jnp.bfloat16)
-        query = jnp.dot(own, qkv_ref[:, :chans], preferred_element_type=jnp.float32)
+        picked = far_picked[...] if extra == "send" else queries(n, own_ref)
         normed = []
         for p in range(2):
             levels = [(2 * p + 1 + lev) % LEVELS for lev in range(WIN_LEV)]
@@ -224,17 +247,16 @@
             normed.append(jnp.concatenate(parts, axis=0).astype(jnp.bfloat16))
         normed = jnp.concatenate(normed, axis=0)
         keys = jnp.dot(normed, qkv_ref[:, chans : 2 * chans], preferred_element_type=jnp.float32)
-        query = query * (head_dim ** (-0.5) * LOG2E)
-        for p in range(2):
-            q = query[p * QUERIES : (p + 1) * QUERIES]
-            picked = [
-                jnp.where((lane >= h * head_dim) & (lane < (h + 1) * head_dim), q, 0.0)
-                for h in range(heads)
-            ]
-            picked = jnp.concatenate(picked, axis=0).astype(jnp.bfloat16)
+        rows = heads * QUERIES
+        for p in range(2):
             k = keys[p * TOKENS : (p + 1) * TOKENS].astype(jnp.bfloat16)
-            scores[n, p] = lax.dot_general(picked, k, NT, preferred_element_type=jnp.float32)
+            scores[n, p] = lax.dot_general(
+                picked[p * rows : (p + 1) * rows], k, NT, preferred_element_type=jnp.float32
+            )
         values[n] = jnp.dot(normed, qkv_ref[:, 2 * chans :], preferred_element_type=jnp.float32)
+    if extra == "ahead":
+        place_own(0, far_ref, WIN_LAT, HALF - odd * HALF, far_keys, far_own)
+        far_picked[...] = queries(0, far_own)
     got = {}
     for n, (_, window) in enumerate(units):
         for p in range(2):
@@ -297,22 +319,25 @@
                 tiles = jnp.concatenate(tiles, axis=1).astype(jnp.bfloat16)
                 out_ref[n, row, :, pair * 2 * chans : (pair + 1) * 2 * chans] = tiles
     if extra == "send":
-        extra_out[0] = extra_ref[0, EDGE:]
-        extra_out[1] = out_ref[0, EDGE:]
-
-
-def run_units(units, near, far, weights, chans, heads, table, extra=None, extra_in=None):
+        send_ref[0] = lower_ref[0, EDGE:]
+        send_ref[1] = out_ref[0, EDGE:]
+
+
+def run_units(units, near, far, weights, chans, heads, table, extra=None, *extra_in):
     count = len(units)
     pieces = [x for is_near, w in units for x in (near[w] if is_near else far)]
     piece = pieces[0]
     outs = [jax.ShapeDtypeStruct((count, WIN_LAT) + piece.shape[1:], piece.dtype)]
-    operands = (*pieces, *weights, table)
+    operands = (*pieces, *weights, table, *extra_in)
     if extra == "send":
         outs.append(jax.ShapeDtypeStruct((2, EDGE) + piece.shape[1:], piece.dtype))
-    elif extra == "tables":
-        outs.append(jax.ShapeDtypeStruct(table.shape, table.dtype))
-    if extra:
-        operands += (extra_in,)
+    elif extra == "ahead":
+        outs += [
+            jax.ShapeDtypeStruct(table.shape, table.dtype),
+            jax.ShapeDtypeStruct((1, 2, LEVELS * QUERIES, LANES), jnp.float32),
+            jax.ShapeDtypeStruct((1, 2, 184, LANES), jnp.float32),
+            jax.ShapeDtypeStruct((2 * heads * QUERIES, chans), jnp.bfloat16),
+        ]
     vmem = pl.BlockSpec(memory_space=pltpu.VMEM)
     return pl.pallas_call(
         functools.partial(units_kernel, chans, heads, units, extra),
@@ -392,8 +417,10 @@
     low, high = ((part, swapped(part, "lon", 0)) for part in near_parts)
     near, far = (high, low), (far, far_halo)
     common = (near, far, weights, chans, heads)
-    near_low, inner = run_units(((True, 1),), *common, table, "tables", inner)
-    far_low, send = run_units(((False, 1),), *common, table, "send", near_low)
+    near_low, inner, *ahead = run_units(
+        ((True, 1),), *common, table, "ahead", inner, far[0]
+    )
+    far_low, send = run_units(((False, 1),), *common, table, "send", *ahead, near_low)
     top = moved(send, "lat", 1)
     (high,) = run_units(((True, 0), (False, 0)), *common, inner)
     done = pl.pallas_call(

time: 20.9 us -> 20.7 us (level)
  transfers between devices with their start and end apart: 5 -> 5, of which waited for: 2 -> 2; matrix products, arithmetic and copies ran while one was open for 0% -> 0% of each run, Pallas kernels for 44% -> 43%
where the time goes in v18:
time: 20.7 us; the launch traced here: 20.5 us
  Pallas kernels  9.66 us (47%)
  starting transfers between devices  9.05 us (44%)
  waiting for transfers between devices  0.92 us (4%)
  local copies, waits for them, and re-layouts  0.83 us (4%)
    pallas_call x3, Pallas kernels, run_units(): pl.pallas_call(functools.partial(units_kernel, chans, heads, units, extra...  6.95 us
    ppermute x2, starting transfers between devices, moved(): return lax.ppermute(x, axis, [(i, (i + by) % size) for i in range(size)])  4.86 us
    ppermute x3, starting transfers between devices, swapped(): return lax.ppermute(x, axis, pairs)  4.18 us
    pallas_call x1, Pallas kernels, shards(): pl.pallas_call(functools.partial(table_kernel, len(weights), heads), out_...  1.95 us
    slice x1, local copies, waits for them, and re-layouts, shards(): south = moved(field[:EDGE], 'lat', -1)  0.83 us
    pallas_call x1, Pallas kernels, shards(): pl.pallas_call(last_kernel, out_shape=jax.ShapeDtypeStruct(field.shape, f...  0.74 us
    ppermute x3, waiting for transfers between devices, swapped(): return lax.ppermute(x, axis, pairs)  0.73 us
  transfers between devices with their start and end apart: 5, of which 2 were waited for; matrix products, arithmetic and copies ran while one was open for 0% of the time, Pallas kernels for 43%

profile of v18, /device:TPU:0, one launch (start us, length us, event | category | flops | bytes accessed | tf_op | source)
XLA Modules:
  0.0 20.5 jit_solution(6906498688797264016)
XLA Ops:
  0.0 0.8 %slice.4 = bf16[3,4,2304]{2,1,0:T(4,128)(2,1)S(1)} slice(bf16[12,4,2304]{2,1,0:T(4,128)(2,1)} %bitcast.9), slice={[0:3], [0:4], [0:2304]} | slice | bytes 110592 | tf_op jit(solution)/shard_map/slice | solution.py:368
  0.8 3.0 %collective-permute-start = (bf16[3,4,2304]{2,1,0:T(4,128)(2,1)S(1)}, bf16[3,4,2304]{2,1,0:T(4,128)(2,1)S(1)}, u32[]{:S(2)}, u32[]{:S(2)}) collective-permute-start(bf16[3,4,2304]{2,1,0:T(4,128)(2,1)S(1)} %slice.4), channel_id=1, source_target_pairs={{0,1},{1,0},{2,3},{3,2},{4,5},{5,4},{6,7},{7,6},{8,9},{9,8},{10,11... | collective-permute-start | bytes 165896 | tf_op jit(solution)/shard_map/ppermute | solution.py:29
  3.8 1.9 %bias_tables.1 = (f32[2,2,2,432,128]{4,3,2,1,0:T(8,128)S(1)}, f32[1944,128]{1,0:T(8,128)S(1)}, bf16[12,4,1152]{2,1,0:T(4,128)(2,1)S(1)}, bf16[12,4,1152]{2,1,0:T...) custom-call(f32[2,6,162,2,128]{4,3,2,1,0:T(2,128)} %bitcast.8, ...), custom_call_target="tpu_custom_call" | custom-call | flops 4000000 | bytes 6000000 | tf_op jit(solution)/shard_map/bias_tables/pallas_call | solution.py:388
  5.8 0.2 collective-permute-done.south_ref
  6.0 3.6 %collective-permute-start.1 = (bf16[12,4,1152]{2,1,0:T(4,128)(2,1)S(1)}, bf16[12,4,1152]{2,1,0:T(4,128)(2,1)S(1)}, u32[]{:S(2)}, u32[]{:S(2)}) collective-permute-start(bf16[12,4,1152]{2,1,0:T(4,128)(2,1)S(1)} %pack_half.2._.refs_10_.refs_0_.refs_2_), channel_id=1, source_target_pairs={{2,4},{4,2},{6,8},{8,6},{10,12},{12,10},{14,16},{16,14},{18,20},{2... | collective-permute-start | bytes 331784 | tf_op jit(solution)/shard_map/ppermute | solution.py:38
  9.6 0.1 collective-permute-start.2
  9.7 0.5 %collective-permute-start.4 = (bf16[6,4,1152]{2,1,0:T(4,128)(2,1)S(1)}, bf16[6,4,1152]{2,1,0:T(4,128)(2,1)S(1)}, u32[]{:S(2)}, u32[]{:S(2)}) collective-permute-start(bf16[6,4,1152]{2,1,0:T(4,128)(2,1)S(1)} %get-tuple-element.40.refs_0_), channel_id=1, source_target_pairs={{0,2},{2,0},{4,6},{6,4},{8,10},{10,8},{12,14},{14,12},{16,18},{18,... | collective-permute-start | bytes 165896 | tf_op jit(solution)/shard_map/ppermute | solution.py:38
  10.2 0.7 %collective-permute-done.2.refs_1_ = bf16[6,4,1152]{2,1,0:T(4,128)(2,1)S(1)} collective-permute-done((bf16[6,4,1152]{2,1,0:T(4,128)(2,1)S(1)}, bf16[6,4,1152]{2,1,0:T(4,128)(2,1)S(1)}, u32[]{:S(2)}, u32[]{:S(2)}) %collective-permute-start.2) | collective-permute-done | bytes 55328 | tf_op jit(solution)/shard_map/ppermute | solution.py:38
  10.9 2.2 %swin_windows.3 = (bf16[1,6,4,1152]{3,2,1,0:T(4,128)(2,1)S(1)}, f32[2,2,2,432,128]{4,3,2,1,0:T(8,128)S(1)}, f32[1,2,288,128]{3,2,1,0:T(8,128)S(1)}, f32[1,2,184,128]{3,2,1,0:T(8,128)S(1)}, bf16[864,192]{1,0:T(8,128)(2,1)S(1)}) custom-call(bf16[6,4,1152]{2,1,0:T(4,128)(2,1)S(1)} %get-tuple-element.33.refs_0_, ...), custom_call_target="tpu_custom_call" | custom-call | flops 200000000 | bytes 3000000 | tf_op jit(solution)/shard_map/swin_windows/pallas_call | solution.py:342
  13.2 0.0 collective-permute-done.1.refs_1_.refs_3_
  13.2 1.9 %swin_windows.4 = (bf16[1,6,4,1152]{3,2,1,0:T(4,128)(2,1)S(1)}, bf16[2,3,4,1152]{3,2,1,0:T(4,128)(2,1)S(1)}) custom-call(bf16[12,4,1152]{2,1,0:T(4,128)(2,1)S(1)} %pack_half.2._.refs_10_.refs_0_.refs_2_, bf16[12,4,1152]{2,1,0:T(4,128)(2,1)S(1)} %collective-permute-done.1.refs_1_.refs_3_, f32[1,192]{1,0:T(1,128)S(1)} %get-tuple-element.25.refs_2_.refs_4_, ...), custom_call_target="tpu_custom_call" | custom-call | flops 200000000 | bytes 3000000 | tf_op jit(solution)/shard_map/swin_windows/pallas_call | solution.py:342
  15.1 1.9 %collective-permute-start.3 = (bf16[2,3,4,1152]{3,2,1,0:T(4,128)(2,1)S(1)}, bf16[2,3,4,1152]{3,2,1,0:T(4,128)(2,1)S(1)}, u32[]{:S(2)}, u32[]{:S(2)}) collective-permute-start(bf16[2,3,4,1152]{3,2,1,0:T(4,128)(2,1)S(1)} %get-tuple-element.39), channel_id=1, source_target_pairs={{0,1},{1,0},{2,3},{3,2},{4,5},{5,4},{6,7},{7,6},{8,9},{9,8},{10,11... | collective-permute-start | bytes 165896 | tf_op jit(solution)/shard_map/ppermute | solution.py:29
  17.0 0.0 collective-permute-done.4.refs_1_
  17.0 2.8 %swin_windows.5.high_ref = bf16[2,6,4,1152]{3,2,1,0:T(4,128)(2,1)S(1)} custom-call(bf16[6,4,1152]{2,1,0:T(4,128)(2,1)S(1)} %get-tuple-element.40.refs_0_, bf16[6,4,1152]{2,1,0:T(4,128)(2,1)S(1)} %collective-permute-done.4.refs_1_, bf16[12,4,1152]{2,1,0:T(4,128)(2,1)S(1)} %pack_half.2._.refs_10_.refs_0_.refs_2_, ...), custom_call_target="tpu_custom_call" | custom-call | flops 400000000 | bytes 3000000 | tf_op jit(solution)/shard_map/swin_windows/pallas_call | solution.py:342
  19.8 0.0 collective-permute-done.3.top_ref
  19.8 0.7 %last_rows.1 = bf16[12,4,2304]{2,1,0:T(4,128)(2,1)} custom-call(bf16[2,3,4,1152]{3,2,1,0:T(4,128)(2,1)S(1)} %collective-permute-done.3.top_ref, bf16[2,6,4,1152]{3,2,1,0:T(4,128)(2,1)S(1)} %swin_windows.5.high_ref, bf16[1,6,4,1152]{3,2,1,0:T(4,128)(2,1)S(1)} %get-tuple-element.38.refs_12_.near_low_ref, bf16[1,6,4,1152]{3,2,1,0:T(4,128)(2,1)S(1)} %get-tuple-element.42.far_low_ref), custom_call_target="tpu_custom_call" | custom-call | bytes 400000 | tf_op jit(solution)/shard_map/last_rows/pallas_call | solution.py:426
  (2 shorter events, 0.0 us)
Async XLA Ops:
  0.8 5.1 %collective-permute-start = (bf16[3,4,2304]{2,1,0:T(4,128)(2,1)S(1)}, bf16[3,4,2304]{2,1,0:T(4,128)(2,1)S(1)}, u32[]{:S(2)}, u32[]{:S(2)}) collective-permute-start(bf16[3,4,2304]{2,1,0:T(4,128)(2,1)S(1)} %slice.4), channel_id=1, source_target_pairs={{0,1},{1,0},{2,3},{3,2},{4,5},{5,4},{6,7},{7,6},{8,9},{9,8},{10,11... | collective-permute-start | bytes 165896 | tf_op jit(solution)/shard_map/ppermute | solution.py:29
  6.0 7.2 %collective-permute-start.1 = (bf16[12,4,1152]{2,1,0:T(4,128)(2,1)S(1)}, bf16[12,4,1152]{2,1,0:T(4,128)(2,1)S(1)}, u32[]{:S(2)}, u32[]{:S(2)}) collective-permute-start(bf16[12,4,1152]{2,1,0:T(4,128)(2,1)S(1)} %pack_half.2._.refs_10_.refs_0_.refs_2_), channel_id=1, source_target_pairs={{2,4},{4,2},{6,8},{8,6},{10,12},{12,10},{14,16},{16,14},{18,20},{2... | collective-permute-start | bytes 331784 | tf_op jit(solution)/shard_map/ppermute | solution.py:38
  9.6 1.3 %collective-permute-start.2 = (bf16[6,4,1152]{2,1,0:T(4,128)(2,1)S(1)}, bf16[6,4,1152]{2,1,0:T(4,128)(2,1)S(1)}, u32[]{:S(2)}, u32[]{:S(2)}) collective-permute-start(bf16[6,4,1152]{2,1,0:T(4,128)(2,1)S(1)} %get-tuple-element.33.refs_0_), channel_id=1, source_target_pairs={{0,2},{2,0},{4,6},{6,4},{8,10},{10,8},{12,14},{14,12},{16,18},{18,... | collective-permute-start | bytes 165896 | tf_op jit(solution)/shard_map/ppermute | solution.py:38
  9.7 7.3 %collective-permute-start.4 = (bf16[6,4,1152]{2,1,0:T(4,128)(2,1)S(1)}, bf16[6,4,1152]{2,1,0:T(4,128)(2,1)S(1)}, u32[]{:S(2)}, u32[]{:S(2)}) collective-permute-start(bf16[6,4,1152]{2,1,0:T(4,128)(2,1)S(1)} %get-tuple-element.40.refs_0_), channel_id=1, source_target_pairs={{0,2},{2,0},{4,6},{6,4},{8,10},{10,8},{12,14},{14,12},{16,18},{18,... | collective-permute-start | bytes 165896 | tf_op jit(solution)/shard_map/ppermute | solution.py:38
  15.1 4.7 %collective-permute-start.3 = (bf16[2,3,4,1152]{3,2,1,0:T(4,128)(2,1)S(1)}, bf16[2,3,4,1152]{3,2,1,0:T(4,128)(2,1)S(1)}, u32[]{:S(2)}, u32[]{:S(2)}) collective-permute-start(bf16[2,3,4,1152]{3,2,1,0:T(4,128)(2,1)S(1)} %get-tuple-element.39), channel_id=1, source_target_pairs={{0,1},{1,0},{2,3},{3,2},{4,5},{5,4},{6,7},{7,6},{8,9},{9,8},{10,11... | collective-permute-start | bytes 165896 | tf_op jit(solution)/shard_map/ppermute | solution.py:29

commit v19 on v18

--- a/solution.py
+++ b/solution.py
@@ -57,15 +57,16 @@
     low_ref[EDGE:] = south_ref[:, :, pl.ds(at, low_ref.shape[2])]
 
 
-def last_kernel(top_ref, high_ref, near_low_ref, far_low_ref, out_ref, sems):
+def last_kernel(top_ref, near_ref, far_low_ref, far_high_ref, out_ref, sems):
     half = top_ref.shape[3]
+    parts = ((near_ref.at[0], near_ref.at[1]), (far_low_ref.at[0], far_high_ref.at[0]))
     copies = []
     for n, at in enumerate(half_places(half)):
         target = out_ref.at[:, :, pl.ds(at, half)]
-        low_ref = (near_low_ref, far_low_ref)[n]
+        low, high = parts[n]
         for source, first in (
-            (high_ref.at[n], EDGE),
-            (low_ref.at[0, :EDGE], EDGE + WIN_LAT),
+            (high, EDGE),
+            (low.at[:EDGE], EDGE + WIN_LAT),
             (top_ref.at[n], 0),
         ):
             rows = pl.ds(first, source.shape[0])
@@ -76,8 +77,8 @@
         copy.wait()
 
 
-def build_tables(bias_ref, table_ref, heads, wrap):
-    lines = bias_ref.shape[0] // heads
+def build_tables(bias_ref, start, table_ref, heads, wrap):
+    lines = bias_ref.shape[0] // 2 // heads
     blocks = WIN_LEV * WIN_LAT // 2
     lane = lax.broadcasted_iota(jnp.int32, (blocks, LANES), 1)
     block = lax.broadcasted_iota(jnp.int32, (blocks, LANES), 0)
@@ -107,7 +108,7 @@
     for h in range(heads):
         for p in range(2):
             for third in range(3):
-                line = h * lines + p + third * 18
+                line = start + h * lines + p + third * 18
                 pieces = [
                     bias_ref[pl.ds(line + 2 * u, blocks, stride=54), :] * LOG2E for u in range(9)
                 ]
@@ -128,17 +129,18 @@
 
 def table_kernel(count, heads, *refs):
     bias_any, field_any, *weights_any = refs[: 2 + count]
-    table_ref, inner_ref, near_ref, far_ref, *weights_ref = refs[2 + count : 6 + 2 * count]
+    high_ref, low_ref, near_ref, far_ref, *weights_ref = refs[2 + count : 6 + 2 * count]
     bias_ref, sems = refs[6 + 2 * count :]
-    lines = bias_ref.shape[0]
+    lines = bias_ref.shape[0] // 2
     flat = bias_any.reshape(2 * lines, LANES)
     rows, half = field_any.shape[0] - EDGE, near_ref.shape[2]
     near_at, far_at = half_places(half)
+    inner, straddling = pl.ds(0, lines), pl.ds(lines, lines)
     fetches = [
-        (flat.at[pl.ds(lines, lines)], bias_ref),
+        (flat.at[straddling], bias_ref.at[straddling]),
+        (flat.at[inner], bias_ref.at[inner]),
         (field_any.at[EDGE:, :, pl.ds(far_at, half)], far_ref.at[:rows]),
         (field_any.at[EDGE:, :, pl.ds(near_at, half)], near_ref.at[:rows]),
-        (flat.at[pl.ds(0, lines)], inner_ref),
     ]
     fetches += list(zip(weights_any, weights_ref))
     fetches = [
@@ -148,8 +150,10 @@
     for copy in fetches:
         copy.start()
     fetches[0].wait()
-    build_tables(bias_ref, table_ref, heads, True)
-    for copy in fetches[1:]:
+    build_tables(bias_ref, lines, low_ref, heads, True)
+    fetches[1].wait()
+    build_tables(bias_ref, 0, high_ref, heads, False)
+    for copy in fetches[2:]:
         copy.wait()
 
 
@@ -167,11 +171,11 @@
 def units_kernel(chans, heads, units, extra, *refs):
     count = len(units)
     pieces, refs = refs[: 2 * count], refs[2 * count :]
-    gain1_ref, qkv_ref, proj_ref, gain2_ref, fc1_ref, fc2_ref, table_ref, *refs = refs
+    gain1_ref, qkv_ref, proj_ref, gain2_ref, fc1_ref, fc2_ref, *refs = refs
+    tables, refs = refs[:2], refs[2:]
     *refs, keys_ref, own_ref, res_ref = refs
     if extra == "ahead":
-        raw_ref, far_ref, out_ref, inner_ref, far_keys, far_own, far_picked = refs
-        build_tables(raw_ref, inner_ref, heads, False)
+        far_ref, out_ref, far_keys, far_own, far_picked = refs
     elif extra == "send":
         far_keys, far_own, far_picked, lower_ref, out_ref, send_ref = refs
     else:
@@ -263,7 +267,7 @@
             probs = []
             for h in range(heads):
                 at = slice(h * QUERIES, (h + 1) * QUERIES)
-                bias = [table_ref[p, rights[n], part, at] for part in range(2)]
+                bias = [tables[window][p, rights[n], part, at] for part in range(2)]
                 bias = jnp.concatenate([bias[0], bias[1][:, : TOKENS - LANES]], axis=1)
                 part = scores[n, p][at] + bias
                 probs.append(jnp.exp2(part - jnp.max(part, axis=1, keepdims=True)))
@@ -323,17 +327,16 @@
         send_ref[1] = out_ref[0, EDGE:]
 
 
-def run_units(units, near, far, weights, chans, heads, table, extra=None, *extra_in):
+def run_units(units, near, far, weights, chans, heads, tables, extra=None, *extra_in):
     count = len(units)
     pieces = [x for is_near, w in units for x in (near[w] if is_near else far)]
     piece = pieces[0]
     outs = [jax.ShapeDtypeStruct((count, WIN_LAT) + piece.shape[1:], piece.dtype)]
-    operands = (*pieces, *weights, table, *extra_in)
+    operands = (*pieces, *weights, *tables, *extra_in)
     if extra == "send":
         outs.append(jax.ShapeDtypeStruct((2, EDGE) + piece.shape[1:], piece.dtype))
     elif extra == "ahead":
         outs += [
-            jax.ShapeDtypeStruct(table.shape, table.dtype),
             jax.ShapeDtypeStruct((1, 2, LEVELS * QUERIES, LANES), jnp.float32),
             jax.ShapeDtypeStruct((1, 2, 184, LANES), jnp.float32),
             jax.ShapeDtypeStruct((2 * heads * QUERIES, chans), jnp.bfloat16),
@@ -382,16 +385,15 @@
     tiles = entries // LANES
     bias = earth_bias.reshape(windows, zwin, heads, tiles, LANES).transpose(0, 2, 3, 1, 4)
     sources = (bias, field) + weights
-    raw = jax.ShapeDtypeStruct((bias.size // windows // LANES, LANES), bias.dtype)
     sources = [pltpu.with_memory_space_constraint(x, pltpu.HBM) for x in sources]
-    outs = [table, raw, piece, piece] + [jax.ShapeDtypeStruct(x.shape, x.dtype) for x in weights]
-    table, inner, near, far, *weights = pl.pallas_call(
+    outs = [table, table, piece, piece] + [jax.ShapeDtypeStruct(x.shape, x.dtype) for x in weights]
+    high_table, low_table, near, far, *weights = pl.pallas_call(
         functools.partial(table_kernel, len(weights), heads),
         out_shape=outs,
         in_specs=[pl.BlockSpec(memory_space=pltpu.HBM)] * len(sources),
         out_specs=[vmem] * len(outs),
         scratch_shapes=[
-            pltpu.VMEM(raw.shape, raw.dtype),
+            pltpu.VMEM((bias.size // LANES, LANES), bias.dtype),
             pltpu.SemaphoreType.DMA((4 + len(weights),)),
         ],
         compiler_params=pltpu.CompilerParams(vmem_limit_bytes=VMEM_BYTES),
@@ -416,13 +418,11 @@
     near_parts = pack(pack_near_kernel, [window, window], south, near, far)
     low, high = ((part, swapped(part, "lon", 0)) for part in near_parts)
     near, far = (high, low), (far, far_halo)
-    common = (near, far, weights, chans, heads)
-    near_low, inner, *ahead = run_units(
-        ((True, 1),), *common, table, "ahead", inner, far[0]
-    )
-    far_low, send = run_units(((False, 1),), *common, table, "send", *ahead, near_low)
+    common = (near, far, weights, chans, heads, (high_table, low_table))
+    near_both, *ahead = run_units(((True, 1), (True, 0)), *common, "ahead", far[0])
+    far_low, send = run_units(((False, 1),), *common, "send", *ahead, near_both)
     top = moved(send, "lat", 1)
-    (high,) = run_units(((True, 0), (False, 0)), *common, inner)
+    (far_high,) = run_units(((False, 0),), *common)
     done = pl.pallas_call(
         last_kernel,
         out_shape=jax.ShapeDtypeStruct(field.shape, field.dtype),
@@ -432,7 +432,7 @@
         compiler_params=pltpu.CompilerParams(vmem_limit_bytes=VMEM_BYTES),
         cost_estimate=pl.CostEstimate(flops=0, bytes_accessed=400_000, transcendentals=0),
         name="last_rows",
-    )(top, high, near_low, far_low)
+    )(top, near_both, far_low, far_high)
     return jnp.transpose(done, (1, 0, 2))
 
 

time: 20.7 us -> 21.8 us (1.053)
  waiting for transfers between devices: 0.92 us -> 2.26 us
  starting transfers between devices: 9.05 us -> 8.11 us
  Pallas kernels: 9.66 us -> 10.3 us
    ppermute x2, waiting for transfers between devices: 0.18 us -> 1.37 us  [moved(): return lax.ppermute(x, axis, [(i, (i + by) % size) for i in range(size)])]
    ppermute x2, starting transfers between devices: 4.86 us -> 3.76 us  [moved(): return lax.ppermute(x, axis, [(i, (i + by) % size) for i in range(size)])]
    pallas_call x1, Pallas kernels: 1.95 us -> 2.57 us  [shards(): pl.pallas_call(functools.partial(table_kernel, len(weights), heads), out_...]
  transfers between devices with their start and end apart: 5 -> 5, of which waited for: 2 -> 3; matrix products, arithmetic and copies ran while one was open for 0% -> 0% of each run, Pallas kernels for 43% -> 35%
where the time goes in v19:
time: 21.8 us; the launch traced here: 21.6 us
  Pallas kernels  10.3 us (47%)
  starting transfers between devices  8.11 us (37%)
  waiting for transfers between devices  2.26 us (10%)
  local copies, waits for them, and re-layouts  0.83 us (4%)
    pallas_call x3, Pallas kernels, run_units(): pl.pallas_call(functools.partial(units_kernel, chans, heads, units, extra...  6.96 us
    ppermute x3, starting transfers between devices, swapped(): return lax.ppermute(x, axis, pairs)  4.35 us
    ppermute x2, starting transfers between devices, moved(): return lax.ppermute(x, axis, [(i, (i + by) % size) for i in range(size)])  3.76 us
    pallas_call x1, Pallas kernels, shards(): pl.pallas_call(functools.partial(table_kernel, len(weights), heads), out_...  2.57 us
    ppermute x2, waiting for transfers between devices, moved(): return lax.ppermute(x, axis, [(i, (i + by) % size) for i in range(size)])  1.37 us
    ppermute x3, waiting for transfers between devices, swapped(): return lax.ppermute(x, axis, pairs)  0.89 us
    slice x1, local copies, waits for them, and re-layouts, shards(): south = moved(field[:EDGE], 'lat', -1)  0.83 us
    pallas_call x1, Pallas kernels, shards(): pl.pallas_call(last_kernel, out_shape=jax.ShapeDtypeStruct(field.shape, f...  0.72 us
  transfers between devices with their start and end apart: 5, of which 3 were waited for; matrix products, arithmetic and copies ran while one was open for 0% of the time, Pallas kernels for 35%

profile of v19, /device:TPU:0, one launch (start us, length us, event | category | flops | bytes accessed | tf_op | source)
XLA Modules:
  0.0 21.6 jit_solution(17689518249125617793)
XLA Ops:
  0.0 0.8 %slice.4 = bf16[3,4,2304]{2,1,0:T(4,128)(2,1)S(1)} slice(bf16[12,4,2304]{2,1,0:T(4,128)(2,1)} %bitcast.9), slice={[0:3], [0:4], [0:2304]} | slice | bytes 110592 | tf_op jit(solution)/shard_map/slice | solution.py:371
  0.8 3.0 %collective-permute-start = (bf16[3,4,2304]{2,1,0:T(4,128)(2,1)S(1)}, bf16[3,4,2304]{2,1,0:T(4,128)(2,1)S(1)}, u32[]{:S(2)}, u32[]{:S(2)}) collective-permute-start(bf16[3,4,2304]{2,1,0:T(4,128)(2,1)S(1)} %slice.4), channel_id=1, source_target_pairs={{0,1},{1,0},{2,3},{3,2},{4,5},{5,4},{6,7},{7,6},{8,9},{9,8},{10,11... | collective-permute-start | bytes 165896 | tf_op jit(solution)/shard_map/ppermute | solution.py:29
  3.8 2.6 %bias_tables.1 = (f32[2,2,2,432,128]{4,3,2,1,0:T(8,128)S(1)}, f32[2,2,2,432,128]{4,3,2,1,0:T(8,128)S(1)}, bf16[12,4,1152]{2,1,0:T(4,128)(2,1)S(1)}, bf16[12,4,11...) custom-call(f32[2,6,162,2,128]{4,3,2,1,0:T(2,128)} %bitcast.8, ...), custom_call_target="tpu_custom_call" | custom-call | flops 4000000 | bytes 6000000 | tf_op jit(solution)/shard_map/bias_tables/pallas_call | solution.py:390
  6.4 0.0 collective-permute-done.south_ref
  6.5 3.8 %collective-permute-start.1 = (bf16[12,4,1152]{2,1,0:T(4,128)(2,1)S(1)}, bf16[12,4,1152]{2,1,0:T(4,128)(2,1)S(1)}, u32[]{:S(2)}, u32[]{:S(2)}) collective-permute-start(bf16[12,4,1152]{2,1,0:T(4,128)(2,1)S(1)} %pack_half.2._.refs_12_.refs_0_), channel_id=1, source_target_pairs={{2,4},{4,2},{6,8},{8,6},{10,12},{12,10},{14,16},{16,14},{18,20},{2... | collective-permute-start | bytes 331784 | tf_op jit(solution)/shard_map/ppermute | solution.py:38
  10.3 0.1 collective-permute-start.2
  10.3 0.5 %collective-permute-start.3 = (bf16[6,4,1152]{2,1,0:T(4,128)(2,1)S(1)}, bf16[6,4,1152]{2,1,0:T(4,128)(2,1)S(1)}, u32[]{:S(2)}, u32[]{:S(2)}) collective-permute-start(bf16[6,4,1152]{2,1,0:T(4,128)(2,1)S(1)} %get-tuple-element.34.refs_2_), channel_id=1, source_target_pairs={{0,2},{2,0},{4,6},{6,4},{8,10},{10,8},{12,14},{14,12},{16,18},{18,... | collective-permute-start | bytes 165896 | tf_op jit(solution)/shard_map/ppermute | solution.py:38
  10.8 0.7 %collective-permute-done.2.refs_1_ = bf16[6,4,1152]{2,1,0:T(4,128)(2,1)S(1)} collective-permute-done((bf16[6,4,1152]{2,1,0:T(4,128)(2,1)S(1)}, bf16[6,4,1152]{2,1,0:T(4,128)(2,1)S(1)}, u32[]{:S(2)}, u32[]{:S(2)}) %collective-permute-start.2) | collective-permute-done | bytes 55328 | tf_op jit(solution)/shard_map/ppermute | solution.py:38
  11.6 0.2 collective-permute-done.3.refs_3_
  11.7 2.9 %swin_windows.3 = (bf16[2,6,4,1152]{3,2,1,0:T(4,128)(2,1)S(1)}, f32[1,2,288,128]{3,2,1,0:T(8,128)S(1)}, f32[1,2,184,128]{3,2,1,0:T(8,128)S(1)}, bf16[864,192]{1,0:T(8,128)(2,1)S(1)}) custom-call(bf16[6,4,1152]{2,1,0:T(4,128)(2,1)S(1)} %get-tuple-element.33.refs_0_, bf16[6,4,1152]{2,1,0:T(4,128)(2,1)S(1)} %collective-permute-done.2.refs_1_, ...), custom_call_target="tpu_custom_call" | custom-call | flops 400000000 | bytes 3000000 | tf_op jit(solution)/shard_map/swin_windows/pallas_call | solution.py:345
  14.7 0.0 collective-permute-done.1.refs_1_
  14.7 2.0 %swin_windows.4 = (bf16[1,6,4,1152]{3,2,1,0:T(4,128)(2,1)S(1)}, bf16[2,3,4,1152]{3,2,1,0:T(4,128)(2,1)S(1)}) custom-call(bf16[12,4,1152]{2,1,0:T(4,128)(2,1)S(1)} %pack_half.2._.refs_12_.refs_0_, bf16[12,4,1152]{2,1,0:T(4,128)(2,1)S(1)} %collective-permute-done.1.refs_1_, f32[1,192]{1,0:T(1,128)S(1)} %get-tuple-element.24.refs_4_.refs_2_, ...), custom_call_target="tpu_custom_call" | custom-call | flops 200000000 | bytes 3000000 | tf_op jit(solution)/shard_map/swin_windows/pallas_call | solution.py:345
  16.6 0.8 %collective-permute-start.4 = (bf16[2,3,4,1152]{3,2,1,0:T(4,128)(2,1)S(1)}, bf16[2,3,4,1152]{3,2,1,0:T(4,128)(2,1)S(1)}, u32[]{:S(2)}, u32[]{:S(2)}) collective-permute-start(bf16[2,3,4,1152]{3,2,1,0:T(4,128)(2,1)S(1)} %get-tuple-element.39), channel_id=1, source_target_pairs={{0,1},{1,0},{2,3},{3,2},{4,5},{5,4},{6,7},{7,6},{8,9},{9,8},{10,11... | collective-permute-start | bytes 165896 | tf_op jit(solution)/shard_map/ppermute | solution.py:29
  17.4 2.1 %swin_windows.5.far_high_ref = bf16[1,6,4,1152]{3,2,1,0:T(4,128)(2,1)S(1)} custom-call(bf16[12,4,1152]{2,1,0:T(4,128)(2,1)S(1)} %pack_half.2._.refs_12_.refs_0_, bf16[12,4,1152]{2,1,0:T(4,128)(2,1)S(1)} %collective-permute-done.1.refs_1_, f32[1,192]{1,0:T(1,128)S(1)} %get-tuple-element.24.refs_4_.refs_2_, ...), custom_call_target="tpu_custom_call" | custom-call | flops 200000000 | bytes 3000000 | tf_op jit(solution)/shard_map/swin_windows/pallas_call | solution.py:345
  19.5 1.4 %collective-permute-done.4.top_ref = bf16[2,3,4,1152]{3,2,1,0:T(4,128)(2,1)S(1)} collective-permute-done((bf16[2,3,4,1152]{3,2,1,0:T(4,128)(2,1)S(1)}, bf16[2,3,4,1152]{3,2,1,0:T(4,128)(2,1)S(1)}, u32[]{:S(2)}, u32[]{:S(2)}) %collective-permute-start.4) | collective-permute-done | bytes 55328 | tf_op jit(solution)/shard_map/ppermute | solution.py:29
  20.8 0.7 %last_rows.1 = bf16[12,4,2304]{2,1,0:T(4,128)(2,1)} custom-call(bf16[2,3,4,1152]{3,2,1,0:T(4,128)(2,1)S(1)} %collective-permute-done.4.top_ref, bf16[2,6,4,1152]{3,2,1,0:T(4,128)(2,1)S(1)} %get-tuple-element.38.refs_13_.near_ref, bf16[1,6,4,1152]{3,2,1,0:T(4,128)(2,1)S(1)} %get-tuple-element.40.far_low_ref, bf16[1,6,4,1152]{3,2,1,0:T(4,128)(2,1)S(1)} %swin_windows.5.far_high_ref), custom_call_target="tpu_custom_call" | custom-call | bytes 400000 | tf_op jit(solution)/shard_map/last_rows/pallas_call | solution.py:426
  (2 shorter events, 0.0 us)
Async XLA Ops:
  0.8 5.6 %collective-permute-start = (bf16[3,4,2304]{2,1,0:T(4,128)(2,1)S(1)}, bf16[3,4,2304]{2,1,0:T(4,128)(2,1)S(1)}, u32[]{:S(2)}, u32[]{:S(2)}) collective-permute-start(bf16[3,4,2304]{2,1,0:T(4,128)(2,1)S(1)} %slice.4), channel_id=1, source_target_pairs={{0,1},{1,0},{2,3},{3,2},{4,5},{5,4},{6,7},{7,6},{8,9},{9,8},{10,11... | collective-permute-start | bytes 165896 | tf_op jit(solution)/shard_map/ppermute | solution.py:29
  6.5 8.2 %collective-permute-start.1 = (bf16[12,4,1152]{2,1,0:T(4,128)(2,1)S(1)}, bf16[12,4,1152]{2,1,0:T(4,128)(2,1)S(1)}, u32[]{:S(2)}, u32[]{:S(2)}) collective-permute-start(bf16[12,4,1152]{2,1,0:T(4,128)(2,1)S(1)} %pack_half.2._.refs_12_.refs_0_), channel_id=1, source_target_pairs={{2,4},{4,2},{6,8},{8,6},{10,12},{12,10},{14,16},{16,14},{18,20},{2... | collective-permute-start | bytes 331784 | tf_op jit(solution)/shard_map/ppermute | solution.py:38
  10.3 1.3 %collective-permute-start.2 = (bf16[6,4,1152]{2,1,0:T(4,128)(2,1)S(1)}, bf16[6,4,1152]{2,1,0:T(4,128)(2,1)S(1)}, u32[]{:S(2)}, u32[]{:S(2)}) collective-permute-start(bf16[6,4,1152]{2,1,0:T(4,128)(2,1)S(1)} %get-tuple-element.33.refs_0_), channel_id=1, source_target_pairs={{0,2},{2,0},{4,6},{6,4},{8,10},{10,8},{12,14},{14,12},{16,18},{18,... | collective-permute-start | bytes 165896 | tf_op jit(solution)/shard_map/ppermute | solution.py:38
  10.3 1.4 %collective-permute-start.3 = (bf16[6,4,1152]{2,1,0:T(4,128)(2,1)S(1)}, bf16[6,4,1152]{2,1,0:T(4,128)(2,1)S(1)}, u32[]{:S(2)}, u32[]{:S(2)}) collective-permute-start(bf16[6,4,1152]{2,1,0:T(4,128)(2,1)S(1)} %get-tuple-element.34.refs_2_), channel_id=1, source_target_pairs={{0,2},{2,0},{4,6},{6,4},{8,10},{10,8},{12,14},{14,12},{16,18},{18,... | collective-permute-start | bytes 165896 | tf_op jit(solution)/shard_map/ppermute | solution.py:38
  16.6 4.2 %collective-permute-start.4 = (bf16[2,3,4,1152]{3,2,1,0:T(4,128)(2,1)S(1)}, bf16[2,3,4,1152]{3,2,1,0:T(4,128)(2,1)S(1)}, u32[]{:S(2)}, u32[]{:S(2)}) collective-permute-start(bf16[2,3,4,1152]{3,2,1,0:T(4,128)(2,1)S(1)} %get-tuple-element.39), channel_id=1, source_target_pairs={{0,1},{1,0},{2,3},{3,2},{4,5},{5,4},{6,7},{7,6},{8,9},{9,8},{10,11... | collective-permute-start | bytes 165896 | tf_op jit(solution)/shard_map/ppermute | solution.py:29

commit v20 on v18

--- a/solution.py
+++ b/solution.py
@@ -20,7 +20,7 @@
 GELU_1 = 0.044715 * GELU_0
 LANES = 128
 SPARE = 64
-VMEM_BYTES = 8 * 2**20
+VMEM_BYTES = 12 * 2**20
 NT = (((1,), (1,)), ((), ()))
 
 
@@ -170,12 +170,13 @@
     gain1_ref, qkv_ref, proj_ref, gain2_ref, fc1_ref, fc2_ref, table_ref, *refs = refs
     *refs, keys_ref, own_ref, res_ref = refs
     if extra == "ahead":
-        raw_ref, far_ref, out_ref, inner_ref, far_keys, far_own, far_picked = refs
+        raw_ref, far_ref, high_ref, out_ref, inner_ref, all_keys, all_own, all_picked = refs
         build_tables(raw_ref, inner_ref, heads, False)
     elif extra == "send":
-        far_keys, far_own, far_picked, lower_ref, out_ref, send_ref = refs
+        all_keys, all_own, all_picked, lower_ref, out_ref, send_ref = refs
     else:
-        (out_ref,) = refs
+        all_keys, all_own, all_picked, out_ref = refs
+    slots = {(True, 1): None, (False, 1): 0, (True, 0): 1, (False, 0): 2}
     head_dim = chans // heads
     low = lax.broadcasted_iota(jnp.int32, (1, LANES), 1) < SPARE
     odd = lax.rem(lax.axis_index("lon"), 2)
@@ -223,13 +224,15 @@
             ]
         return jnp.concatenate(picked, axis=0).astype(jnp.bfloat16)
 
-    if extra == "send":
-        keys_ref[...] = far_keys[...]
-        own_ref = far_own
+    owns = {n: (own_ref, n) for n in range(count)}
     for n, (near, window) in enumerate(units):
+        if extra != "ahead":
+            slot = slots[near, window]
+            keys_ref[n] = all_keys[slot]
+            owns[n] = (all_own, slot)
         own_piece, halo_piece = pieces[2 * n], pieces[2 * n + 1]
         first = 0 if near else window * WIN_LAT
-        if extra != "send":
+        if extra == "ahead":
             place_own(n, own_piece, first, HALF - rights[n] * HALF, keys_ref, own_ref)
         place_keys(n, halo_piece, first, rights[n] * HALF, keys_ref)
 
@@ -238,7 +241,7 @@
     ones = jnp.ones((TOKENS, 2 * LANES - chans), jnp.float32)
     scores, values, mixed = {}, {}, []
     for n in range(count):
-        picked = far_picked[...] if extra == "send" else queries(n, own_ref)
+        picked = queries(n, own_ref) if extra == "ahead" else all_picked[owns[n][1]]
         normed = []
         for p in range(2):
             levels = [(2 * p + 1 + lev) % LEVELS for lev in range(WIN_LEV)]
@@ -255,8 +258,10 @@
             )
         values[n] = jnp.dot(normed, qkv_ref[:, 2 * chans :], preferred_element_type=jnp.float32)
     if extra == "ahead":
-        place_own(0, far_ref, WIN_LAT, HALF - odd * HALF, far_keys, far_own)
-        far_picked[...] = queries(0, far_own)
+        ahead = ((far_ref, WIN_LAT, odd), (high_ref, 0, 1 - odd), (far_ref, 0, odd))
+        for slot, (ref, first, right) in enumerate(ahead):
+            place_own(slot, ref, first, HALF - right * HALF, all_keys, all_own)
+            all_picked[slot] = queries(slot, all_own)
     got = {}
     for n, (_, window) in enumerate(units):
         for p in range(2):
@@ -284,7 +289,7 @@
     attn = attn.astype(jnp.bfloat16).astype(jnp.float32)
     resid, normed = [], []
     for n in range(count):
-        part = tokens_of(own_ref, n, 40, 144) + attn[n * 144 : (n + 1) * 144]
+        part = tokens_of(*owns[n], 40, 144) + attn[n * 144 : (n + 1) * 144]
         resid.append(part.astype(jnp.bfloat16).astype(jnp.float32))
         normed.append(layer_norm(resid[n], gain2_ref[...]).astype(jnp.bfloat16))
     result, normed = jnp.concatenate(resid, axis=0), jnp.concatenate(normed, axis=0)
@@ -334,9 +339,9 @@
     elif extra == "ahead":
         outs += [
             jax.ShapeDtypeStruct(table.shape, table.dtype),
-            jax.ShapeDtypeStruct((1, 2, LEVELS * QUERIES, LANES), jnp.float32),
-            jax.ShapeDtypeStruct((1, 2, 184, LANES), jnp.float32),
-            jax.ShapeDtypeStruct((2 * heads * QUERIES, chans), jnp.bfloat16),
+            jax.ShapeDtypeStruct((3, 2, LEVELS * QUERIES, LANES), jnp.float32),
+            jax.ShapeDtypeStruct((3, 2, 184, LANES), jnp.float32),
+            jax.ShapeDtypeStruct((3, 2 * heads * QUERIES, chans), jnp.bfloat16),
         ]
     vmem = pl.BlockSpec(memory_space=pltpu.VMEM)
     return pl.pallas_call(
@@ -418,11 +423,11 @@
     near, far = (high, low), (far, far_halo)
     common = (near, far, weights, chans, heads)
     near_low, inner, *ahead = run_units(
-        ((True, 1),), *common, table, "ahead", inner, far[0]
+        ((True, 1),), *common, table, "ahead", inner, far[0], high[0]
     )
     far_low, send = run_units(((False, 1),), *common, table, "send", *ahead, near_low)
     top = moved(send, "lat", 1)
-    (high,) = run_units(((True, 0), (False, 0)), *common, inner)
+    (high,) = run_units(((True, 0), (False, 0)), *common, inner, None, *ahead)
     done = pl.pallas_call(
         last_kernel,
         out_shape=jax.ShapeDtypeStruct(field.shape, field.dtype),

time: 20.7 us -> 20.6 us (level)
  starting transfers between devices: 9.05 us -> 8.81 us
    ppermute x2, starting transfers between devices: 4.86 us -> 4.63 us  [moved(): return lax.ppermute(x, axis, [(i, (i + by) % size) for i in range(size)])]
  transfers between devices with their start and end apart: 5 -> 5, of which waited for: 2 -> 2; matrix products, arithmetic and copies ran while one was open for 0% -> 0% of each run, Pallas kernels for 43% -> 44%
where the time goes in v20:
time: 20.6 us; the launch traced here: 20.4 us
  Pallas kernels  9.72 us (47%)
  starting transfers between devices  8.81 us (43%)
  waiting for transfers between devices  0.92 us (4%)
  local copies, waits for them, and re-layouts  0.83 us (4%)
    pallas_call x3, Pallas kernels, run_units(): pl.pallas_call(functools.partial(units_kernel, chans, heads, units, extra...  7 us
    ppermute x2, starting transfers between devices, moved(): return lax.ppermute(x, axis, [(i, (i + by) % size) for i in range(size)])  4.63 us
    ppermute x3, starting transfers between devices, swapped(): return lax.ppermute(x, axis, pairs)  4.18 us
    pallas_call x1, Pallas kernels, shards(): pl.pallas_call(functools.partial(table_kernel, len(weights), heads), out_...  1.95 us
    slice x1, local copies, waits for them, and re-layouts, shards(): south = moved(field[:EDGE], 'lat', -1)  0.83 us
    pallas_call x1, Pallas kernels, shards(): pl.pallas_call(last_kernel, out_shape=jax.ShapeDtypeStruct(field.shape, f...  0.74 us
    ppermute x3, waiting for transfers between devices, swapped(): return lax.ppermute(x, axis, pairs)  0.73 us
  transfers between devices with their start and end apart: 5, of which 2 were waited for; matrix products, arithmetic and copies ran while one was open for 0% of the time, Pallas kernels for 44%

profile of v20, /device:TPU:0, one launch (start us, length us, event | category | flops | bytes accessed | tf_op | source)
XLA Modules:
  0.0 20.4 jit_solution(17319554069491587785)
XLA Ops:
  0.0 0.8 %slice.4 = bf16[3,4,2304]{2,1,0:T(4,128)(2,1)S(1)} slice(bf16[12,4,2304]{2,1,0:T(4,128)(2,1)} %bitcast.9), slice={[0:3], [0:4], [0:2304]} | slice | bytes 110592 | tf_op jit(solution)/shard_map/slice | solution.py:373
  0.8 3.0 %collective-permute-start = (bf16[3,4,2304]{2,1,0:T(4,128)(2,1)S(1)}, bf16[3,4,2304]{2,1,0:T(4,128)(2,1)S(1)}, u32[]{:S(2)}, u32[]{:S(2)}) collective-permute-start(bf16[3,4,2304]{2,1,0:T(4,128)(2,1)S(1)} %slice.4), channel_id=1, source_target_pairs={{0,1},{1,0},{2,3},{3,2},{4,5},{5,4},{6,7},{7,6},{8,9},{9,8},{10,11... | collective-permute-start | bytes 165896 | tf_op jit(solution)/shard_map/ppermute | solution.py:29
  3.8 1.9 %bias_tables.1 = (f32[2,2,2,432,128]{4,3,2,1,0:T(8,128)S(1)}, f32[1944,128]{1,0:T(8,128)S(1)}, bf16[12,4,1152]{2,1,0:T(4,128)(2,1)S(1)}, bf16[12,4,1152]{2,1,0:T...) custom-call(f32[2,6,162,2,128]{4,3,2,1,0:T(2,128)} %bitcast.8, ...), custom_call_target="tpu_custom_call" | custom-call | flops 4000000 | bytes 6000000 | tf_op jit(solution)/shard_map/bias_tables/pallas_call | solution.py:393
  5.8 0.2 collective-permute-done.south_ref
  6.0 3.6 %collective-permute-start.1 = (bf16[12,4,1152]{2,1,0:T(4,128)(2,1)S(1)}, bf16[12,4,1152]{2,1,0:T(4,128)(2,1)S(1)}, u32[]{:S(2)}, u32[]{:S(2)}) collective-permute-start(bf16[12,4,1152]{2,1,0:T(4,128)(2,1)S(1)} %pack_half.2._.refs_10_.refs_0_.refs_2_), channel_id=1, source_target_pairs={{2,4},{4,2},{6,8},{8,6},{10,12},{12,10},{14,16},{16,14},{18,20},{2... | collective-permute-start | bytes 331784 | tf_op jit(solution)/shard_map/ppermute | solution.py:38
  9.6 0.1 collective-permute-start.2
  9.7 0.5 %collective-permute-start.4 = (bf16[6,4,1152]{2,1,0:T(4,128)(2,1)S(1)}, bf16[6,4,1152]{2,1,0:T(4,128)(2,1)S(1)}, u32[]{:S(2)}, u32[]{:S(2)}) collective-permute-start(bf16[6,4,1152]{2,1,0:T(4,128)(2,1)S(1)} %get-tuple-element.35.refs_11_.refs_0_), channel_id=1, source_target_pairs={{0,2},{2,0},{4,6},{6,4},{8,10},{10,8},{12,14},{14,12},{16,18},{18,... | collective-permute-start | bytes 165896 | tf_op jit(solution)/shard_map/ppermute | solution.py:38
  10.2 0.7 %collective-permute-done.2.refs_1_ = bf16[6,4,1152]{2,1,0:T(4,128)(2,1)S(1)} collective-permute-done((bf16[6,4,1152]{2,1,0:T(4,128)(2,1)S(1)}, bf16[6,4,1152]{2,1,0:T(4,128)(2,1)S(1)}, u32[]{:S(2)}, u32[]{:S(2)}) %collective-permute-start.2) | collective-permute-done | bytes 55328 | tf_op jit(solution)/shard_map/ppermute | solution.py:38
  10.9 2.4 %swin_windows.3 = (bf16[1,6,4,1152]{3,2,1,0:T(4,128)(2,1)S(1)}, f32[2,2,2,432,128]{4,3,2,1,0:T(8,128)S(1)}, f32[3,2,288,128]{3,2,1,0:T(8,128)S(1)}, f32[3,2,184,...) custom-call(bf16[6,4,1152]{2,1,0:T(4,128)(2,1)S(1)} %get-tuple-element.33.refs_0_, ...), custom_call_target="tpu_custom_call" | custom-call | flops 200000000 | bytes 3000000 | tf_op jit(solution)/shard_map/swin_windows/pallas_call | solution.py:347
  13.4 0.0 collective-permute-done.1.refs_1_.refs_3_
  13.4 2.0 %swin_windows.4 = (bf16[1,6,4,1152]{3,2,1,0:T(4,128)(2,1)S(1)}, bf16[2,3,4,1152]{3,2,1,0:T(4,128)(2,1)S(1)}) custom-call(bf16[12,4,1152]{2,1,0:T(4,128)(2,1)S(1)} %pack_half.2._.refs_10_.refs_0_.refs_2_, bf16[12,4,1152]{2,1,0:T(4,128)(2,1)S(1)} %collective-permute-done.1.refs_1_.refs_3_, f32[1,192]{1,0:T(1,128)S(1)} %get-tuple-element.25.refs_2_.refs_4_, ...), custom_call_target="tpu_custom_call" | custom-call | flops 200000000 | bytes 3000000 | tf_op jit(solution)/shard_map/swin_windows/pallas_call | solution.py:347
  15.4 1.6 %collective-permute-start.3 = (bf16[2,3,4,1152]{3,2,1,0:T(4,128)(2,1)S(1)}, bf16[2,3,4,1152]{3,2,1,0:T(4,128)(2,1)S(1)}, u32[]{:S(2)}, u32[]{:S(2)}) collective-permute-start(bf16[2,3,4,1152]{3,2,1,0:T(4,128)(2,1)S(1)} %get-tuple-element.40), channel_id=1, source_target_pairs={{0,1},{1,0},{2,3},{3,2},{4,5},{5,4},{6,7},{7,6},{8,9},{9,8},{10,11... | collective-permute-start | bytes 165896 | tf_op jit(solution)/shard_map/ppermute | solution.py:29
  17.0 0.0 collective-permute-done.4.refs_1_
  17.0 2.6 %swin_windows.5.high_ref = bf16[2,6,4,1152]{3,2,1,0:T(4,128)(2,1)S(1)} custom-call(bf16[6,4,1152]{2,1,0:T(4,128)(2,1)S(1)} %get-tuple-element.35.refs_11_.refs_0_, bf16[6,4,1152]{2,1,0:T(4,128)(2,1)S(1)} %collective-permute-done.4.refs_1_, bf16[12,4,1152]{2,1,0:T(4,128)(2,1)S(1)} %pack_half.2._.refs_10_.refs_0_.refs_2_, ...), custom_call_target="tpu_custom_call" | custom-call | flops 400000000 | bytes 3000000 | tf_op jit(solution)/shard_map/swin_windows/pallas_call | solution.py:347
  19.6 0.0 collective-permute-done.3.top_ref
  19.6 0.7 %last_rows.1 = bf16[12,4,2304]{2,1,0:T(4,128)(2,1)} custom-call(bf16[2,3,4,1152]{3,2,1,0:T(4,128)(2,1)S(1)} %collective-permute-done.3.top_ref, bf16[2,6,4,1152]{3,2,1,0:T(4,128)(2,1)S(1)} %swin_windows.5.high_ref, bf16[1,6,4,1152]{3,2,1,0:T(4,128)(2,1)S(1)} %get-tuple-element.39.refs_12_.near_low_ref, bf16[1,6,4,1152]{3,2,1,0:T(4,128)(2,1)S(1)} %get-tuple-element.42.far_low_ref), custom_call_target="tpu_custom_call" | custom-call | bytes 400000 | tf_op jit(solution)/shard_map/last_rows/pallas_call | solution.py:431
  (2 shorter events, 0.0 us)
Async XLA Ops:
  0.8 5.1 %collective-permute-start = (bf16[3,4,2304]{2,1,0:T(4,128)(2,1)S(1)}, bf16[3,4,2304]{2,1,0:T(4,128)(2,1)S(1)}, u32[]{:S(2)}, u32[]{:S(2)}) collective-permute-start(bf16[3,4,2304]{2,1,0:T(4,128)(2,1)S(1)} %slice.4), channel_id=1, source_target_pairs={{0,1},{1,0},{2,3},{3,2},{4,5},{5,4},{6,7},{7,6},{8,9},{9,8},{10,11... | collective-permute-start | bytes 165896 | tf_op jit(solution)/shard_map/ppermute | solution.py:29
  6.0 7.4 %collective-permute-start.1 = (bf16[12,4,1152]{2,1,0:T(4,128)(2,1)S(1)}, bf16[12,4,1152]{2,1,0:T(4,128)(2,1)S(1)}, u32[]{:S(2)}, u32[]{:S(2)}) collective-permute-start(bf16[12,4,1152]{2,1,0:T(4,128)(2,1)S(1)} %pack_half.2._.refs_10_.refs_0_.refs_2_), channel_id=1, source_target_pairs={{2,4},{4,2},{6,8},{8,6},{10,12},{12,10},{14,16},{16,14},{18,20},{2... | collective-permute-start | bytes 331784 | tf_op jit(solution)/shard_map/ppermute | solution.py:38
  9.6 1.3 %collective-permute-start.2 = (bf16[6,4,1152]{2,1,0:T(4,128)(2,1)S(1)}, bf16[6,4,1152]{2,1,0:T(4,128)(2,1)S(1)}, u32[]{:S(2)}, u32[]{:S(2)}) collective-permute-start(bf16[6,4,1152]{2,1,0:T(4,128)(2,1)S(1)} %get-tuple-element.33.refs_0_), channel_id=1, source_target_pairs={{0,2},{2,0},{4,6},{6,4},{8,10},{10,8},{12,14},{14,12},{16,18},{18,... | collective-permute-start | bytes 165896 | tf_op jit(solution)/shard_map/ppermute | solution.py:38
  9.7 7.3 %collective-permute-start.4 = (bf16[6,4,1152]{2,1,0:T(4,128)(2,1)S(1)}, bf16[6,4,1152]{2,1,0:T(4,128)(2,1)S(1)}, u32[]{:S(2)}, u32[]{:S(2)}) collective-permute-start(bf16[6,4,1152]{2,1,0:T(4,128)(2,1)S(1)} %get-tuple-element.35.refs_11_.refs_0_), channel_id=1, source_target_pairs={{0,2},{2,0},{4,6},{6,4},{8,10},{10,8},{12,14},{14,12},{16,18},{18,... | collective-permute-start | bytes 165896 | tf_op jit(solution)/shard_map/ppermute | solution.py:38
  15.4 4.3 %collective-permute-start.3 = (bf16[2,3,4,1152]{3,2,1,0:T(4,128)(2,1)S(1)}, bf16[2,3,4,1152]{3,2,1,0:T(4,128)(2,1)S(1)}, u32[]{:S(2)}, u32[]{:S(2)}) collective-permute-start(bf16[2,3,4,1152]{3,2,1,0:T(4,128)(2,1)S(1)} %get-tuple-element.40), channel_id=1, source_target_pairs={{0,1},{1,0},{2,3},{3,2},{4,5},{5,4},{6,7},{7,6},{8,9},{9,8},{10,11... | collective-permute-start | bytes 165896 | tf_op jit(solution)/shard_map/ppermute | solution.py:29

commit v21 on v20

--- a/solution.py
+++ b/solution.py
@@ -160,8 +160,9 @@
 
 
 def gelu(x):
-    half = 0.5 * x
-    return half + half * jnp.tanh(x * (GELU_0 + GELU_1 * (x * x)))
+    one, zero = jnp.asarray(GELU_1, x.dtype), jnp.asarray(GELU_0, x.dtype)
+    half = jnp.asarray(0.5, x.dtype) * x
+    return half + half * jnp.tanh(x * (zero + one * (x * x)))
 
 
 def units_kernel(chans, heads, units, extra, *refs):
@@ -301,7 +302,7 @@
     hidden = first_product(blocks[0])
     for b, at in enumerate(blocks):
         following = first_product(blocks[b + 1]) if b + 1 < len(blocks) else None
-        active = gelu(hidden).astype(jnp.bfloat16)
+        active = gelu(hidden.astype(jnp.bfloat16))
         result = result + lax.dot_general(
             active, fc2_ref[:, at], NT, preferred_element_type=jnp.float32
         )

time: 20.6 us -> 20.5 us (level)
  no operation moved by 1% of the time
where the time goes in v21:
time: 20.5 us; the launch traced here: 20.3 us
  Pallas kernels  9.62 us (47%)
  starting transfers between devices  8.85 us (43%)
  waiting for transfers between devices  0.92 us (4%)
  local copies, waits for them, and re-layouts  0.83 us (4%)
    pallas_call x3, Pallas kernels, run_units(): pl.pallas_call(functools.partial(units_kernel, chans, heads, units, extra...  6.9 us
    ppermute x2, starting transfers between devices, moved(): return lax.ppermute(x, axis, [(i, (i + by) % size) for i in range(size)])  4.67 us
    ppermute x3, starting transfers between devices, swapped(): return lax.ppermute(x, axis, pairs)  4.18 us
    pallas_call x1, Pallas kernels, shards(): pl.pallas_call(functools.partial(table_kernel, len(weights), heads), out_...  1.95 us
    slice x1, local copies, waits for them, and re-layouts, shards(): south = moved(field[:EDGE], 'lat', -1)  0.83 us
    pallas_call x1, Pallas kernels, shards(): pl.pallas_call(last_kernel, out_shape=jax.ShapeDtypeStruct(field.shape, f...  0.74 us
    ppermute x3, waiting for transfers between devices, swapped(): return lax.ppermute(x, axis, pairs)  0.73 us
  transfers between devices with their start and end apart: 5, of which 2 were waited for; matrix products, arithmetic and copies ran while one was open for 0% of the time, Pallas kernels for 44%

profile of v21, /device:TPU:0, one launch (start us, length us, event | category | flops | bytes accessed | tf_op | source)
XLA Modules:
  0.0 20.3 jit_solution(1173374841796861978)
XLA Ops:
  0.0 0.8 %slice.4 = bf16[3,4,2304]{2,1,0:T(4,128)(2,1)S(1)} slice(bf16[12,4,2304]{2,1,0:T(4,128)(2,1)} %bitcast.9), slice={[0:3], [0:4], [0:2304]} | slice | bytes 110592 | tf_op jit(solution)/shard_map/slice | solution.py:374
  0.8 3.0 %collective-permute-start = (bf16[3,4,2304]{2,1,0:T(4,128)(2,1)S(1)}, bf16[3,4,2304]{2,1,0:T(4,128)(2,1)S(1)}, u32[]{:S(2)}, u32[]{:S(2)}) collective-permute-start(bf16[3,4,2304]{2,1,0:T(4,128)(2,1)S(1)} %slice.4), channel_id=1, source_target_pairs={{0,1},{1,0},{2,3},{3,2},{4,5},{5,4},{6,7},{7,6},{8,9},{9,8},{10,11... | collective-permute-start | bytes 165896 | tf_op jit(solution)/shard_map/ppermute | solution.py:29
  3.8 1.9 %bias_tables.1 = (f32[2,2,2,432,128]{4,3,2,1,0:T(8,128)S(1)}, f32[1944,128]{1,0:T(8,128)S(1)}, bf16[12,4,1152]{2,1,0:T(4,128)(2,1)S(1)}, bf16[12,4,1152]{2,1,0:T...) custom-call(f32[2,6,162,2,128]{4,3,2,1,0:T(2,128)} %bitcast.8, ...), custom_call_target="tpu_custom_call" | custom-call | flops 4000000 | bytes 6000000 | tf_op jit(solution)/shard_map/bias_tables/pallas_call | solution.py:394
  5.8 0.2 collective-permute-done.south_ref
  6.0 3.6 %collective-permute-start.1 = (bf16[12,4,1152]{2,1,0:T(4,128)(2,1)S(1)}, bf16[12,4,1152]{2,1,0:T(4,128)(2,1)S(1)}, u32[]{:S(2)}, u32[]{:S(2)}) collective-permute-start(bf16[12,4,1152]{2,1,0:T(4,128)(2,1)S(1)} %pack_half.2._.refs_10_.refs_0_.refs_2_), channel_id=1, source_target_pairs={{2,4},{4,2},{6,8},{8,6},{10,12},{12,10},{14,16},{16,14},{18,20},{2... | collective-permute-start | bytes 331784 | tf_op jit(solution)/shard_map/ppermute | solution.py:38
  9.6 0.1 collective-permute-start.2
  9.7 0.5 %collective-permute-start.4 = (bf16[6,4,1152]{2,1,0:T(4,128)(2,1)S(1)}, bf16[6,4,1152]{2,1,0:T(4,128)(2,1)S(1)}, u32[]{:S(2)}, u32[]{:S(2)}) collective-permute-start(bf16[6,4,1152]{2,1,0:T(4,128)(2,1)S(1)} %get-tuple-element.35.refs_11_.refs_0_), channel_id=1, source_target_pairs={{0,2},{2,0},{4,6},{6,4},{8,10},{10,8},{12,14},{14,12},{16,18},{18,... | collective-permute-start | bytes 165896 | tf_op jit(solution)/shard_map/ppermute | solution.py:38
  10.2 0.7 %collective-permute-done.2.refs_1_ = bf16[6,4,1152]{2,1,0:T(4,128)(2,1)S(1)} collective-permute-done((bf16[6,4,1152]{2,1,0:T(4,128)(2,1)S(1)}, bf16[6,4,1152]{2,1,0:T(4,128)(2,1)S(1)}, u32[]{:S(2)}, u32[]{:S(2)}) %collective-permute-start.2) | collective-permute-done | bytes 55328 | tf_op jit(solution)/shard_map/ppermute | solution.py:38
  10.9 2.4 %swin_windows.3 = (bf16[1,6,4,1152]{3,2,1,0:T(4,128)(2,1)S(1)}, f32[2,2,2,432,128]{4,3,2,1,0:T(8,128)S(1)}, f32[3,2,288,128]{3,2,1,0:T(8,128)S(1)}, f32[3,2,184,...) custom-call(bf16[6,4,1152]{2,1,0:T(4,128)(2,1)S(1)} %get-tuple-element.33.refs_0_, ...), custom_call_target="tpu_custom_call" | custom-call | flops 200000000 | bytes 3000000 | tf_op jit(solution)/shard_map/swin_windows/pallas_call | solution.py:348
  13.3 0.0 collective-permute-done.1.refs_1_.refs_3_
  13.4 2.0 %swin_windows.4 = (bf16[1,6,4,1152]{3,2,1,0:T(4,128)(2,1)S(1)}, bf16[2,3,4,1152]{3,2,1,0:T(4,128)(2,1)S(1)}) custom-call(bf16[12,4,1152]{2,1,0:T(4,128)(2,1)S(1)} %pack_half.2._.refs_10_.refs_0_.refs_2_, bf16[12,4,1152]{2,1,0:T(4,128)(2,1)S(1)} %collective-permute-done.1.refs_1_.refs_3_, f32[1,192]{1,0:T(1,128)S(1)} %get-tuple-element.25.refs_2_.refs_4_, ...), custom_call_target="tpu_custom_call" | custom-call | flops 200000000 | bytes 3000000 | tf_op jit(solution)/shard_map/swin_windows/pallas_call | solution.py:348
  15.3 1.7 %collective-permute-start.3 = (bf16[2,3,4,1152]{3,2,1,0:T(4,128)(2,1)S(1)}, bf16[2,3,4,1152]{3,2,1,0:T(4,128)(2,1)S(1)}, u32[]{:S(2)}, u32[]{:S(2)}) collective-permute-start(bf16[2,3,4,1152]{3,2,1,0:T(4,128)(2,1)S(1)} %get-tuple-element.40), channel_id=1, source_target_pairs={{0,1},{1,0},{2,3},{3,2},{4,5},{5,4},{6,7},{7,6},{8,9},{9,8},{10,11... | collective-permute-start | bytes 165896 | tf_op jit(solution)/shard_map/ppermute | solution.py:29
  17.0 0.0 collective-permute-done.4.refs_1_
  17.0 2.6 %swin_windows.5.high_ref = bf16[2,6,4,1152]{3,2,1,0:T(4,128)(2,1)S(1)} custom-call(bf16[6,4,1152]{2,1,0:T(4,128)(2,1)S(1)} %get-tuple-element.35.refs_11_.refs_0_, bf16[6,4,1152]{2,1,0:T(4,128)(2,1)S(1)} %collective-permute-done.4.refs_1_, bf16[12,4,1152]{2,1,0:T(4,128)(2,1)S(1)} %pack_half.2._.refs_10_.refs_0_.refs_2_, ...), custom_call_target="tpu_custom_call" | custom-call | flops 400000000 | bytes 3000000 | tf_op jit(solution)/shard_map/swin_windows/pallas_call | solution.py:348
  19.6 0.0 collective-permute-done.3.top_ref
  19.6 0.7 %last_rows.1 = bf16[12,4,2304]{2,1,0:T(4,128)(2,1)} custom-call(bf16[2,3,4,1152]{3,2,1,0:T(4,128)(2,1)S(1)} %collective-permute-done.3.top_ref, bf16[2,6,4,1152]{3,2,1,0:T(4,128)(2,1)S(1)} %swin_windows.5.high_ref, bf16[1,6,4,1152]{3,2,1,0:T(4,128)(2,1)S(1)} %get-tuple-element.39.refs_12_.near_low_ref, bf16[1,6,4,1152]{3,2,1,0:T(4,128)(2,1)S(1)} %get-tuple-element.42.far_low_ref), custom_call_target="tpu_custom_call" | custom-call | bytes 400000 | tf_op jit(solution)/shard_map/last_rows/pallas_call | solution.py:432
  (2 shorter events, 0.0 us)
Async XLA Ops:
  0.8 5.1 %collective-permute-start = (bf16[3,4,2304]{2,1,0:T(4,128)(2,1)S(1)}, bf16[3,4,2304]{2,1,0:T(4,128)(2,1)S(1)}, u32[]{:S(2)}, u32[]{:S(2)}) collective-permute-start(bf16[3,4,2304]{2,1,0:T(4,128)(2,1)S(1)} %slice.4), channel_id=1, source_target_pairs={{0,1},{1,0},{2,3},{3,2},{4,5},{5,4},{6,7},{7,6},{8,9},{9,8},{10,11... | collective-permute-start | bytes 165896 | tf_op jit(solution)/shard_map/ppermute | solution.py:29
  6.0 7.3 %collective-permute-start.1 = (bf16[12,4,1152]{2,1,0:T(4,128)(2,1)S(1)}, bf16[12,4,1152]{2,1,0:T(4,128)(2,1)S(1)}, u32[]{:S(2)}, u32[]{:S(2)}) collective-permute-start(bf16[12,4,1152]{2,1,0:T(4,128)(2,1)S(1)} %pack_half.2._.refs_10_.refs_0_.refs_2_), channel_id=1, source_target_pairs={{2,4},{4,2},{6,8},{8,6},{10,12},{12,10},{14,16},{16,14},{18,20},{2... | collective-permute-start | bytes 331784 | tf_op jit(solution)/shard_map/ppermute | solution.py:38
  9.6 1.3 %collective-permute-start.2 = (bf16[6,4,1152]{2,1,0:T(4,128)(2,1)S(1)}, bf16[6,4,1152]{2,1,0:T(4,128)(2,1)S(1)}, u32[]{:S(2)}, u32[]{:S(2)}) collective-permute-start(bf16[6,4,1152]{2,1,0:T(4,128)(2,1)S(1)} %get-tuple-element.33.refs_0_), channel_id=1, source_target_pairs={{0,2},{2,0},{4,6},{6,4},{8,10},{10,8},{12,14},{14,12},{16,18},{18,... | collective-permute-start | bytes 165896 | tf_op jit(solution)/shard_map/ppermute | solution.py:38
  9.7 7.3 %collective-permute-start.4 = (bf16[6,4,1152]{2,1,0:T(4,128)(2,1)S(1)}, bf16[6,4,1152]{2,1,0:T(4,128)(2,1)S(1)}, u32[]{:S(2)}, u32[]{:S(2)}) collective-permute-start(bf16[6,4,1152]{2,1,0:T(4,128)(2,1)S(1)} %get-tuple-element.35.refs_11_.refs_0_), channel_id=1, source_target_pairs={{0,2},{2,0},{4,6},{6,4},{8,10},{10,8},{12,14},{14,12},{16,18},{18,... | collective-permute-start | bytes 165896 | tf_op jit(solution)/shard_map/ppermute | solution.py:38
  15.3 4.2 %collective-permute-start.3 = (bf16[2,3,4,1152]{3,2,1,0:T(4,128)(2,1)S(1)}, bf16[2,3,4,1152]{3,2,1,0:T(4,128)(2,1)S(1)}, u32[]{:S(2)}, u32[]{:S(2)}) collective-permute-start(bf16[2,3,4,1152]{3,2,1,0:T(4,128)(2,1)S(1)} %get-tuple-element.40), channel_id=1, source_target_pairs={{0,1},{1,0},{2,3},{3,2},{4,5},{5,4},{6,7},{7,6},{8,9},{9,8},{10,11... | collective-permute-start | bytes 165896 | tf_op jit(solution)/shard_map/ppermute | solution.py:29

commit v22 on v21

--- a/solution.py
+++ b/solution.py
@@ -282,7 +282,9 @@
             out = None
             for h in range(heads):
                 part = got[n, p][h * QUERIES : (h + 1) * QUERIES]
-                scaled = part[:, :chans] * (1.0 / part[:, chans : chans + 1])
+                total = part[:, chans : chans + 1]
+                inverse = pl.reciprocal(total, approx=True)
+                scaled = part[:, :chans] * (inverse * (2.0 - total * inverse))
                 out = jnp.where(lane >= h * head_dim, scaled, out) if h else scaled
             mixed.append(out)
     mixed = jnp.concatenate(mixed, axis=0).astype(jnp.bfloat16)

time: 20.5 us -> 20.5 us (level)
  no operation moved by 1% of the time
where the time goes in v22:
time: 20.5 us; the launch traced here: 20.3 us
  Pallas kernels  9.62 us (47%)
  starting transfers between devices  8.86 us (43%)
  waiting for transfers between devices  0.92 us (4%)
  local copies, waits for them, and re-layouts  0.83 us (4%)
    pallas_call x3, Pallas kernels, run_units(): pl.pallas_call(functools.partial(units_kernel, chans, heads, units, extra...  6.9 us
    ppermute x2, starting transfers between devices, moved(): return lax.ppermute(x, axis, [(i, (i + by) % size) for i in range(size)])  4.68 us
    ppermute x3, starting transfers between devices, swapped(): return lax.ppermute(x, axis, pairs)  4.18 us
    pallas_call x1, Pallas kernels, shards(): pl.pallas_call(functools.partial(table_kernel, len(weights), heads), out_...  1.95 us
    slice x1, local copies, waits for them, and re-layouts, shards(): south = moved(field[:EDGE], 'lat', -1)  0.83 us
    pallas_call x1, Pallas kernels, shards(): pl.pallas_call(last_kernel, out_shape=jax.ShapeDtypeStruct(field.shape, f...  0.74 us
    ppermute x3, waiting for transfers between devices, swapped(): return lax.ppermute(x, axis, pairs)  0.73 us
  transfers between devices with their start and end apart: 5, of which 2 were waited for; matrix products, arithmetic and copies ran while one was open for 0% of the time, Pallas kernels for 44%

profile of v22, /device:TPU:0, one launch (start us, length us, event | category | flops | bytes accessed | tf_op | source)
XLA Modules:
  0.0 20.3 jit_solution(866397857353024730)
XLA Ops:
  0.0 0.8 %slice.4 = bf16[3,4,2304]{2,1,0:T(4,128)(2,1)S(1)} slice(bf16[12,4,2304]{2,1,0:T(4,128)(2,1)} %bitcast.9), slice={[0:3], [0:4], [0:2304]} | slice | bytes 110592 | tf_op jit(solution)/shard_map/slice | solution.py:376
  0.8 3.0 %collective-permute-start = (bf16[3,4,2304]{2,1,0:T(4,128)(2,1)S(1)}, bf16[3,4,2304]{2,1,0:T(4,128)(2,1)S(1)}, u32[]{:S(2)}, u32[]{:S(2)}) collective-permute-start(bf16[3,4,2304]{2,1,0:T(4,128)(2,1)S(1)} %slice.4), channel_id=1, source_target_pairs={{0,1},{1,0},{2,3},{3,2},{4,5},{5,4},{6,7},{7,6},{8,9},{9,8},{10,11... | collective-permute-start | bytes 165896 | tf_op jit(solution)/shard_map/ppermute | solution.py:29
  3.8 1.9 %bias_tables.1 = (f32[2,2,2,432,128]{4,3,2,1,0:T(8,128)S(1)}, f32[1944,128]{1,0:T(8,128)S(1)}, bf16[12,4,1152]{2,1,0:T(4,128)(2,1)S(1)}, bf16[12,4,1152]{2,1,0:T...) custom-call(f32[2,6,162,2,128]{4,3,2,1,0:T(2,128)} %bitcast.8, ...), custom_call_target="tpu_custom_call" | custom-call | flops 4000000 | bytes 6000000 | tf_op jit(solution)/shard_map/bias_tables/pallas_call | solution.py:396
  5.8 0.2 collective-permute-done.south_ref
  6.0 3.6 %collective-permute-start.1 = (bf16[12,4,1152]{2,1,0:T(4,128)(2,1)S(1)}, bf16[12,4,1152]{2,1,0:T(4,128)(2,1)S(1)}, u32[]{:S(2)}, u32[]{:S(2)}) collective-permute-start(bf16[12,4,1152]{2,1,0:T(4,128)(2,1)S(1)} %pack_half.2._.refs_10_.refs_0_.refs_2_), channel_id=1, source_target_pairs={{2,4},{4,2},{6,8},{8,6},{10,12},{12,10},{14,16},{16,14},{18,20},{2... | collective-permute-start | bytes 331784 | tf_op jit(solution)/shard_map/ppermute | solution.py:38
  9.6 0.1 collective-permute-start.2
  9.7 0.5 %collective-permute-start.4 = (bf16[6,4,1152]{2,1,0:T(4,128)(2,1)S(1)}, bf16[6,4,1152]{2,1,0:T(4,128)(2,1)S(1)}, u32[]{:S(2)}, u32[]{:S(2)}) collective-permute-start(bf16[6,4,1152]{2,1,0:T(4,128)(2,1)S(1)} %get-tuple-element.35.refs_11_.refs_0_), channel_id=1, source_target_pairs={{0,2},{2,0},{4,6},{6,4},{8,10},{10,8},{12,14},{14,12},{16,18},{18,... | collective-permute-start | bytes 165896 | tf_op jit(solution)/shard_map/ppermute | solution.py:38
  10.2 0.7 %collective-permute-done.2.refs_1_ = bf16[6,4,1152]{2,1,0:T(4,128)(2,1)S(1)} collective-permute-done((bf16[6,4,1152]{2,1,0:T(4,128)(2,1)S(1)}, bf16[6,4,1152]{2,1,0:T(4,128)(2,1)S(1)}, u32[]{:S(2)}, u32[]{:S(2)}) %collective-permute-start.2) | collective-permute-done | bytes 55328 | tf_op jit(solution)/shard_map/ppermute | solution.py:38
  10.9 2.4 %swin_windows.3 = (bf16[1,6,4,1152]{3,2,1,0:T(4,128)(2,1)S(1)}, f32[2,2,2,432,128]{4,3,2,1,0:T(8,128)S(1)}, f32[3,2,288,128]{3,2,1,0:T(8,128)S(1)}, f32[3,2,184,...) custom-call(bf16[6,4,1152]{2,1,0:T(4,128)(2,1)S(1)} %get-tuple-element.33.refs_0_, ...), custom_call_target="tpu_custom_call" | custom-call | flops 200000000 | bytes 3000000 | tf_op jit(solution)/shard_map/swin_windows/pallas_call | solution.py:350
  13.3 0.0 collective-permute-done.1.refs_1_.refs_3_
  13.3 2.0 %swin_windows.4 = (bf16[1,6,4,1152]{3,2,1,0:T(4,128)(2,1)S(1)}, bf16[2,3,4,1152]{3,2,1,0:T(4,128)(2,1)S(1)}) custom-call(bf16[12,4,1152]{2,1,0:T(4,128)(2,1)S(1)} %pack_half.2._.refs_10_.refs_0_.refs_2_, bf16[12,4,1152]{2,1,0:T(4,128)(2,1)S(1)} %collective-permute-done.1.refs_1_.refs_3_, f32[1,192]{1,0:T(1,128)S(1)} %get-tuple-element.25.refs_2_.refs_4_, ...), custom_call_target="tpu_custom_call" | custom-call | flops 200000000 | bytes 3000000 | tf_op jit(solution)/shard_map/swin_windows/pallas_call | solution.py:350
  15.3 1.7 %collective-permute-start.3 = (bf16[2,3,4,1152]{3,2,1,0:T(4,128)(2,1)S(1)}, bf16[2,3,4,1152]{3,2,1,0:T(4,128)(2,1)S(1)}, u32[]{:S(2)}, u32[]{:S(2)}) collective-permute-start(bf16[2,3,4,1152]{3,2,1,0:T(4,128)(2,1)S(1)} %get-tuple-element.40), channel_id=1, source_target_pairs={{0,1},{1,0},{2,3},{3,2},{4,5},{5,4},{6,7},{7,6},{8,9},{9,8},{10,11... | collective-permute-start | bytes 165896 | tf_op jit(solution)/shard_map/ppermute | solution.py:29
  17.0 0.0 collective-permute-done.4.refs_1_
  17.0 2.6 %swin_windows.5.high_ref = bf16[2,6,4,1152]{3,2,1,0:T(4,128)(2,1)S(1)} custom-call(bf16[6,4,1152]{2,1,0:T(4,128)(2,1)S(1)} %get-tuple-element.35.refs_11_.refs_0_, bf16[6,4,1152]{2,1,0:T(4,128)(2,1)S(1)} %collective-permute-done.4.refs_1_, bf16[12,4,1152]{2,1,0:T(4,128)(2,1)S(1)} %pack_half.2._.refs_10_.refs_0_.refs_2_, ...), custom_call_target="tpu_custom_call" | custom-call | flops 400000000 | bytes 3000000 | tf_op jit(solution)/shard_map/swin_windows/pallas_call | solution.py:350
  19.6 0.0 collective-permute-done.3.top_ref
  19.6 0.7 %last_rows.1 = bf16[12,4,2304]{2,1,0:T(4,128)(2,1)} custom-call(bf16[2,3,4,1152]{3,2,1,0:T(4,128)(2,1)S(1)} %collective-permute-done.3.top_ref, bf16[2,6,4,1152]{3,2,1,0:T(4,128)(2,1)S(1)} %swin_windows.5.high_ref, bf16[1,6,4,1152]{3,2,1,0:T(4,128)(2,1)S(1)} %get-tuple-element.39.refs_12_.near_low_ref, bf16[1,6,4,1152]{3,2,1,0:T(4,128)(2,1)S(1)} %get-tuple-element.42.far_low_ref), custom_call_target="tpu_custom_call" | custom-call | bytes 400000 | tf_op jit(solution)/shard_map/last_rows/pallas_call | solution.py:434
  (2 shorter events, 0.0 us)
Async XLA Ops:
  0.8 5.1 %collective-permute-start = (bf16[3,4,2304]{2,1,0:T(4,128)(2,1)S(1)}, bf16[3,4,2304]{2,1,0:T(4,128)(2,1)S(1)}, u32[]{:S(2)}, u32[]{:S(2)}) collective-permute-start(bf16[3,4,2304]{2,1,0:T(4,128)(2,1)S(1)} %slice.4), channel_id=1, source_target_pairs={{0,1},{1,0},{2,3},{3,2},{4,5},{5,4},{6,7},{7,6},{8,9},{9,8},{10,11... | collective-permute-start | bytes 165896 | tf_op jit(solution)/shard_map/ppermute | solution.py:29
  6.0 7.3 %collective-permute-start.1 = (bf16[12,4,1152]{2,1,0:T(4,128)(2,1)S(1)}, bf16[12,4,1152]{2,1,0:T(4,128)(2,1)S(1)}, u32[]{:S(2)}, u32[]{:S(2)}) collective-permute-start(bf16[12,4,1152]{2,1,0:T(4,128)(2,1)S(1)} %pack_half.2._.refs_10_.refs_0_.refs_2_), channel_id=1, source_target_pairs={{2,4},{4,2},{6,8},{8,6},{10,12},{12,10},{14,16},{16,14},{18,20},{2... | collective-permute-start | bytes 331784 | tf_op jit(solution)/shard_map/ppermute | solution.py:38
  9.6 1.3 %collective-permute-start.2 = (bf16[6,4,1152]{2,1,0:T(4,128)(2,1)S(1)}, bf16[6,4,1152]{2,1,0:T(4,128)(2,1)S(1)}, u32[]{:S(2)}, u32[]{:S(2)}) collective-permute-start(bf16[6,4,1152]{2,1,0:T(4,128)(2,1)S(1)} %get-tuple-element.33.refs_0_), channel_id=1, source_target_pairs={{0,2},{2,0},{4,6},{6,4},{8,10},{10,8},{12,14},{14,12},{16,18},{18,... | collective-permute-start | bytes 165896 | tf_op jit(solution)/shard_map/ppermute | solution.py:38
  9.7 7.3 %collective-permute-start.4 = (bf16[6,4,1152]{2,1,0:T(4,128)(2,1)S(1)}, bf16[6,4,1152]{2,1,0:T(4,128)(2,1)S(1)}, u32[]{:S(2)}, u32[]{:S(2)}) collective-permute-start(bf16[6,4,1152]{2,1,0:T(4,128)(2,1)S(1)} %get-tuple-element.35.refs_11_.refs_0_), channel_id=1, source_target_pairs={{0,2},{2,0},{4,6},{6,4},{8,10},{10,8},{12,14},{14,12},{16,18},{18,... | collective-permute-start | bytes 165896 | tf_op jit(solution)/shard_map/ppermute | solution.py:38
  15.3 4.3 %collective-permute-start.3 = (bf16[2,3,4,1152]{3,2,1,0:T(4,128)(2,1)S(1)}, bf16[2,3,4,1152]{3,2,1,0:T(4,128)(2,1)S(1)}, u32[]{:S(2)}, u32[]{:S(2)}) collective-permute-start(bf16[2,3,4,1152]{3,2,1,0:T(4,128)(2,1)S(1)} %get-tuple-element.40), channel_id=1, source_target_pairs={{0,1},{1,0},{2,3},{3,2},{4,5},{5,4},{6,7},{7,6},{8,9},{9,8},{10,11... | collective-permute-start | bytes 165896 | tf_op jit(solution)/shard_map/ppermute | solution.py:29

commit v23 on v21

--- a/solution.py
+++ b/solution.py
@@ -77,7 +77,7 @@
 
 
 def build_tables(bias_ref, table_ref, heads, wrap):
-    lines = bias_ref.shape[0] // heads
+    lines = 2 * TOKENS * TOKENS // LANES
     blocks = WIN_LEV * WIN_LAT // 2
     lane = lax.broadcasted_iota(jnp.int32, (blocks, LANES), 1)
     block = lax.broadcasted_iota(jnp.int32, (blocks, LANES), 0)
@@ -130,15 +130,15 @@
     bias_any, field_any, *weights_any = refs[: 2 + count]
     table_ref, inner_ref, near_ref, far_ref, *weights_ref = refs[2 + count : 6 + 2 * count]
     bias_ref, sems = refs[6 + 2 * count :]
-    lines = bias_ref.shape[0]
+    lines = heads * 2 * TOKENS * TOKENS // LANES
     flat = bias_any.reshape(2 * lines, LANES)
     rows, half = field_any.shape[0] - EDGE, near_ref.shape[2]
     near_at, far_at = half_places(half)
     fetches = [
-        (flat.at[pl.ds(lines, lines)], bias_ref),
+        (flat.at[pl.ds(lines, lines)], bias_ref.at[pl.ds(0, lines)]),
         (field_any.at[EDGE:, :, pl.ds(far_at, half)], far_ref.at[:rows]),
         (field_any.at[EDGE:, :, pl.ds(near_at, half)], near_ref.at[:rows]),
-        (flat.at[pl.ds(0, lines)], inner_ref),
+        (flat.at[pl.ds(0, lines)], inner_ref.at[pl.ds(0, lines)]),
     ]
     fetches += list(zip(weights_any, weights_ref))
     fetches = [
@@ -340,8 +340,8 @@
     elif extra == "ahead":
         outs += [
             jax.ShapeDtypeStruct(table.shape, table.dtype),
-            jax.ShapeDtypeStruct((3, 2, LEVELS * QUERIES, LANES), jnp.float32),
-            jax.ShapeDtypeStruct((3, 2, 184, LANES), jnp.float32),
+            jax.ShapeDtypeStruct((4, 2, LEVELS * QUERIES, LANES), jnp.float32),
+            jax.ShapeDtypeStruct((4, 2, 184, LANES), jnp.float32),
             jax.ShapeDtypeStruct((3, 2 * heads * QUERIES, chans), jnp.bfloat16),
         ]
     vmem = pl.BlockSpec(memory_space=pltpu.VMEM)
@@ -351,9 +351,9 @@
         in_specs=[vmem] * len(operands),
         out_specs=[vmem] * len(outs),
         scratch_shapes=[
-            pltpu.VMEM((count, 2, LEVELS * QUERIES, LANES), jnp.float32),
-            pltpu.VMEM((count, 2, 184, LANES), jnp.float32),
-            pltpu.VMEM((count, 2, 184, LANES), jnp.float32),
+            pltpu.VMEM((count + 1, 2, LEVELS * QUERIES, LANES), jnp.float32),
+            pltpu.VMEM((count + 1, 2, 184, LANES), jnp.float32),
+            pltpu.VMEM((count + 1, 2, 184, LANES), jnp.float32),
         ],
         compiler_params=pltpu.CompilerParams(vmem_limit_bytes=VMEM_BYTES),
         cost_estimate=pl.CostEstimate(
@@ -383,12 +383,12 @@
     vmem = pl.BlockSpec(memory_space=pltpu.VMEM)
     anywhere = pl.BlockSpec(memory_space=pl.ANY)
     piece = jax.ShapeDtypeStruct((rows, levels, half), field.dtype)
-    table = jax.ShapeDtypeStruct((2, 2, 2, heads * QUERIES, LANES), jnp.float32)
+    table = jax.ShapeDtypeStruct((2, 2, 2, heads * QUERIES + 24, LANES), jnp.float32)
     windows, zwin, _, entries = earth_bias.shape
     tiles = entries // LANES
     bias = earth_bias.reshape(windows, zwin, heads, tiles, LANES).transpose(0, 2, 3, 1, 4)
     sources = (bias, field) + weights
-    raw = jax.ShapeDtypeStruct((bias.size // windows // LANES, LANES), bias.dtype)
+    raw = jax.ShapeDtypeStruct((bias.size // windows // LANES + 112, LANES), bias.dtype)
     sources = [pltpu.with_memory_space_constraint(x, pltpu.HBM) for x in sources]
     outs = [table, raw, piece, piece] + [jax.ShapeDtypeStruct(x.shape, x.dtype) for x in weights]
     table, inner, near, far, *weights = pl.pallas_call(

time: 20.5 us -> 20.5 us (level)
  transfers between devices with their start and end apart: 5 -> 5, of which waited for: 2 -> 2; matrix products, arithmetic and copies ran while one was open for 0% -> 0% of each run, Pallas kernels for 44% -> 43%
where the time goes in v23:
time: 20.5 us; the launch traced here: 20.3 us
  Pallas kernels  9.57 us (47%)
  starting transfers between devices  8.89 us (43%)
  waiting for transfers between devices  0.92 us (4%)
  local copies, waits for them, and re-layouts  0.83 us (4%)
    pallas_call x3, Pallas kernels, run_units(): pl.pallas_call(functools.partial(units_kernel, chans, heads, units, extra...  6.85 us
    ppermute x2, starting transfers between devices, moved(): return lax.ppermute(x, axis, [(i, (i + by) % size) for i in range(size)])  4.7 us
    ppermute x3, starting transfers between devices, swapped(): return lax.ppermute(x, axis, pairs)  4.18 us
    pallas_call x1, Pallas kernels, shards(): pl.pallas_call(functools.partial(table_kernel, len(weights), heads), out_...  1.95 us
    slice x1, local copies, waits for them, and re-layouts, shards(): south = moved(field[:EDGE], 'lat', -1)  0.83 us
    pallas_call x1, Pallas kernels, shards(): pl.pallas_call(last_kernel, out_shape=jax.ShapeDtypeStruct(field.shape, f...  0.74 us
    ppermute x3, waiting for transfers between devices, swapped(): return lax.ppermute(x, axis, pairs)  0.73 us
  transfers between devices with their start and end apart: 5, of which 2 were waited for; matrix products, arithmetic and copies ran while one was open for 0% of the time, Pallas kernels for 43%

profile of v23, /device:TPU:0, one launch (start us, length us, event | category | flops | bytes accessed | tf_op | source)
XLA Modules:
  0.0 20.3 jit_solution(11861302599956778123)
XLA Ops:
  0.0 0.8 %slice.4 = bf16[3,4,2304]{2,1,0:T(4,128)(2,1)S(1)} slice(bf16[12,4,2304]{2,1,0:T(4,128)(2,1)} %bitcast.9), slice={[0:3], [0:4], [0:2304]} | slice | bytes 110592 | tf_op jit(solution)/shard_map/slice | solution.py:374
  0.8 3.0 %collective-permute-start = (bf16[3,4,2304]{2,1,0:T(4,128)(2,1)S(1)}, bf16[3,4,2304]{2,1,0:T(4,128)(2,1)S(1)}, u32[]{:S(2)}, u32[]{:S(2)}) collective-permute-start(bf16[3,4,2304]{2,1,0:T(4,128)(2,1)S(1)} %slice.4), channel_id=1, source_target_pairs={{0,1},{1,0},{2,3},{3,2},{4,5},{5,4},{6,7},{7,6},{8,9},{9,8},{10,11... | collective-permute-start | bytes 165896 | tf_op jit(solution)/shard_map/ppermute | solution.py:29
  3.8 1.9 %bias_tables.1 = (f32[2,2,2,456,128]{4,3,2,1,0:T(8,128)S(1)}, f32[2056,128]{1,0:T(8,128)S(1)}, bf16[12,4,1152]{2,1,0:T(4,128)(2,1)S(1)}, bf16[12,4,1152]{2,1,0:T...) custom-call(f32[2,6,162,2,128]{4,3,2,1,0:T(2,128)} %bitcast.8, ...), custom_call_target="tpu_custom_call" | custom-call | flops 4000000 | bytes 6000000 | tf_op jit(solution)/shard_map/bias_tables/pallas_call | solution.py:394
  5.8 0.2 collective-permute-done.south_ref
  6.0 3.6 %collective-permute-start.1 = (bf16[12,4,1152]{2,1,0:T(4,128)(2,1)S(1)}, bf16[12,4,1152]{2,1,0:T(4,128)(2,1)S(1)}, u32[]{:S(2)}, u32[]{:S(2)}) collective-permute-start(bf16[12,4,1152]{2,1,0:T(4,128)(2,1)S(1)} %pack_half.2._.refs_10_.refs_0_.refs_2_), channel_id=1, source_target_pairs={{2,4},{4,2},{6,8},{8,6},{10,12},{12,10},{14,16},{16,14},{18,20},{2... | collective-permute-start | bytes 331784 | tf_op jit(solution)/shard_map/ppermute | solution.py:38
  9.6 0.1 collective-permute-start.2
  9.7 0.5 %collective-permute-start.4 = (bf16[6,4,1152]{2,1,0:T(4,128)(2,1)S(1)}, bf16[6,4,1152]{2,1,0:T(4,128)(2,1)S(1)}, u32[]{:S(2)}, u32[]{:S(2)}) collective-permute-start(bf16[6,4,1152]{2,1,0:T(4,128)(2,1)S(1)} %get-tuple-element.35.refs_11_.refs_0_), channel_id=1, source_target_pairs={{0,2},{2,0},{4,6},{6,4},{8,10},{10,8},{12,14},{14,12},{16,18},{18,... | collective-permute-start | bytes 165896 | tf_op jit(solution)/shard_map/ppermute | solution.py:38
  10.2 0.7 %collective-permute-done.2.refs_1_ = bf16[6,4,1152]{2,1,0:T(4,128)(2,1)S(1)} collective-permute-done((bf16[6,4,1152]{2,1,0:T(4,128)(2,1)S(1)}, bf16[6,4,1152]{2,1,0:T(4,128)(2,1)S(1)}, u32[]{:S(2)}, u32[]{:S(2)}) %collective-permute-start.2) | collective-permute-done | bytes 55328 | tf_op jit(solution)/shard_map/ppermute | solution.py:38
  10.9 2.4 %swin_windows.3 = (bf16[1,6,4,1152]{3,2,1,0:T(4,128)(2,1)S(1)}, f32[2,2,2,456,128]{4,3,2,1,0:T(8,128)S(1)}, f32[4,2,288,128]{3,2,1,0:T(8,128)S(1)}, f32[4,2,184,...) custom-call(bf16[6,4,1152]{2,1,0:T(4,128)(2,1)S(1)} %get-tuple-element.33.refs_0_, ...), custom_call_target="tpu_custom_call" | custom-call | flops 200000000 | bytes 3000000 | tf_op jit(solution)/shard_map/swin_windows/pallas_call | solution.py:348
  13.3 0.0 collective-permute-done.1.refs_1_.refs_3_
  13.3 1.9 %swin_windows.4 = (bf16[1,6,4,1152]{3,2,1,0:T(4,128)(2,1)S(1)}, bf16[2,3,4,1152]{3,2,1,0:T(4,128)(2,1)S(1)}) custom-call(bf16[12,4,1152]{2,1,0:T(4,128)(2,1)S(1)} %pack_half.2._.refs_10_.refs_0_.refs_2_, bf16[12,4,1152]{2,1,0:T(4,128)(2,1)S(1)} %collective-permute-done.1.refs_1_.refs_3_, f32[1,192]{1,0:T(1,128)S(1)} %get-tuple-element.25.refs_2_.refs_4_, ...), custom_call_target="tpu_custom_call" | custom-call | flops 200000000 | bytes 3000000 | tf_op jit(solution)/shard_map/swin_windows/pallas_call | solution.py:348
  15.3 1.7 %collective-permute-start.3 = (bf16[2,3,4,1152]{3,2,1,0:T(4,128)(2,1)S(1)}, bf16[2,3,4,1152]{3,2,1,0:T(4,128)(2,1)S(1)}, u32[]{:S(2)}, u32[]{:S(2)}) collective-permute-start(bf16[2,3,4,1152]{3,2,1,0:T(4,128)(2,1)S(1)} %get-tuple-element.40), channel_id=1, source_target_pairs={{0,1},{1,0},{2,3},{3,2},{4,5},{5,4},{6,7},{7,6},{8,9},{9,8},{10,11... | collective-permute-start | bytes 165896 | tf_op jit(solution)/shard_map/ppermute | solution.py:29
  17.0 0.0 collective-permute-done.4.refs_1_
  17.0 2.6 %swin_windows.5.high_ref = bf16[2,6,4,1152]{3,2,1,0:T(4,128)(2,1)S(1)} custom-call(bf16[6,4,1152]{2,1,0:T(4,128)(2,1)S(1)} %get-tuple-element.35.refs_11_.refs_0_, bf16[6,4,1152]{2,1,0:T(4,128)(2,1)S(1)} %collective-permute-done.4.refs_1_, bf16[12,4,1152]{2,1,0:T(4,128)(2,1)S(1)} %pack_half.2._.refs_10_.refs_0_.refs_2_, ...), custom_call_target="tpu_custom_call" | custom-call | flops 400000000 | bytes 3000000 | tf_op jit(solution)/shard_map/swin_windows/pallas_call | solution.py:348
  19.5 0.0 collective-permute-done.3.top_ref
  19.5 0.7 %last_rows.1 = bf16[12,4,2304]{2,1,0:T(4,128)(2,1)} custom-call(bf16[2,3,4,1152]{3,2,1,0:T(4,128)(2,1)S(1)} %collective-permute-done.3.top_ref, bf16[2,6,4,1152]{3,2,1,0:T(4,128)(2,1)S(1)} %swin_windows.5.high_ref, bf16[1,6,4,1152]{3,2,1,0:T(4,128)(2,1)S(1)} %get-tuple-element.39.refs_12_.near_low_ref, bf16[1,6,4,1152]{3,2,1,0:T(4,128)(2,1)S(1)} %get-tuple-element.42.far_low_ref), custom_call_target="tpu_custom_call" | custom-call | bytes 400000 | tf_op jit(solution)/shard_map/last_rows/pallas_call | solution.py:432
  (2 shorter events, 0.0 us)
Async XLA Ops:
  0.8 5.1 %collective-permute-start = (bf16[3,4,2304]{2,1,0:T(4,128)(2,1)S(1)}, bf16[3,4,2304]{2,1,0:T(4,128)(2,1)S(1)}, u32[]{:S(2)}, u32[]{:S(2)}) collective-permute-start(bf16[3,4,2304]{2,1,0:T(4,128)(2,1)S(1)} %slice.4), channel_id=1, source_target_pairs={{0,1},{1,0},{2,3},{3,2},{4,5},{5,4},{6,7},{7,6},{8,9},{9,8},{10,11... | collective-permute-start | bytes 165896 | tf_op jit(solution)/shard_map/ppermute | solution.py:29
  6.0 7.3 %collective-permute-start.1 = (bf16[12,4,1152]{2,1,0:T(4,128)(2,1)S(1)}, bf16[12,4,1152]{2,1,0:T(4,128)(2,1)S(1)}, u32[]{:S(2)}, u32[]{:S(2)}) collective-permute-start(bf16[12,4,1152]{2,1,0:T(4,128)(2,1)S(1)} %pack_half.2._.refs_10_.refs_0_.refs_2_), channel_id=1, source_target_pairs={{2,4},{4,2},{6,8},{8,6},{10,12},{12,10},{14,16},{16,14},{18,20},{2... | collective-permute-start | bytes 331784 | tf_op jit(solution)/shard_map/ppermute | solution.py:38
  9.6 1.3 %collective-permute-start.2 = (bf16[6,4,1152]{2,1,0:T(4,128)(2,1)S(1)}, bf16[6,4,1152]{2,1,0:T(4,128)(2,1)S(1)}, u32[]{:S(2)}, u32[]{:S(2)}) collective-permute-start(bf16[6,4,1152]{2,1,0:T(4,128)(2,1)S(1)} %get-tuple-element.33.refs_0_), channel_id=1, source_target_pairs={{0,2},{2,0},{4,6},{6,4},{8,10},{10,8},{12,14},{14,12},{16,18},{18,... | collective-permute-start | bytes 165896 | tf_op jit(solution)/shard_map/ppermute | solution.py:38
  9.7 7.3 %collective-permute-start.4 = (bf16[6,4,1152]{2,1,0:T(4,128)(2,1)S(1)}, bf16[6,4,1152]{2,1,0:T(4,128)(2,1)S(1)}, u32[]{:S(2)}, u32[]{:S(2)}) collective-permute-start(bf16[6,4,1152]{2,1,0:T(4,128)(2,1)S(1)} %get-tuple-element.35.refs_11_.refs_0_), channel_id=1, source_target_pairs={{0,2},{2,0},{4,6},{6,4},{8,10},{10,8},{12,14},{14,12},{16,18},{18,... | collective-permute-start | bytes 165896 | tf_op jit(solution)/shard_map/ppermute | solution.py:38
  15.3 4.3 %collective-permute-start.3 = (bf16[2,3,4,1152]{3,2,1,0:T(4,128)(2,1)S(1)}, bf16[2,3,4,1152]{3,2,1,0:T(4,128)(2,1)S(1)}, u32[]{:S(2)}, u32[]{:S(2)}) collective-permute-start(bf16[2,3,4,1152]{3,2,1,0:T(4,128)(2,1)S(1)} %get-tuple-element.40), channel_id=1, source_target_pairs={{0,1},{1,0},{2,3},{3,2},{4,5},{5,4},{6,7},{7,6},{8,9},{9,8},{10,11... | collective-permute-start | bytes 165896 | tf_op jit(solution)/shard_map/ppermute | solution.py:29
